TPU v7x, 32 devices: a whole 2x2x4 slice. The times are simulated.
32 devices in a mesh: groups: 2 (over x), pts: 8 (over z, y), probe: 2 (over core).
Axes of the slice: x: 2, y: 2, z: 4, core: 2. Of those that a mesh axis runs over, the one named last changes fastest.
Arguments:
- systems: float32 [32, 12288], P('probe', ('groups', 'pts')), parts along dimension 1, may hold values from -16 to 16, as said below
- features: float32 [8, 12288], P(None, ('groups', 'pts')), parts along dimension 1, may hold values from -4 to 4
- task_ids: int32 [12288], P(('groups', 'pts')), parts along dimension 0, may hold values from 0 to 15
- pattern: int32 [48, 7], P(('groups', 'pts')), parts along dimension 0, may hold values from 0 to 1, as said below
- aggregate: int32 [12288], P(('groups', 'pts')), parts along dimension 0, may hold values from 0 to 23
- coarse_inverse: float32 [48, 24], P(('groups', 'pts')), parts along dimension 0, as said below
- task_cov: float32 [32, 16], P('groups'), parts along dimension 0, as said below
- lengthscales: float32 [16], P('groups'), parts along dimension 0, may hold values from 1.5 to 4
- noise: float32 [32], P('groups'), parts along dimension 0, may hold values from 0.3 to 1
Outputs:
- solution: float32 [32, 12288], P('probe', ('groups', 'pts')), parts along dimension 1
- grad_lengths: float32 [16], P('groups'), parts along dimension 0
- grad_tasks: float32 [32, 16], P('groups'), parts along dimension 0
There are 2 independent parts, one for each index of `groups`. A program takes and returns all parts, laid end to end along the dimension named above; each array names one. Nothing has to cross between parts.
Inputs may be any that keep to these rules, and one draw needn't show every extreme that they name: pattern[I, 3] = 1 for every block I; pattern[I, 3 + o] = pattern[I + o, 3 - o]; entries whose block I + o lies outside 0 to 23 are 0. `coarse_inverse`: symmetric and positive definite. `task_cov`: symmetric and positive definite. `systems`: row 0 holds the targets, the other rows probe vectors.
All inputs are finite; a program needn't handle non-finite values.
Results may differ from a plain program's by a relative error of at most 0.0003.
Values sent between devices are 32-bit elements; how exact they have to be, the bound alone decides.
No kernel may reach another device: no remote copies, remote signals or barrier semaphores. Data moves between devices by JAX's collectives and lax.ppermute only.
A program may use at most 128 MiB of HBM per device.

v0:
```python
import jax
import jax.numpy as jnp
from jax import lax
from jax.sharding import PartitionSpec as P

BS = 256
REACH = 3
FEAT = 8
TASKS = 16
ITERS = 3


highest = lax.Precision.HIGHEST


def extended(cells, sides, width):
    for axis, dim in sides:
        count = lax.axis_size(axis)
        ends = count - 1
        head = lax.slice_in_dim(cells, 0, width, axis=dim)
        tail = lax.slice_in_dim(cells, cells.shape[dim] - width, cells.shape[dim], axis=dim)
        cells = jnp.concatenate(
            [
                lax.ppermute(tail, axis, [(i, (i + 1) % count) for i in range(ends)]),
                cells,
                lax.ppermute(head, axis, [((i + 1) % count, i) for i in range(ends)]),
            ],
            axis=dim,
        )
    return cells


def window(padded, offset, width):
    return lax.slice_in_dim(padded, offset * BS, offset * BS + width, axis=1)


def slot_terms(left_scaled, left_table, near_scaled_all, near_table_all, task_cov, weights, offset):
    blocks = left_scaled.shape[1]
    width = blocks * BS
    right_scaled = window(near_scaled_all, offset, width).reshape(FEAT, blocks, BS)
    right_table = window(near_table_all, offset, width).reshape(TASKS, blocks, BS)
    cross = jnp.einsum("fbi,fbj->bij", left_scaled, right_scaled, precision=highest)
    left_norm = jnp.sum(left_scaled * left_scaled, axis=0)
    right_norm = jnp.sum(right_scaled * right_scaled, axis=0)
    distance = left_norm[:, :, None] + right_norm[:, None, :] - 2.0 * cross
    task_rows = jnp.einsum("tbi,ts->sbi", left_table, task_cov, precision=highest)
    pair = jnp.einsum("sbi,sbj->bij", task_rows, right_table, precision=highest)
    similar = weights[:, offset][:, None, None] * jnp.exp(-0.5 * distance)
    return (similar * pair, similar)


def shards(
    systems, features, task_ids, pattern, aggregate, coarse_inverse, task_cov, lengthscales, noise
):
    count, width = systems.shape
    blocks = width // BS
    slots = 2 * REACH + 1
    coarse_size = coarse_inverse.shape[1]
    scaled = features / lengthscales[:, None]
    task_table = (task_ids[None, :] == jnp.arange(TASKS, dtype=jnp.int32)[:, None]).astype(
        jnp.float32
    )
    joined = extended(jnp.concatenate([scaled, task_table], axis=0), (("pts", 1),), REACH * BS)
    near_scaled_all = joined[:FEAT]
    near_table_all = joined[FEAT:]
    left_scaled = scaled.reshape(FEAT, blocks, BS)
    left_table = task_table.reshape(TASKS, blocks, BS)
    column = jnp.arange(slots, dtype=jnp.int32)[None, :]
    weights = jnp.where(column == REACH, jnp.sum(pattern, axis=1)[:, None], pattern).astype(
        jnp.float32
    )
    noise_points = jnp.dot(noise, task_table, precision=highest)
    kernels = []
    similars = []
    for offset in range(slots):

        def build(offset=offset):
            return slot_terms(
                left_scaled, left_table, near_scaled_all, near_table_all, task_cov, weights, offset
            )

        kernel, similar = build()
        kernels.append(kernel)
        similars.append(similar)
    kernel_all = jnp.stack(kernels, axis=0)
    identity = jnp.eye(BS, dtype=jnp.float32)
    diagonal = kernels[REACH] + identity[None, :, :] * noise_points.reshape(blocks, 1, BS)
    factors = jnp.linalg.cholesky(diagonal)
    jacobi = jax.vmap(lambda factor: jax.scipy.linalg.cho_solve((factor, True), identity))(factors)
    spread = (aggregate[:, None] == jnp.arange(coarse_size, dtype=jnp.int32)[None, :]).astype(
        jnp.float32
    )
    contract = (((1,), (1,)), ((), ()))

    def operate(vectors):
        padded = extended(vectors, (("pts", 1),), REACH * BS)
        shifted = jnp.stack(
            [window(padded, offset, width) for offset in range(slots)], axis=0
        ).reshape(slots, count, blocks, BS)
        image = jnp.einsum("obij,orbj->rbi", kernel_all, shifted, precision=highest)
        return image.reshape(count, width) + noise_points[None, :] * vectors

    def precondition(residual):
        local = jnp.einsum(
            "bij,rbj->rbi", jacobi, residual.reshape(count, blocks, BS), precision=highest
        ).reshape(count, width)
        partial_value = jnp.dot(residual, spread, precision=highest)
        totals = lax.psum(partial_value, "pts")
        owned = lax.dot_general(totals, coarse_inverse, contract, precision=highest)
        coarse = lax.all_gather(owned, "pts", axis=1, tiled=True)
        return local + lax.dot_general(coarse, spread, contract, precision=highest)

    def fitted(residual, pre):
        return lax.psum(jnp.sum(residual * pre, axis=1), "pts")

    solution = jnp.zeros_like(systems)
    residual = systems
    pre = precondition(residual)
    direction = pre
    gamma = fitted(residual, pre)
    for step in range(ITERS):
        image = operate(direction)
        alpha = gamma / lax.psum(jnp.sum(direction * image, axis=1), "pts")
        solution = solution + alpha[:, None] * direction
        residual = residual - alpha[:, None] * image
        if step + 1 < ITERS:
            pre = precondition(residual)
            gamma_new = fitted(residual, pre)
            direction = pre + (gamma_new / gamma)[:, None] * direction
            gamma = gamma_new
    rows = lax.axis_index("probe") * count + jnp.arange(count, dtype=jnp.int32)
    total_points = lax.axis_size("pts") * width
    total_sides = lax.axis_size("probe") * count
    coef = jnp.where(rows == 0, 0.5, -0.5 / (total_sides - 1)) / total_points
    right = jnp.where((rows == 0)[:, None], solution, systems)
    right_all = extended(right, (("pts", 1),), REACH * BS)
    weighted = (solution * coef[:, None]).reshape(count, blocks, BS)
    length_grad = jnp.zeros((FEAT,), jnp.float32)
    task_grad = jnp.zeros((TASKS, TASKS), jnp.float32)
    for offset in range(slots):
        near = window(right_all, offset, width).reshape(count, blocks, BS)
        right_scaled = window(near_scaled_all, offset, width).reshape(FEAT, blocks, BS)
        right_table = window(near_table_all, offset, width).reshape(TASKS, blocks, BS)
        outer = jnp.einsum("rbi,rbj->bij", weighted, near, precision=highest)
        energy = outer * kernel_all[offset]
        held = outer * similars[offset]
        projected = jnp.einsum("bij,fbj->fbi", energy, right_scaled, precision=highest)
        length_grad = length_grad + jnp.sum(
            left_scaled * left_scaled * jnp.sum(energy, axis=2)[None], axis=(1, 2)
        )
        length_grad = length_grad + jnp.sum(
            right_scaled * right_scaled * jnp.sum(energy, axis=1)[None], axis=(1, 2)
        )
        length_grad = length_grad - 2.0 * jnp.sum(left_scaled * projected, axis=(1, 2))
        task_rows = jnp.einsum("tbi,bij->tbj", left_table, held, precision=highest)
        task_grad = task_grad + jnp.einsum("tbj,sbj->ts", task_rows, right_table, precision=highest)
    length_grad, task_grad = lax.psum((length_grad, task_grad), ("pts", "probe"))
    return (solution, length_grad, task_grad)


def solution(mesh):
    return jax.shard_map(
        shards,
        mesh=mesh,
        in_specs=(
            P("probe", ("groups", "pts")),
            P(None, ("groups", "pts")),
            P(("groups", "pts")),
            P(("groups", "pts"), None),
            P(("groups", "pts")),
            P(("groups", "pts"), None),
            P("groups", None),
            P("groups"),
            P("groups"),
        ),
        out_specs=(P("probe", ("groups", "pts")), P("groups"), P("groups", None)),
        check_vma=False,
    )
```

profile of v0, /device:TPU:0, one launch (start us, length us, event | category | flops | bytes accessed | tf_op | source)
XLA Modules:
  0.0 654.4 jit_solution(1153504129598168912)
XLA Ops:
  7.1 23.4 %psum.77 = f32[16,24]{1,0:T(8,128)S(1)} all-reduce(f32[16,24]{1,0:T(8,128)S(1)} %convolution_bitcast_fusion.25), channel_id=1, replica_groups=mesh['groups'=2,'pts'=8,'probe'=2] {'pts'}, use_global_device_ids=true, to_apply=%region_6.7 | all-reduce | flops 384 | bytes 3072 | tf_op jit(solution)/shard_map/psum | solution.py:108
  31.3 26.1 %all-gather = f32[8,3,16]{2,1,0:T(4,128)S(1)} all-gather(f32[1,3,16]{2,1,0:T(4,128)S(1)} %convolution_bitcast_fusion.28), channel_id=1, replica_groups=mesh['groups'=2,'pts'=8,'probe'=2] {'pts'}, dimensions={0}, use_global_device_ids=true | all-gather | bytes 1728 | tf_op jit(solution)/shard_map/all_gather | solution.py:110
  68.6 35.4 %custom-call.20 = f32[3,128,128]{2,1,0:T(8,128)S(1)} custom-call(f32[3,128,128]{2,1,0:T(8,128)S(1)} %cholesky.122), custom_call_target="Cholesky" | custom-call | tf_op jit(solution)/shard_map/jit(cholesky)/cholesky | solution.py:88
  104.0 30.1 %custom-call.21 = f32[3,1,128,128]{2,3,1,0:T(8,128)} custom-call(f32[3,1,128,128]{3,2,1,0:T(8,128)S(1)} %select_bitcast_fusion), custom_call_target="InvertDiagBlocksLowerTriangular" | custom-call | tf_op jit(solution)/shard_map/jit(cholesky)/cholesky | solution.py:88
  137.7 36.6 %custom-call.22 = f32[3,128,128]{2,1,0:T(8,128)} custom-call(f32[3,128,128]{2,1,0:T(8,128)} %convolution_subtract_fusion.2), custom_call_target="Cholesky" | custom-call | tf_op jit(solution)/shard_map/jit(cholesky)/cholesky | solution.py:88
  177.6 5.4 while.1
  182.9 60.2 %custom-call.23 = f32[3,2,128,128]{2,3,1,0:T(8,128)S(1)} custom-call(f32[3,2,128,128]{3,2,1,0:T(8,128)} %bitcast.458), custom_call_target="InvertDiagBlocksLowerTriangular" | custom-call | tf_op jit(solution)/shard_map/vmap(jit(_cho_solve))/triangular_solve | solution.py:89
  253.3 4.5 collective-permute-start
  260.6 4.5 collective-permute-start.2
  285.5 2.6 bitcast_dynamic-update-slice_fusion.5
  288.2 2.6 bitcast_dynamic-update-slice_fusion.4
  301.5 4.7 fusion.30
  306.9 18.7 %all-reduce.2 = (f32[16]{0:T(128)}, f32[16]{0:T(128)}) all-reduce(f32[16]{0:T(128)} %get-tuple-element.26, f32[16]{0:T(128)} %get-tuple-element.25), channel_id=1, replica_groups=mesh['groups'=2,'pts'=8,'probe'=2] {'pts'}, use_global_device_ids=true, to_apply=%region_8.9 | all-reduce | flops 32 | bytes 256 | tf_op jit(solution)/shard_map/psum | solution.py:114
  329.9 19.2 %psum.80 = f32[16,24]{1,0:T(8,128)} all-reduce(f32[16,24]{1,0:T(8,128)} %fusion.73), channel_id=1, replica_groups=mesh['groups'=2,'pts'=8,'probe'=2] {'pts'}, use_global_device_ids=true, to_apply=%region_17.18 | all-reduce | flops 384 | bytes 3072 | tf_op jit(solution)/shard_map/psum | solution.py:108
  349.9 26.6 %all-gather.1 = f32[8,3,16]{2,1,0:T(4,128)} all-gather(f32[1,3,16]{2,1,0:T(4,128)S(1)} %convolution_bitcast_fusion.27), channel_id=1, replica_groups=mesh['groups'=2,'pts'=8,'probe'=2] {'pts'}, dimensions={0}, use_global_device_ids=true | all-gather | bytes 1728 | tf_op jit(solution)/shard_map/all_gather | solution.py:110
  379.6 2.5 multiply_reduce_fusion.3
  382.1 17.7 %psum.81 = f32[16]{0:T(128)} all-reduce(f32[16]{0:T(128)} %get-tuple-element.132), channel_id=1, replica_groups=mesh['groups'=2,'pts'=8,'probe'=2] {'pts'}, use_global_device_ids=true, to_apply=%region_19.20 | all-reduce | flops 16 | bytes 128 | tf_op jit(solution)/shard_map/psum | solution.py:114
  403.3 5.2 collective-permute-start.4
  430.5 7.2 %fusion.33 = f32[3,2,8,256]{3,2,1,0:T(8,128)S(1)} fusion(f32[7,16,3,256]{3,1,0,2:T(8,128)} %constant_dynamic-update-slice_fusion.8, f32[7,3,256,256]{3,2,1,0:T(8,128)} %copy-done.1), kind=kOutput, calls=%fused_computation.49 | convolution fusion | flops 264241152 | bytes 5898240 | tf_op jit(solution)/shard_map/obij,orbj->rbi/dot_general | solution.py:100
  439.7 20.6 %psum.82 = f32[16]{0:T(128)} all-reduce(f32[16]{0:T(128)} %multiply_reduce_fusion.2), channel_id=1, replica_groups=mesh['groups'=2,'pts'=8,'probe'=2] {'pts'}, use_global_device_ids=true, to_apply=%region_21.22 | all-reduce | flops 16 | bytes 128 | tf_op jit(solution)/shard_map/psum | solution.py:123
  465.4 18.0 %psum.83 = f32[16,24]{1,0:T(8,128)S(1)} all-reduce(f32[16,24]{1,0:T(8,128)} %fusion.72), channel_id=1, replica_groups=mesh['groups'=2,'pts'=8,'probe'=2] {'pts'}, use_global_device_ids=true, to_apply=%region_22.23 | all-reduce | flops 384 | bytes 3072 | tf_op jit(solution)/shard_map/psum | solution.py:108
  484.3 26.0 %all-gather.2 = f32[8,3,16]{2,1,0:T(4,128)S(1)} all-gather(f32[1,3,16]{2,1,0:T(4,128)S(1)} %convolution_bitcast_fusion.26), channel_id=1, replica_groups=mesh['groups'=2,'pts'=8,'probe'=2] {'pts'}, dimensions={0}, use_global_device_ids=true | all-gather | bytes 1728 | tf_op jit(solution)/shard_map/all_gather | solution.py:110
  511.6 17.1 %psum.84 = f32[16]{0:T(128)S(1)} all-reduce(f32[16]{0:T(128)S(1)} %get-tuple-element.134), channel_id=1, replica_groups=mesh['groups'=2,'pts'=8,'probe'=2] {'pts'}, use_global_device_ids=true, to_apply=%region_24.25 | all-reduce | flops 16 | bytes 128 | tf_op jit(solution)/shard_map/psum | solution.py:114
  531.6 4.5 collective-permute-start.6
  551.5 7.2 %fusion.36 = f32[3,2,8,256]{3,2,1,0:T(8,128)S(1)} fusion(f32[7,16,3,256]{3,1,0,2:T(8,128)} %constant_dynamic-update-slice_fusion.15, f32[7,3,256,256]{3,2,1,0:T(8,128)} %copy-done.1), kind=kOutput, calls=%fused_computation.50 | convolution fusion | flops 264241152 | bytes 5898240 | tf_op jit(solution)/shard_map/obij,orbj->rbi/dot_general | solution.py:100
  558.8 20.2 %psum.85 = f32[16]{0:T(128)S(1)} all-reduce(f32[16]{0:T(128)S(1)} %multiply_reduce_fusion), channel_id=1, replica_groups=mesh['groups'=2,'pts'=8,'probe'=2] {'pts'}, use_global_device_ids=true, to_apply=%region_26.27 | all-reduce | flops 16 | bytes 128 | tf_op jit(solution)/shard_map/psum | solution.py:123
  581.9 4.8 collective-permute-start.8
  592.1 2.7 multiply_reduce_fusion.32
  594.8 2.6 fusion.50
  599.0 2.7 multiply_reduce_fusion.28
  601.7 2.6 fusion.52
  623.1 31.0 %all-reduce.1 = (f32[8]{0:T(128)}, f32[16,16]{1,0:T(8,128)}) all-reduce(f32[8]{0:T(128)S(1)} %multiply_subtract_fusion.2, f32[16,16]{1,0:T(8,128)S(1)} %fusion.58), channel_id=1, replica_groups=mesh['groups'=2,'pts'=8,'probe'=2] {'pts','probe'}, use_global_device_ids=true, to_apply=%region_62.63 | all-reduce | flops 264 | bytes 2112 | tf_op jit(solution)/shard_map/psum | solution.py:157
  (420 shorter events, 163.9 us)
Async XLA Ops:
  0.6 61.1 %copy-start = (f32[16,16]{1,0:T(8,128)S(1)}, f32[16,16]{1,0:T(8,128)}, u32[]{:S(2)}) copy-start(f32[16,16]{1,0:T(8,128)} %param.15) | copy-start | bytes 3076
  31.3 34.6 %copy-start.84 = (f32[3]{0:T(128)S(1)}, f32[3]{0:T(128)}, u32[]{:S(2)}) copy-start(f32[3]{0:T(128)} %get-tuple-element.43) | copy-start | bytes 40
  64.8 112.7 %copy-start.101 = (s32[2]{0:T(128)S(1)}, s32[2]{0:T(128)}, u32[]{:S(2)}) copy-start(s32[2]{0:T(128)} %iota_multiply_fusion) | copy-start | bytes 28
  243.2 14.7 %copy-start.80 = (s32[768]{0:T(1024)S(1)}, s32[768]{0:T(1024)}, u32[]{:S(2)}) copy-start(s32[768]{0:T(1024)} %param.11) | copy-start | bytes 9220
  252.0 27.9 %copy-start.24 = (f32[16,768]{1,0:T(8,128)}, f32[16,768]{1,0:T(8,128)S(1)}, u32[]{:S(2)}) copy-start(f32[16,768]{1,0:T(8,128)S(1)} %convolution_add_fusion.2) | copy-start | bytes 147460
  252.0 14.4 %collective-permute-start.1 = (f32[16,768]{1,0:T(8,128)S(1)}, f32[16,768]{1,0:T(8,128)S(1)}, u32[]{:S(2)}, u32[]{:S(2)}) collective-permute-start(f32[16,768]{1,0:T(8,128)S(1)} %convolution_add_fusion.2), channel_id=1, source_target_pairs={{2,0},{4,2},{6,4},{8,6},{10,8},{12,10},{14,12},{3,1},{5,3},{7,5},{... | collective-permute-start | bytes 147464 | tf_op jit(solution)/shard_map/ppermute | solution.py:26
  253.3 13.1 %collective-permute-start = (f32[16,768]{1,0:T(8,128)S(1)}, f32[16,768]{1,0:T(8,128)S(1)}, u32[]{:S(2)}, u32[]{:S(2)}) collective-permute-start(f32[16,768]{1,0:T(8,128)S(1)} %convolution_add_fusion.2), channel_id=1, source_target_pairs={{0,2},{2,4},{4,6},{6,8},{8,10},{10,12},{12,14},{1,3},{3,5},{5,7},{... | collective-permute-start | bytes 147464 | tf_op jit(solution)/shard_map/ppermute | solution.py:24
  259.3 13.2 %collective-permute-start.3 = (f32[24,768]{1,0:T(8,128)}, f32[24,768]{1,0:T(8,128)S(1)}, u32[]{:S(2)}, u32[]{:S(2)}) collective-permute-start(f32[24,768]{1,0:T(8,128)} %pad_maximum_fusion.5), channel_id=1, source_target_pairs={{2,0},{4,2},{6,4},{8,6},{10,8},{12,10},{14,12},{3,1},{5,3},{7,5},{... | collective-permute-start | bytes 221192 | tf_op jit(solution)/shard_map/ppermute | solution.py:26
  260.6 12.0 %collective-permute-start.2 = (f32[24,768]{1,0:T(8,128)}, f32[24,768]{1,0:T(8,128)S(1)}, u32[]{:S(2)}, u32[]{:S(2)}) collective-permute-start(f32[24,768]{1,0:T(8,128)} %pad_maximum_fusion.5), channel_id=1, source_target_pairs={{0,2},{2,4},{4,6},{6,8},{8,10},{10,12},{12,14},{1,3},{3,5},{5,7},{... | collective-permute-start | bytes 221192 | tf_op jit(solution)/shard_map/ppermute | solution.py:24
  278.0 15.8 %copy-start.41 = (f32[16,768]{1,0:T(8,128)}, f32[16,768]{1,0:T(8,128)S(1)}, u32[]{:S(2)}) copy-start(f32[16,768]{1,0:T(8,128)S(1)} %slice.286) | copy-start | bytes 147460
  278.0 12.7 %copy-start.39 = (f32[16,768]{1,0:T(8,128)}, f32[16,768]{1,0:T(8,128)S(1)}, u32[]{:S(2)}) copy-start(f32[16,768]{1,0:T(8,128)S(1)} %slice.285) | copy-start | bytes 147460
  278.0 12.7 %copy-start.9 = (f32[1,3,256,256]{3,2,1,0:T(8,128)S(1)}, f32[1,3,256,256]{3,2,1,0:T(8,128)}, u32[]{:S(2)}) copy-start(f32[1,3,256,256]{3,2,1,0:T(8,128)} %copy.268) | copy-start | bytes 2359300
  279.9 15.7 %copy-start.45 = (f32[16,768]{1,0:T(8,128)}, f32[16,768]{1,0:T(8,128)S(1)}, u32[]{:S(2)}) copy-start(f32[16,768]{1,0:T(8,128)S(1)} %get-tuple-element.96) | copy-start | bytes 147460
  279.9 17.4 %copy-start.49 = (f32[16,768]{1,0:T(8,128)}, f32[16,768]{1,0:T(8,128)S(1)}, u32[]{:S(2)}) copy-start(f32[16,768]{1,0:T(8,128)S(1)} %get-tuple-element.95) | copy-start | bytes 147460
  402.1 7.9 %collective-permute-start.5 = (f32[16,768]{1,0:T(8,128)}, f32[16,768]{1,0:T(8,128)}, u32[]{:S(2)}, u32[]{:S(2)}) collective-permute-start(f32[16,768]{1,0:T(8,128)} %multiply_add_fusion.4), channel_id=1, source_target_pairs={{2,0},{4,2},{6,4},{8,6},{10,8},{12,10},{14,12},{3,1},{5,3},{7,5},{... | collective-permute-start | bytes 147464 | tf_op jit(solution)/shard_map/ppermute | solution.py:26
  403.3 6.6 %collective-permute-start.4 = (f32[16,768]{1,0:T(8,128)}, f32[16,768]{1,0:T(8,128)}, u32[]{:S(2)}, u32[]{:S(2)}) collective-permute-start(f32[16,768]{1,0:T(8,128)} %multiply_add_fusion.4), channel_id=1, source_target_pairs={{0,2},{2,4},{4,6},{6,8},{8,10},{10,12},{12,14},{1,3},{3,5},{5,7},{... | collective-permute-start | bytes 147464 | tf_op jit(solution)/shard_map/ppermute | solution.py:24
  465.3 113.8 %copy-start.26 = (f32[16,768]{1,0:T(8,128)S(1)}, f32[16,768]{1,0:T(8,128)}, u32[]{:S(2)}) copy-start(f32[16,768]{1,0:T(8,128)} %copy-done.24) | copy-start | bytes 147460
  465.3 113.7 %copy-start.90 = (f32[16]{0:T(128)S(1)}, f32[16]{0:T(128)}, u32[]{:S(2)}) copy-start(f32[16]{0:T(128)} %copy-done.89) | copy-start | bytes 196
  465.4 113.7 %copy-start.92 = (f32[16]{0:T(128)S(1)}, f32[16]{0:T(128)}, u32[]{:S(2)}) copy-start(f32[16]{0:T(128)} %copy-done.91) | copy-start | bytes 196
  465.4 114.6 %copy-start.32 = (f32[16,768]{1,0:T(8,128)S(1)}, f32[16,768]{1,0:T(8,128)}, u32[]{:S(2)}) copy-start(f32[16,768]{1,0:T(8,128)} %param.9) | copy-start | bytes 147460
  530.3 6.0 collective-permute-start.7
  531.6 6.3 collective-permute-start.6
  548.8 40.1 %copy-start.8 = (f32[8,768]{1,0:T(8,128)S(1)}, f32[8,768]{1,0:T(8,128)}, u32[]{:S(2)}) copy-start(f32[8,768]{1,0:T(8,128)} %copy-done.6) | copy-start | bytes 73732
  558.7 36.1 %copy-start.57 = (f32[8,768]{1,0:T(8,128)S(1)}, f32[8,768]{1,0:T(8,128)}, u32[]{:S(2)}) copy-start(f32[8,768]{1,0:T(8,128)} %get-tuple-element.76) | copy-start | bytes 73732
  580.6 11.4 %collective-permute-start.9 = (f32[16,768]{1,0:T(8,128)S(1)}, f32[16,768]{1,0:T(8,128)S(1)}, u32[]{:S(2)}, u32[]{:S(2)}) collective-permute-start(f32[16,768]{1,0:T(8,128)S(1)} %broadcast_select_fusion), channel_id=1, source_target_pairs={{2,0},{4,2},{6,4},{8,6},{10,8},{12,10},{14,12},{3,1},{5,3},{7,5},{... | collective-permute-start | bytes 147464 | tf_op jit(solution)/shard_map/ppermute | solution.py:26
  581.9 10.2 %collective-permute-start.8 = (f32[16,768]{1,0:T(8,128)S(1)}, f32[16,768]{1,0:T(8,128)S(1)}, u32[]{:S(2)}, u32[]{:S(2)}) collective-permute-start(f32[16,768]{1,0:T(8,128)S(1)} %broadcast_select_fusion), channel_id=1, source_target_pairs={{0,2},{2,4},{4,6},{6,8},{8,10},{10,12},{12,14},{1,3},{3,5},{5,7},{... | collective-permute-start | bytes 147464 | tf_op jit(solution)/shard_map/ppermute | solution.py:24
  587.6 14.1 %copy-start.70 = (f32[8,768]{1,0:T(8,128)S(1)}, f32[8,768]{1,0:T(8,128)}, u32[]{:S(2)}) copy-start(f32[8,768]{1,0:T(8,128)} %get-tuple-element.106) | copy-start | bytes 73732
  590.1 16.4 %copy-start.4 = (f32[3,256,256]{2,1,0:T(8,128)S(1)}, f32[3,256,256]{2,1,0:T(8,128)}, u32[]{:S(2)}) copy-start(f32[3,256,256]{2,1,0:T(8,128)} %get-tuple-element.125) | copy-start | bytes 2359300
  592.1 15.9 %copy-start.55 = (f32[8,768]{1,0:T(8,128)S(1)}, f32[8,768]{1,0:T(8,128)}, u32[]{:S(2)}) copy-start(f32[8,768]{1,0:T(8,128)} %get-tuple-element.103) | copy-start | bytes 73732
  594.8 14.7 %copy-start.18 = (f32[3,256,256]{2,1,0:T(8,128)S(1)}, f32[3,256,256]{2,1,0:T(8,128)}, u32[]{:S(2)}) copy-start(f32[3,256,256]{2,1,0:T(8,128)} %copy-done.17) | copy-start | bytes 2359300
  597.3 13.2 %copy-start.2 = (f32[3,256,256]{2,1,0:T(8,128)S(1)}, f32[3,256,256]{2,1,0:T(8,128)}, u32[]{:S(2)}) copy-start(f32[3,256,256]{2,1,0:T(8,128)} %get-tuple-element.123) | copy-start | bytes 2359300
  599.0 13.1 %copy-start.54 = (f32[8,768]{1,0:T(8,128)S(1)}, f32[8,768]{1,0:T(8,128)}, u32[]{:S(2)}) copy-start(f32[8,768]{1,0:T(8,128)} %get-tuple-element.101) | copy-start | bytes 73732
  (80 other events, 523.1 us)
where the time goes:
time: 662 us; the launch traced here: 654 us
  blocking collectives  265 us (40%)
  other arithmetic  189 us (29%)
  matrix products  101 us (15%)
  local copies, waits for them, and re-layouts  65.2 us (10%)
  starting transfers between devices  30 us (5%)
    another operation x9, other arithmetic, shards(): factors = jnp.linalg.cholesky(diagonal)  103 us
    all_gather x3, blocking collectives, precondition(): coarse = lax.all_gather(owned, 'pts', axis=1, tiled=True)  78.7 us
    another operation x4, other arithmetic, shards(): jax.scipy.linalg.cho_solve((factor, True), identity)  62 us
    psum x3, blocking collectives, precondition(): totals = lax.psum(partial_value, 'pts')  60.6 us
    psum x3, blocking collectives, fitted(): return lax.psum(jnp.sum(residual * pre, axis=1), 'pts')  53.6 us
    psum x2, blocking collectives, shards(): alpha = gamma / lax.psum(jnp.sum(direction * image, axis=1), 'pts')  40.9 us
    psum x1, blocking collectives, shards(): lax.psum((length_grad, task_grad), ('pts', 'probe'))  31 us
    unnamed x226, local copies, waits for them, and re-layouts  28.3 us
  transfers between devices with their start and end apart: 10, of which 2 were waited for; matrix products, arithmetic and copies ran while one was open for 2% of the time, Pallas kernels for 0%

commit v1 on v0

v1 whole, which is shorter than its diff:
```python
import functools

import jax
import jax.numpy as jnp
from jax import lax
from jax.experimental import pallas as pl
from jax.experimental.pallas import tpu as pltpu
from jax.sharding import PartitionSpec as P

BS = 256
REACH = 3
FEAT = 8
TASKS = 16
ITERS = 3
SLOTS = 2 * REACH + 1
BAND = SLOTS * BS
BASE = 32
GROUP = 4
LANES = 128

highest = lax.Precision.HIGHEST
f32 = jnp.float32
bf16 = jnp.bfloat16
NN = (((1,), (0,)), ((), ()))
NT = (((1,), (1,)), ((), ()))
TN = (((0,), (0,)), ((), ()))


def dot(a, b, dims=NN, precision=None):
    return lax.dot_general(a, b, dims, precision=precision, preferred_element_type=f32)


def iota(shape, dim):
    return lax.broadcasted_iota(jnp.int32, shape, dim)


def split(x, parts):
    out = []
    for _ in range(parts - 1):
        head = x.astype(bf16).astype(f32)
        out.append(head)
        x = x - head
    out.append(x.astype(bf16).astype(f32))
    return out


def column(ref, size):
    rows = iota((size, 1), 0)
    out = jnp.zeros((size, 1), f32)
    for i in range(size):
        out = jnp.where(rows == i, ref[i], out)
    return out


def one_hot(ids, size):
    return (iota((size, ids.shape[1]), 0).astype(f32) == ids).astype(f32)


def noise_row(noise_ref, ids):
    out = jnp.zeros(ids.shape, f32)
    for t in range(TASKS):
        out = jnp.where(ids == float(t), noise_ref[t], out)
    return out


def weight(pat_ref, block, offset):
    if offset != REACH:
        return pat_ref[block, offset].astype(f32)
    total = pat_ref[block, 0]
    for o in range(1, SLOTS):
        total = total + pat_ref[block, o]
    return total.astype(f32)


def near_stack(scaled, table):
    s0, s1, s2 = split(scaled, 3)
    n0, n1, n2 = split(-0.5 * jnp.sum(scaled * scaled, axis=0, keepdims=True), 3)
    rows = iota(scaled.shape, 0)
    norms = jnp.where(rows == 0, n0, jnp.where(rows == 1, n1, jnp.where(rows == 2, n2, 0.0)))
    pad = jnp.zeros((LANES - 7 * FEAT - 3 * TASKS, scaled.shape[1]), f32)
    return jnp.concatenate(
        [s0, s0, s1, s1, s0, s2, norms, table, table, table, pad], axis=0
    ).astype(bf16)


def own_stack(scaled, table, cov):
    s0, s1, s2 = split(scaled, 3)
    rows = iota(scaled.shape, 0)
    ones = jnp.where(rows < 3, 1.0, 0.0)
    count = scaled.shape[1]
    c0, c1, c2 = split(cov, 3)
    picked = dot(
        jnp.concatenate([c0, c1, c2], axis=0).astype(bf16), table.astype(bf16)
    )
    tail = LANES - 7 * FEAT - 3 * TASKS
    left = jnp.concatenate(
        [s0, s1, s0, s1, s2, s0, ones, jnp.zeros((3 * TASKS + tail, count), f32)], axis=0
    ).astype(bf16)
    right = jnp.concatenate(
        [jnp.zeros((7 * FEAT, count), f32), picked, jnp.zeros((tail, count), f32)], axis=0
    ).astype(bf16)
    return left, right, -0.5 * jnp.sum(scaled * scaled, axis=0, keepdims=True)


def small_inverse(p):
    n = len(p)
    if n == 1:
        return [[1.0 / p[0][0]]]
    if n == 2:
        a, b, d = p[0][0], p[0][1], p[1][1]
        r = 1.0 / (a * d - b * b)
        off = -b * r
        return [[d * r, off], [off, a * r]]
    h = n // 2
    ainv = small_inverse([row[:h] for row in p[:h]])
    b = [row[h:] for row in p[:h]]
    t = [[sum(ainv[i][k] * b[k][j] for k in range(h)) for j in range(h)] for i in range(h)]
    s = [[None] * h for _ in range(h)]
    for i in range(h):
        for j in range(i, h):
            s[i][j] = s[j][i] = p[h + i][h + j] - sum(b[k][i] * t[k][j] for k in range(h))
    sinv = small_inverse(s)
    u = [[sum(t[i][k] * sinv[k][j] for k in range(h)) for j in range(h)] for i in range(h)]
    out = [[None] * n for _ in range(n)]
    for i in range(h):
        for j in range(h):
            out[h + i][h + j] = sinv[i][j]
            out[i][h + j] = out[h + j][i] = -u[i][j]
    for i in range(h):
        for j in range(i, h):
            out[i][j] = out[j][i] = ainv[i][j] + sum(u[i][k] * t[j][k] for k in range(h))
    return out


def sweep_base(cells):
    lane = iota((BASE, LANES), 1)
    start = lane - lane % BASE
    inner = iota((1, LANES), 1) % BASE
    sub = iota((BASE, 1), 0)
    for g in range(BASE // GROUP):
        first = g * GROUP
        cols = [
            jnp.take_along_axis(cells, start + (first + t), axis=1, mode="promise_in_bounds")
            for t in range(GROUP)
        ]
        rows = [cells[first + t : first + t + 1, :] for t in range(GROUP)]
        pivots = [[cols[u][first + t : first + t + 1, :] for u in range(GROUP)] for t in range(GROUP)]
        inv = small_inverse(pivots)
        rows = [jnp.where(inner == first + t, -1.0, rows[t]) for t in range(GROUP)]
        group = (inner >= first) & (inner < first + GROUP)
        for t in range(GROUP):
            rows[t] = jnp.where(group & (inner != first + t), 0.0, rows[t])
        new = [sum(inv[t][u] * rows[u] for u in range(GROUP)) for t in range(GROUP)]
        cells = jnp.where(group, 0.0, cells)
        for t in range(GROUP):
            cells = cells - cols[t] * new[t]
        for t in range(GROUP):
            cells = jnp.where(sub == first + t, new[t], cells)
    return cells


def invert_kernel(pat_ref, len_ref, noise_ref, pack_ref, cov_ref, jac_ref, pre_ref, work):
    blocks = work.shape[0]
    scaled = pack_ref[0:FEAT, :] / column(len_ref, FEAT)
    ids = pack_ref[FEAT : FEAT + 1, :]
    table = one_hot(ids, TASKS)
    noise = noise_row(noise_ref, ids)
    cov = cov_ref[...]
    near = near_stack(scaled, table)
    left, right, norm = own_stack(scaled, table, cov)
    eye = iota((BS, BS), 0) == iota((BS, BS), 1)
    for m in range(blocks):
        at = slice(m * BS, (m + 1) * BS)
        exponent = dot(near[:, at], left[:, at], TN) + norm[:, at]
        pair = dot(near[:, at], right[:, at], TN)
        block = weight(pat_ref, m, REACH) * jnp.exp(exponent) * pair
        work[m] = block + jnp.where(eye, noise[:, at], 0.0)
    seg = iota((BASE, LANES), 1) // BASE
    wide = iota((BASE, BS), 1)
    deep = iota((BASE, BS), 0)
    for k in range(BS // BASE):
        first = k * BASE
        tile, inside = first // LANES, first % LANES
        strips = [work[m, first : first + BASE, :] for m in range(blocks)]
        cells = jnp.where(iota((BASE, LANES), 1) % BASE == iota((BASE, LANES), 0), 1.0, 0.0)
        for m in range(blocks):
            piece = strips[m][:, tile * LANES : (tile + 1) * LANES]
            shift = (BASE * m - inside) % LANES
            if shift:
                piece = pltpu.roll(piece, shift, axis=1)
            cells = jnp.where(seg == m, piece, cells)
        inv = -sweep_base(cells)
        held = (wide >= first) & (wide < first + BASE)
        minus = jnp.where(wide - first == deep, -1.0, 0.0)
        stack = jnp.concatenate(
            [jnp.where(held, minus, s) for s in strips]
            + [jnp.zeros((LANES - blocks * BASE, BS), f32)],
            axis=0,
        )
        spread = jnp.concatenate([jnp.where(seg == m, inv, 0.0) for m in range(blocks)], axis=0)
        new = dot(spread, stack, precision=highest)
        gone = (iota((1, BS), 1) >= first) & (iota((1, BS), 1) < first + BASE)
        for m in range(blocks):
            row = new[m * BASE : (m + 1) * BASE, :]
            r0, r1, r2 = split(strips[m], 3)
            p0, p1, p2 = split(row, 3)
            a = jnp.concatenate([r0, r0, r1, r1, r0, r2], axis=0).astype(bf16)
            b = jnp.concatenate([p0, p1, p0, p1, p2, p0], axis=0).astype(bf16)
            work[m] = jnp.where(gone, 0.0, work[m]) - dot(a, b, TN)
            work[m, first : first + BASE, :] = row
    base = FEAT + 8
    for m in range(blocks):
        at = slice(m * BS, (m + 1) * BS)
        inv = -work[m]
        jac_ref[m] = inv
        pre_ref[:, at] = dot(pack_ref[base:, at], inv, precision=highest)


def build_kernel(
    pat_ref, len_ref, own_ref, left_ref, right_ref, cov_ref, hi_ref, lo_ref, sim_ref
):
    blocks = hi_ref.shape[0]
    lens = column(len_ref, FEAT)
    pack = jnp.concatenate(
        [left_ref[0 : FEAT + 8, :], own_ref[0 : FEAT + 8, :], right_ref[0 : FEAT + 8, :]], axis=1
    )
    scaled = pack[0:FEAT] / lens
    table = one_hot(pack[FEAT : FEAT + 1], TASKS)
    near = near_stack(scaled, table)
    width = blocks * BS
    own = slice(width, 2 * width)
    left, right, norm = own_stack(scaled[:, own], table[:, own], cov_ref[...])
    edge = width - REACH * BS
    for m in range(blocks):
        at = slice(m * BS, (m + 1) * BS)
        for o in range(SLOTS):
            j = edge + (m + o) * BS
            part = near[:, j : j + BS]
            exponent = dot(part, left[:, at], TN) + norm[:, at]
            pair = dot(part, right[:, at], TN)
            similar = weight(pat_ref, m, o) * jnp.exp(exponent)
            kernel = similar * pair
            head = kernel.astype(bf16)
            rows = slice(o * BS, (o + 1) * BS)
            sim_ref[m, rows, :] = similar
            hi_ref[m, rows, :] = head
            lo_ref[m, rows, :] = (kernel - head.astype(f32)).astype(bf16)


def operate(vectors, noise, own, hi_ref, lo_ref):
    rows = vectors.shape[0]
    head, tail = (part.astype(bf16) for part in split(vectors, 2))
    both = jnp.concatenate([head, tail], axis=0)
    out = []
    for m in range(hi_ref.shape[0]):
        at = slice(m * BS, m * BS + BAND)
        first = dot(both[:, at], hi_ref[m])
        out.append(first[:rows] + first[rows:] + dot(head[:, at], lo_ref[m]))
    return jnp.concatenate(out, axis=1) + noise * own


def smooth(image, jac_ref):
    return jnp.concatenate(
        [
            dot(image[:, m * BS : (m + 1) * BS], jac_ref[m], precision=highest)
            for m in range(jac_ref.shape[0])
        ],
        axis=1,
    )


def first_kernel(
    noise_ref, own_ref, left_ref, right_ref, pre_ref, prel_ref, prer_ref, hi_ref, lo_ref, jac_ref,
    image_ref, next_ref,
):
    count, width = pre_ref.shape
    coarse = image_ref.shape[0] - count
    pre = jnp.concatenate([prel_ref[...], pre_ref[...], prer_ref[...]], axis=1)
    row = slice(FEAT + 1, FEAT + 2)
    which = jnp.concatenate([left_ref[row, :], own_ref[row, :], right_ref[row, :]], axis=1)
    ext = jnp.concatenate([pre, one_hot(which, coarse)], axis=0)
    edge = width - REACH * BS
    noise = noise_row(noise_ref, own_ref[FEAT : FEAT + 1, :])
    image = operate(
        ext[:, edge : 3 * width - edge], noise, ext[:, width : 2 * width], hi_ref, lo_ref
    )
    image_ref[...] = image
    next_ref[...] = smooth(image, jac_ref)


def second_kernel(
    noise_ref, own_ref, vec_ref, vecl_ref, vecr_ref, hi_ref, lo_ref, jac_ref, image_ref, next_ref
):
    width = vec_ref.shape[1]
    edge = width - REACH * BS
    ext = jnp.concatenate([vecl_ref[:, edge:], vec_ref[...], vecr_ref[:, : width - edge]], axis=1)
    noise = noise_row(noise_ref, own_ref[FEAT : FEAT + 1, :])
    image = operate(ext, noise, vec_ref[...], hi_ref, lo_ref)
    image_ref[...] = image
    next_ref[...] = smooth(image, jac_ref)


def moment_kernel(
    noise_ref, own_ref, vec_ref, vecl_ref, vecr_ref, hi_ref, lo_ref, pre_ref, d1_ref, v0_ref,
    v1_ref, coarse_ref, out_ref,
):
    count, width = pre_ref.shape
    rows = vec_ref.shape[0]
    coarse = rows - count
    lanes = out_ref.shape[1]
    pitch = pitch_of(coarse)
    edge = width - REACH * BS
    ext = jnp.concatenate([vecl_ref[:, edge:], vec_ref[...], vecr_ref[:, : width - edge]], axis=1)
    noise = noise_row(noise_ref, own_ref[FEAT : FEAT + 1, :])
    d2 = vec_ref[...]
    v2 = operate(ext, noise, d2, hi_ref, lo_ref)
    base = FEAT + 8
    systems = own_ref[base:, :]
    pre = pre_ref[...]
    z = one_hot(own_ref[FEAT + 1 : FEAT + 2, :], coarse)
    d1, v0, v1 = d1_ref[...], v0_ref[...], v1_ref[...]
    gap = jnp.zeros((pitch - coarse, width), f32)

    def stacked(parts):
        cells = []
        for k in range(lanes // pitch):
            if k in parts:
                cells.append(jnp.concatenate([parts[k], gap], axis=0))
            else:
                cells.append(jnp.zeros((pitch, width), f32))
        return jnp.concatenate(cells, axis=0)

    high = lax.Precision.HIGH
    residual = jnp.concatenate([systems, jnp.zeros((coarse, width), f32)], axis=0)
    total = dot(v0, stacked({0: z, 1: d1[count:]}), NT, high)
    total = total + dot(v1, stacked({2: d1[count:], 3: d2[count:]}), NT, high)
    total = total + dot(v2, stacked({4: d2[count:]}), NT, high)
    total = total + dot(residual, stacked({5: z}), NT, high)
    own = [
        pre * v0[:count],
        d1[:count] * v0[:count],
        d1[:count] * v1[:count],
        d2[:count] * v1[:count],
        d2[:count] * v2[:count],
        systems * pre,
    ]
    lane = iota((count, lanes), 1)
    top = total[:count]
    for k, value in enumerate(own):
        top = jnp.where(lane == k * pitch + coarse, jnp.sum(value, axis=1, keepdims=True), top)
    out_ref[...] = jnp.concatenate([top, total[count:]], axis=0) + coarse_ref[...]


def pitch_of(coarse):
    return BASE if coarse < BASE else -(-(coarse + 1) // LANES) * LANES


def lanes_of(coarse):
    return -(-7 * pitch_of(coarse) // LANES) * LANES


def final_kernel(
    scalar_ref, len_ref, gram_ref, own_ref, left_ref, right_ref, pre_ref, prel_ref, prer_ref,
    d1_ref, d1l_ref, d1r_ref, d2_ref, d2l_ref, d2r_ref, hi_ref, lo_ref, sim_ref, coef_ref, cov_ref,
    sol_ref, grad_ref,
):
    count, width = pre_ref.shape
    rows = d1_ref.shape[0]
    coarse = rows - count
    pitch = pitch_of(coarse)
    wide = -(-3 * pitch // LANES) * LANES
    blocks = width // BS
    edge = width - REACH * BS
    gram = gram_ref[...]
    lane = iota((1, wide), 1)
    slot, inside = lane // pitch, lane % pitch
    live = lane < 3 * pitch
    is_vec = live & (inside < coarse)
    is_one = live & (inside == coarse)

    def shifted(j):
        return jnp.where(live, gram[:, j * pitch : j * pitch + wide], 0.0)

    moved = [shifted(j) for j in range(3)]
    own = [m[:count] for m in moved]
    gap = jnp.zeros((pitch - coarse, wide), f32)
    hankel = jnp.concatenate(
        [
            jnp.concatenate([jnp.where(is_vec, m[count:], 0.0), gap], axis=0)
            for m in moved
        ]
        + ([jnp.zeros((wide - 3 * pitch, wide), f32)] if wide > 3 * pitch else []),
        axis=0,
    )
    block0 = lane < pitch
    inverse = gram[:coarse, 6 * pitch : 7 * pitch]
    if pitch < wide:
        inverse = jnp.concatenate([inverse, jnp.zeros((coarse, wide - pitch), f32)], axis=1)
    inverse = jnp.where(lane < coarse, inverse, 0.0)
    inverse = jnp.concatenate([inverse, jnp.zeros((wide - coarse, wide), f32)], axis=0)
    start = gram[:count, 5 * pitch : 6 * pitch]
    if pitch < wide:
        start = jnp.concatenate([start, jnp.zeros((count, wide - pitch), f32)], axis=1)
    against = jnp.where(
        block0, start, jnp.where(live, pltpu.roll(jnp.where(live, own[0], 0.0), pitch, axis=1), 0.0)
    )

    def total(x):
        return jnp.sum(x, axis=1, keepdims=True)

    def scalars(u, i):
        return total(jnp.where(lane == i * pitch + coarse, u, 0.0))

    def metric(u):
        out = dot(jnp.where(is_vec, u, 0.0), hankel, precision=highest)
        for j in range(3):
            out = out + scalars(u, j) * own[j]
        out = jnp.where(is_vec, out, 0.0)
        for i in range(3):
            out = jnp.where(lane == i * pitch + coarse, total(u * own[i]), out)
        return out

    def corrected(w):
        return dot(jnp.where(lane < coarse, w, 0.0), inverse, precision=highest)

    pre = corrected(against) + jnp.where(lane == coarse, 1.0, 0.0)
    direction = pre
    gamma = total(pre * against)
    answer = jnp.zeros_like(pre)
    image_sum = jnp.zeros_like(pre)
    for step in range(ITERS):
        image = metric(direction)
        alpha = gamma / total(direction * image)
        answer = answer + alpha * direction
        if step + 1 < ITERS:
            image_sum = image_sum + alpha * image
            moved_on = jnp.where(live & (slot > 0), pltpu.roll(direction, pitch, axis=1), 0.0)
            pre = pre - alpha * (moved_on + corrected(image))
            gamma_new = total(pre * (against - image_sum))
            direction = pre + (gamma_new / gamma) * direction
            gamma = gamma_new

    row = slice(FEAT + 1, FEAT + 2)
    which = jnp.concatenate(
        [left_ref[row, edge:], own_ref[row, :], right_ref[row, : width - edge]], axis=1
    )
    z = one_hot(which, coarse)
    q0 = jnp.concatenate([prel_ref[:, edge:], pre_ref[...], prer_ref[:, : width - edge]], axis=1)
    d1 = jnp.concatenate([d1l_ref[:, edge:], d1_ref[...], d1r_ref[:, : width - edge]], axis=1)
    d2 = jnp.concatenate([d2l_ref[:, edge:], d2_ref[...], d2r_ref[:, : width - edge]], axis=1)
    span = q0.shape[1]
    pad = jnp.zeros((pitch - coarse, span), f32)
    basis = [z, pad, d1[count:], pad, d2[count:], pad]
    if wide > 3 * pitch:
        basis.append(jnp.zeros((wide - 3 * pitch, span), f32))
    x = dot(jnp.where(is_vec, answer, 0.0), jnp.concatenate(basis, axis=0), precision=highest)
    x = x + scalars(answer, 0) * q0 + scalars(answer, 1) * d1[:count]
    x = x + scalars(answer, 2) * d2[:count]
    mine = slice(REACH * BS, REACH * BS + width)
    sol_ref[...] = x[:, mine]

    base = FEAT + 8
    systems = jnp.concatenate(
        [left_ref[base:, edge:], own_ref[base:, :], right_ref[base:, : width - edge]], axis=1
    )
    target = (iota((count, 1), 0) == 0) & (scalar_ref[0] == 0)
    right = jnp.where(target, x, systems)
    weighted = x[:, mine] * coef_ref[...][:, 0:1]
    r0, r1 = split(right, 2)
    w0, w1 = split(weighted, 2)
    near = jnp.concatenate([r0, r1, r0], axis=0).astype(bf16)
    mate = jnp.concatenate([w0, w0, w1], axis=0).astype(bf16)
    pack = jnp.concatenate(
        [left_ref[0:16, edge:], own_ref[0:16, :], right_ref[0:16, : width - edge]], axis=1
    )
    scaled = pack[0:FEAT] / column(len_ref, FEAT)
    table = one_hot(pack[FEAT : FEAT + 1], TASKS)
    ones = jnp.ones((8, span), f32)
    terms = jnp.concatenate([scaled, ones, scaled * scaled], axis=0)
    t0, t1 = split(terms, 2)
    pad8 = jnp.zeros((8, span), f32)
    both = jnp.concatenate([t0, pad8, t1, pad8], axis=0).astype(bf16)
    heads = jnp.concatenate([t0, pad8], axis=0).astype(bf16)
    tables = table.astype(bf16)
    high = 32
    length_total = jnp.zeros((FEAT, 1), f32)
    task_total = jnp.zeros((TASKS, TASKS), f32)
    for m in range(blocks):
        at = slice(m * BS, (m + 1) * BS)
        sums = jnp.zeros((high, BS), f32)
        held_sums = jnp.zeros((TASKS, BS), f32)
        for o in range(SLOTS):
            j = slice((m + o) * BS, (m + o + 1) * BS)
            rows_at = slice(o * BS, (o + 1) * BS)
            outer = dot(near[:, j], mate[:, at], TN)
            kernel = hi_ref[m, rows_at, :].astype(f32) + lo_ref[m, rows_at, :].astype(f32)
            energy = outer * kernel
            held = outer * sim_ref[m, rows_at, :]
            e0, e1 = (part.astype(bf16) for part in split(energy, 2))
            h0, h1 = (part.astype(bf16) for part in split(held, 2))
            first = dot(both[:, j], e0)
            sums = sums + first[:high] + first[high:] + dot(heads[:, j], e1)
            held_sums = held_sums + dot(tables[:, j], h0) + dot(tables[:, j], h1)
        mid = slice((REACH + m) * BS, (REACH + m + 1) * BS)
        left = scaled[:, mid]
        value = left * left * sums[FEAT : FEAT + 1] + sums[2 * FEAT : 3 * FEAT]
        value = value - 2.0 * left * sums[:FEAT]
        length_total = length_total + jnp.sum(value, axis=1, keepdims=True)
        task_total = task_total + dot(table[:, mid], held_sums, NT, highest)
    lane = iota((TASKS, LANES), 1)
    lengths = jnp.concatenate([length_total, jnp.zeros((TASKS - FEAT, 1), f32)], axis=0)
    wide_tasks = jnp.concatenate([task_total, jnp.zeros((TASKS, LANES - TASKS), f32)], axis=1)
    grad_ref[...] = jnp.where(lane == TASKS, lengths, wide_tasks)


def call(body, outs, args, smem, name, scratch=(), flops=0):
    vm = pl.BlockSpec(memory_space=pltpu.VMEM)
    sm = pl.BlockSpec(memory_space=pltpu.SMEM)
    return pl.pallas_call(
        body,
        out_shape=outs,
        in_specs=[sm] * smem + [vm] * (len(args) - smem),
        out_specs=[vm] * len(outs),
        scratch_shapes=scratch,
        compiler_params=pltpu.CompilerParams(vmem_limit_bytes=48 * 1024 * 1024),
        cost_estimate=pl.CostEstimate(flops=flops, bytes_accessed=1 << 20, transcendentals=0),
        name=name,
    )(*args)


def both_sides(cells):
    count = lax.axis_size("pts")
    up = [(i, i + 1) for i in range(count - 1)]
    down = [(i + 1, i) for i in range(count - 1)]
    return lax.ppermute(cells, "pts", up), lax.ppermute(cells, "pts", down)


def shards(
    systems, features, task_ids, pattern, aggregate, coarse_inverse, task_cov, lengthscales, noise
):
    count, width = systems.shape
    blocks = width // BS
    coarse = coarse_inverse.shape[1]
    rows = count + coarse
    pitch, lanes = pitch_of(coarse), lanes_of(coarse)

    def shape(*dims, kind=f32):
        return jax.ShapeDtypeStruct(dims, kind)

    pack = jnp.concatenate(
        [
            features,
            task_ids.astype(f32)[None],
            aggregate.astype(f32)[None],
            jnp.zeros((6, width), f32),
            systems,
        ],
        axis=0,
    )
    pack_l, pack_r = both_sides(pack)
    jac, pre = call(
        invert_kernel,
        [shape(blocks, BS, BS), shape(count, width)],
        [pattern, lengthscales, noise, pack, task_cov],
        3,
        "invert",
        [pltpu.VMEM((blocks, BS, BS), f32)],
        flops=10**10,
    )
    pre_l, pre_r = both_sides(pre)
    hi, lo, sim = call(
        build_kernel,
        [
            shape(blocks, BAND, BS, kind=bf16),
            shape(blocks, BAND, BS, kind=bf16),
            shape(blocks, BAND, BS),
        ],
        [pattern, lengthscales, pack, pack_l, pack_r, task_cov],
        2,
        "build",
        flops=3 * 10**9,
    )
    v0, d1 = call(
        first_kernel,
        [shape(rows, width), shape(rows, width)],
        [noise, pack, pack_l, pack_r, pre, pre_l, pre_r, hi, lo, jac],
        1,
        "first",
        flops=10**9,
    )
    d1_l, d1_r = both_sides(d1)
    v1, d2 = call(
        second_kernel,
        [shape(rows, width), shape(rows, width)],
        [noise, pack, d1, d1_l, d1_r, hi, lo, jac],
        1,
        "second",
        flops=10**9,
    )
    d2_l, d2_r = both_sides(d2)
    own_rows = coarse_inverse.shape[0]
    placed = lax.dynamic_update_slice(
        jnp.zeros((rows, lanes), f32),
        coarse_inverse,
        (lax.axis_index("pts") * own_rows, 6 * pitch),
    )
    (partial_gram,) = call(
        moment_kernel,
        [shape(rows, lanes)],
        [noise, pack, d2, d2_l, d2_r, hi, lo, pre, d1, v0, v1, placed],
        1,
        "moments",
        flops=10**9,
    )
    gram = lax.psum(partial_gram, "pts")
    probe = lax.axis_index("probe")
    line = probe * count + jnp.arange(count, dtype=jnp.int32)
    total_points = lax.axis_size("pts") * width
    total_sides = lax.axis_size("probe") * count
    coef = jnp.where(line == 0, 0.5, -0.5 / (total_sides - 1)) / total_points
    coef = jnp.broadcast_to(coef[:, None], (count, LANES)).astype(f32)
    answer, grads = call(
        final_kernel,
        [shape(count, width), shape(TASKS, LANES)],
        [
            probe.astype(jnp.int32)[None], lengthscales, gram, pack, pack_l, pack_r, pre, pre_l,
            pre_r, d1, d1_l, d1_r, d2, d2_l, d2_r, hi, lo, sim, coef, task_cov,
        ],
        2,
        "final",
        flops=10**9,
    )
    grads = lax.psum(grads, ("pts", "probe"))
    return answer, grads[:FEAT, TASKS], grads[:, :TASKS]


def solution(mesh):
    return jax.shard_map(
        shards,
        mesh=mesh,
        in_specs=(
            P("probe", ("groups", "pts")),
            P(None, ("groups", "pts")),
            P(("groups", "pts")),
            P(("groups", "pts"), None),
            P(("groups", "pts")),
            P(("groups", "pts"), None),
            P("groups", None),
            P("groups"),
            P("groups"),
        ),
        out_specs=(P("probe", ("groups", "pts")), P("groups"), P("groups", None)),
        check_vma=False,
    )
```

time: 662 us -> 165 us (0.25)
  blocking collectives: 265 us -> 65.3 us
  other arithmetic: 189 us -> 1.89 us
  matrix products: 101 us -> 0 us
  local copies, waits for them, and re-layouts: 65.2 us -> 19.7 us
  Pallas kernels: 0 us -> 42.5 us
  waiting for transfers between devices: 1.7 us -> 8.88 us
    another operation x13 -> x0, other arithmetic: 165 us -> none  [the longest x9 103 us: shards(): factors = jnp.linalg.cholesky(diagonal)]
    psum x9 -> x2, blocking collectives: 186 us -> 65.3 us  [the longest x1 35.3 us: shards(): gram = lax.psum(partial_gram, 'pts')]
    dot_general x59 -> x0, matrix products: 90.7 us -> none  [the longest x3 19 us: operate(): image = jnp.einsum('obij,orbj->rbi', kernel_all, shifted, precision=highest)]
    all_gather x3 -> x0, blocking collectives: 78.7 us -> none  [precondition(): coarse = lax.all_gather(owned, 'pts', axis=1, tiled=True)]
    pallas_call x0 -> x6, Pallas kernels: none -> 42.5 us  [call(): pl.pallas_call(body, out_shape=outs, in_specs=[sm] * smem + [vm] * (len(a...]
    another operation x37 -> x0, local copies, waits for them, and re-layouts: 29.4 us -> none  [the longest x24 21.1 us: operate(): jnp.stack([window(padded, offset, width) for offset in range(slots)], axi...]
    unnamed x226 -> x56, local copies, waits for them, and re-layouts: 28.3 us -> 14.9 us
    another operation x8 -> x0, matrix products: 10.4 us -> none  [the longest x6 6.85 us: shards(): jax.scipy.linalg.cho_solve((factor, True), identity)]
  transfers between devices with their start and end apart: 10 -> 8, of which waited for: 2 -> 3; matrix products, arithmetic and copies ran while one was open for 2% -> 1% of each run, Pallas kernels for 0% -> 13%
where the time goes in v1:
time: 165 us; the launch traced here: 164 us
  blocking collectives  65.3 us (40%)
  Pallas kernels  42.5 us (26%)
  starting transfers between devices  24.7 us (15%)
  local copies, waits for them, and re-layouts  19.7 us (12%)
  waiting for transfers between devices  8.88 us (5%)
  other arithmetic  1.89 us (1%)
    pallas_call x6, Pallas kernels, call(): pl.pallas_call(body, out_shape=outs, in_specs=[sm] * smem + [vm] * (len(a...  42.5 us
    psum x1, blocking collectives, shards(): gram = lax.psum(partial_gram, 'pts')  35.3 us
    psum x1, blocking collectives, shards(): grads = lax.psum(grads, ('pts', 'probe'))  30 us
    ppermute x8, starting transfers between devices, both_sides(): return (lax.ppermute(cells, 'pts', up), lax.ppermute(cells, 'pts', down))  24.7 us
    unnamed x56, local copies, waits for them, and re-layouts  14.9 us
    ppermute x8, waiting for transfers between devices, both_sides(): return (lax.ppermute(cells, 'pts', up), lax.ppermute(cells, 'pts', down))  8.88 us
  transfers between devices with their start and end apart: 8, of which 3 were waited for; matrix products, arithmetic and copies ran while one was open for 1% of the time, Pallas kernels for 13%

profile of v1, /device:TPU:0, one launch (start us, length us, event | category | flops | bytes accessed | tf_op | source)
XLA Modules:
  0.0 163.9 jit_solution(11572734822434079810)
XLA Ops:
  2.1 1.6 concatenate.3.pack_ref.own_ref
  3.6 4.9 %collective-permute-start = (f32[32,768]{1,0:T(8,128)S(1)}, f32[32,768]{1,0:T(8,128)S(1)}, u32[]{:S(2)}, u32[]{:S(2)}) collective-permute-start(f32[32,768]{1,0:T(8,128)S(1)} %concatenate.3.pack_ref.own_ref), channel_id=1, source_target_pairs={{0,2},{2,4},{4,6},{6,8},{8,10},{10,12},{12,14},{1,3},{3,5},{5,7},{... | collective-permute-start | bytes 294920 | tf_op jit(solution)/shard_map/ppermute | solution.py:535
  8.5 1.3 collective-permute-start.1
  12.5 16.7 %invert.1 = (f32[3,256,256]{2,1,0:T(8,128)S(1)}, f32[16,768]{1,0:T(8,128)S(1)}) custom-call(s32[3,7]{1,0:T(4,128)S(1)} %copy-done.25, f32[8]{0:T(128)S(1)} %copy-done.22, f32[16]{0:T(128)S(1)} %copy-done.19, f32[32,768]{1,0:T(8,128)S(1)} %concatenate.3.pack_ref.own_ref, f32[16,16]{1,0:T(8,128)S(1)} %copy-done.16), custom_call_target="tpu_custom_call" | custom-call | flops 10000000000 | bytes 1048576 | tf_op jit(solution)/shard_map/invert/pallas_call | solution.py:519
  29.3 4.7 %collective-permute-start.2 = (f32[16,768]{1,0:T(8,128)S(1)}, f32[16,768]{1,0:T(8,128)S(1)}, u32[]{:S(2)}, u32[]{:S(2)}) collective-permute-start(f32[16,768]{1,0:T(8,128)S(1)} %get-tuple-element.14.pre_ref), channel_id=1, source_target_pairs={{0,2},{2,4},{4,6},{6,8},{8,10},{10,12},{12,14},{1,3},{3,5},{5,7},{... | collective-permute-start | bytes 147464 | tf_op jit(solution)/shard_map/ppermute | solution.py:535
  34.0 1.3 collective-permute-start.3
  35.3 5.1 %build.1 = (bf16[3,1792,256]{2,1,0:T(8,128)(2,1)S(1)}, bf16[3,1792,256]{2,1,0:T(8,128)(2,1)S(1)}, f32[3,1792,256]{2,1,0:T(8,128)}) custom-call(s32[3,7]{1,0:T(4,128)S(1)} %copy-done.26, f32[8]{0:T(128)S(1)} %copy-done.23, f32[32,768]{1,0:T(8,128)S(1)} %concatenate.3.pack_ref.own_ref, f32[32,768]{1,0:T(8,128)S(1)} %collective-permute-done.left_ref, ...), custom_call_target="tpu_custom_call" | custom-call | flops 3000000000 | bytes 1048576 | tf_op jit(solution)/shard_map/build/pallas_call | solution.py:519
  40.4 1.6 copy-done
  42.0 3.2 %first.1 = (f32[40,768]{1,0:T(8,128)S(1)}, f32[40,768]{1,0:T(8,128)S(1)}) custom-call(f32[16]{0:T(128)S(1)} %copy-done.20, f32[32,768]{1,0:T(8,128)S(1)} %concatenate.3.pack_ref.own_ref, f32[32,768]{1,0:T(8,128)S(1)} %collective-permute-done.left_ref, f32[32,768]{1,0:T(8,128)S(1)} %collective-permute-done.1.right_ref, ...), custom_call_target="tpu_custom_call" | custom-call | flops 1000000000 | bytes 1048576 | tf_op jit(solution)/shard_map/first/pallas_call | solution.py:519
  45.9 4.9 %collective-permute-start.4 = (f32[40,768]{1,0:T(8,128)S(1)}, f32[40,768]{1,0:T(8,128)S(1)}, u32[]{:S(2)}, u32[]{:S(2)}) collective-permute-start(f32[40,768]{1,0:T(8,128)S(1)} %get-tuple-element.18.vec_ref.d1_ref), channel_id=1, source_target_pairs={{0,2},{2,4},{4,6},{6,8},{8,10},{10,12},{12,14},{1,3},{3,5},{5,7},{... | collective-permute-start | bytes 368648 | tf_op jit(solution)/shard_map/ppermute | solution.py:535
  50.9 1.5 collective-permute-start.5
  52.3 0.9 collective-permute-done.4.vecl_ref.d1l_ref
  53.3 5.2 %collective-permute-done.5.vecr_ref.d1r_ref = f32[40,768]{1,0:T(8,128)S(1)} collective-permute-done((f32[40,768]{1,0:T(8,128)S(1)}, f32[40,768]{1,0:T(8,128)S(1)}, u32[]{:S(2)}, u32[]{:S(2)}) %collective-permute-start.5) | collective-permute-done | bytes 122912 | tf_op jit(solution)/shard_map/ppermute | solution.py:535
  58.5 3.2 %second.1 = (f32[40,768]{1,0:T(8,128)S(1)}, f32[40,768]{1,0:T(8,128)S(1)}) custom-call(f32[16]{0:T(128)S(1)} %copy-done.20, f32[32,768]{1,0:T(8,128)S(1)} %concatenate.3.pack_ref.own_ref, f32[40,768]{1,0:T(8,128)S(1)} %get-tuple-element.18.vec_ref.d1_ref, f32[40,768]{1,0:T(8,128)S(1)} %collective-permute-done.4.vecl_ref.d1l_ref, ...), custom_call_target="tpu_custom_call" | custom-call | flops 1000000000 | bytes 1048576 | tf_op jit(solution)/shard_map/second/pallas_call | solution.py:519
  62.4 4.8 %collective-permute-start.6 = (f32[40,768]{1,0:T(8,128)S(1)}, f32[40,768]{1,0:T(8,128)S(1)}, u32[]{:S(2)}, u32[]{:S(2)}) collective-permute-start(f32[40,768]{1,0:T(8,128)S(1)} %get-tuple-element.19.vec_ref.d2_ref), channel_id=1, source_target_pairs={{0,2},{2,4},{4,6},{6,8},{8,10},{10,12},{12,14},{1,3},{3,5},{5,7},{... | collective-permute-start | bytes 368648 | tf_op jit(solution)/shard_map/ppermute | solution.py:535
  67.2 1.3 collective-permute-start.7
  68.6 1.7 %dynamic_update_slice.3.coarse_ref = f32[40,256]{1,0:T(8,128)S(1)} dynamic-update-slice(f32[40,256]{1,0:T(8,128)S(1)} %broadcast_in_dim.33, f32[3,24]{1,0:T(4,128)} %param.14, s32[]{:T(128)S(6)} %select_n.11, s32[]{:T(128)} %constant.7.clone.1) | dynamic-update-slice | bytes 580 | tf_op jit(solution)/shard_map/dynamic_update_slice | solution.py:602
  71.4 2.7 %collective-permute-done.7.vecr_ref.d2r_ref = f32[40,768]{1,0:T(8,128)} collective-permute-done((f32[40,768]{1,0:T(8,128)S(1)}, f32[40,768]{1,0:T(8,128)}, u32[]{:S(2)}, u32[]{:S(2)}) %collective-permute-start.7) | collective-permute-done | bytes 122912 | tf_op jit(solution)/shard_map/ppermute | solution.py:535
  74.1 0.8 copy-done.10
  74.9 0.9 copy-done.13
  75.8 0.9 copy-done.15
  77.4 3.5 %moments.1 = f32[40,256]{1,0:T(8,128)S(1)} custom-call(f32[16]{0:T(128)S(1)} %copy-done.21, f32[32,768]{1,0:T(8,128)S(1)} %concatenate.3.pack_ref.own_ref, f32[40,768]{1,0:T(8,128)S(1)} %get-tuple-element.19.vec_ref.d2_ref, f32[40,768]{1,0:T(8,128)S(1)} %collective-permute-done.6.vecl_ref.d2l_ref, f32[40,768]{1,0:T(8,128)} %collective-permute-done.7.vecr_ref.d2r_ref, ...), custom_call_target="tpu_custom_call" | custom-call | flops 1000000000 | bytes 1048576 | tf_op jit(solution)/shard_map/moments/pallas_call | solution.py:519
  80.9 35.3 %psum.14.gram_ref = f32[40,256]{1,0:T(8,128)} all-reduce(f32[40,256]{1,0:T(8,128)S(1)} %moments.1), channel_id=1, replica_groups=mesh['groups'=2,'pts'=8,'probe'=2] {'pts'}, use_global_device_ids=true, to_apply=%region_0.0 | all-reduce | flops 10240 | bytes 81920 | tf_op jit(solution)/shard_map/psum | solution.py:615
  116.2 0.7 broadcast_in_dim.36.coef_ref
  116.9 0.9 copy-done.2
  117.8 0.9 copy-done.4
  118.7 0.8 copy-done.6
  119.5 0.8 copy-done.8
  120.3 0.8 copy-done.11
  121.1 0.7 copy-done.18
  122.4 10.8 %final.1 = (f32[16,768]{1,0:T(8,128)}, f32[16,128]{1,0:T(8,128)S(1)}) custom-call(s32[1]{0:T(128)} %bitcast.scalar_ref, f32[8]{0:T(128)S(1)} %copy-done.24, f32[40,256]{1,0:T(8,128)S(1)} %copy-done.11, f32[32,768]{1,0:T(8,128)S(1)} %concatenate.3.pack_ref.own_ref, f32[32,768]{1,0:T(8,128)S(1)} %copy-done.2, f32[32,768]{1,0:T(8,128)S(1)} %copy-done.4, ...), custom_call_target="tpu_custom_call" | custom-call | flops 1000000000 | bytes 1048576 | tf_op jit(solution)/shard_map/final/pallas_call | solution.py:519
  133.2 30.0 %psum.15 = f32[16,128]{1,0:T(8,128)S(1)} all-reduce(f32[16,128]{1,0:T(8,128)S(1)} %get-tuple-element.24), channel_id=1, replica_groups=mesh['groups'=2,'pts'=8,'probe'=2] {'pts','probe'}, use_global_device_ids=true, to_apply=%region_1.2 | all-reduce | flops 2048 | bytes 16384 | tf_op jit(solution)/shard_map/psum | solution.py:633
  (59 shorter events, 8.6 us)
Async XLA Ops:
  2.0 33.3 %copy-start.17 = (f32[16,16]{1,0:T(8,128)S(1)}, f32[16,16]{1,0:T(8,128)}, u32[]{:S(2)}) copy-start(f32[16,16]{1,0:T(8,128)} %cov_ref.5) | copy-start | bytes 3076
  2.0 33.3 %copy-start.23 = (f32[8]{0:T(128)S(1)}, f32[8]{0:T(128)}, u32[]{:S(2)}) copy-start(f32[8]{0:T(128)} %len_ref.5) | copy-start | bytes 100
  2.0 33.3 %copy-start.26 = (s32[3,7]{1,0:T(4,128)S(1)}, s32[3,7]{1,0:T(4,128)}, u32[]{:S(2)}) copy-start(s32[3,7]{1,0:T(4,128)} %pat_ref.3) | copy-start | bytes 256
  3.6 31.6 %collective-permute-start = (f32[32,768]{1,0:T(8,128)S(1)}, f32[32,768]{1,0:T(8,128)S(1)}, u32[]{:S(2)}, u32[]{:S(2)}) collective-permute-start(f32[32,768]{1,0:T(8,128)S(1)} %concatenate.3.pack_ref.own_ref), channel_id=1, source_target_pairs={{0,2},{2,4},{4,6},{6,8},{8,10},{10,12},{12,14},{1,3},{3,5},{5,7},{... | collective-permute-start | bytes 294920 | tf_op jit(solution)/shard_map/ppermute | solution.py:535
  8.5 26.8 %collective-permute-start.1 = (f32[32,768]{1,0:T(8,128)S(1)}, f32[32,768]{1,0:T(8,128)S(1)}, u32[]{:S(2)}, u32[]{:S(2)}) collective-permute-start(f32[32,768]{1,0:T(8,128)S(1)} %concatenate.3.pack_ref.own_ref), channel_id=1, source_target_pairs={{2,0},{4,2},{6,4},{8,6},{10,8},{12,10},{14,12},{3,1},{5,3},{7,5},{... | collective-permute-start | bytes 294920 | tf_op jit(solution)/shard_map/ppermute | solution.py:535
  9.8 0.7 copy-start.16
  10.5 0.7 copy-start.19
  11.8 0.7 copy-start.25
  29.3 12.7 %copy-start.20 = (f32[16]{0:T(128)S(1)}, f32[16]{0:T(128)}, u32[]{:S(2)}) copy-start(f32[16]{0:T(128)} %noise_ref.7) | copy-start | bytes 196
  29.3 12.7 %collective-permute-start.2 = (f32[16,768]{1,0:T(8,128)S(1)}, f32[16,768]{1,0:T(8,128)S(1)}, u32[]{:S(2)}, u32[]{:S(2)}) collective-permute-start(f32[16,768]{1,0:T(8,128)S(1)} %get-tuple-element.14.pre_ref), channel_id=1, source_target_pairs={{0,2},{2,4},{4,6},{6,8},{8,10},{10,12},{12,14},{1,3},{3,5},{5,7},{... | collective-permute-start | bytes 147464 | tf_op jit(solution)/shard_map/ppermute | solution.py:535
  34.0 8.0 %collective-permute-start.3 = (f32[16,768]{1,0:T(8,128)S(1)}, f32[16,768]{1,0:T(8,128)S(1)}, u32[]{:S(2)}, u32[]{:S(2)}) collective-permute-start(f32[16,768]{1,0:T(8,128)S(1)} %get-tuple-element.14.pre_ref), channel_id=1, source_target_pairs={{2,0},{4,2},{6,4},{8,6},{10,8},{12,10},{14,12},{3,1},{5,3},{7,5},{... | collective-permute-start | bytes 147464 | tf_op jit(solution)/shard_map/ppermute | solution.py:535
  35.3 6.7 %copy-start.1 = (f32[32,768]{1,0:T(8,128)}, f32[32,768]{1,0:T(8,128)S(1)}, u32[]{:S(2)}) copy-start(f32[32,768]{1,0:T(8,128)S(1)} %collective-permute-done.left_ref) | copy-start | bytes 294916
  35.3 6.7 %copy-start.3 = (f32[32,768]{1,0:T(8,128)}, f32[32,768]{1,0:T(8,128)S(1)}, u32[]{:S(2)}) copy-start(f32[32,768]{1,0:T(8,128)S(1)} %collective-permute-done.1.right_ref) | copy-start | bytes 294916
  40.4 1.6 copy-start
  42.0 3.3 %copy-start.5 = (f32[16,768]{1,0:T(8,128)}, f32[16,768]{1,0:T(8,128)S(1)}, u32[]{:S(2)}) copy-start(f32[16,768]{1,0:T(8,128)S(1)} %collective-permute-done.2.prel_ref) | copy-start | bytes 147460
  42.0 3.3 %copy-start.7 = (f32[16,768]{1,0:T(8,128)}, f32[16,768]{1,0:T(8,128)S(1)}, u32[]{:S(2)}) copy-start(f32[16,768]{1,0:T(8,128)S(1)} %collective-permute-done.3.prer_ref) | copy-start | bytes 147460
  45.9 7.4 %collective-permute-start.4 = (f32[40,768]{1,0:T(8,128)S(1)}, f32[40,768]{1,0:T(8,128)S(1)}, u32[]{:S(2)}, u32[]{:S(2)}) collective-permute-start(f32[40,768]{1,0:T(8,128)S(1)} %get-tuple-element.18.vec_ref.d1_ref), channel_id=1, source_target_pairs={{0,2},{2,4},{4,6},{6,8},{8,10},{10,12},{12,14},{1,3},{3,5},{5,7},{... | collective-permute-start | bytes 368648 | tf_op jit(solution)/shard_map/ppermute | solution.py:535
  50.9 7.7 %collective-permute-start.5 = (f32[40,768]{1,0:T(8,128)S(1)}, f32[40,768]{1,0:T(8,128)S(1)}, u32[]{:S(2)}, u32[]{:S(2)}) collective-permute-start(f32[40,768]{1,0:T(8,128)S(1)} %get-tuple-element.18.vec_ref.d1_ref), channel_id=1, source_target_pairs={{2,0},{4,2},{6,4},{8,6},{10,8},{12,10},{14,12},{3,1},{5,3},{7,5},{... | collective-permute-start | bytes 368648 | tf_op jit(solution)/shard_map/ppermute | solution.py:535
  61.7 0.7 copy-start.14
  62.4 9.0 %collective-permute-start.6 = (f32[40,768]{1,0:T(8,128)S(1)}, f32[40,768]{1,0:T(8,128)S(1)}, u32[]{:S(2)}, u32[]{:S(2)}) collective-permute-start(f32[40,768]{1,0:T(8,128)S(1)} %get-tuple-element.19.vec_ref.d2_ref), channel_id=1, source_target_pairs={{0,2},{2,4},{4,6},{6,8},{8,10},{10,12},{12,14},{1,3},{3,5},{5,7},{... | collective-permute-start | bytes 368648 | tf_op jit(solution)/shard_map/ppermute | solution.py:535
  67.2 6.9 %collective-permute-start.7 = (f32[40,768]{1,0:T(8,128)S(1)}, f32[40,768]{1,0:T(8,128)}, u32[]{:S(2)}, u32[]{:S(2)}) collective-permute-start(f32[40,768]{1,0:T(8,128)S(1)} %get-tuple-element.19.vec_ref.d2_ref), channel_id=1, source_target_pairs={{2,0},{4,2},{6,4},{8,6},{10,8},{12,10},{14,12},{3,1},{5,3},{7,5},{... | collective-permute-start | bytes 368648 | tf_op jit(solution)/shard_map/ppermute | solution.py:535
  74.1 0.8 copy-start.10
  74.9 0.9 copy-start.13
  75.8 0.9 copy-start.15
  76.7 0.7 copy-start.21
  116.9 0.9 copy-start.2
  117.8 0.9 copy-start.4
  118.7 0.8 copy-start.6
  119.5 0.8 copy-start.8
  120.3 0.8 copy-start.11
  121.1 0.7 copy-start.18
  163.2 0.7 copy-start.27
  (4 other events, 2.6 us)

commit v2 on v1

--- a/solution.py
+++ b/solution.py
@@ -17,6 +17,7 @@
 BASE = 32
 GROUP = 4
 LANES = 128
+SYS = 2 * FEAT
 
 highest = lax.Precision.HIGHEST
 f32 = jnp.float32
@@ -83,21 +84,18 @@
     ).astype(bf16)
 
 
-def own_stack(scaled, table, cov):
+def own_stack(scaled, picked):
     s0, s1, s2 = split(scaled, 3)
     rows = iota(scaled.shape, 0)
     ones = jnp.where(rows < 3, 1.0, 0.0)
     count = scaled.shape[1]
-    c0, c1, c2 = split(cov, 3)
-    picked = dot(
-        jnp.concatenate([c0, c1, c2], axis=0).astype(bf16), table.astype(bf16)
-    )
     tail = LANES - 7 * FEAT - 3 * TASKS
     left = jnp.concatenate(
         [s0, s1, s0, s1, s2, s0, ones, jnp.zeros((3 * TASKS + tail, count), f32)], axis=0
     ).astype(bf16)
     right = jnp.concatenate(
-        [jnp.zeros((7 * FEAT, count), f32), picked, jnp.zeros((tail, count), f32)], axis=0
+        [jnp.zeros((7 * FEAT, count), f32)] + split(picked, 3) + [jnp.zeros((tail, count), f32)],
+        axis=0,
     ).astype(bf16)
     return left, right, -0.5 * jnp.sum(scaled * scaled, axis=0, keepdims=True)
 
@@ -159,15 +157,53 @@
     return cells
 
 
-def invert_kernel(pat_ref, len_ref, noise_ref, pack_ref, cov_ref, jac_ref, pre_ref, work):
+def invert_kernel(
+    feat_hbm, ids_hbm, agg_hbm, sys_hbm, cov_hbm, coarse_hbm, pat_hbm, len_hbm, noise_hbm,
+    jac_ref, pack_ref, extra_ref,
+    work, feat_ref, ids_ref, agg_ref, sys_ref, cov_ref, coarse_ref, pat_ref, len_ref, noise_ref, sems,
+):
     blocks = work.shape[0]
-    scaled = pack_ref[0:FEAT, :] / column(len_ref, FEAT)
-    ids = pack_ref[FEAT : FEAT + 1, :]
+    width = blocks * BS
+    pairs = [
+        (feat_hbm, feat_ref), (ids_hbm, ids_ref), (agg_hbm, agg_ref), (cov_hbm, cov_ref),
+        (pat_hbm, pat_ref), (len_hbm, len_ref), (noise_hbm, noise_ref), (coarse_hbm, coarse_ref),
+        (sys_hbm, sys_ref),
+    ]
+    copies = [pltpu.make_async_copy(a, b, sems.at[i]) for i, (a, b) in enumerate(pairs)]
+    for copy in copies:
+        copy.start()
+    for copy in copies:
+        copy.wait()
+    scaled = feat_ref[...] / column(len_ref, FEAT)
+    ids = ids_ref[...].astype(f32)
     table = one_hot(ids, TASKS)
     noise = noise_row(noise_ref, ids)
-    cov = cov_ref[...]
+    c0, c1, c2 = split(cov_ref[...], 3)
+    tab = table.astype(bf16)
+    picked = (dot(c2.astype(bf16), tab) + dot(c1.astype(bf16), tab)) + dot(c0.astype(bf16), tab)
+    rows = iota((FEAT, width), 0)
+    weights = jnp.zeros((1, width), f32)
+    places = iota((1, width), 1)
+    for m in range(blocks):
+        for o in range(SLOTS):
+            weights = jnp.where(places == m * SLOTS + o, weight(pat_ref, m, o), weights)
+    pack_ref[0:FEAT, :] = scaled
+    pack_ref[FEAT : 2 * FEAT, :] = jnp.where(
+        rows == 0, ids, jnp.where(rows == 1, agg_ref[...].astype(f32), 0.0)
+    )
+    count = sys_ref.shape[0]
+    pack_ref[SYS : SYS + count, :] = sys_ref[...]
+    extra_ref[0:TASKS, :] = picked
+    tail = jnp.where(rows == 0, noise, jnp.where(rows == 1, weights, 0.0))
+    held = coarse_ref.shape[0]
+    inverse = jnp.concatenate(
+        [coarse_ref[...], jnp.zeros((held, width - coarse_ref.shape[1]), f32)], axis=1
+    )
+    for r in range(held):
+        tail = jnp.where(rows == 2 + r, inverse[r : r + 1], tail)
+    extra_ref[TASKS : TASKS + FEAT, :] = tail
     near = near_stack(scaled, table)
-    left, right, norm = own_stack(scaled, table, cov)
+    left, right, norm = own_stack(scaled, picked)
     eye = iota((BS, BS), 0) == iota((BS, BS), 1)
     for m in range(blocks):
         at = slice(m * BS, (m + 1) * BS)
@@ -208,28 +244,22 @@
             b = jnp.concatenate([p0, p1, p0, p1, p2, p0], axis=0).astype(bf16)
             work[m] = jnp.where(gone, 0.0, work[m]) - dot(a, b, TN)
             work[m, first : first + BASE, :] = row
-    base = FEAT + 8
     for m in range(blocks):
         at = slice(m * BS, (m + 1) * BS)
         inv = -work[m]
         jac_ref[m] = inv
-        pre_ref[:, at] = dot(pack_ref[base:, at], inv, precision=highest)
-
-
-def build_kernel(
-    pat_ref, len_ref, own_ref, left_ref, right_ref, cov_ref, hi_ref, lo_ref, sim_ref
-):
+        pack_ref[SYS + count :, at] = dot(sys_ref[:, at], inv, precision=highest)
+
+
+def build_kernel(own_ref, left_ref, right_ref, extra_ref, hi_ref, lo_ref, sim_ref):
     blocks = hi_ref.shape[0]
-    lens = column(len_ref, FEAT)
-    pack = jnp.concatenate(
-        [left_ref[0 : FEAT + 8, :], own_ref[0 : FEAT + 8, :], right_ref[0 : FEAT + 8, :]], axis=1
-    )
-    scaled = pack[0:FEAT] / lens
+    pack = jnp.concatenate([left_ref[0:SYS, :], own_ref[0:SYS, :], right_ref[0:SYS, :]], axis=1)
+    scaled = pack[0:FEAT]
     table = one_hot(pack[FEAT : FEAT + 1], TASKS)
     near = near_stack(scaled, table)
     width = blocks * BS
-    own = slice(width, 2 * width)
-    left, right, norm = own_stack(scaled[:, own], table[:, own], cov_ref[...])
+    left, right, norm = own_stack(own_ref[0:FEAT, :], extra_ref[0:TASKS, :])
+    weights = extra_ref[TASKS + 1 : TASKS + 2, :]
     edge = width - REACH * BS
     for m in range(blocks):
         at = slice(m * BS, (m + 1) * BS)
@@ -238,7 +268,8 @@
             part = near[:, j : j + BS]
             exponent = dot(part, left[:, at], TN) + norm[:, at]
             pair = dot(part, right[:, at], TN)
-            similar = weight(pat_ref, m, o) * jnp.exp(exponent)
+            place = m * SLOTS + o
+            similar = weights[:, place : place + 1] * jnp.exp(exponent)
             kernel = similar * pair
             head = kernel.astype(bf16)
             rows = slice(o * BS, (o + 1) * BS)
@@ -269,54 +300,52 @@
     )
 
 
-def first_kernel(
-    noise_ref, own_ref, left_ref, right_ref, pre_ref, prel_ref, prer_ref, hi_ref, lo_ref, jac_ref,
-    image_ref, next_ref,
-):
-    count, width = pre_ref.shape
+def first_kernel(own_ref, left_ref, right_ref, extra_ref, hi_ref, lo_ref, jac_ref, image_ref, next_ref):
+    width = own_ref.shape[1]
+    count = (own_ref.shape[0] - SYS) // 2
     coarse = image_ref.shape[0] - count
-    pre = jnp.concatenate([prel_ref[...], pre_ref[...], prer_ref[...]], axis=1)
-    row = slice(FEAT + 1, FEAT + 2)
-    which = jnp.concatenate([left_ref[row, :], own_ref[row, :], right_ref[row, :]], axis=1)
-    ext = jnp.concatenate([pre, one_hot(which, coarse)], axis=0)
     edge = width - REACH * BS
-    noise = noise_row(noise_ref, own_ref[FEAT : FEAT + 1, :])
-    image = operate(
-        ext[:, edge : 3 * width - edge], noise, ext[:, width : 2 * width], hi_ref, lo_ref
-    )
+    pack = jnp.concatenate(
+        [left_ref[:, edge:], own_ref[...], right_ref[:, : width - edge]], axis=1
+    )
+    ext = jnp.concatenate(
+        [pack[SYS + count :], one_hot(pack[FEAT + 1 : FEAT + 2], coarse)], axis=0
+    )
+    noise = extra_ref[TASKS : TASKS + 1, :]
+    image = operate(ext, noise, ext[:, REACH * BS : REACH * BS + width], hi_ref, lo_ref)
     image_ref[...] = image
     next_ref[...] = smooth(image, jac_ref)
 
 
 def second_kernel(
-    noise_ref, own_ref, vec_ref, vecl_ref, vecr_ref, hi_ref, lo_ref, jac_ref, image_ref, next_ref
+    extra_ref, vec_ref, vecl_ref, vecr_ref, hi_ref, lo_ref, jac_ref, image_ref, next_ref
 ):
     width = vec_ref.shape[1]
     edge = width - REACH * BS
     ext = jnp.concatenate([vecl_ref[:, edge:], vec_ref[...], vecr_ref[:, : width - edge]], axis=1)
-    noise = noise_row(noise_ref, own_ref[FEAT : FEAT + 1, :])
+    noise = extra_ref[TASKS : TASKS + 1, :]
     image = operate(ext, noise, vec_ref[...], hi_ref, lo_ref)
     image_ref[...] = image
     next_ref[...] = smooth(image, jac_ref)
 
 
 def moment_kernel(
-    noise_ref, own_ref, vec_ref, vecl_ref, vecr_ref, hi_ref, lo_ref, pre_ref, d1_ref, v0_ref,
-    v1_ref, coarse_ref, out_ref,
+    place_ref, own_ref, extra_ref, vec_ref, vecl_ref, vecr_ref, hi_ref, lo_ref, d1_ref, v0_ref,
+    v1_ref, out_ref, *, held,
 ):
-    count, width = pre_ref.shape
+    width = own_ref.shape[1]
+    count = (own_ref.shape[0] - SYS) // 2
     rows = vec_ref.shape[0]
     coarse = rows - count
-    lanes = out_ref.shape[1]
+    copies, _, lanes = out_ref.shape
     pitch = pitch_of(coarse)
     edge = width - REACH * BS
     ext = jnp.concatenate([vecl_ref[:, edge:], vec_ref[...], vecr_ref[:, : width - edge]], axis=1)
-    noise = noise_row(noise_ref, own_ref[FEAT : FEAT + 1, :])
+    noise = extra_ref[TASKS : TASKS + 1, :]
     d2 = vec_ref[...]
     v2 = operate(ext, noise, d2, hi_ref, lo_ref)
-    base = FEAT + 8
-    systems = own_ref[base:, :]
-    pre = pre_ref[...]
+    systems = own_ref[SYS : SYS + count, :]
+    pre = own_ref[SYS + count :, :]
     z = one_hot(own_ref[FEAT + 1 : FEAT + 2, :], coarse)
     d1, v0, v1 = d1_ref[...], v0_ref[...], v1_ref[...]
     gap = jnp.zeros((pitch - coarse, width), f32)
@@ -348,7 +377,17 @@
     top = total[:count]
     for k, value in enumerate(own):
         top = jnp.where(lane == k * pitch + coarse, jnp.sum(value, axis=1, keepdims=True), top)
-    out_ref[...] = jnp.concatenate([top, total[count:]], axis=0) + coarse_ref[...]
+    value = jnp.concatenate([top, total[count:]], axis=0)
+    row = iota((rows, 1), 0)
+    start = place_ref[0] * held
+    front = jnp.zeros((1, 6 * pitch), f32)
+    back = jnp.zeros((1, lanes - 6 * pitch - coarse), f32)
+    for r in range(held):
+        line = extra_ref[TASKS + 2 + r : TASKS + 3 + r, 0:coarse]
+        line = jnp.concatenate([front, line, back], axis=1)
+        value = value + jnp.where(row == start + r, line, 0.0)
+    for c in range(copies):
+        out_ref[c] = value
 
 
 def pitch_of(coarse):
@@ -360,18 +399,20 @@
 
 
 def final_kernel(
-    scalar_ref, len_ref, gram_ref, own_ref, left_ref, right_ref, pre_ref, prel_ref, prer_ref,
-    d1_ref, d1l_ref, d1r_ref, d2_ref, d2l_ref, d2r_ref, hi_ref, lo_ref, sim_ref, coef_ref, cov_ref,
-    sol_ref, grad_ref,
+    probe_ref, gram_ref, own_ref, left_ref, right_ref, d1_ref, d1l_ref, d1r_ref, d2_ref, d2l_ref,
+    d2r_ref, hi_ref, lo_ref, sim_ref, sol_ref, grad_ref, *, sides, points,
 ):
-    count, width = pre_ref.shape
+    width = own_ref.shape[1]
+    count = (own_ref.shape[0] - SYS) // 2
     rows = d1_ref.shape[0]
     coarse = rows - count
     pitch = pitch_of(coarse)
     wide = -(-3 * pitch // LANES) * LANES
     blocks = width // BS
     edge = width - REACH * BS
-    gram = gram_ref[...]
+    gram = gram_ref[0]
+    for c in range(1, gram_ref.shape[0]):
+        gram = gram + gram_ref[c]
     lane = iota((1, wide), 1)
     slot, inside = lane // pitch, lane % pitch
     live = lane < 3 * pitch
@@ -440,12 +481,11 @@
             direction = pre + (gamma_new / gamma) * direction
             gamma = gamma_new
 
-    row = slice(FEAT + 1, FEAT + 2)
-    which = jnp.concatenate(
-        [left_ref[row, edge:], own_ref[row, :], right_ref[row, : width - edge]], axis=1
-    )
-    z = one_hot(which, coarse)
-    q0 = jnp.concatenate([prel_ref[:, edge:], pre_ref[...], prer_ref[:, : width - edge]], axis=1)
+    pack = jnp.concatenate(
+        [left_ref[:, edge:], own_ref[...], right_ref[:, : width - edge]], axis=1
+    )
+    z = one_hot(pack[FEAT + 1 : FEAT + 2], coarse)
+    q0 = pack[SYS + count :]
     d1 = jnp.concatenate([d1l_ref[:, edge:], d1_ref[...], d1r_ref[:, : width - edge]], axis=1)
     d2 = jnp.concatenate([d2l_ref[:, edge:], d2_ref[...], d2r_ref[:, : width - edge]], axis=1)
     span = q0.shape[1]
@@ -459,21 +499,16 @@
     mine = slice(REACH * BS, REACH * BS + width)
     sol_ref[...] = x[:, mine]
 
-    base = FEAT + 8
-    systems = jnp.concatenate(
-        [left_ref[base:, edge:], own_ref[base:, :], right_ref[base:, : width - edge]], axis=1
-    )
-    target = (iota((count, 1), 0) == 0) & (scalar_ref[0] == 0)
-    right = jnp.where(target, x, systems)
-    weighted = x[:, mine] * coef_ref[...][:, 0:1]
+    systems = pack[SYS : SYS + count]
+    line = iota((count, 1), 0) + probe_ref[0] * count
+    right = jnp.where(line == 0, x, systems)
+    coef = jnp.where(line == 0, 0.5 / points, -0.5 / (sides - 1) / points)
+    weighted = x[:, mine] * coef
     r0, r1 = split(right, 2)
     w0, w1 = split(weighted, 2)
     near = jnp.concatenate([r0, r1, r0], axis=0).astype(bf16)
     mate = jnp.concatenate([w0, w0, w1], axis=0).astype(bf16)
-    pack = jnp.concatenate(
-        [left_ref[0:16, edge:], own_ref[0:16, :], right_ref[0:16, : width - edge]], axis=1
-    )
-    scaled = pack[0:FEAT] / column(len_ref, FEAT)
+    scaled = pack[0:FEAT]
     table = one_hot(pack[FEAT : FEAT + 1], TASKS)
     ones = jnp.ones((8, span), f32)
     terms = jnp.concatenate([scaled, ones, scaled * scaled], axis=0)
@@ -510,19 +545,25 @@
     lane = iota((TASKS, LANES), 1)
     lengths = jnp.concatenate([length_total, jnp.zeros((TASKS - FEAT, 1), f32)], axis=0)
     wide_tasks = jnp.concatenate([task_total, jnp.zeros((TASKS, LANES - TASKS), f32)], axis=1)
-    grad_ref[...] = jnp.where(lane == TASKS, lengths, wide_tasks)
-
-
-def call(body, outs, args, smem, name, scratch=(), flops=0):
+    value = jnp.where(lane == TASKS, lengths, wide_tasks)
+    for c in range(grad_ref.shape[0]):
+        grad_ref[c] = value
+
+
+MIB = 1024 * 1024
+
+
+def call(body, outs, args, name, smem=0, hbm=0, scratch=(), flops=0, limit=16):
     vm = pl.BlockSpec(memory_space=pltpu.VMEM)
     sm = pl.BlockSpec(memory_space=pltpu.SMEM)
+    far = pl.BlockSpec(memory_space=pltpu.HBM)
     return pl.pallas_call(
         body,
         out_shape=outs,
-        in_specs=[sm] * smem + [vm] * (len(args) - smem),
+        in_specs=[sm] * smem + [far] * hbm + [vm] * (len(args) - smem - hbm),
         out_specs=[vm] * len(outs),
         scratch_shapes=scratch,
-        compiler_params=pltpu.CompilerParams(vmem_limit_bytes=48 * 1024 * 1024),
+        compiler_params=pltpu.CompilerParams(vmem_limit_bytes=limit * MIB),
         cost_estimate=pl.CostEstimate(flops=flops, bytes_accessed=1 << 20, transcendentals=0),
         name=name,
     )(*args)
@@ -542,32 +583,36 @@
     blocks = width // BS
     coarse = coarse_inverse.shape[1]
     rows = count + coarse
-    pitch, lanes = pitch_of(coarse), lanes_of(coarse)
+    lanes = lanes_of(coarse)
+    ranks = lax.axis_size("pts")
+    sides = lax.axis_size("probe")
 
     def shape(*dims, kind=f32):
         return jax.ShapeDtypeStruct(dims, kind)
 
-    pack = jnp.concatenate(
-        [
-            features,
-            task_ids.astype(f32)[None],
-            aggregate.astype(f32)[None],
-            jnp.zeros((6, width), f32),
-            systems,
+    ids, which = task_ids[None], aggregate[None]
+    jac, pack, extra = call(
+        invert_kernel,
+        [shape(blocks, BS, BS), shape(SYS + 2 * count, width), shape(TASKS + FEAT, width)],
+        [features, ids, which, systems, task_cov, coarse_inverse, pattern, lengthscales, noise],
+        "invert",
+        hbm=9,
+        scratch=[
+            pltpu.VMEM((blocks, BS, BS), f32),
+            pltpu.VMEM(features.shape, f32),
+            pltpu.VMEM(ids.shape, jnp.int32),
+            pltpu.VMEM(which.shape, jnp.int32),
+            pltpu.VMEM(systems.shape, f32),
+            pltpu.VMEM(task_cov.shape, f32),
+            pltpu.VMEM(coarse_inverse.shape, f32),
+            pltpu.SMEM(pattern.shape, jnp.int32),
+            pltpu.SMEM(lengthscales.shape, f32),
+            pltpu.SMEM(noise.shape, f32),
+            pltpu.SemaphoreType.DMA((9,)),
         ],
-        axis=0,
+        flops=10**10,
     )
     pack_l, pack_r = both_sides(pack)
-    jac, pre = call(
-        invert_kernel,
-        [shape(blocks, BS, BS), shape(count, width)],
-        [pattern, lengthscales, noise, pack, task_cov],
-        3,
-        "invert",
-        [pltpu.VMEM((blocks, BS, BS), f32)],
-        flops=10**10,
-    )
-    pre_l, pre_r = both_sides(pre)
     hi, lo, sim = call(
         build_kernel,
         [
@@ -575,16 +620,15 @@
             shape(blocks, BAND, BS, kind=bf16),
             shape(blocks, BAND, BS),
         ],
-        [pattern, lengthscales, pack, pack_l, pack_r, task_cov],
-        2,
+        [pack, pack_l, pack_r, extra],
         "build",
         flops=3 * 10**9,
+        limit=24,
     )
     v0, d1 = call(
         first_kernel,
         [shape(rows, width), shape(rows, width)],
-        [noise, pack, pack_l, pack_r, pre, pre_l, pre_r, hi, lo, jac],
-        1,
+        [pack, pack_l, pack_r, extra, hi, lo, jac],
         "first",
         flops=10**9,
     )
@@ -592,45 +636,33 @@
     v1, d2 = call(
         second_kernel,
         [shape(rows, width), shape(rows, width)],
-        [noise, pack, d1, d1_l, d1_r, hi, lo, jac],
-        1,
+        [extra, d1, d1_l, d1_r, hi, lo, jac],
         "second",
         flops=10**9,
     )
     d2_l, d2_r = both_sides(d2)
-    own_rows = coarse_inverse.shape[0]
-    placed = lax.dynamic_update_slice(
-        jnp.zeros((rows, lanes), f32),
-        coarse_inverse,
-        (lax.axis_index("pts") * own_rows, 6 * pitch),
-    )
-    (partial_gram,) = call(
-        moment_kernel,
-        [shape(rows, lanes)],
-        [noise, pack, d2, d2_l, d2_r, hi, lo, pre, d1, v0, v1, placed],
-        1,
+    place = lax.axis_index("pts").astype(jnp.int32)[None]
+    probe = lax.axis_index("probe").astype(jnp.int32)[None]
+    (gram,) = call(
+        functools.partial(moment_kernel, held=coarse_inverse.shape[0]),
+        [shape(ranks, rows, lanes)],
+        [place, pack, extra, d2, d2_l, d2_r, hi, lo, d1, v0, v1],
         "moments",
+        smem=1,
         flops=10**9,
     )
-    gram = lax.psum(partial_gram, "pts")
-    probe = lax.axis_index("probe")
-    line = probe * count + jnp.arange(count, dtype=jnp.int32)
-    total_points = lax.axis_size("pts") * width
-    total_sides = lax.axis_size("probe") * count
-    coef = jnp.where(line == 0, 0.5, -0.5 / (total_sides - 1)) / total_points
-    coef = jnp.broadcast_to(coef[:, None], (count, LANES)).astype(f32)
+    gram = lax.all_to_all(gram, "pts", 0, 0, tiled=True)
     answer, grads = call(
-        final_kernel,
-        [shape(count, width), shape(TASKS, LANES)],
-        [
-            probe.astype(jnp.int32)[None], lengthscales, gram, pack, pack_l, pack_r, pre, pre_l,
-            pre_r, d1, d1_l, d1_r, d2, d2_l, d2_r, hi, lo, sim, coef, task_cov,
-        ],
-        2,
+        functools.partial(final_kernel, sides=sides * count, points=ranks * width),
+        [shape(count, width), shape(ranks * sides, TASKS, LANES)],
+        [probe, gram, pack, pack_l, pack_r, d1, d1_l, d1_r, d2, d2_l, d2_r, hi, lo, sim],
         "final",
+        smem=1,
         flops=10**9,
-    )
-    grads = lax.psum(grads, ("pts", "probe"))
+        limit=24,
+    )
+    grads = lax.all_to_all(grads, ("pts", "probe"), 0, 0, tiled=True)
+    grads = jnp.sum(grads, axis=0)
     return answer, grads[:FEAT, TASKS], grads[:, :TASKS]
 
 

time: 165 us -> 119 us (0.72)
  blocking collectives: 65.3 us -> 11.4 us
  waiting for transfers between devices: 8.88 us -> 26.9 us
  Pallas kernels: 42.5 us -> 34.2 us
  local copies, waits for them, and re-layouts: 19.7 us -> 22.5 us
  starting transfers between devices: 24.7 us -> 22.4 us
  other arithmetic: 1.89 us -> 0.02 us
    psum x2 -> x0, blocking collectives: 65.3 us -> none  [the longest x1 35.3 us: shards(): gram = lax.psum(partial_gram, 'pts')]
    all_to_all x0 -> x1, blocking collectives: none -> 11.4 us  [shards(): grads = lax.all_to_all(grads, ('pts', 'probe'), 0, 0, tiled=True)]
    all_to_all x0 -> x1, waiting for transfers between devices: none -> 10 us  [shards(): gram = lax.all_to_all(gram, 'pts', 0, 0, tiled=True)]
    pallas_call x6, Pallas kernels: 42.5 us -> 34.2 us  [call(): pl.pallas_call(body, out_shape=outs, in_specs=[sm] * smem + [far] * hbm +...]
    ppermute x8 -> x6, waiting for transfers between devices: 8.88 us -> 16.9 us  [both_sides(): return (lax.ppermute(cells, 'pts', up), lax.ppermute(cells, 'pts', down))]
    ppermute x8 -> x6, starting transfers between devices: 24.7 us -> 17.6 us  [both_sides(): return (lax.ppermute(cells, 'pts', up), lax.ppermute(cells, 'pts', down))]
    unnamed x56 -> x54, local copies, waits for them, and re-layouts: 14.9 us -> 20.5 us
    all_to_all x0 -> x1, starting transfers between devices: none -> 4.86 us  [shards(): gram = lax.all_to_all(gram, 'pts', 0, 0, tiled=True)]
  transfers between devices with their start and end apart: 8 -> 7, of which waited for: 3 -> 7; matrix products, arithmetic and copies ran while one was open for 1% -> 0% of each run, Pallas kernels for 13% -> 0%
where the time goes in v2:
time: 119 us; the launch traced here: 118 us
  Pallas kernels  34.2 us (29%)
  waiting for transfers between devices  26.9 us (23%)
  local copies, waits for them, and re-layouts  22.5 us (19%)
  starting transfers between devices  22.4 us (19%)
  blocking collectives  11.4 us (10%)
    pallas_call x6, Pallas kernels, call(): pl.pallas_call(body, out_shape=outs, in_specs=[sm] * smem + [far] * hbm +...  34.2 us
    unnamed x54, local copies, waits for them, and re-layouts  20.5 us
    ppermute x6, starting transfers between devices, both_sides(): return (lax.ppermute(cells, 'pts', up), lax.ppermute(cells, 'pts', down))  17.6 us
    ppermute x6, waiting for transfers between devices, both_sides(): return (lax.ppermute(cells, 'pts', up), lax.ppermute(cells, 'pts', down))  16.9 us
    all_to_all x1, blocking collectives, shards(): grads = lax.all_to_all(grads, ('pts', 'probe'), 0, 0, tiled=True)  11.4 us
    all_to_all x1, waiting for transfers between devices, shards(): gram = lax.all_to_all(gram, 'pts', 0, 0, tiled=True)  10 us
    all_to_all x1, starting transfers between devices, shards(): gram = lax.all_to_all(gram, 'pts', 0, 0, tiled=True)  4.86 us
  transfers between devices with their start and end apart: 7, of which 7 were waited for; matrix products, arithmetic and copies ran while one was open for 0% of the time, Pallas kernels for 0%

profile of v2, /device:TPU:0, one launch (start us, length us, event | category | flops | bytes accessed | tf_op | source)
XLA Modules:
  0.0 118.3 jit_solution(2509905124304908871)
XLA Ops:
  6.9 16.8 %invert.1 = (f32[3,256,256]{2,1,0:T(8,128)S(1)}, f32[48,768]{1,0:T(8,128)S(1)}, f32[24,768]{1,0:T(8,128)S(1)}) custom-call(f32[8,768]{1,0:T(8,128)S(1)} %copy-done.20, s32[1,768]{1,0:T(1,128)S(1)} %broadcast_in_dim.14.ids_hbm, s32[1,768]{1,0:T(1,128)S(1)} %broadcast_in_dim.15.agg_hbm, f32[16,768]{1,0:T(8,128)S(1)} %copy-done.19, f32[16,16]{1,0:T(8,128)S(1)} %copy-done.21, ...), custom_call_target="tpu_custom_call" | custom-call | flops 10000000000 | bytes 1048576 | tf_op jit(solution)/shard_map/invert/pallas_call | solution.py:560
  23.7 4.9 %collective-permute-start = (f32[48,768]{1,0:T(8,128)S(1)}, f32[48,768]{1,0:T(8,128)S(1)}, u32[]{:S(2)}, u32[]{:S(2)}) collective-permute-start(f32[48,768]{1,0:T(8,128)S(1)} %get-tuple-element.15.own_ref), channel_id=1, source_target_pairs={{0,2},{2,4},{4,6},{6,8},{8,10},{10,12},{12,14},{1,3},{3,5},{5,7},{... | collective-permute-start | bytes 442376 | tf_op jit(solution)/shard_map/ppermute | solution.py:576
  28.6 1.3 %collective-permute-start.1 = (f32[48,768]{1,0:T(8,128)S(1)}, f32[48,768]{1,0:T(8,128)S(1)}, u32[]{:S(2)}, u32[]{:S(2)}) collective-permute-start(f32[48,768]{1,0:T(8,128)S(1)} %get-tuple-element.15.own_ref), channel_id=1, source_target_pairs={{2,0},{4,2},{6,4},{8,6},{10,8},{12,10},{14,12},{3,1},{5,3},{7,5},{... | collective-permute-start | bytes 442376 | tf_op jit(solution)/shard_map/ppermute | solution.py:576
  29.9 1.8 %collective-permute-done.left_ref = f32[48,768]{1,0:T(8,128)S(1)} collective-permute-done((f32[48,768]{1,0:T(8,128)S(1)}, f32[48,768]{1,0:T(8,128)S(1)}, u32[]{:S(2)}, u32[]{:S(2)}) %collective-permute-start) | collective-permute-done | bytes 147488 | tf_op jit(solution)/shard_map/ppermute | solution.py:576
  31.7 4.1 %collective-permute-done.1.right_ref = f32[48,768]{1,0:T(8,128)S(1)} collective-permute-done((f32[48,768]{1,0:T(8,128)S(1)}, f32[48,768]{1,0:T(8,128)S(1)}, u32[]{:S(2)}, u32[]{:S(2)}) %collective-permute-start.1) | collective-permute-done | bytes 147488 | tf_op jit(solution)/shard_map/ppermute | solution.py:576
  35.8 2.1 %build.1 = (bf16[3,1792,256]{2,1,0:T(8,128)(2,1)S(1)}, bf16[3,1792,256]{2,1,0:T(8,128)(2,1)S(1)}, f32[3,1792,256]{2,1,0:T(8,128)S(1)}) custom-call(f32[48,768]{1,0:T(8,128)S(1)} %get-tuple-element.15.own_ref, f32[48,768]{1,0:T(8,128)S(1)} %collective-permute-done.left_ref, f32[48,768]{1,0:T(8,128)S(1)} %collective-permute-done.1.right_ref, ...), custom_call_target="tpu_custom_call" | custom-call | flops 3000000000 | bytes 1048576 | tf_op jit(solution)/shard_map/build/pallas_call | solution.py:560
  37.9 2.4 %copy-done.3 = f32[3,1792,256]{2,1,0:T(8,128)} copy-done((f32[3,1792,256]{2,1,0:T(8,128)}, f32[3,1792,256]{2,1,0:T(8,128)S(1)}, u32[]{:S(2)}) %copy-start.3) | copy-done | bytes 5505048
  40.3 1.5 %first.1 = (f32[40,768]{1,0:T(8,128)S(1)}, f32[40,768]{1,0:T(8,128)S(1)}) custom-call(f32[48,768]{1,0:T(8,128)S(1)} %get-tuple-element.15.own_ref, f32[48,768]{1,0:T(8,128)S(1)} %collective-permute-done.left_ref, f32[48,768]{1,0:T(8,128)S(1)} %collective-permute-done.1.right_ref, f32[24,768]{1,0:T(8,128)S(1)} %get-tuple-element.16.extra_ref, ...), custom_call_target="tpu_custom_call" | custom-call | flops 1000000000 | bytes 1048576 | tf_op jit(solution)/shard_map/first/pallas_call | solution.py:560
  41.8 4.3 %collective-permute-start.2 = (f32[40,768]{1,0:T(8,128)S(1)}, f32[40,768]{1,0:T(8,128)S(1)}, u32[]{:S(2)}, u32[]{:S(2)}) collective-permute-start(f32[40,768]{1,0:T(8,128)S(1)} %get-tuple-element.20.vec_ref.d1_ref), channel_id=1, source_target_pairs={{0,2},{2,4},{4,6},{6,8},{8,10},{10,12},{12,14},{1,3},{3,5},{5,7},{... | collective-permute-start | bytes 368648 | tf_op jit(solution)/shard_map/ppermute | solution.py:576
  46.2 1.5 %collective-permute-start.3 = (f32[40,768]{1,0:T(8,128)S(1)}, f32[40,768]{1,0:T(8,128)S(1)}, u32[]{:S(2)}, u32[]{:S(2)}) collective-permute-start(f32[40,768]{1,0:T(8,128)S(1)} %get-tuple-element.20.vec_ref.d1_ref), channel_id=1, source_target_pairs={{2,0},{4,2},{6,4},{8,6},{10,8},{12,10},{14,12},{3,1},{5,3},{7,5},{... | collective-permute-start | bytes 368648 | tf_op jit(solution)/shard_map/ppermute | solution.py:576
  47.7 0.9 collective-permute-done.2.vecl_ref.d1l_ref
  48.6 4.4 %collective-permute-done.3.vecr_ref.d1r_ref = f32[40,768]{1,0:T(8,128)S(1)} collective-permute-done((f32[40,768]{1,0:T(8,128)S(1)}, f32[40,768]{1,0:T(8,128)S(1)}, u32[]{:S(2)}, u32[]{:S(2)}) %collective-permute-start.3) | collective-permute-done | bytes 122912 | tf_op jit(solution)/shard_map/ppermute | solution.py:576
  52.9 2.2 %second.1 = (f32[40,768]{1,0:T(8,128)S(1)}, f32[40,768]{1,0:T(8,128)}) custom-call(f32[24,768]{1,0:T(8,128)S(1)} %get-tuple-element.16.extra_ref, f32[40,768]{1,0:T(8,128)S(1)} %get-tuple-element.20.vec_ref.d1_ref, f32[40,768]{1,0:T(8,128)S(1)} %collective-permute-done.2.vecl_ref.d1l_ref, f32[40,768]{1,0:T(8,128)S(1)} %collective-permute-done.3.vecr_ref.d1r_ref, ...), custom_call_target="tpu_custom_call" | custom-call | flops 1000000000 | bytes 1048576 | tf_op jit(solution)/shard_map/second/pallas_call | solution.py:560
  55.8 4.3 %collective-permute-start.4 = (f32[40,768]{1,0:T(8,128)}, f32[40,768]{1,0:T(8,128)S(1)}, u32[]{:S(2)}, u32[]{:S(2)}) collective-permute-start(f32[40,768]{1,0:T(8,128)} %get-tuple-element.21.vec_ref.d2_ref), channel_id=1, source_target_pairs={{0,2},{2,4},{4,6},{6,8},{8,10},{10,12},{12,14},{1,3},{3,5},{5,7},{... | collective-permute-start | bytes 368648 | tf_op jit(solution)/shard_map/ppermute | solution.py:576
  60.1 1.3 %collective-permute-start.5 = (f32[40,768]{1,0:T(8,128)}, f32[40,768]{1,0:T(8,128)S(1)}, u32[]{:S(2)}, u32[]{:S(2)}) collective-permute-start(f32[40,768]{1,0:T(8,128)} %get-tuple-element.21.vec_ref.d2_ref), channel_id=1, source_target_pairs={{2,0},{4,2},{6,4},{8,6},{10,8},{12,10},{14,12},{3,1},{5,3},{7,5},{... | collective-permute-start | bytes 368648 | tf_op jit(solution)/shard_map/ppermute | solution.py:576
  61.4 1.4 %collective-permute-done.4.vecl_ref.d2l_ref = f32[40,768]{1,0:T(8,128)S(1)} collective-permute-done((f32[40,768]{1,0:T(8,128)}, f32[40,768]{1,0:T(8,128)S(1)}, u32[]{:S(2)}, u32[]{:S(2)}) %collective-permute-start.4) | collective-permute-done | bytes 122912 | tf_op jit(solution)/shard_map/ppermute | solution.py:576
  62.8 4.2 %collective-permute-done.5.vecr_ref.d2r_ref = f32[40,768]{1,0:T(8,128)S(1)} collective-permute-done((f32[40,768]{1,0:T(8,128)}, f32[40,768]{1,0:T(8,128)S(1)}, u32[]{:S(2)}, u32[]{:S(2)}) %collective-permute-start.5) | collective-permute-done | bytes 122912 | tf_op jit(solution)/shard_map/ppermute | solution.py:576
  67.1 1.8 %copy-done.1 = bf16[3,1792,256]{2,1,0:T(8,128)(2,1)S(1)} copy-done((bf16[3,1792,256]{2,1,0:T(8,128)(2,1)S(1)}, bf16[3,1792,256]{2,1,0:T(8,128)(2,1)}, u32[]{:S(2)}) %copy-start.1) | copy-done | bytes 2752536
  68.9 0.9 copy-done.16
  69.8 0.9 copy-done.18
  70.7 3.4 %moments.1 = f32[8,40,256]{2,1,0:T(8,128)} custom-call(s32[1]{0:T(128)} %bitcast.1.place_ref, f32[48,768]{1,0:T(8,128)S(1)} %get-tuple-element.15.own_ref, f32[24,768]{1,0:T(8,128)S(1)} %get-tuple-element.16.extra_ref, f32[40,768]{1,0:T(8,128)} %get-tuple-element.21.vec_ref.d2_ref, f32[40,768]{1,0:T(8,128)S(1)} %collective-permute-done.4.vecl_ref.d2l_ref, ...), custom_call_target="tpu_custom_call" | custom-call | flops 1000000000 | bytes 1048576 | tf_op jit(solution)/shard_map/moments/pallas_call | solution.py:560
  74.1 4.9 %all-to-all-start = ((f32[8,40,256]{2,1,0:T(8,128)}), f32[8,40,256]{2,1,0:T(8,128)S(1)}, u32[]{:S(2)}, u32[]{:S(2)}) async-start(f32[8,40,256]{2,1,0:T(8,128)} %moments.1), calls=%async_computation | async-start | bytes 655360 | tf_op jit(solution)/shard_map/all_to_all | solution.py:654
  78.9 10.0 %all-to-all-done.gram_ref = f32[8,40,256]{2,1,0:T(8,128)S(1)} async-done(((f32[8,40,256]{2,1,0:T(8,128)}), f32[8,40,256]{2,1,0:T(8,128)S(1)}, u32[]{:S(2)}, u32[]{:S(2)}) %all-to-all-start) | async-done | bytes 327712 | tf_op jit(solution)/shard_map/all_to_all | solution.py:654
  89.0 1.8 %copy-done.2 = bf16[3,1792,256]{2,1,0:T(8,128)(2,1)S(1)} copy-done((bf16[3,1792,256]{2,1,0:T(8,128)(2,1)S(1)}, bf16[3,1792,256]{2,1,0:T(8,128)(2,1)}, u32[]{:S(2)}) %copy-start.2) | copy-done | bytes 2752536
  90.7 2.6 %copy-done.4 = f32[3,1792,256]{2,1,0:T(8,128)S(1)} copy-done((f32[3,1792,256]{2,1,0:T(8,128)S(1)}, f32[3,1792,256]{2,1,0:T(8,128)}, u32[]{:S(2)}) %copy-start.4) | copy-done | bytes 5505048
  93.3 0.9 copy-done.6
  94.2 0.9 copy-done.8
  95.1 0.9 copy-done.10
  96.0 0.9 copy-done.12
  96.9 0.9 copy-done.14
  97.8 8.3 %final.1 = (f32[16,768]{1,0:T(8,128)}, f32[16,16,128]{2,1,0:T(8,128)S(1)}) custom-call(s32[1]{0:T(128)} %bitcast.probe_ref, f32[8,40,256]{2,1,0:T(8,128)S(1)} %all-to-all-done.gram_ref, f32[48,768]{1,0:T(8,128)S(1)} %get-tuple-element.15.own_ref, f32[48,768]{1,0:T(8,128)S(1)} %collective-permute-done.left_ref, f32[48,768]{1,0:T(8,128)S(1)} %copy-done.6, ...), custom_call_target="tpu_custom_call" | custom-call | flops 1000000000 | bytes 1048576 | tf_op jit(solution)/shard_map/final/pallas_call | solution.py:560
  106.1 11.4 %all_to_all.10 = f32[16,16,128]{2,1,0:T(8,128)S(1)} all-to-all(f32[16,16,128]{2,1,0:T(8,128)S(1)} %get-tuple-element.26), channel_id=1, replica_groups=mesh['groups'=2,'pts'=8,'probe'=2] {'pts','probe'}, dimensions={0} | all-to-all | bytes 262144 | tf_op jit(solution)/shard_map/all_to_all | solution.py:664
  (47 shorter events, 7.7 us)
Async XLA Ops:
  2.0 0.8 copy-start.19
  2.8 0.7 copy-start.20
  3.5 0.7 copy-start.21
  4.2 0.7 copy-start.22
  4.9 0.7 copy-start.23
  6.3 0.7 copy-start.25
  23.7 8.0 %collective-permute-start = (f32[48,768]{1,0:T(8,128)S(1)}, f32[48,768]{1,0:T(8,128)S(1)}, u32[]{:S(2)}, u32[]{:S(2)}) collective-permute-start(f32[48,768]{1,0:T(8,128)S(1)} %get-tuple-element.15.own_ref), channel_id=1, source_target_pairs={{0,2},{2,4},{4,6},{6,8},{8,10},{10,12},{12,14},{1,3},{3,5},{5,7},{... | collective-permute-start | bytes 442376 | tf_op jit(solution)/shard_map/ppermute | solution.py:576
  28.6 7.2 %collective-permute-start.1 = (f32[48,768]{1,0:T(8,128)S(1)}, f32[48,768]{1,0:T(8,128)S(1)}, u32[]{:S(2)}, u32[]{:S(2)}) collective-permute-start(f32[48,768]{1,0:T(8,128)S(1)} %get-tuple-element.15.own_ref), channel_id=1, source_target_pairs={{2,0},{4,2},{6,4},{8,6},{10,8},{12,10},{14,12},{3,1},{5,3},{7,5},{... | collective-permute-start | bytes 442376 | tf_op jit(solution)/shard_map/ppermute | solution.py:576
  35.8 4.5 %copy-start.5 = (f32[48,768]{1,0:T(8,128)}, f32[48,768]{1,0:T(8,128)S(1)}, u32[]{:S(2)}) copy-start(f32[48,768]{1,0:T(8,128)S(1)} %collective-permute-done.1.right_ref) | copy-start | bytes 442372
  37.9 2.4 %copy-start.3 = (f32[3,1792,256]{2,1,0:T(8,128)}, f32[3,1792,256]{2,1,0:T(8,128)S(1)}, u32[]{:S(2)}) copy-start(f32[3,1792,256]{2,1,0:T(8,128)S(1)} %get-tuple-element.24.sim_ref) | copy-start | bytes 16515076
  40.3 12.6 %copy-start = (bf16[3,1792,256]{2,1,0:T(8,128)(2,1)}, bf16[3,1792,256]{2,1,0:T(8,128)(2,1)S(1)}, u32[]{:S(2)}) copy-start(bf16[3,1792,256]{2,1,0:T(8,128)(2,1)S(1)} %get-tuple-element.18.lo_ref) | copy-start | bytes 8257540
  41.8 13.3 %copy-start.15 = (f32[40,768]{1,0:T(8,128)}, f32[40,768]{1,0:T(8,128)S(1)}, u32[]{:S(2)}) copy-start(f32[40,768]{1,0:T(8,128)S(1)} %get-tuple-element.22.v0_ref) | copy-start | bytes 368644
  41.8 6.7 %collective-permute-start.2 = (f32[40,768]{1,0:T(8,128)S(1)}, f32[40,768]{1,0:T(8,128)S(1)}, u32[]{:S(2)}, u32[]{:S(2)}) collective-permute-start(f32[40,768]{1,0:T(8,128)S(1)} %get-tuple-element.20.vec_ref.d1_ref), channel_id=1, source_target_pairs={{0,2},{2,4},{4,6},{6,8},{8,10},{10,12},{12,14},{1,3},{3,5},{5,7},{... | collective-permute-start | bytes 368648 | tf_op jit(solution)/shard_map/ppermute | solution.py:576
  46.2 6.8 %collective-permute-start.3 = (f32[40,768]{1,0:T(8,128)S(1)}, f32[40,768]{1,0:T(8,128)S(1)}, u32[]{:S(2)}, u32[]{:S(2)}) collective-permute-start(f32[40,768]{1,0:T(8,128)S(1)} %get-tuple-element.20.vec_ref.d1_ref), channel_id=1, source_target_pairs={{2,0},{4,2},{6,4},{8,6},{10,8},{12,10},{14,12},{3,1},{5,3},{7,5},{... | collective-permute-start | bytes 368648 | tf_op jit(solution)/shard_map/ppermute | solution.py:576
  48.6 6.5 %copy-start.7 = (f32[40,768]{1,0:T(8,128)}, f32[40,768]{1,0:T(8,128)S(1)}, u32[]{:S(2)}) copy-start(f32[40,768]{1,0:T(8,128)S(1)} %collective-permute-done.2.vecl_ref.d1l_ref) | copy-start | bytes 368644
  52.9 2.2 %copy-start.9 = (f32[40,768]{1,0:T(8,128)}, f32[40,768]{1,0:T(8,128)S(1)}, u32[]{:S(2)}) copy-start(f32[40,768]{1,0:T(8,128)S(1)} %collective-permute-done.3.vecr_ref.d1r_ref) | copy-start | bytes 368644
  55.8 7.1 %collective-permute-start.4 = (f32[40,768]{1,0:T(8,128)}, f32[40,768]{1,0:T(8,128)S(1)}, u32[]{:S(2)}, u32[]{:S(2)}) collective-permute-start(f32[40,768]{1,0:T(8,128)} %get-tuple-element.21.vec_ref.d2_ref), channel_id=1, source_target_pairs={{0,2},{2,4},{4,6},{6,8},{8,10},{10,12},{12,14},{1,3},{3,5},{5,7},{... | collective-permute-start | bytes 368648 | tf_op jit(solution)/shard_map/ppermute | solution.py:576
  60.1 7.0 %collective-permute-start.5 = (f32[40,768]{1,0:T(8,128)}, f32[40,768]{1,0:T(8,128)S(1)}, u32[]{:S(2)}, u32[]{:S(2)}) collective-permute-start(f32[40,768]{1,0:T(8,128)} %get-tuple-element.21.vec_ref.d2_ref), channel_id=1, source_target_pairs={{2,0},{4,2},{6,4},{8,6},{10,8},{12,10},{14,12},{3,1},{5,3},{7,5},{... | collective-permute-start | bytes 368648 | tf_op jit(solution)/shard_map/ppermute | solution.py:576
  62.8 11.2 %copy-start.11 = (f32[40,768]{1,0:T(8,128)}, f32[40,768]{1,0:T(8,128)S(1)}, u32[]{:S(2)}) copy-start(f32[40,768]{1,0:T(8,128)S(1)} %collective-permute-done.4.vecl_ref.d2l_ref) | copy-start | bytes 368644
  67.1 7.0 %copy-start.13 = (f32[40,768]{1,0:T(8,128)}, f32[40,768]{1,0:T(8,128)S(1)}, u32[]{:S(2)}) copy-start(f32[40,768]{1,0:T(8,128)S(1)} %collective-permute-done.5.vecr_ref.d2r_ref) | copy-start | bytes 368644
  67.1 1.8 %copy-start.1 = (bf16[3,1792,256]{2,1,0:T(8,128)(2,1)S(1)}, bf16[3,1792,256]{2,1,0:T(8,128)(2,1)}, u32[]{:S(2)}) copy-start(bf16[3,1792,256]{2,1,0:T(8,128)(2,1)} %copy-done) | copy-start | bytes 8257540
  68.9 0.9 copy-start.16
  69.8 0.9 copy-start.18
  74.1 14.9 %all-to-all-start = ((f32[8,40,256]{2,1,0:T(8,128)}), f32[8,40,256]{2,1,0:T(8,128)S(1)}, u32[]{:S(2)}, u32[]{:S(2)}) async-start(f32[8,40,256]{2,1,0:T(8,128)} %moments.1), calls=%async_computation | async-start | bytes 655360 | tf_op jit(solution)/shard_map/all_to_all | solution.py:654
  89.0 1.8 %copy-start.2 = (bf16[3,1792,256]{2,1,0:T(8,128)(2,1)S(1)}, bf16[3,1792,256]{2,1,0:T(8,128)(2,1)}, u32[]{:S(2)}) copy-start(bf16[3,1792,256]{2,1,0:T(8,128)(2,1)} %copy-done) | copy-start | bytes 8257540
  90.7 2.6 %copy-start.4 = (f32[3,1792,256]{2,1,0:T(8,128)S(1)}, f32[3,1792,256]{2,1,0:T(8,128)}, u32[]{:S(2)}) copy-start(f32[3,1792,256]{2,1,0:T(8,128)} %copy-done.3) | copy-start | bytes 16515076
  93.3 0.9 copy-start.6
  94.2 0.9 copy-start.8
  95.1 0.9 copy-start.10
  96.0 0.9 copy-start.12
  96.9 0.9 copy-start.14
  117.6 0.7 copy-start.26
  (2 other events, 1.3 us)

commit v3 on v2

--- a/solution.py
+++ b/solution.py
@@ -157,6 +157,13 @@
     return cells
 
 
+def fetch(pairs, sems):
+    copies = [pltpu.make_async_copy(a, b, sems.at[i]) for i, (a, b) in enumerate(pairs)]
+    for copy in copies:
+        copy.start()
+    return copies
+
+
 def invert_kernel(
     feat_hbm, ids_hbm, agg_hbm, sys_hbm, cov_hbm, coarse_hbm, pat_hbm, len_hbm, noise_hbm,
     jac_ref, pack_ref, extra_ref,
@@ -169,13 +176,11 @@
         (pat_hbm, pat_ref), (len_hbm, len_ref), (noise_hbm, noise_ref), (coarse_hbm, coarse_ref),
         (sys_hbm, sys_ref),
     ]
-    copies = [pltpu.make_async_copy(a, b, sems.at[i]) for i, (a, b) in enumerate(pairs)]
-    for copy in copies:
-        copy.start()
-    for copy in copies:
+    for copy in fetch(pairs, sems):
         copy.wait()
     scaled = feat_ref[...] / column(len_ref, FEAT)
-    ids = ids_ref[...].astype(f32)
+    ids = ids_ref[...].astype(f32).reshape(1, width)
+    which = agg_ref[...].astype(f32).reshape(1, width)
     table = one_hot(ids, TASKS)
     noise = noise_row(noise_ref, ids)
     c0, c1, c2 = split(cov_ref[...], 3)
@@ -189,7 +194,7 @@
             weights = jnp.where(places == m * SLOTS + o, weight(pat_ref, m, o), weights)
     pack_ref[0:FEAT, :] = scaled
     pack_ref[FEAT : 2 * FEAT, :] = jnp.where(
-        rows == 0, ids, jnp.where(rows == 1, agg_ref[...].astype(f32), 0.0)
+        rows == 0, ids, jnp.where(rows == 1, which, 0.0)
     )
     count = sys_ref.shape[0]
     pack_ref[SYS : SYS + count, :] = sys_ref[...]
@@ -251,7 +256,9 @@
         pack_ref[SYS + count :, at] = dot(sys_ref[:, at], inv, precision=highest)
 
 
-def build_kernel(own_ref, left_ref, right_ref, extra_ref, hi_ref, lo_ref, sim_ref):
+def build_kernel(
+    own_ref, left_ref, right_ref, extra_ref, hi_ref, lo_ref, sim_hbm, sim_ref, sems
+):
     blocks = hi_ref.shape[0]
     pack = jnp.concatenate([left_ref[0:SYS, :], own_ref[0:SYS, :], right_ref[0:SYS, :]], axis=1)
     scaled = pack[0:FEAT]
@@ -276,6 +283,9 @@
             sim_ref[m, rows, :] = similar
             hi_ref[m, rows, :] = head
             lo_ref[m, rows, :] = (kernel - head.astype(f32)).astype(bf16)
+        pltpu.make_async_copy(sim_ref.at[m], sim_hbm.at[m], sems.at[m]).start()
+    for m in range(blocks):
+        pltpu.make_async_copy(sim_ref.at[m], sim_hbm.at[m], sems.at[m]).wait()
 
 
 def operate(vectors, noise, own, hi_ref, lo_ref):
@@ -329,79 +339,98 @@
     next_ref[...] = smooth(image, jac_ref)
 
 
-def moment_kernel(
-    place_ref, own_ref, extra_ref, vec_ref, vecl_ref, vecr_ref, hi_ref, lo_ref, d1_ref, v0_ref,
-    v1_ref, out_ref, *, held,
-):
-    width = own_ref.shape[1]
+def pitch_of(coarse):
+    return coarse + 1
+
+
+def shape_of(count, coarse):
+    lanes = -(-5 * pitch_of(coarse) // LANES) * LANES
+    return count + coarse, max(count, coarse), lanes, -(-pitch_of(coarse) // BASE) * BASE
+
+
+def moment(vectors, images, pairs):
+    count = pairs.shape[0]
+    table = dot(images, vectors, NT, lax.Precision.HIGH)
+    own = jnp.sum(pairs, axis=1, keepdims=True)
+    if images.shape[0] > count:
+        own = jnp.concatenate([own, jnp.zeros((images.shape[0] - count, 1), f32)], axis=0)
+    return jnp.concatenate([table, own], axis=1)
+
+
+def spread_out(parts, lanes):
+    rows, pitch = next(iter(parts.values())).shape
+    cells = [parts.get(k, jnp.zeros((rows, pitch), f32)) for k in range(5)]
+    if lanes > 5 * pitch:
+        cells.append(jnp.zeros((rows, lanes - 5 * pitch), f32))
+    return jnp.concatenate(cells, axis=1)
+
+
+def early_moments_kernel(own_ref, d1_ref, v0_ref, out_ref):
     count = (own_ref.shape[0] - SYS) // 2
-    rows = vec_ref.shape[0]
-    coarse = rows - count
-    copies, _, lanes = out_ref.shape
-    pitch = pitch_of(coarse)
-    edge = width - REACH * BS
-    ext = jnp.concatenate([vecl_ref[:, edge:], vec_ref[...], vecr_ref[:, : width - edge]], axis=1)
-    noise = extra_ref[TASKS : TASKS + 1, :]
-    d2 = vec_ref[...]
-    v2 = operate(ext, noise, d2, hi_ref, lo_ref)
+    coarse = d1_ref.shape[0] - count
+    rows, below, lanes, _ = shape_of(count, coarse)
     systems = own_ref[SYS : SYS + count, :]
     pre = own_ref[SYS + count :, :]
     z = one_hot(own_ref[FEAT + 1 : FEAT + 2, :], coarse)
-    d1, v0, v1 = d1_ref[...], v0_ref[...], v1_ref[...]
-    gap = jnp.zeros((pitch - coarse, width), f32)
-
-    def stacked(parts):
-        cells = []
-        for k in range(lanes // pitch):
-            if k in parts:
-                cells.append(jnp.concatenate([parts[k], gap], axis=0))
-            else:
-                cells.append(jnp.zeros((pitch, width), f32))
-        return jnp.concatenate(cells, axis=0)
-
-    high = lax.Precision.HIGH
-    residual = jnp.concatenate([systems, jnp.zeros((coarse, width), f32)], axis=0)
-    total = dot(v0, stacked({0: z, 1: d1[count:]}), NT, high)
-    total = total + dot(v1, stacked({2: d1[count:], 3: d2[count:]}), NT, high)
-    total = total + dot(v2, stacked({4: d2[count:]}), NT, high)
-    total = total + dot(residual, stacked({5: z}), NT, high)
-    own = [
-        pre * v0[:count],
-        d1[:count] * v0[:count],
-        d1[:count] * v1[:count],
-        d2[:count] * v1[:count],
-        d2[:count] * v2[:count],
-        systems * pre,
-    ]
-    lane = iota((count, lanes), 1)
-    top = total[:count]
-    for k, value in enumerate(own):
-        top = jnp.where(lane == k * pitch + coarse, jnp.sum(value, axis=1, keepdims=True), top)
-    value = jnp.concatenate([top, total[count:]], axis=0)
-    row = iota((rows, 1), 0)
+    d1, v0 = d1_ref[...], v0_ref[...]
+    parts = {
+        0: moment(z, v0, pre * v0[:count]),
+        1: moment(d1[count:], v0, d1[:count] * v0[:count]),
+    }
+    out_ref[0:rows, :] = spread_out(parts, lanes)
+    start = spread_out({0: moment(z, systems, systems * pre)}, lanes)
+    if below > count:
+        start = jnp.concatenate([start, jnp.zeros((below - count, lanes), f32)], axis=0)
+    out_ref[rows:, :] = start
+
+
+def late_moments_kernel(before_ref, d1_ref, d2_ref, v1_ref, out_ref, *, count):
+    rows = d1_ref.shape[0]
+    d1, d2, v1 = d1_ref[...], d2_ref[...], v1_ref[...]
+    parts = {
+        2: moment(d1[count:], v1, d1[:count] * v1[:count]),
+        3: moment(d2[count:], v1, d2[:count] * v1[:count]),
+    }
+    out_ref[0:rows, :] = before_ref[0:rows, :] + spread_out(parts, out_ref.shape[1])
+    out_ref[rows:, :] = before_ref[rows:, :]
+
+
+def third_kernel(
+    place_ref, extra_ref, before_ref, vec_ref, vecl_ref, vecr_ref, hi_ref, lo_ref, out_ref,
+    *, count, held,
+):
+    width = vec_ref.shape[1]
+    coarse = vec_ref.shape[0] - count
+    rows, below, lanes, stand = shape_of(count, coarse)
+    edge = width - REACH * BS
+    ext = jnp.concatenate([vecl_ref[:, edge:], vec_ref[...], vecr_ref[:, : width - edge]], axis=1)
+    d2 = vec_ref[...]
+    v2 = operate(ext, extra_ref[TASKS : TASKS + 1, :], d2, hi_ref, lo_ref)
+    last = spread_out({4: moment(d2[count:], v2, d2[:count] * v2[:count])}, lanes)
+    top = before_ref[0:rows, :] + last
+    row = iota((below, 1), 0)
     start = place_ref[0] * held
-    front = jnp.zeros((1, 6 * pitch), f32)
-    back = jnp.zeros((1, lanes - 6 * pitch - coarse), f32)
+    bottom = before_ref[rows:, :]
+    front = jnp.zeros((1, stand), f32)
+    back = jnp.zeros((1, lanes - stand - coarse), f32)
     for r in range(held):
         line = extra_ref[TASKS + 2 + r : TASKS + 3 + r, 0:coarse]
         line = jnp.concatenate([front, line, back], axis=1)
-        value = value + jnp.where(row == start + r, line, 0.0)
-    for c in range(copies):
-        out_ref[c] = value
-
-
-def pitch_of(coarse):
-    return BASE if coarse < BASE else -(-(coarse + 1) // LANES) * LANES
-
-
-def lanes_of(coarse):
-    return -(-7 * pitch_of(coarse) // LANES) * LANES
+        bottom = bottom + jnp.where(row == start + r, line, 0.0)
+    for c in range(out_ref.shape[0]):
+        out_ref[c, 0:rows, :] = top
+        out_ref[c, rows:, :] = bottom
 
 
 def final_kernel(
-    probe_ref, gram_ref, own_ref, left_ref, right_ref, d1_ref, d1l_ref, d1r_ref, d2_ref, d2l_ref,
-    d2r_ref, hi_ref, lo_ref, sim_ref, sol_ref, grad_ref, *, sides, points,
+    probe_ref, gram_ref, *refs, sides, points,
 ):
+    far, (sol_ref, grad_ref), near_refs, sems = refs[:12], refs[12:14], refs[14:26], refs[26]
+    copies = fetch(list(zip(far, near_refs)), sems)
+    (
+        own_ref, left_ref, right_ref, d1_ref, d1l_ref, d1r_ref, d2_ref, d2l_ref, d2r_ref,
+        hi_ref, lo_ref, sim_ref,
+    ) = near_refs
     width = own_ref.shape[1]
     count = (own_ref.shape[0] - SYS) // 2
     rows = d1_ref.shape[0]
@@ -413,6 +442,9 @@
     gram = gram_ref[0]
     for c in range(1, gram_ref.shape[0]):
         gram = gram + gram_ref[c]
+    _, _, lanes, stand = shape_of(count, coarse)
+    bottom = gram[rows:, :]
+    gram = jnp.concatenate([gram[:rows], jnp.zeros((rows, wide), f32)], axis=1)
     lane = iota((1, wide), 1)
     slot, inside = lane // pitch, lane % pitch
     live = lane < 3 * pitch
@@ -434,14 +466,11 @@
         axis=0,
     )
     block0 = lane < pitch
-    inverse = gram[:coarse, 6 * pitch : 7 * pitch]
-    if pitch < wide:
-        inverse = jnp.concatenate([inverse, jnp.zeros((coarse, wide - pitch), f32)], axis=1)
-    inverse = jnp.where(lane < coarse, inverse, 0.0)
+    inverse = bottom[:coarse, stand : stand + coarse]
+    inverse = jnp.concatenate([inverse, jnp.zeros((coarse, wide - coarse), f32)], axis=1)
     inverse = jnp.concatenate([inverse, jnp.zeros((wide - coarse, wide), f32)], axis=0)
-    start = gram[:count, 5 * pitch : 6 * pitch]
-    if pitch < wide:
-        start = jnp.concatenate([start, jnp.zeros((count, wide - pitch), f32)], axis=1)
+    start = bottom[:count, :pitch]
+    start = jnp.concatenate([start, jnp.zeros((count, wide - pitch), f32)], axis=1)
     against = jnp.where(
         block0, start, jnp.where(live, pltpu.roll(jnp.where(live, own[0], 0.0), pitch, axis=1), 0.0)
     )
@@ -481,6 +510,8 @@
             direction = pre + (gamma_new / gamma) * direction
             gamma = gamma_new
 
+    for copy in copies[:9]:
+        copy.wait()
     pack = jnp.concatenate(
         [left_ref[:, edge:], own_ref[...], right_ref[:, : width - edge]], axis=1
     )
@@ -489,11 +520,21 @@
     d1 = jnp.concatenate([d1l_ref[:, edge:], d1_ref[...], d1r_ref[:, : width - edge]], axis=1)
     d2 = jnp.concatenate([d2l_ref[:, edge:], d2_ref[...], d2r_ref[:, : width - edge]], axis=1)
     span = q0.shape[1]
-    pad = jnp.zeros((pitch - coarse, span), f32)
-    basis = [z, pad, d1[count:], pad, d2[count:], pad]
-    if wide > 3 * pitch:
-        basis.append(jnp.zeros((wide - 3 * pitch, span), f32))
-    x = dot(jnp.where(is_vec, answer, 0.0), jnp.concatenate(basis, axis=0), precision=highest)
+    step = -(-coarse // FEAT) * FEAT
+    deep = -(-3 * step // LANES) * LANES
+    parts, basis = [], []
+    for i, rest in enumerate((z, d1[count:], d2[count:])):
+        parts.append(answer[:, i * pitch : i * pitch + coarse])
+        basis.append(rest)
+        if step > coarse:
+            parts.append(jnp.zeros((count, step - coarse), f32))
+            basis.append(jnp.zeros((step - coarse, span), f32))
+    if deep > 3 * step:
+        parts.append(jnp.zeros((count, deep - 3 * step), f32))
+        basis.append(jnp.zeros((deep - 3 * step, span), f32))
+    x = dot(
+        jnp.concatenate(parts, axis=1), jnp.concatenate(basis, axis=0), precision=highest
+    )
     x = x + scalars(answer, 0) * q0 + scalars(answer, 1) * d1[:count]
     x = x + scalars(answer, 2) * d2[:count]
     mine = slice(REACH * BS, REACH * BS + width)
@@ -518,6 +559,8 @@
     heads = jnp.concatenate([t0, pad8], axis=0).astype(bf16)
     tables = table.astype(bf16)
     high = 32
+    for copy in copies[9:]:
+        copy.wait()
     length_total = jnp.zeros((FEAT, 1), f32)
     task_total = jnp.zeros((TASKS, TASKS), f32)
     for m in range(blocks):
@@ -553,15 +596,19 @@
 MIB = 1024 * 1024
 
 
-def call(body, outs, args, name, smem=0, hbm=0, scratch=(), flops=0, limit=16):
+def call(body, outs, args, name, smem=0, hbm=0, far_outs=0, scratch=(), flops=0, limit=16):
+    if hbm:
+        args = args[:-hbm] + [pltpu.with_memory_space_constraint(a, pltpu.HBM) for a in args[-hbm:]]
+    if far_outs:
+        outs = outs[:-far_outs] + [pltpu.HBM(o.shape, o.dtype) for o in outs[-far_outs:]]
     vm = pl.BlockSpec(memory_space=pltpu.VMEM)
     sm = pl.BlockSpec(memory_space=pltpu.SMEM)
     far = pl.BlockSpec(memory_space=pltpu.HBM)
     return pl.pallas_call(
         body,
         out_shape=outs,
-        in_specs=[sm] * smem + [far] * hbm + [vm] * (len(args) - smem - hbm),
-        out_specs=[vm] * len(outs),
+        in_specs=[sm] * smem + [vm] * (len(args) - smem - hbm) + [far] * hbm,
+        out_specs=[vm] * (len(outs) - far_outs) + [far] * far_outs,
         scratch_shapes=scratch,
         compiler_params=pltpu.CompilerParams(vmem_limit_bytes=limit * MIB),
         cost_estimate=pl.CostEstimate(flops=flops, bytes_accessed=1 << 20, transcendentals=0),
@@ -583,25 +630,24 @@
     blocks = width // BS
     coarse = coarse_inverse.shape[1]
     rows = count + coarse
-    lanes = lanes_of(coarse)
+    top, below, lanes, _ = shape_of(count, coarse)
     ranks = lax.axis_size("pts")
     sides = lax.axis_size("probe")
 
     def shape(*dims, kind=f32):
         return jax.ShapeDtypeStruct(dims, kind)
 
-    ids, which = task_ids[None], aggregate[None]
     jac, pack, extra = call(
         invert_kernel,
         [shape(blocks, BS, BS), shape(SYS + 2 * count, width), shape(TASKS + FEAT, width)],
-        [features, ids, which, systems, task_cov, coarse_inverse, pattern, lengthscales, noise],
+        [features, task_ids, aggregate, systems, task_cov, coarse_inverse, pattern, lengthscales, noise],
         "invert",
         hbm=9,
         scratch=[
             pltpu.VMEM((blocks, BS, BS), f32),
             pltpu.VMEM(features.shape, f32),
-            pltpu.VMEM(ids.shape, jnp.int32),
-            pltpu.VMEM(which.shape, jnp.int32),
+            pltpu.VMEM(task_ids.shape, jnp.int32),
+            pltpu.VMEM(aggregate.shape, jnp.int32),
             pltpu.VMEM(systems.shape, f32),
             pltpu.VMEM(task_cov.shape, f32),
             pltpu.VMEM(coarse_inverse.shape, f32),
@@ -622,6 +668,8 @@
         ],
         [pack, pack_l, pack_r, extra],
         "build",
+        far_outs=1,
+        scratch=[pltpu.VMEM((blocks, BAND, BS), f32), pltpu.SemaphoreType.DMA((blocks,))],
         flops=3 * 10**9,
         limit=24,
     )
@@ -633,6 +681,9 @@
         flops=10**9,
     )
     d1_l, d1_r = both_sides(d1)
+    (early,) = call(
+        early_moments_kernel, [shape(top + below, lanes)], [pack, d1, v0], "early", flops=10**9
+    )
     v1, d2 = call(
         second_kernel,
         [shape(rows, width), shape(rows, width)],
@@ -641,25 +692,36 @@
         flops=10**9,
     )
     d2_l, d2_r = both_sides(d2)
+    (late,) = call(
+        functools.partial(late_moments_kernel, count=count),
+        [shape(top + below, lanes)],
+        [early, d1, d2, v1],
+        "late",
+        flops=10**9,
+    )
     place = lax.axis_index("pts").astype(jnp.int32)[None]
     probe = lax.axis_index("probe").astype(jnp.int32)[None]
     (gram,) = call(
-        functools.partial(moment_kernel, held=coarse_inverse.shape[0]),
-        [shape(ranks, rows, lanes)],
-        [place, pack, extra, d2, d2_l, d2_r, hi, lo, d1, v0, v1],
-        "moments",
+        functools.partial(third_kernel, count=count, held=coarse_inverse.shape[0]),
+        [shape(ranks, top + below, lanes)],
+        [place, extra, late, d2, d2_l, d2_r, hi, lo],
+        "third",
         smem=1,
         flops=10**9,
     )
     gram = lax.all_to_all(gram, "pts", 0, 0, tiled=True)
+    stored = [pack, pack_l, pack_r, d1, d1_l, d1_r, d2, d2_l, d2_r, hi, lo, sim]
     answer, grads = call(
         functools.partial(final_kernel, sides=sides * count, points=ranks * width),
         [shape(count, width), shape(ranks * sides, TASKS, LANES)],
-        [probe, gram, pack, pack_l, pack_r, d1, d1_l, d1_r, d2, d2_l, d2_r, hi, lo, sim],
+        [probe, gram] + stored,
         "final",
         smem=1,
+        hbm=len(stored),
+        scratch=[pltpu.VMEM(a.shape, a.dtype) for a in stored]
+        + [pltpu.SemaphoreType.DMA((len(stored),))],
         flops=10**9,
-        limit=24,
+        limit=32,
     )
     grads = lax.all_to_all(grads, ("pts", "probe"), 0, 0, tiled=True)
     grads = jnp.sum(grads, axis=0)

time: 119 us -> 104 us (0.87)
  local copies, waits for them, and re-layouts: 22.5 us -> 4.06 us
  waiting for transfers between devices: 26.9 us -> 19.5 us
  Pallas kernels: 34.2 us -> 41 us
  starting transfers between devices: 22.4 us -> 26.3 us
    unnamed x54 -> x32, local copies, waits for them, and re-layouts: 20.5 us -> 3.36 us
    pallas_call x6 -> x8, Pallas kernels: 34.2 us -> 41 us  [call(): pl.pallas_call(body, out_shape=outs, in_specs=[sm] * smem + [vm] * (len(a...]
    ppermute x6, waiting for transfers between devices: 16.9 us -> 11 us  [both_sides(): return (lax.ppermute(cells, 'pts', up), lax.ppermute(cells, 'pts', down))]
    ppermute x6, starting transfers between devices: 17.6 us -> 20.1 us  [both_sides(): return (lax.ppermute(cells, 'pts', up), lax.ppermute(cells, 'pts', down))]
    all_to_all x1, waiting for transfers between devices: 10 us -> 8.53 us  [shards(): gram = lax.all_to_all(gram, 'pts', 0, 0, tiled=True)]
    all_to_all x1, starting transfers between devices: 4.86 us -> 6.25 us  [shards(): gram = lax.all_to_all(gram, 'pts', 0, 0, tiled=True)]
    broadcast_in_dim x2 -> x0, local copies, waits for them, and re-layouts: 1.38 us -> none  [shards(): ids, which = (task_ids[None], aggregate[None])]
  transfers between devices with their start and end apart: 7 -> 7, of which waited for: 7 -> 6; matrix products, arithmetic and copies ran while one was open for 0% -> 0% of each run, Pallas kernels for 0% -> 2%
where the time goes in v3:
time: 104 us; the launch traced here: 103 us
  Pallas kernels  41 us (39%)
  starting transfers between devices  26.3 us (25%)
  waiting for transfers between devices  19.5 us (19%)
  blocking collectives  11.4 us (11%)
  local copies, waits for them, and re-layouts  4.06 us (4%)
    pallas_call x8, Pallas kernels, call(): pl.pallas_call(body, out_shape=outs, in_specs=[sm] * smem + [vm] * (len(a...  41 us
    ppermute x6, starting transfers between devices, both_sides(): return (lax.ppermute(cells, 'pts', up), lax.ppermute(cells, 'pts', down))  20.1 us
    all_to_all x1, blocking collectives, shards(): grads = lax.all_to_all(grads, ('pts', 'probe'), 0, 0, tiled=True)  11.4 us
    ppermute x6, waiting for transfers between devices, both_sides(): return (lax.ppermute(cells, 'pts', up), lax.ppermute(cells, 'pts', down))  11 us
    all_to_all x1, waiting for transfers between devices, shards(): gram = lax.all_to_all(gram, 'pts', 0, 0, tiled=True)  8.53 us
    all_to_all x1, starting transfers between devices, shards(): gram = lax.all_to_all(gram, 'pts', 0, 0, tiled=True)  6.25 us
    unnamed x32, local copies, waits for them, and re-layouts  3.36 us
  transfers between devices with their start and end apart: 7, of which 6 were waited for; matrix products, arithmetic and copies ran while one was open for 0% of the time, Pallas kernels for 2%

profile of v3, /device:TPU:0, one launch (start us, length us, event | category | flops | bytes accessed | tf_op | source)
XLA Modules:
  0.0 103.1 jit_solution(5526100954570480167)
XLA Ops:
  0.6 17.1 %invert.1 = (f32[3,256,256]{2,1,0:T(8,128)S(1)}, f32[48,768]{1,0:T(8,128)S(1)}, f32[24,768]{1,0:T(8,128)S(1)}) custom-call(f32[8,768]{1,0:T(8,128)} %feat_hbm.1, s32[768]{0:T(1024)} %ids_hbm.1, s32[768]{0:T(1024)} %agg_hbm.1, f32[16,768]{1,0:T(8,128)} %sys_hbm.1, f32[16,16]{1,0:T(8,128)} %cov_hbm.1, f32[3,24]{1,0:T(4,128)} %coarse_hbm.1, s32[3,7]{1,0:T(4,128)} %pat_hbm.1, ...), custom_call_target="tpu_custom_call" | custom-call | flops 10000000000 | bytes 1048576 | tf_op jit(solution)/shard_map/invert/pallas_call | solution.py:607
  17.7 1.3 %collective-permute-start.1 = (f32[48,768]{1,0:T(8,128)S(1)}, f32[48,768]{1,0:T(8,128)S(1)}, u32[]{:S(2)}, u32[]{:S(2)}) collective-permute-start(f32[48,768]{1,0:T(8,128)S(1)} %get-tuple-element.16.own_ref.refs_0_), channel_id=1, source_target_pairs={{2,0},{4,2},{6,4},{8,6},{10,8},{12,10},{14,12},{3,1},{5,3},{7,5},{... | collective-permute-start | bytes 442376 | tf_op jit(solution)/shard_map/ppermute | solution.py:623
  19.0 5.5 %collective-permute-start = (f32[48,768]{1,0:T(8,128)S(1)}, f32[48,768]{1,0:T(8,128)S(1)}, u32[]{:S(2)}, u32[]{:S(2)}) collective-permute-start(f32[48,768]{1,0:T(8,128)S(1)} %get-tuple-element.16.own_ref.refs_0_), channel_id=1, source_target_pairs={{0,2},{2,4},{4,6},{6,8},{8,10},{10,12},{12,14},{1,3},{3,5},{5,7},{... | collective-permute-start | bytes 442376 | tf_op jit(solution)/shard_map/ppermute | solution.py:623
  24.6 1.9 %collective-permute-done.1.right_ref.refs_2_ = f32[48,768]{1,0:T(8,128)S(1)} collective-permute-done((f32[48,768]{1,0:T(8,128)S(1)}, f32[48,768]{1,0:T(8,128)S(1)}, u32[]{:S(2)}, u32[]{:S(2)}) %collective-permute-start.1) | collective-permute-done | bytes 147488 | tf_op jit(solution)/shard_map/ppermute | solution.py:623
  26.5 3.3 %collective-permute-done.left_ref.refs_1_ = f32[48,768]{1,0:T(8,128)S(1)} collective-permute-done((f32[48,768]{1,0:T(8,128)S(1)}, f32[48,768]{1,0:T(8,128)S(1)}, u32[]{:S(2)}, u32[]{:S(2)}) %collective-permute-start) | collective-permute-done | bytes 147488 | tf_op jit(solution)/shard_map/ppermute | solution.py:623
  29.8 3.4 %build.1 = (bf16[3,1792,256]{2,1,0:T(8,128)(2,1)S(1)}, bf16[3,1792,256]{2,1,0:T(8,128)(2,1)S(1)}, f32[3,1792,256]{2,1,0:T(8,128)}) custom-call(f32[48,768]{1,0:T(8,128)S(1)} %get-tuple-element.16.own_ref.refs_0_, f32[48,768]{1,0:T(8,128)S(1)} %collective-permute-done.left_ref.refs_1_, f32[48,768]{1,0:T(8,128)S(1)} %collective-permute-done.1.right_ref.refs_2_, ...), custom_call_target="tpu_custom_call" | custom-call | flops 3000000000 | bytes 1048576 | tf_op jit(solution)/shard_map/build/pallas_call | solution.py:607
  33.2 2.4 %first.1 = (f32[40,768]{1,0:T(8,128)S(1)}, f32[40,768]{1,0:T(8,128)}) custom-call(f32[48,768]{1,0:T(8,128)S(1)} %get-tuple-element.16.own_ref.refs_0_, f32[48,768]{1,0:T(8,128)S(1)} %collective-permute-done.left_ref.refs_1_, f32[48,768]{1,0:T(8,128)S(1)} %collective-permute-done.1.right_ref.refs_2_, f32[24,768]{1,0:T(8,128)S(1)} %get-tuple-element.15.extra_ref, ...), custom_call_target="tpu_custom_call" | custom-call | flops 1000000000 | bytes 1048576 | tf_op jit(solution)/shard_map/first/pallas_call | solution.py:607
  35.6 0.6 copy-done.13
  36.3 1.3 %collective-permute-start.3 = (f32[40,768]{1,0:T(8,128)}, f32[40,768]{1,0:T(8,128)}, u32[]{:S(2)}, u32[]{:S(2)}) collective-permute-start(f32[40,768]{1,0:T(8,128)} %get-tuple-element.20.d1_ref.vec_ref.refs_3_), channel_id=1, source_target_pairs={{2,0},{4,2},{6,4},{8,6},{10,8},{12,10},{14,12},{3,1},{5,3},{7,5},{... | collective-permute-start | bytes 368648 | tf_op jit(solution)/shard_map/ppermute | solution.py:623
  37.6 5.7 %collective-permute-start.2 = (f32[40,768]{1,0:T(8,128)}, f32[40,768]{1,0:T(8,128)}, u32[]{:S(2)}, u32[]{:S(2)}) collective-permute-start(f32[40,768]{1,0:T(8,128)} %get-tuple-element.20.d1_ref.vec_ref.refs_3_), channel_id=1, source_target_pairs={{0,2},{2,4},{4,6},{6,8},{8,10},{10,12},{12,14},{1,3},{3,5},{5,7},{... | collective-permute-start | bytes 368648 | tf_op jit(solution)/shard_map/ppermute | solution.py:623
  43.2 1.2 %collective-permute-done.3.vecr_ref.refs_5_ = f32[40,768]{1,0:T(8,128)} collective-permute-done((f32[40,768]{1,0:T(8,128)}, f32[40,768]{1,0:T(8,128)}, u32[]{:S(2)}, u32[]{:S(2)}) %collective-permute-start.3) | collective-permute-done | bytes 122912 | tf_op jit(solution)/shard_map/ppermute | solution.py:623
  44.5 2.8 %collective-permute-done.2.vecl_ref.refs_4_ = f32[40,768]{1,0:T(8,128)} collective-permute-done((f32[40,768]{1,0:T(8,128)}, f32[40,768]{1,0:T(8,128)}, u32[]{:S(2)}, u32[]{:S(2)}) %collective-permute-start.2) | collective-permute-done | bytes 122912 | tf_op jit(solution)/shard_map/ppermute | solution.py:623
  47.3 1.8 %copy-done.2 = bf16[3,1792,256]{2,1,0:T(8,128)(2,1)S(1)} copy-done((bf16[3,1792,256]{2,1,0:T(8,128)(2,1)S(1)}, bf16[3,1792,256]{2,1,0:T(8,128)(2,1)}, u32[]{:S(2)}) %copy-start.2) | copy-done | bytes 2752536
  49.0 0.9 copy-done.4
  49.9 2.5 %second.1 = (f32[40,768]{1,0:T(8,128)S(1)}, f32[40,768]{1,0:T(8,128)S(1)}) custom-call(f32[24,768]{1,0:T(8,128)S(1)} %copy-done.4, f32[40,768]{1,0:T(8,128)} %get-tuple-element.20.d1_ref.vec_ref.refs_3_, f32[40,768]{1,0:T(8,128)} %collective-permute-done.2.vecl_ref.refs_4_, f32[40,768]{1,0:T(8,128)} %collective-permute-done.3.vecr_ref.refs_5_, ...), custom_call_target="tpu_custom_call" | custom-call | flops 1000000000 | bytes 1048576 | tf_op jit(solution)/shard_map/second/pallas_call | solution.py:607
  52.5 0.0 copy-start.10
  52.5 1.3 %collective-permute-start.5 = (f32[40,768]{1,0:T(8,128)S(1)}, f32[40,768]{1,0:T(8,128)S(1)}, u32[]{:S(2)}, u32[]{:S(2)}) collective-permute-start(f32[40,768]{1,0:T(8,128)S(1)} %get-tuple-element.22.d2_ref.vec_ref.refs_6_), channel_id=1, source_target_pairs={{2,0},{4,2},{6,4},{8,6},{10,8},{12,10},{14,12},{3,1},{5,3},{7,5},{... | collective-permute-start | bytes 368648 | tf_op jit(solution)/shard_map/ppermute | solution.py:623
  53.8 5.0 %collective-permute-start.4 = (f32[40,768]{1,0:T(8,128)S(1)}, f32[40,768]{1,0:T(8,128)S(1)}, u32[]{:S(2)}, u32[]{:S(2)}) collective-permute-start(f32[40,768]{1,0:T(8,128)S(1)} %get-tuple-element.22.d2_ref.vec_ref.refs_6_), channel_id=1, source_target_pairs={{0,2},{2,4},{4,6},{6,8},{8,10},{10,12},{12,14},{1,3},{3,5},{5,7},{... | collective-permute-start | bytes 368648 | tf_op jit(solution)/shard_map/ppermute | solution.py:623
  58.8 0.0 copy-done.7
  58.8 0.0 copy-done.14
  58.8 1.2 %early.1.before_ref = f32[64,128]{1,0:T(8,128)S(1)} custom-call(f32[48,768]{1,0:T(8,128)S(1)} %copy-done.7, f32[40,768]{1,0:T(8,128)} %get-tuple-element.20.d1_ref.vec_ref.refs_3_, f32[40,768]{1,0:T(8,128)S(1)} %copy-done.14), custom_call_target="tpu_custom_call" | custom-call | flops 1000000000 | bytes 1048576 | tf_op jit(solution)/shard_map/early/pallas_call | solution.py:607
  60.1 1.3 %late.1.before_ref = f32[64,128]{1,0:T(8,128)S(1)} custom-call(f32[64,128]{1,0:T(8,128)S(1)} %early.1.before_ref, f32[40,768]{1,0:T(8,128)} %get-tuple-element.20.d1_ref.vec_ref.refs_3_, f32[40,768]{1,0:T(8,128)S(1)} %get-tuple-element.22.d2_ref.vec_ref.refs_6_, f32[40,768]{1,0:T(8,128)S(1)} %get-tuple-element.23.v1_ref), custom_call_target="tpu_custom_call" | custom-call | flops 1000000000 | bytes 1048576 | tf_op jit(solution)/shard_map/late/pallas_call | solution.py:607
  61.3 0.0 collective-permute-done.5.vecr_ref.refs_8_
  61.4 1.8 %collective-permute-done.4.vecl_ref.refs_7_ = f32[40,768]{1,0:T(8,128)S(1)} collective-permute-done((f32[40,768]{1,0:T(8,128)S(1)}, f32[40,768]{1,0:T(8,128)S(1)}, u32[]{:S(2)}, u32[]{:S(2)}) %collective-permute-start.4) | collective-permute-done | bytes 122912 | tf_op jit(solution)/shard_map/ppermute | solution.py:623
  63.2 0.0 copy-done.5
  63.2 2.0 %third.1 = f32[8,64,128]{2,1,0:T(8,128)} custom-call(s32[1]{0:T(128)} %bitcast.1.place_ref, f32[24,768]{1,0:T(8,128)S(1)} %copy-done.5, f32[64,128]{1,0:T(8,128)S(1)} %late.1.before_ref, f32[40,768]{1,0:T(8,128)S(1)} %get-tuple-element.22.d2_ref.vec_ref.refs_6_, f32[40,768]{1,0:T(8,128)S(1)} %collective-permute-done.4.vecl_ref.refs_7_, ...), custom_call_target="tpu_custom_call" | custom-call | flops 1000000000 | bytes 1048576 | tf_op jit(solution)/shard_map/third/pallas_call | solution.py:607
  65.2 6.2 %all-to-all-start = ((f32[8,64,128]{2,1,0:T(8,128)}), f32[8,64,128]{2,1,0:T(8,128)S(1)}, u32[]{:S(2)}, u32[]{:S(2)}) async-start(f32[8,64,128]{2,1,0:T(8,128)} %third.1), calls=%async_computation | async-start | bytes 524288 | tf_op jit(solution)/shard_map/all_to_all | solution.py:712
  71.4 8.5 %all-to-all-done.gram_ref = f32[8,64,128]{2,1,0:T(8,128)S(1)} async-done(((f32[8,64,128]{2,1,0:T(8,128)}), f32[8,64,128]{2,1,0:T(8,128)S(1)}, u32[]{:S(2)}, u32[]{:S(2)}) %all-to-all-start) | async-done | bytes 262176 | tf_op jit(solution)/shard_map/all_to_all | solution.py:712
  79.9 11.1 %final.1 = (f32[16,768]{1,0:T(8,128)}, f32[16,16,128]{2,1,0:T(8,128)S(1)}) custom-call(s32[1]{0:T(128)} %bitcast.probe_ref, f32[8,64,128]{2,1,0:T(8,128)S(1)} %all-to-all-done.gram_ref, f32[48,768]{1,0:T(8,128)} %copy-done.6, f32[48,768]{1,0:T(8,128)} %copy-done.9, f32[48,768]{1,0:T(8,128)} %copy-done.8, f32[40,768]{1,0:T(8,128)} %get-tuple-element.20.d1_ref.vec_ref.refs_3_, ...), custom_call_target="tpu_custom_call" | custom-call | flops 1000000000 | bytes 1048576 | tf_op jit(solution)/shard_map/final/pallas_call | solution.py:607
  91.0 11.4 %all_to_all.10 = f32[16,16,128]{2,1,0:T(8,128)S(1)} all-to-all(f32[16,16,128]{2,1,0:T(8,128)S(1)} %get-tuple-element.26), channel_id=1, replica_groups=mesh['groups'=2,'pts'=8,'probe'=2] {'pts','probe'}, dimensions={0} | all-to-all | bytes 262144 | tf_op jit(solution)/shard_map/all_to_all | solution.py:726
  102.4 0.0 copy-start.15
  102.4 0.7 slice_reduce_fusion
  (25 shorter events, 0.1 us)
Async XLA Ops:
  17.7 15.5 %copy-start.3 = (f32[24,768]{1,0:T(8,128)}, f32[24,768]{1,0:T(8,128)S(1)}, u32[]{:S(2)}) copy-start(f32[24,768]{1,0:T(8,128)S(1)} %get-tuple-element.15.extra_ref) | copy-start | bytes 221188
  17.7 15.5 %copy-start.6 = (f32[48,768]{1,0:T(8,128)}, f32[48,768]{1,0:T(8,128)S(1)}, u32[]{:S(2)}) copy-start(f32[48,768]{1,0:T(8,128)S(1)} %get-tuple-element.16.own_ref.refs_0_) | copy-start | bytes 442372
  17.7 8.7 %collective-permute-start.1 = (f32[48,768]{1,0:T(8,128)S(1)}, f32[48,768]{1,0:T(8,128)S(1)}, u32[]{:S(2)}, u32[]{:S(2)}) collective-permute-start(f32[48,768]{1,0:T(8,128)S(1)} %get-tuple-element.16.own_ref.refs_0_), channel_id=1, source_target_pairs={{2,0},{4,2},{6,4},{8,6},{10,8},{12,10},{14,12},{3,1},{5,3},{7,5},{... | collective-permute-start | bytes 442376 | tf_op jit(solution)/shard_map/ppermute | solution.py:623
  19.0 10.7 %collective-permute-start = (f32[48,768]{1,0:T(8,128)S(1)}, f32[48,768]{1,0:T(8,128)S(1)}, u32[]{:S(2)}, u32[]{:S(2)}) collective-permute-start(f32[48,768]{1,0:T(8,128)S(1)} %get-tuple-element.16.own_ref.refs_0_), channel_id=1, source_target_pairs={{0,2},{2,4},{4,6},{6,8},{8,10},{10,12},{12,14},{1,3},{3,5},{5,7},{... | collective-permute-start | bytes 442376 | tf_op jit(solution)/shard_map/ppermute | solution.py:623
  26.5 6.7 %copy-start.8 = (f32[48,768]{1,0:T(8,128)}, f32[48,768]{1,0:T(8,128)S(1)}, u32[]{:S(2)}) copy-start(f32[48,768]{1,0:T(8,128)S(1)} %collective-permute-done.1.right_ref.refs_2_) | copy-start | bytes 442372
  29.8 3.4 %copy-start.9 = (f32[48,768]{1,0:T(8,128)}, f32[48,768]{1,0:T(8,128)S(1)}, u32[]{:S(2)}) copy-start(f32[48,768]{1,0:T(8,128)S(1)} %collective-permute-done.left_ref.refs_1_) | copy-start | bytes 442372
  33.2 2.5 %copy-start.1 = (bf16[3,1792,256]{2,1,0:T(8,128)(2,1)}, bf16[3,1792,256]{2,1,0:T(8,128)(2,1)S(1)}, u32[]{:S(2)}) copy-start(bf16[3,1792,256]{2,1,0:T(8,128)(2,1)S(1)} %get-tuple-element.18.lo_ref.refs_10_) | copy-start | bytes 8257540
  33.2 30.0 %copy-start = (bf16[3,1792,256]{2,1,0:T(8,128)(2,1)}, bf16[3,1792,256]{2,1,0:T(8,128)(2,1)S(1)}, u32[]{:S(2)}) copy-start(bf16[3,1792,256]{2,1,0:T(8,128)(2,1)S(1)} %get-tuple-element.17.hi_ref.refs_9_) | copy-start | bytes 8257540
  35.6 0.6 copy-start.13
  36.3 8.2 %collective-permute-start.3 = (f32[40,768]{1,0:T(8,128)}, f32[40,768]{1,0:T(8,128)}, u32[]{:S(2)}, u32[]{:S(2)}) collective-permute-start(f32[40,768]{1,0:T(8,128)} %get-tuple-element.20.d1_ref.vec_ref.refs_3_), channel_id=1, source_target_pairs={{2,0},{4,2},{6,4},{8,6},{10,8},{12,10},{14,12},{3,1},{5,3},{7,5},{... | collective-permute-start | bytes 368648 | tf_op jit(solution)/shard_map/ppermute | solution.py:623
  37.6 9.7 %collective-permute-start.2 = (f32[40,768]{1,0:T(8,128)}, f32[40,768]{1,0:T(8,128)}, u32[]{:S(2)}, u32[]{:S(2)}) collective-permute-start(f32[40,768]{1,0:T(8,128)} %get-tuple-element.20.d1_ref.vec_ref.refs_3_), channel_id=1, source_target_pairs={{0,2},{2,4},{4,6},{6,8},{8,10},{10,12},{12,14},{1,3},{3,5},{5,7},{... | collective-permute-start | bytes 368648 | tf_op jit(solution)/shard_map/ppermute | solution.py:623
  47.2 1.8 %copy-start.2 = (bf16[3,1792,256]{2,1,0:T(8,128)(2,1)S(1)}, bf16[3,1792,256]{2,1,0:T(8,128)(2,1)}, u32[]{:S(2)}) copy-start(bf16[3,1792,256]{2,1,0:T(8,128)(2,1)} %copy-done.1) | copy-start | bytes 8257540
  49.0 0.9 copy-start.4
  49.9 8.9 %copy-start.7 = (f32[48,768]{1,0:T(8,128)S(1)}, f32[48,768]{1,0:T(8,128)}, u32[]{:S(2)}) copy-start(f32[48,768]{1,0:T(8,128)} %copy-done.6) | copy-start | bytes 442372
  49.9 8.9 %copy-start.14 = (f32[40,768]{1,0:T(8,128)S(1)}, f32[40,768]{1,0:T(8,128)}, u32[]{:S(2)}) copy-start(f32[40,768]{1,0:T(8,128)} %copy-done.13) | copy-start | bytes 368644
  52.5 10.7 %copy-start.10 = (f32[40,768]{1,0:T(8,128)}, f32[40,768]{1,0:T(8,128)S(1)}, u32[]{:S(2)}) copy-start(f32[40,768]{1,0:T(8,128)S(1)} %get-tuple-element.22.d2_ref.vec_ref.refs_6_) | copy-start | bytes 368644
  52.5 8.9 %collective-permute-start.5 = (f32[40,768]{1,0:T(8,128)S(1)}, f32[40,768]{1,0:T(8,128)S(1)}, u32[]{:S(2)}, u32[]{:S(2)}) collective-permute-start(f32[40,768]{1,0:T(8,128)S(1)} %get-tuple-element.22.d2_ref.vec_ref.refs_6_), channel_id=1, source_target_pairs={{2,0},{4,2},{6,4},{8,6},{10,8},{12,10},{14,12},{3,1},{5,3},{7,5},{... | collective-permute-start | bytes 368648 | tf_op jit(solution)/shard_map/ppermute | solution.py:623
  53.8 9.4 %collective-permute-start.4 = (f32[40,768]{1,0:T(8,128)S(1)}, f32[40,768]{1,0:T(8,128)S(1)}, u32[]{:S(2)}, u32[]{:S(2)}) collective-permute-start(f32[40,768]{1,0:T(8,128)S(1)} %get-tuple-element.22.d2_ref.vec_ref.refs_6_), channel_id=1, source_target_pairs={{0,2},{2,4},{4,6},{6,8},{8,10},{10,12},{12,14},{1,3},{3,5},{5,7},{... | collective-permute-start | bytes 368648 | tf_op jit(solution)/shard_map/ppermute | solution.py:623
  60.1 3.1 %copy-start.5 = (f32[24,768]{1,0:T(8,128)S(1)}, f32[24,768]{1,0:T(8,128)}, u32[]{:S(2)}) copy-start(f32[24,768]{1,0:T(8,128)} %copy-done.3) | copy-start | bytes 221188
  61.4 3.8 %copy-start.11 = (f32[40,768]{1,0:T(8,128)}, f32[40,768]{1,0:T(8,128)S(1)}, u32[]{:S(2)}) copy-start(f32[40,768]{1,0:T(8,128)S(1)} %collective-permute-done.5.vecr_ref.refs_8_) | copy-start | bytes 368644
  63.1 2.0 %copy-start.12 = (f32[40,768]{1,0:T(8,128)}, f32[40,768]{1,0:T(8,128)S(1)}, u32[]{:S(2)}) copy-start(f32[40,768]{1,0:T(8,128)S(1)} %collective-permute-done.4.vecl_ref.refs_7_) | copy-start | bytes 368644
  65.2 14.8 %all-to-all-start = ((f32[8,64,128]{2,1,0:T(8,128)}), f32[8,64,128]{2,1,0:T(8,128)S(1)}, u32[]{:S(2)}, u32[]{:S(2)}) async-start(f32[8,64,128]{2,1,0:T(8,128)} %third.1), calls=%async_computation | async-start | bytes 524288 | tf_op jit(solution)/shard_map/all_to_all | solution.py:712
  102.4 0.7 copy-start.15

commit v4 on v3

--- a/solution.py
+++ b/solution.py
@@ -79,9 +79,8 @@
     rows = iota(scaled.shape, 0)
     norms = jnp.where(rows == 0, n0, jnp.where(rows == 1, n1, jnp.where(rows == 2, n2, 0.0)))
     pad = jnp.zeros((LANES - 7 * FEAT - 3 * TASKS, scaled.shape[1]), f32)
-    return jnp.concatenate(
-        [s0, s0, s1, s1, s0, s2, norms, table, table, table, pad], axis=0
-    ).astype(bf16)
+    stack = jnp.concatenate([s0, s0, s1, s1, s0, s2, norms, table, table, table, pad], axis=0)
+    return stack.T.astype(bf16)
 
 
 def own_stack(scaled, picked):
@@ -97,7 +96,11 @@
         [jnp.zeros((7 * FEAT, count), f32)] + split(picked, 3) + [jnp.zeros((tail, count), f32)],
         axis=0,
     ).astype(bf16)
-    return left, right, -0.5 * jnp.sum(scaled * scaled, axis=0, keepdims=True)
+    sides = [
+        jnp.concatenate([left[:, i : i + BS], right[:, i : i + BS]], axis=1)
+        for i in range(0, count, BS)
+    ]
+    return sides, -0.5 * jnp.sum(scaled * scaled, axis=0, keepdims=True)
 
 
 def small_inverse(p):
@@ -208,13 +211,12 @@
         tail = jnp.where(rows == 2 + r, inverse[r : r + 1], tail)
     extra_ref[TASKS : TASKS + FEAT, :] = tail
     near = near_stack(scaled, table)
-    left, right, norm = own_stack(scaled, picked)
+    mates, norm = own_stack(scaled, picked)
     eye = iota((BS, BS), 0) == iota((BS, BS), 1)
     for m in range(blocks):
         at = slice(m * BS, (m + 1) * BS)
-        exponent = dot(near[:, at], left[:, at], TN) + norm[:, at]
-        pair = dot(near[:, at], right[:, at], TN)
-        block = weight(pat_ref, m, REACH) * jnp.exp(exponent) * pair
+        both = dot(near[at], mates[m])
+        block = weight(pat_ref, m, REACH) * jnp.exp(both[:, :BS] + norm[:, at]) * both[:, BS:]
         work[m] = block + jnp.where(eye, noise[:, at], 0.0)
     seg = iota((BASE, LANES), 1) // BASE
     wide = iota((BASE, BS), 1)
@@ -252,34 +254,39 @@
     for m in range(blocks):
         at = slice(m * BS, (m + 1) * BS)
         inv = -work[m]
-        jac_ref[m] = inv
+        for i, part in enumerate(split(inv, 3)):
+            jac_ref[i, m] = part.astype(bf16)
         pack_ref[SYS + count :, at] = dot(sys_ref[:, at], inv, precision=highest)
 
 
-def build_kernel(
-    own_ref, left_ref, right_ref, extra_ref, hi_ref, lo_ref, sim_hbm, sim_ref, sems
-):
+def own_places(m):
+    return [(j, j, REACH + j - m) for j in range(REACH)]
+
+
+def halo_places(m):
+    lefts = [(j - m, j, j - m) for j in range(m, REACH)]
+    return lefts + [(REACH - m + j, REACH + j, 2 * REACH - m + j) for j in range(m + 1)]
+
+
+def build_kernel(*refs, places, sides):
+    cells, (own_ref, extra_ref) = refs[:sides], refs[sides : sides + 2]
+    hi_ref, lo_ref, sim_hbm, sim_ref, sems = refs[sides + 2 :]
     blocks = hi_ref.shape[0]
-    pack = jnp.concatenate([left_ref[0:SYS, :], own_ref[0:SYS, :], right_ref[0:SYS, :]], axis=1)
-    scaled = pack[0:FEAT]
-    table = one_hot(pack[FEAT : FEAT + 1], TASKS)
-    near = near_stack(scaled, table)
-    width = blocks * BS
-    left, right, norm = own_stack(own_ref[0:FEAT, :], extra_ref[0:TASKS, :])
+    near = []
+    for ref in cells:
+        near.append(near_stack(ref[0:FEAT, :], one_hot(ref[FEAT : FEAT + 1, :], TASKS)))
+    mates, norm = own_stack(own_ref[0:FEAT, :], extra_ref[0:TASKS, :])
     weights = extra_ref[TASKS + 1 : TASKS + 2, :]
-    edge = width - REACH * BS
     for m in range(blocks):
-        at = slice(m * BS, (m + 1) * BS)
-        for o in range(SLOTS):
-            j = edge + (m + o) * BS
-            part = near[:, j : j + BS]
-            exponent = dot(part, left[:, at], TN) + norm[:, at]
-            pair = dot(part, right[:, at], TN)
+        for row, j, o in places(m):
+            part = near[j // REACH][(j % REACH) * BS : (j % REACH + 1) * BS]
+            both = dot(part, mates[m])
             place = m * SLOTS + o
+            exponent = both[:, :BS] + norm[:, m * BS : (m + 1) * BS]
             similar = weights[:, place : place + 1] * jnp.exp(exponent)
-            kernel = similar * pair
+            kernel = similar * both[:, BS:]
             head = kernel.astype(bf16)
-            rows = slice(o * BS, (o + 1) * BS)
+            rows = slice(row * BS, (row + 1) * BS)
             sim_ref[m, rows, :] = similar
             hi_ref[m, rows, :] = head
             lo_ref[m, rows, :] = (kernel - head.astype(f32)).astype(bf16)
@@ -288,53 +295,55 @@
         pltpu.make_async_copy(sim_ref.at[m], sim_hbm.at[m], sems.at[m]).wait()
 
 
-def operate(vectors, noise, own, hi_ref, lo_ref):
-    rows = vectors.shape[0]
-    head, tail = (part.astype(bf16) for part in split(vectors, 2))
-    both = jnp.concatenate([head, tail], axis=0)
+def operate(own, left, right, noise, own_hi, own_lo, halo_hi, halo_lo):
+    rows = own.shape[0]
+    width = own.shape[1]
+
+    def pieces(vectors):
+        head, tail = split(vectors, 2)
+        return jnp.concatenate([head, tail], axis=0).astype(bf16)
+
+    mine, lefts, rights = pieces(own), pieces(left), pieces(right)
     out = []
-    for m in range(hi_ref.shape[0]):
-        at = slice(m * BS, m * BS + BAND)
-        first = dot(both[:, at], hi_ref[m])
-        out.append(first[:rows] + first[rows:] + dot(head[:, at], lo_ref[m]))
+    for m in range(REACH):
+        beyond = jnp.concatenate([lefts[:, m * BS :], rights[:, : (m + 1) * BS]], axis=1)
+        first = dot(mine, own_hi[m]) + dot(beyond, halo_hi[m])
+        second = dot(mine[:rows], own_lo[m]) + dot(beyond[:rows], halo_lo[m])
+        out.append(first[:rows] + first[rows:] + second)
     return jnp.concatenate(out, axis=1) + noise * own
 
 
 def smooth(image, jac_ref):
-    return jnp.concatenate(
-        [
-            dot(image[:, m * BS : (m + 1) * BS], jac_ref[m], precision=highest)
-            for m in range(jac_ref.shape[0])
-        ],
-        axis=1,
-    )
-
-
-def first_kernel(own_ref, left_ref, right_ref, extra_ref, hi_ref, lo_ref, jac_ref, image_ref, next_ref):
-    width = own_ref.shape[1]
+    rows = image.shape[0]
+    out = []
+    for m in range(jac_ref.shape[1]):
+        pieces = jnp.concatenate(split(image[:, m * BS : (m + 1) * BS], 3), axis=0).astype(bf16)
+        a = dot(pieces, jac_ref[0, m])
+        b = dot(pieces[: 2 * rows], jac_ref[1, m])
+        c = dot(pieces[:rows], jac_ref[2, m])
+        out.append(a[:rows] + (a[rows : 2 * rows] + b[:rows] + (a[2 * rows :] + b[rows:] + c)))
+    return jnp.concatenate(out, axis=1)
+
+
+def first_kernel(own_ref, left_ref, right_ref, extra_ref, *refs):
+    kernel, (jac_ref, image_ref, next_ref) = refs[:4], refs[4:]
     count = (own_ref.shape[0] - SYS) // 2
     coarse = image_ref.shape[0] - count
-    edge = width - REACH * BS
-    pack = jnp.concatenate(
-        [left_ref[:, edge:], own_ref[...], right_ref[:, : width - edge]], axis=1
-    )
-    ext = jnp.concatenate(
-        [pack[SYS + count :], one_hot(pack[FEAT + 1 : FEAT + 2], coarse)], axis=0
-    )
+
+    def basis(ref):
+        z = one_hot(ref[FEAT + 1 : FEAT + 2, :], coarse)
+        return jnp.concatenate([ref[SYS + count :, :], z], axis=0)
+
     noise = extra_ref[TASKS : TASKS + 1, :]
-    image = operate(ext, noise, ext[:, REACH * BS : REACH * BS + width], hi_ref, lo_ref)
+    image = operate(basis(own_ref), basis(left_ref), basis(right_ref), noise, *kernel)
     image_ref[...] = image
     next_ref[...] = smooth(image, jac_ref)
 
 
-def second_kernel(
-    extra_ref, vec_ref, vecl_ref, vecr_ref, hi_ref, lo_ref, jac_ref, image_ref, next_ref
-):
-    width = vec_ref.shape[1]
-    edge = width - REACH * BS
-    ext = jnp.concatenate([vecl_ref[:, edge:], vec_ref[...], vecr_ref[:, : width - edge]], axis=1)
+def second_kernel(extra_ref, vec_ref, left_ref, right_ref, early_ref, *refs):
+    kernel, (jac_ref, image_ref, next_ref) = refs[:4], refs[4:]
     noise = extra_ref[TASKS : TASKS + 1, :]
-    image = operate(ext, noise, vec_ref[...], hi_ref, lo_ref)
+    image = operate(vec_ref[...], left_ref[...], right_ref[...], noise, *kernel)
     image_ref[...] = image
     next_ref[...] = smooth(image, jac_ref)
 
@@ -343,9 +352,8 @@
     return coarse + 1
 
 
-def shape_of(count, coarse):
-    lanes = -(-5 * pitch_of(coarse) // LANES) * LANES
-    return count + coarse, max(count, coarse), lanes, -(-pitch_of(coarse) // BASE) * BASE
+def lanes_of(coarse):
+    return -(-5 * pitch_of(coarse) // LANES) * LANES
 
 
 def moment(vectors, images, pairs):
@@ -365,71 +373,85 @@
     return jnp.concatenate(cells, axis=1)
 
 
+def folded(low, high):
+    order = low.shape[0]
+    row, col = iota((order, order), 0), iota((order, order), 1)
+    diagonal = jnp.sum(jnp.where(row == col, high, 0.0), axis=1, keepdims=True)
+    return jnp.concatenate([jnp.where(row >= col, low, high), diagonal], axis=1)
+
+
+def unfolded(cells):
+    order = cells.shape[0]
+    row, col = iota((order, order), 0), iota((order, order), 1)
+    square = cells[:, :order]
+    turned = dot(square, jnp.where(row == col, 1.0, 0.0), TN, highest)
+    low = jnp.where(row >= col, square, turned)
+    high = jnp.where(row < col, square, jnp.where(row > col, turned, cells[:, order:]))
+    return low, high
+
+
 def early_moments_kernel(own_ref, d1_ref, v0_ref, out_ref):
     count = (own_ref.shape[0] - SYS) // 2
     coarse = d1_ref.shape[0] - count
-    rows, below, lanes, _ = shape_of(count, coarse)
+    lanes = out_ref.shape[1]
+    pitch = pitch_of(coarse)
     systems = own_ref[SYS : SYS + count, :]
     pre = own_ref[SYS + count :, :]
     z = one_hot(own_ref[FEAT + 1 : FEAT + 2, :], coarse)
     d1, v0 = d1_ref[...], v0_ref[...]
-    parts = {
-        0: moment(z, v0, pre * v0[:count]),
-        1: moment(d1[count:], v0, d1[:count] * v0[:count]),
-    }
-    out_ref[0:rows, :] = spread_out(parts, lanes)
-    start = spread_out({0: moment(z, systems, systems * pre)}, lanes)
-    if below > count:
-        start = jnp.concatenate([start, jnp.zeros((below - count, lanes), f32)], axis=0)
-    out_ref[rows:, :] = start
+    m0 = moment(z, v0, pre * v0[:count])
+    m1 = moment(d1[count:], v0, d1[:count] * v0[:count])
+    out_ref[0:count, :] = spread_out({0: m0[:count], 1: m1[:count]}, lanes)
+    start = moment(z, systems, systems * pre)
+    if coarse > count:
+        start = jnp.concatenate([start, jnp.zeros((coarse - count, pitch), f32)], axis=0)
+    fold = folded(m0[count:, :coarse], m1[count:, :coarse])
+    out_ref[count:, :] = spread_out({0: fold, 3: start}, lanes)
 
 
 def late_moments_kernel(before_ref, d1_ref, d2_ref, v1_ref, out_ref, *, count):
-    rows = d1_ref.shape[0]
+    lanes = out_ref.shape[1]
     d1, d2, v1 = d1_ref[...], d2_ref[...], v1_ref[...]
-    parts = {
-        2: moment(d1[count:], v1, d1[:count] * v1[:count]),
-        3: moment(d2[count:], v1, d2[:count] * v1[:count]),
-    }
-    out_ref[0:rows, :] = before_ref[0:rows, :] + spread_out(parts, out_ref.shape[1])
-    out_ref[rows:, :] = before_ref[rows:, :]
+    coarse = d1.shape[0] - count
+    m2 = moment(d1[count:], v1, d1[:count] * v1[:count])
+    m3 = moment(d2[count:], v1, d2[:count] * v1[:count])
+    out_ref[0:count, :] = before_ref[0:count, :] + spread_out({2: m2[:count], 3: m3[:count]}, lanes)
+    fold = folded(m2[count:, :coarse], m3[count:, :coarse])
+    out_ref[count:, :] = before_ref[count:, :] + spread_out({1: fold}, lanes)
 
 
 def third_kernel(
-    place_ref, extra_ref, before_ref, vec_ref, vecl_ref, vecr_ref, hi_ref, lo_ref, out_ref,
-    *, count, held,
+    place_ref, extra_ref, before_ref, vec_ref, left_ref, right_ref, *refs, count, held
 ):
-    width = vec_ref.shape[1]
+    kernel, out_ref = refs[:4], refs[4]
     coarse = vec_ref.shape[0] - count
-    rows, below, lanes, stand = shape_of(count, coarse)
-    edge = width - REACH * BS
-    ext = jnp.concatenate([vecl_ref[:, edge:], vec_ref[...], vecr_ref[:, : width - edge]], axis=1)
+    lanes = out_ref.shape[2]
+    pitch = pitch_of(coarse)
     d2 = vec_ref[...]
-    v2 = operate(ext, extra_ref[TASKS : TASKS + 1, :], d2, hi_ref, lo_ref)
-    last = spread_out({4: moment(d2[count:], v2, d2[:count] * v2[:count])}, lanes)
-    top = before_ref[0:rows, :] + last
-    row = iota((below, 1), 0)
+    noise = extra_ref[TASKS : TASKS + 1, :]
+    v2 = operate(d2, left_ref[...], right_ref[...], noise, *kernel)
+    m4 = moment(d2[count:], v2, d2[:count] * v2[:count])
+    row = iota((coarse, 1), 0)
     start = place_ref[0] * held
-    bottom = before_ref[rows:, :]
-    front = jnp.zeros((1, stand), f32)
-    back = jnp.zeros((1, lanes - stand - coarse), f32)
+    inverse = jnp.zeros((coarse, pitch), f32)
     for r in range(held):
-        line = extra_ref[TASKS + 2 + r : TASKS + 3 + r, 0:coarse]
-        line = jnp.concatenate([front, line, back], axis=1)
-        bottom = bottom + jnp.where(row == start + r, line, 0.0)
+        line = extra_ref[TASKS + 2 + r : TASKS + 3 + r, 0:pitch]
+        inverse = jnp.where(row == start + r, line, inverse)
+    top = before_ref[0:count, :] + spread_out({4: m4[:count]}, lanes)
+    bottom = before_ref[count:, :] + spread_out({2: m4[count:], 4: inverse}, lanes)
     for c in range(out_ref.shape[0]):
-        out_ref[c, 0:rows, :] = top
-        out_ref[c, rows:, :] = bottom
+        out_ref[c, 0:count, :] = top
+        out_ref[c, count:, :] = bottom
 
 
 def final_kernel(
     probe_ref, gram_ref, *refs, sides, points,
 ):
-    far, (sol_ref, grad_ref), near_refs, sems = refs[:12], refs[12:14], refs[14:26], refs[26]
+    far, (sol_ref, grad_ref), near_refs, sems = refs[:15], refs[15:17], refs[17:32], refs[32]
     copies = fetch(list(zip(far, near_refs)), sems)
     (
         own_ref, left_ref, right_ref, d1_ref, d1l_ref, d1r_ref, d2_ref, d2l_ref, d2r_ref,
-        hi_ref, lo_ref, sim_ref,
+        *kernel_refs,
     ) = near_refs
     width = own_ref.shape[1]
     count = (own_ref.shape[0] - SYS) // 2
@@ -442,9 +464,10 @@
     gram = gram_ref[0]
     for c in range(1, gram_ref.shape[0]):
         gram = gram + gram_ref[c]
-    _, _, lanes, stand = shape_of(count, coarse)
-    bottom = gram[rows:, :]
-    gram = jnp.concatenate([gram[:rows], jnp.zeros((rows, wide), f32)], axis=1)
+    bottom = gram[count:]
+    gram = jnp.concatenate([gram[:count], jnp.zeros((count, wide), f32)], axis=1)
+    squares = list(unfolded(bottom[:, :pitch])) + list(unfolded(bottom[:, pitch : 2 * pitch]))
+    squares.append(bottom[:, 2 * pitch : 2 * pitch + coarse])
     lane = iota((1, wide), 1)
     slot, inside = lane // pitch, lane % pitch
     live = lane < 3 * pitch
@@ -454,22 +477,22 @@
     def shifted(j):
         return jnp.where(live, gram[:, j * pitch : j * pitch + wide], 0.0)
 
-    moved = [shifted(j) for j in range(3)]
-    own = [m[:count] for m in moved]
-    gap = jnp.zeros((pitch - coarse, wide), f32)
-    hankel = jnp.concatenate(
-        [
-            jnp.concatenate([jnp.where(is_vec, m[count:], 0.0), gap], axis=0)
-            for m in moved
-        ]
-        + ([jnp.zeros((wide - 3 * pitch, wide), f32)] if wide > 3 * pitch else []),
-        axis=0,
-    )
+    own = [shifted(j) for j in range(3)]
+    gap = jnp.zeros((coarse, 1), f32)
+    rest = jnp.zeros((coarse, wide - 3 * pitch), f32)
+    hankel = []
+    for i in range(3):
+        line = [squares[i], gap, squares[i + 1], gap, squares[i + 2], gap]
+        hankel.append(jnp.concatenate(line + ([rest] if wide > 3 * pitch else []), axis=1))
+        hankel.append(jnp.zeros((1, wide), f32))
+    if wide > 3 * pitch:
+        hankel.append(jnp.zeros((wide - 3 * pitch, wide), f32))
+    hankel = jnp.concatenate(hankel, axis=0)
     block0 = lane < pitch
-    inverse = bottom[:coarse, stand : stand + coarse]
+    inverse = bottom[:, 4 * pitch : 4 * pitch + coarse]
     inverse = jnp.concatenate([inverse, jnp.zeros((coarse, wide - coarse), f32)], axis=1)
     inverse = jnp.concatenate([inverse, jnp.zeros((wide - coarse, wide), f32)], axis=0)
-    start = bottom[:count, :pitch]
+    start = bottom[:count, 3 * pitch : 4 * pitch]
     start = jnp.concatenate([start, jnp.zeros((count, wide - pitch), f32)], axis=1)
     against = jnp.where(
         block0, start, jnp.where(live, pltpu.roll(jnp.where(live, own[0], 0.0), pitch, axis=1), 0.0)
@@ -567,9 +590,12 @@
         at = slice(m * BS, (m + 1) * BS)
         sums = jnp.zeros((high, BS), f32)
         held_sums = jnp.zeros((TASKS, BS), f32)
-        for o in range(SLOTS):
-            j = slice((m + o) * BS, (m + o + 1) * BS)
-            rows_at = slice(o * BS, (o + 1) * BS)
+        places = [(0, row, j + REACH) for row, j, _ in own_places(m)]
+        places += [(1, row, j if j < REACH else j + REACH) for row, j, _ in halo_places(m)]
+        for side, row, block in places:
+            hi_ref, lo_ref, sim_ref = kernel_refs[3 * side : 3 * side + 3]
+            j = slice(block * BS, (block + 1) * BS)
+            rows_at = slice(row * BS, (row + 1) * BS)
             outer = dot(near[:, j], mate[:, at], TN)
             kernel = hi_ref[m, rows_at, :].astype(f32) + lo_ref[m, rows_at, :].astype(f32)
             energy = outer * kernel
@@ -630,7 +656,8 @@
     blocks = width // BS
     coarse = coarse_inverse.shape[1]
     rows = count + coarse
-    top, below, lanes, _ = shape_of(count, coarse)
+    lanes = lanes_of(coarse)
+    assert blocks == REACH
     ranks = lax.axis_size("pts")
     sides = lax.axis_size("probe")
 
@@ -639,7 +666,7 @@
 
     jac, pack, extra = call(
         invert_kernel,
-        [shape(blocks, BS, BS), shape(SYS + 2 * count, width), shape(TASKS + FEAT, width)],
+        [shape(3, blocks, BS, BS, kind=bf16), shape(SYS + 2 * count, width), shape(TASKS + FEAT, width)],
         [features, task_ids, aggregate, systems, task_cov, coarse_inverse, pattern, lengthscales, noise],
         "invert",
         hbm=9,
@@ -659,42 +686,49 @@
         flops=10**10,
     )
     pack_l, pack_r = both_sides(pack)
-    hi, lo, sim = call(
-        build_kernel,
-        [
-            shape(blocks, BAND, BS, kind=bf16),
-            shape(blocks, BAND, BS, kind=bf16),
-            shape(blocks, BAND, BS),
-        ],
-        [pack, pack_l, pack_r, extra],
-        "build",
-        far_outs=1,
-        scratch=[pltpu.VMEM((blocks, BAND, BS), f32), pltpu.SemaphoreType.DMA((blocks,))],
-        flops=3 * 10**9,
-        limit=24,
-    )
+
+    def build(places, deep, cells, name):
+        return call(
+            functools.partial(build_kernel, places=places, sides=len(cells)),
+            [
+                shape(blocks, deep, BS, kind=bf16),
+                shape(blocks, deep, BS, kind=bf16),
+                shape(blocks, deep, BS),
+            ],
+            cells + [pack, extra],
+            name,
+            far_outs=1,
+            scratch=[pltpu.VMEM((blocks, deep, BS), f32), pltpu.SemaphoreType.DMA((blocks,))],
+            flops=10**9,
+        )
+
+    own_hi, own_lo, own_sim = build(own_places, width, [pack], "build_own")
+    halo_hi, halo_lo, halo_sim = build(
+        halo_places, BAND - width, [pack_l, pack_r], "build_halo"
+    )
+    kernel = [own_hi, own_lo, halo_hi, halo_lo]
     v0, d1 = call(
         first_kernel,
         [shape(rows, width), shape(rows, width)],
-        [pack, pack_l, pack_r, extra, hi, lo, jac],
+        [pack, pack_l, pack_r, extra] + kernel + [jac],
         "first",
         flops=10**9,
     )
     d1_l, d1_r = both_sides(d1)
     (early,) = call(
-        early_moments_kernel, [shape(top + below, lanes)], [pack, d1, v0], "early", flops=10**9
+        early_moments_kernel, [shape(rows, lanes)], [pack, d1, v0], "early", flops=10**9
     )
     v1, d2 = call(
         second_kernel,
         [shape(rows, width), shape(rows, width)],
-        [extra, d1, d1_l, d1_r, hi, lo, jac],
+        [extra, d1, d1_l, d1_r, early] + kernel + [jac],
         "second",
         flops=10**9,
     )
     d2_l, d2_r = both_sides(d2)
     (late,) = call(
         functools.partial(late_moments_kernel, count=count),
-        [shape(top + below, lanes)],
+        [shape(rows, lanes)],
         [early, d1, d2, v1],
         "late",
         flops=10**9,
@@ -703,14 +737,15 @@
     probe = lax.axis_index("probe").astype(jnp.int32)[None]
     (gram,) = call(
         functools.partial(third_kernel, count=count, held=coarse_inverse.shape[0]),
-        [shape(ranks, top + below, lanes)],
-        [place, extra, late, d2, d2_l, d2_r, hi, lo],
+        [shape(ranks, rows, lanes)],
+        [place, extra, late, d2, d2_l, d2_r] + kernel,
         "third",
         smem=1,
         flops=10**9,
     )
     gram = lax.all_to_all(gram, "pts", 0, 0, tiled=True)
-    stored = [pack, pack_l, pack_r, d1, d1_l, d1_r, d2, d2_l, d2_r, hi, lo, sim]
+    stored = [pack, pack_l, pack_r, d1, d1_l, d1_r, d2, d2_l, d2_r]
+    stored += [own_hi, own_lo, own_sim, halo_hi, halo_lo, halo_sim]
     answer, grads = call(
         functools.partial(final_kernel, sides=sides * count, points=ranks * width),
         [shape(count, width), shape(ranks * sides, TASKS, LANES)],

time: 104 us -> 96 us (0.923)
  starting transfers between devices: 26.3 us -> 22.4 us
  Pallas kernels: 41 us -> 38.7 us
    ppermute x6, starting transfers between devices: 20.1 us -> 17.6 us  [both_sides(): return (lax.ppermute(cells, 'pts', up), lax.ppermute(cells, 'pts', down))]
    pallas_call x8 -> x9, Pallas kernels: 41 us -> 38.7 us  [call(): pl.pallas_call(body, out_shape=outs, in_specs=[sm] * smem + [vm] * (len(a...]
    all_to_all x1, starting transfers between devices: 6.25 us -> 4.85 us  [shards(): gram = lax.all_to_all(gram, 'pts', 0, 0, tiled=True)]
    ppermute x6, waiting for transfers between devices: 11 us -> 12.2 us  [both_sides(): return (lax.ppermute(cells, 'pts', up), lax.ppermute(cells, 'pts', down))]
    unnamed x32 -> x36, local copies, waits for them, and re-layouts: 3.36 us -> 2.5 us
  transfers between devices with their start and end apart: 7 -> 7, of which waited for: 6 -> 5; matrix products, arithmetic and copies ran while one was open for 0% -> 0% of each run, Pallas kernels for 2% -> 3%
where the time goes in v4:
time: 96 us; the launch traced here: 95.5 us
  Pallas kernels  38.7 us (40%)
  starting transfers between devices  22.4 us (23%)
  waiting for transfers between devices  19.7 us (21%)
  blocking collectives  10.5 us (11%)
  local copies, waits for them, and re-layouts  3.19 us (3%)
    pallas_call x9, Pallas kernels, call(): pl.pallas_call(body, out_shape=outs, in_specs=[sm] * smem + [vm] * (len(a...  38.7 us
    ppermute x6, starting transfers between devices, both_sides(): return (lax.ppermute(cells, 'pts', up), lax.ppermute(cells, 'pts', down))  17.6 us
    ppermute x6, waiting for transfers between devices, both_sides(): return (lax.ppermute(cells, 'pts', up), lax.ppermute(cells, 'pts', down))  12.2 us
    all_to_all x1, blocking collectives, shards(): grads = lax.all_to_all(grads, ('pts', 'probe'), 0, 0, tiled=True)  10.5 us
    all_to_all x1, waiting for transfers between devices, shards(): gram = lax.all_to_all(gram, 'pts', 0, 0, tiled=True)  7.56 us
    all_to_all x1, starting transfers between devices, shards(): gram = lax.all_to_all(gram, 'pts', 0, 0, tiled=True)  4.85 us
    unnamed x36, local copies, waits for them, and re-layouts  2.5 us
  transfers between devices with their start and end apart: 7, of which 5 were waited for; matrix products, arithmetic and copies ran while one was open for 0% of the time, Pallas kernels for 3%

profile of v4, /device:TPU:0, one launch (start us, length us, event | category | flops | bytes accessed | tf_op | source)
XLA Modules:
  0.0 95.5 jit_solution(6767437684806550713)
XLA Ops:
  0.6 17.1 %invert.1 = (bf16[3,3,256,256]{3,2,1,0:T(8,128)(2,1)S(1)}, f32[48,768]{1,0:T(8,128)S(1)}, f32[24,768]{1,0:T(8,128)S(1)}) custom-call(f32[8,768]{1,0:T(8,128)} %feat_hbm.1, s32[768]{0:T(1024)} %ids_hbm.1, s32[768]{0:T(1024)} %agg_hbm.1, f32[16,768]{1,0:T(8,128)} %sys_hbm.1, f32[16,16]{1,0:T(8,128)} %cov_hbm.1, f32[3,24]{1,0:T(4,128)} %coarse_hbm.1, ...), custom_call_target="tpu_custom_call" | custom-call | flops 10000000000 | bytes 1048576 | tf_op jit(solution)/shard_map/invert/pallas_call | solution.py:633
  17.8 4.9 %collective-permute-start = (f32[48,768]{1,0:T(8,128)S(1)}, f32[48,768]{1,0:T(8,128)S(1)}, u32[]{:S(2)}, u32[]{:S(2)}) collective-permute-start(f32[48,768]{1,0:T(8,128)S(1)} %get-tuple-element.19.refs_0_.refs_1_.refs_2_.own_ref), channel_id=1, source_target_pairs={{0,2},{2,4},{4,6},{6,8},{8,10},{10,12},{12,14},{1,3},{3,5},{5,7},{... | collective-permute-start | bytes 442376 | tf_op jit(solution)/shard_map/ppermute | solution.py:649
  22.7 1.3 %collective-permute-start.1 = (f32[48,768]{1,0:T(8,128)S(1)}, f32[48,768]{1,0:T(8,128)S(1)}, u32[]{:S(2)}, u32[]{:S(2)}) collective-permute-start(f32[48,768]{1,0:T(8,128)S(1)} %get-tuple-element.19.refs_0_.refs_1_.refs_2_.own_ref), channel_id=1, source_target_pairs={{2,0},{4,2},{6,4},{8,6},{10,8},{12,10},{14,12},{3,1},{5,3},{7,5},{... | collective-permute-start | bytes 442376 | tf_op jit(solution)/shard_map/ppermute | solution.py:649
  24.0 2.0 %build_own.1 = (bf16[3,768,256]{2,1,0:T(8,128)(2,1)S(1)}, bf16[3,768,256]{2,1,0:T(8,128)(2,1)S(1)}, f32[3,768,256]{2,1,0:T(8,128)}) custom-call(f32[48,768]{1,0:T(8,128)S(1)} %get-tuple-element.19.refs_0_.refs_1_.refs_2_.own_ref, f32[48,768]{1,0:T(8,128)S(1)} %get-tuple-element.19.refs_0_.refs_1_.refs_2_.own_ref, ...), custom_call_target="tpu_custom_call" | custom-call | flops 1000000000 | bytes 1048576 | tf_op jit(solution)/shard_map/build_own/pallas_call | solution.py:633
  26.0 0.0 collective-permute-done.refs_0_.left_ref.refs_1_
  26.0 0.0 copy-start.7
  26.0 3.9 %collective-permute-done.1.refs_1_.right_ref.refs_2_ = f32[48,768]{1,0:T(8,128)S(1)} collective-permute-done((f32[48,768]{1,0:T(8,128)S(1)}, f32[48,768]{1,0:T(8,128)S(1)}, u32[]{:S(2)}, u32[]{:S(2)}) %collective-permute-start.1) | collective-permute-done | bytes 147488 | tf_op jit(solution)/shard_map/ppermute | solution.py:649
  29.9 2.4 %build_halo.1 = (bf16[3,1024,256]{2,1,0:T(8,128)(2,1)S(1)}, bf16[3,1024,256]{2,1,0:T(8,128)(2,1)S(1)}, f32[3,1024,256]{2,1,0:T(8,128)}) custom-call(f32[48,768]{1,0:T(8,128)S(1)} %collective-permute-done.refs_0_.left_ref.refs_1_, f32[48,768]{1,0:T(8,128)S(1)} %collective-permute-done.1.refs_1_.right_ref.refs_2_, ...), custom_call_target="tpu_custom_call" | custom-call | flops 1000000000 | bytes 1048576 | tf_op jit(solution)/shard_map/build_halo/pallas_call | solution.py:633
  32.3 1.2 %first.1 = (f32[40,768]{1,0:T(8,128)S(1)}, f32[40,768]{1,0:T(8,128)S(1)}) custom-call(f32[48,768]{1,0:T(8,128)S(1)} %get-tuple-element.19.refs_0_.refs_1_.refs_2_.own_ref, f32[48,768]{1,0:T(8,128)S(1)} %collective-permute-done.refs_0_.left_ref.refs_1_, f32[48,768]{1,0:T(8,128)S(1)} %collective-permute-done.1.refs_1_.right_ref.refs_2_, ...), custom_call_target="tpu_custom_call" | custom-call | flops 1000000000 | bytes 1048576 | tf_op jit(solution)/shard_map/first/pallas_call | solution.py:633
  33.6 0.0 copy-start.9
  33.6 4.3 %collective-permute-start.2 = (f32[40,768]{1,0:T(8,128)S(1)}, f32[40,768]{1,0:T(8,128)S(1)}, u32[]{:S(2)}, u32[]{:S(2)}) collective-permute-start(f32[40,768]{1,0:T(8,128)S(1)} %get-tuple-element.25.d1_ref.vec_ref.refs_3_), channel_id=1, source_target_pairs={{0,2},{2,4},{4,6},{6,8},{8,10},{10,12},{12,14},{1,3},{3,5},{5,7},{... | collective-permute-start | bytes 368648 | tf_op jit(solution)/shard_map/ppermute | solution.py:649
  37.9 1.5 %collective-permute-start.3 = (f32[40,768]{1,0:T(8,128)S(1)}, f32[40,768]{1,0:T(8,128)S(1)}, u32[]{:S(2)}, u32[]{:S(2)}) collective-permute-start(f32[40,768]{1,0:T(8,128)S(1)} %get-tuple-element.25.d1_ref.vec_ref.refs_3_), channel_id=1, source_target_pairs={{2,0},{4,2},{6,4},{8,6},{10,8},{12,10},{14,12},{3,1},{5,3},{7,5},{... | collective-permute-start | bytes 368648 | tf_op jit(solution)/shard_map/ppermute | solution.py:649
  39.4 0.4 early.1.early_ref.before_ref
  39.8 0.6 collective-permute-done.2.left_ref.refs_4_
  40.3 4.4 %collective-permute-done.3.right_ref.refs_5_ = f32[40,768]{1,0:T(8,128)S(1)} collective-permute-done((f32[40,768]{1,0:T(8,128)S(1)}, f32[40,768]{1,0:T(8,128)S(1)}, u32[]{:S(2)}, u32[]{:S(2)}) %collective-permute-start.3) | collective-permute-done | bytes 122912 | tf_op jit(solution)/shard_map/ppermute | solution.py:649
  44.7 0.0 copy-done.2
  44.7 1.2 %second.1 = (f32[40,768]{1,0:T(8,128)S(1)}, f32[40,768]{1,0:T(8,128)S(1)}) custom-call(f32[24,768]{1,0:T(8,128)S(1)} %get-tuple-element.18.refs_2_.refs_3_.extra_ref, f32[40,768]{1,0:T(8,128)S(1)} %get-tuple-element.25.d1_ref.vec_ref.refs_3_, f32[40,768]{1,0:T(8,128)S(1)} %collective-permute-done.2.left_ref.refs_4_, ...), custom_call_target="tpu_custom_call" | custom-call | flops 1000000000 | bytes 1048576 | tf_op jit(solution)/shard_map/second/pallas_call | solution.py:633
  45.9 0.6 copy-done.15
  46.6 4.3 %collective-permute-start.4 = (f32[40,768]{1,0:T(8,128)S(1)}, f32[40,768]{1,0:T(8,128)S(1)}, u32[]{:S(2)}, u32[]{:S(2)}) collective-permute-start(f32[40,768]{1,0:T(8,128)S(1)} %get-tuple-element.27.d2_ref.vec_ref.refs_6_), channel_id=1, source_target_pairs={{0,2},{2,4},{4,6},{6,8},{8,10},{10,12},{12,14},{1,3},{3,5},{5,7},{... | collective-permute-start | bytes 368648 | tf_op jit(solution)/shard_map/ppermute | solution.py:649
  50.9 1.3 %collective-permute-start.5 = (f32[40,768]{1,0:T(8,128)S(1)}, f32[40,768]{1,0:T(8,128)}, u32[]{:S(2)}, u32[]{:S(2)}) collective-permute-start(f32[40,768]{1,0:T(8,128)S(1)} %get-tuple-element.27.d2_ref.vec_ref.refs_6_), channel_id=1, source_target_pairs={{2,0},{4,2},{6,4},{8,6},{10,8},{12,10},{14,12},{3,1},{5,3},{7,5},{... | collective-permute-start | bytes 368648 | tf_op jit(solution)/shard_map/ppermute | solution.py:649
  52.2 0.9 copy-done.10
  53.1 0.9 copy-done.16
  54.0 0.4 late.1.before_ref
  54.4 0.0 collective-permute-done.4.left_ref.refs_7_
  54.4 3.4 %collective-permute-done.5.right_ref.refs_8_ = f32[40,768]{1,0:T(8,128)} collective-permute-done((f32[40,768]{1,0:T(8,128)S(1)}, f32[40,768]{1,0:T(8,128)}, u32[]{:S(2)}, u32[]{:S(2)}) %collective-permute-start.5) | collective-permute-done | bytes 122912 | tf_op jit(solution)/shard_map/ppermute | solution.py:649
  57.8 2.8 %third.1 = f32[8,40,128]{2,1,0:T(8,128)} custom-call(s32[1]{0:T(128)} %bitcast.1.place_ref, f32[24,768]{1,0:T(8,128)S(1)} %get-tuple-element.18.refs_2_.refs_3_.extra_ref, f32[40,128]{1,0:T(8,128)S(1)} %late.1.before_ref, f32[40,768]{1,0:T(8,128)S(1)} %get-tuple-element.27.d2_ref.vec_ref.refs_6_, f32[40,768]{1,0:T(8,128)S(1)} %collective-permute-done.4.left_ref.refs_7_, ...), custom_call_target="tpu_custom_call" | custom-call | flops 1000000000 | bytes 1048576 | tf_op jit(solution)/shard_map/third/pallas_call | solution.py:633
  60.7 4.8 %all-to-all-start = ((f32[8,40,128]{2,1,0:T(8,128)}), f32[8,40,128]{2,1,0:T(8,128)S(1)}, u32[]{:S(2)}, u32[]{:S(2)}) async-start(f32[8,40,128]{2,1,0:T(8,128)} %third.1), calls=%async_computation | async-start | bytes 327680 | tf_op jit(solution)/shard_map/all_to_all | solution.py:746
  65.5 7.6 %all-to-all-done.gram_ref = f32[8,40,128]{2,1,0:T(8,128)S(1)} async-done(((f32[8,40,128]{2,1,0:T(8,128)}), f32[8,40,128]{2,1,0:T(8,128)S(1)}, u32[]{:S(2)}, u32[]{:S(2)}) %all-to-all-start) | async-done | bytes 163872 | tf_op jit(solution)/shard_map/all_to_all | solution.py:746
  73.1 11.1 %final.1 = (f32[16,768]{1,0:T(8,128)}, f32[16,16,128]{2,1,0:T(8,128)S(1)}) custom-call(s32[1]{0:T(128)} %bitcast.probe_ref, f32[8,40,128]{2,1,0:T(8,128)S(1)} %all-to-all-done.gram_ref, f32[48,768]{1,0:T(8,128)} %copy-done.6, f32[48,768]{1,0:T(8,128)} %copy-done.7, f32[48,768]{1,0:T(8,128)} %copy-done.8, f32[40,768]{1,0:T(8,128)} %copy-done.9, ...), custom_call_target="tpu_custom_call" | custom-call | flops 1000000000 | bytes 1048576 | tf_op jit(solution)/shard_map/final/pallas_call | solution.py:633
  84.2 10.5 %all_to_all.10 = f32[16,16,128]{2,1,0:T(8,128)S(1)} all-to-all(f32[16,16,128]{2,1,0:T(8,128)S(1)} %get-tuple-element.32), channel_id=1, replica_groups=mesh['groups'=2,'pts'=8,'probe'=2] {'pts','probe'}, dimensions={0} | all-to-all | bytes 262144 | tf_op jit(solution)/shard_map/all_to_all | solution.py:761
  94.8 0.0 copy-start.17
  94.8 0.7 slice_reduce_fusion
  (30 shorter events, 0.1 us)
Async XLA Ops:
  17.8 21.6 %copy-start.6 = (f32[48,768]{1,0:T(8,128)}, f32[48,768]{1,0:T(8,128)S(1)}, u32[]{:S(2)}) copy-start(f32[48,768]{1,0:T(8,128)S(1)} %get-tuple-element.19.refs_0_.refs_1_.refs_2_.own_ref) | copy-start | bytes 442372
  17.8 8.2 %collective-permute-start = (f32[48,768]{1,0:T(8,128)S(1)}, f32[48,768]{1,0:T(8,128)S(1)}, u32[]{:S(2)}, u32[]{:S(2)}) collective-permute-start(f32[48,768]{1,0:T(8,128)S(1)} %get-tuple-element.19.refs_0_.refs_1_.refs_2_.own_ref), channel_id=1, source_target_pairs={{0,2},{2,4},{4,6},{6,8},{8,10},{10,12},{12,14},{1,3},{3,5},{5,7},{... | collective-permute-start | bytes 442376 | tf_op jit(solution)/shard_map/ppermute | solution.py:649
  22.7 7.2 %collective-permute-start.1 = (f32[48,768]{1,0:T(8,128)S(1)}, f32[48,768]{1,0:T(8,128)S(1)}, u32[]{:S(2)}, u32[]{:S(2)}) collective-permute-start(f32[48,768]{1,0:T(8,128)S(1)} %get-tuple-element.19.refs_0_.refs_1_.refs_2_.own_ref), channel_id=1, source_target_pairs={{2,0},{4,2},{6,4},{8,6},{10,8},{12,10},{14,12},{3,1},{5,3},{7,5},{... | collective-permute-start | bytes 442376 | tf_op jit(solution)/shard_map/ppermute | solution.py:649
  25.9 18.7 %copy-start.2 = (bf16[3,768,256]{2,1,0:T(8,128)(2,1)}, bf16[3,768,256]{2,1,0:T(8,128)(2,1)S(1)}, u32[]{:S(2)}) copy-start(bf16[3,768,256]{2,1,0:T(8,128)(2,1)S(1)} %get-tuple-element.20.refs_0_.refs_9_) | copy-start | bytes 3538948
  26.0 18.7 %copy-start.4 = (bf16[3,768,256]{2,1,0:T(8,128)(2,1)}, bf16[3,768,256]{2,1,0:T(8,128)(2,1)S(1)}, u32[]{:S(2)}) copy-start(bf16[3,768,256]{2,1,0:T(8,128)(2,1)S(1)} %get-tuple-element.21.refs_1_.refs_10_) | copy-start | bytes 3538948
  26.0 6.3 %copy-start.7 = (f32[48,768]{1,0:T(8,128)}, f32[48,768]{1,0:T(8,128)S(1)}, u32[]{:S(2)}) copy-start(f32[48,768]{1,0:T(8,128)S(1)} %collective-permute-done.refs_0_.left_ref.refs_1_) | copy-start | bytes 442372
  29.9 2.4 %copy-start.8 = (f32[48,768]{1,0:T(8,128)}, f32[48,768]{1,0:T(8,128)S(1)}, u32[]{:S(2)}) copy-start(f32[48,768]{1,0:T(8,128)S(1)} %collective-permute-done.1.refs_1_.right_ref.refs_2_) | copy-start | bytes 442372
  32.3 25.5 %copy-start = (bf16[3,1024,256]{2,1,0:T(8,128)(2,1)}, bf16[3,1024,256]{2,1,0:T(8,128)(2,1)S(1)}, u32[]{:S(2)}) copy-start(bf16[3,1024,256]{2,1,0:T(8,128)(2,1)S(1)} %get-tuple-element.22.refs_2_.refs_12_) | copy-start | bytes 4718596
  32.3 25.5 %copy-start.1 = (bf16[3,1024,256]{2,1,0:T(8,128)(2,1)}, bf16[3,1024,256]{2,1,0:T(8,128)(2,1)S(1)}, u32[]{:S(2)}) copy-start(bf16[3,1024,256]{2,1,0:T(8,128)(2,1)S(1)} %get-tuple-element.23.refs_3_.refs_13_) | copy-start | bytes 4718596
  33.6 11.1 %copy-start.9 = (f32[40,768]{1,0:T(8,128)}, f32[40,768]{1,0:T(8,128)S(1)}, u32[]{:S(2)}) copy-start(f32[40,768]{1,0:T(8,128)S(1)} %get-tuple-element.25.d1_ref.vec_ref.refs_3_) | copy-start | bytes 368644
  33.6 6.8 %collective-permute-start.2 = (f32[40,768]{1,0:T(8,128)S(1)}, f32[40,768]{1,0:T(8,128)S(1)}, u32[]{:S(2)}, u32[]{:S(2)}) collective-permute-start(f32[40,768]{1,0:T(8,128)S(1)} %get-tuple-element.25.d1_ref.vec_ref.refs_3_), channel_id=1, source_target_pairs={{0,2},{2,4},{4,6},{6,8},{8,10},{10,12},{12,14},{1,3},{3,5},{5,7},{... | collective-permute-start | bytes 368648 | tf_op jit(solution)/shard_map/ppermute | solution.py:649
  37.9 6.8 %collective-permute-start.3 = (f32[40,768]{1,0:T(8,128)S(1)}, f32[40,768]{1,0:T(8,128)S(1)}, u32[]{:S(2)}, u32[]{:S(2)}) collective-permute-start(f32[40,768]{1,0:T(8,128)S(1)} %get-tuple-element.25.d1_ref.vec_ref.refs_3_), channel_id=1, source_target_pairs={{2,0},{4,2},{6,4},{8,6},{10,8},{12,10},{14,12},{3,1},{5,3},{7,5},{... | collective-permute-start | bytes 368648 | tf_op jit(solution)/shard_map/ppermute | solution.py:649
  40.3 5.6 %copy-start.11 = (f32[40,768]{1,0:T(8,128)}, f32[40,768]{1,0:T(8,128)S(1)}, u32[]{:S(2)}) copy-start(f32[40,768]{1,0:T(8,128)S(1)} %collective-permute-done.2.left_ref.refs_4_) | copy-start | bytes 368644
  44.7 1.2 %copy-start.12 = (f32[40,768]{1,0:T(8,128)}, f32[40,768]{1,0:T(8,128)S(1)}, u32[]{:S(2)}) copy-start(f32[40,768]{1,0:T(8,128)S(1)} %collective-permute-done.3.right_ref.refs_5_) | copy-start | bytes 368644
  45.9 0.6 copy-start.15
  46.6 11.2 %copy-start.13 = (f32[40,768]{1,0:T(8,128)}, f32[40,768]{1,0:T(8,128)S(1)}, u32[]{:S(2)}) copy-start(f32[40,768]{1,0:T(8,128)S(1)} %get-tuple-element.27.d2_ref.vec_ref.refs_6_) | copy-start | bytes 368644
  46.6 7.8 %collective-permute-start.4 = (f32[40,768]{1,0:T(8,128)S(1)}, f32[40,768]{1,0:T(8,128)S(1)}, u32[]{:S(2)}, u32[]{:S(2)}) collective-permute-start(f32[40,768]{1,0:T(8,128)S(1)} %get-tuple-element.27.d2_ref.vec_ref.refs_6_), channel_id=1, source_target_pairs={{0,2},{2,4},{4,6},{6,8},{8,10},{10,12},{12,14},{1,3},{3,5},{5,7},{... | collective-permute-start | bytes 368648 | tf_op jit(solution)/shard_map/ppermute | solution.py:649
  50.9 6.9 %collective-permute-start.5 = (f32[40,768]{1,0:T(8,128)S(1)}, f32[40,768]{1,0:T(8,128)}, u32[]{:S(2)}, u32[]{:S(2)}) collective-permute-start(f32[40,768]{1,0:T(8,128)S(1)} %get-tuple-element.27.d2_ref.vec_ref.refs_6_), channel_id=1, source_target_pairs={{2,0},{4,2},{6,4},{8,6},{10,8},{12,10},{14,12},{3,1},{5,3},{7,5},{... | collective-permute-start | bytes 368648 | tf_op jit(solution)/shard_map/ppermute | solution.py:649
  52.2 0.9 copy-start.10
  53.1 0.9 copy-start.16
  54.0 3.8 %copy-start.3 = (bf16[3,768,256]{2,1,0:T(8,128)(2,1)S(1)}, bf16[3,768,256]{2,1,0:T(8,128)(2,1)}, u32[]{:S(2)}) copy-start(bf16[3,768,256]{2,1,0:T(8,128)(2,1)} %copy-done.2) | copy-start | bytes 3538948
  54.0 3.8 %copy-start.5 = (bf16[3,768,256]{2,1,0:T(8,128)(2,1)S(1)}, bf16[3,768,256]{2,1,0:T(8,128)(2,1)}, u32[]{:S(2)}) copy-start(bf16[3,768,256]{2,1,0:T(8,128)(2,1)} %copy-done.4) | copy-start | bytes 3538948
  54.4 6.2 %copy-start.14 = (f32[40,768]{1,0:T(8,128)}, f32[40,768]{1,0:T(8,128)S(1)}, u32[]{:S(2)}) copy-start(f32[40,768]{1,0:T(8,128)S(1)} %collective-permute-done.4.left_ref.refs_7_) | copy-start | bytes 368644
  60.7 12.4 %all-to-all-start = ((f32[8,40,128]{2,1,0:T(8,128)}), f32[8,40,128]{2,1,0:T(8,128)S(1)}, u32[]{:S(2)}, u32[]{:S(2)}) async-start(f32[8,40,128]{2,1,0:T(8,128)} %third.1), calls=%async_computation | async-start | bytes 327680 | tf_op jit(solution)/shard_map/all_to_all | solution.py:746
  94.8 0.7 copy-start.17

commit v5 on v4

--- a/solution.py
+++ b/solution.py
@@ -199,8 +199,6 @@
     pack_ref[FEAT : 2 * FEAT, :] = jnp.where(
         rows == 0, ids, jnp.where(rows == 1, which, 0.0)
     )
-    count = sys_ref.shape[0]
-    pack_ref[SYS : SYS + count, :] = sys_ref[...]
     extra_ref[0:TASKS, :] = picked
     tail = jnp.where(rows == 0, noise, jnp.where(rows == 1, weights, 0.0))
     held = coarse_ref.shape[0]
@@ -256,7 +254,7 @@
         inv = -work[m]
         for i, part in enumerate(split(inv, 3)):
             jac_ref[i, m] = part.astype(bf16)
-        pack_ref[SYS + count :, at] = dot(sys_ref[:, at], inv, precision=highest)
+        pack_ref[SYS:, at] = dot(sys_ref[:, at], inv, precision=highest)
 
 
 def own_places(m):
@@ -270,7 +268,7 @@
 
 def build_kernel(*refs, places, sides):
     cells, (own_ref, extra_ref) = refs[:sides], refs[sides : sides + 2]
-    hi_ref, lo_ref, sim_hbm, sim_ref, sems = refs[sides + 2 :]
+    hi_ref, lo_ref, sim_ref = refs[sides + 2 :]
     blocks = hi_ref.shape[0]
     near = []
     for ref in cells:
@@ -290,9 +288,6 @@
             sim_ref[m, rows, :] = similar
             hi_ref[m, rows, :] = head
             lo_ref[m, rows, :] = (kernel - head.astype(f32)).astype(bf16)
-        pltpu.make_async_copy(sim_ref.at[m], sim_hbm.at[m], sems.at[m]).start()
-    for m in range(blocks):
-        pltpu.make_async_copy(sim_ref.at[m], sim_hbm.at[m], sems.at[m]).wait()
 
 
 def operate(own, left, right, noise, own_hi, own_lo, halo_hi, halo_lo):
@@ -327,12 +322,12 @@
 
 def first_kernel(own_ref, left_ref, right_ref, extra_ref, *refs):
     kernel, (jac_ref, image_ref, next_ref) = refs[:4], refs[4:]
-    count = (own_ref.shape[0] - SYS) // 2
+    count = own_ref.shape[0] - SYS
     coarse = image_ref.shape[0] - count
 
     def basis(ref):
         z = one_hot(ref[FEAT + 1 : FEAT + 2, :], coarse)
-        return jnp.concatenate([ref[SYS + count :, :], z], axis=0)
+        return jnp.concatenate([ref[SYS:, :], z], axis=0)
 
     noise = extra_ref[TASKS : TASKS + 1, :]
     image = operate(basis(own_ref), basis(left_ref), basis(right_ref), noise, *kernel)
@@ -390,13 +385,15 @@
     return low, high
 
 
-def early_moments_kernel(own_ref, d1_ref, v0_ref, out_ref):
-    count = (own_ref.shape[0] - SYS) // 2
+def early_moments_kernel(own_ref, sys_ref, d1_ref, v0_ref, *refs):
+    sources, (out_ref, *stashes), sems = refs[:6], refs[6:13], refs[13]
+    copies = fetch(list(zip(sources, stashes)), sems)
+    count = own_ref.shape[0] - SYS
     coarse = d1_ref.shape[0] - count
     lanes = out_ref.shape[1]
     pitch = pitch_of(coarse)
-    systems = own_ref[SYS : SYS + count, :]
-    pre = own_ref[SYS + count :, :]
+    systems = sys_ref[...]
+    pre = own_ref[SYS:, :]
     z = one_hot(own_ref[FEAT + 1 : FEAT + 2, :], coarse)
     d1, v0 = d1_ref[...], v0_ref[...]
     m0 = moment(z, v0, pre * v0[:count])
@@ -407,6 +404,8 @@
         start = jnp.concatenate([start, jnp.zeros((coarse - count, pitch), f32)], axis=0)
     fold = folded(m0[count:, :coarse], m1[count:, :coarse])
     out_ref[count:, :] = spread_out({0: fold, 3: start}, lanes)
+    for copy in copies:
+        copy.wait()
 
 
 def late_moments_kernel(before_ref, d1_ref, d2_ref, v1_ref, out_ref, *, count):
@@ -447,14 +446,14 @@
 def final_kernel(
     probe_ref, gram_ref, *refs, sides, points,
 ):
-    far, (sol_ref, grad_ref), near_refs, sems = refs[:15], refs[15:17], refs[17:32], refs[32]
+    far, (sol_ref, grad_ref), near_refs, sems = refs[:16], refs[16:18], refs[18:34], refs[34]
     copies = fetch(list(zip(far, near_refs)), sems)
     (
-        own_ref, left_ref, right_ref, d1_ref, d1l_ref, d1r_ref, d2_ref, d2l_ref, d2r_ref,
+        sys_ref, own_ref, left_ref, right_ref, d1_ref, d1l_ref, d1r_ref, d2_ref, d2l_ref, d2r_ref,
         *kernel_refs,
     ) = near_refs
     width = own_ref.shape[1]
-    count = (own_ref.shape[0] - SYS) // 2
+    count = own_ref.shape[0] - SYS
     rows = d1_ref.shape[0]
     coarse = rows - count
     pitch = pitch_of(coarse)
@@ -533,13 +532,13 @@
             direction = pre + (gamma_new / gamma) * direction
             gamma = gamma_new
 
-    for copy in copies[:9]:
+    for copy in copies[:10]:
         copy.wait()
     pack = jnp.concatenate(
         [left_ref[:, edge:], own_ref[...], right_ref[:, : width - edge]], axis=1
     )
     z = one_hot(pack[FEAT + 1 : FEAT + 2], coarse)
-    q0 = pack[SYS + count :]
+    q0 = pack[SYS:]
     d1 = jnp.concatenate([d1l_ref[:, edge:], d1_ref[...], d1r_ref[:, : width - edge]], axis=1)
     d2 = jnp.concatenate([d2l_ref[:, edge:], d2_ref[...], d2r_ref[:, : width - edge]], axis=1)
     span = q0.shape[1]
@@ -563,15 +562,14 @@
     mine = slice(REACH * BS, REACH * BS + width)
     sol_ref[...] = x[:, mine]
 
-    systems = pack[SYS : SYS + count]
     line = iota((count, 1), 0) + probe_ref[0] * count
-    right = jnp.where(line == 0, x, systems)
+    right = jnp.where(line == 0, x[:, mine], sys_ref[...])
     coef = jnp.where(line == 0, 0.5 / points, -0.5 / (sides - 1) / points)
-    weighted = x[:, mine] * coef
     r0, r1 = split(right, 2)
-    w0, w1 = split(weighted, 2)
-    near = jnp.concatenate([r0, r1, r0], axis=0).astype(bf16)
-    mate = jnp.concatenate([w0, w0, w1], axis=0).astype(bf16)
+    w0, w1 = split(x * coef, 2)
+    rest = LANES - 3 * count
+    near = jnp.concatenate([w0, w1, w0, jnp.zeros((rest, span), f32)], axis=0).T.astype(bf16)
+    mate = jnp.concatenate([r0, r0, r1, jnp.zeros((rest, width), f32)], axis=0).astype(bf16)
     scaled = pack[0:FEAT]
     table = one_hot(pack[FEAT : FEAT + 1], TASKS)
     ones = jnp.ones((8, span), f32)
@@ -582,7 +580,7 @@
     heads = jnp.concatenate([t0, pad8], axis=0).astype(bf16)
     tables = table.astype(bf16)
     high = 32
-    for copy in copies[9:]:
+    for copy in copies[10:]:
         copy.wait()
     length_total = jnp.zeros((FEAT, 1), f32)
     task_total = jnp.zeros((TASKS, TASKS), f32)
@@ -596,7 +594,7 @@
             hi_ref, lo_ref, sim_ref = kernel_refs[3 * side : 3 * side + 3]
             j = slice(block * BS, (block + 1) * BS)
             rows_at = slice(row * BS, (row + 1) * BS)
-            outer = dot(near[:, j], mate[:, at], TN)
+            outer = dot(near[j], mate[:, at])
             kernel = hi_ref[m, rows_at, :].astype(f32) + lo_ref[m, rows_at, :].astype(f32)
             energy = outer * kernel
             held = outer * sim_ref[m, rows_at, :]
@@ -610,13 +608,29 @@
         value = left * left * sums[FEAT : FEAT + 1] + sums[2 * FEAT : 3 * FEAT]
         value = value - 2.0 * left * sums[:FEAT]
         length_total = length_total + jnp.sum(value, axis=1, keepdims=True)
-        task_total = task_total + dot(table[:, mid], held_sums, NT, highest)
-    lane = iota((TASKS, LANES), 1)
-    lengths = jnp.concatenate([length_total, jnp.zeros((TASKS - FEAT, 1), f32)], axis=0)
-    wide_tasks = jnp.concatenate([task_total, jnp.zeros((TASKS, LANES - TASKS), f32)], axis=1)
-    value = jnp.where(lane == TASKS, lengths, wide_tasks)
+        task_total = task_total + dot(held_sums, table[:, mid], NT, highest)
+    half = TASKS // 2
+    value = jnp.concatenate(
+        [
+            task_total[:half],
+            task_total[half:],
+            length_total,
+            jnp.zeros((half, LANES - 2 * TASKS - 1), f32),
+        ],
+        axis=1,
+    )
     for c in range(grad_ref.shape[0]):
         grad_ref[c] = value
+
+
+def tail_kernel(parts_ref, length_ref, task_ref):
+    total = parts_ref[0]
+    for c in range(1, parts_ref.shape[0]):
+        total = total + parts_ref[c]
+    half = TASKS // 2
+    task_ref[0:half, :] = total[:, :TASKS]
+    task_ref[half:, :] = total[:, TASKS : 2 * TASKS]
+    length_ref[...] = total[:, 2 * TASKS : 2 * TASKS + 1]
 
 
 MIB = 1024 * 1024
@@ -666,7 +680,7 @@
 
     jac, pack, extra = call(
         invert_kernel,
-        [shape(3, blocks, BS, BS, kind=bf16), shape(SYS + 2 * count, width), shape(TASKS + FEAT, width)],
+        [shape(3, blocks, BS, BS, kind=bf16), shape(SYS + count, width), shape(TASKS + FEAT, width)],
         [features, task_ids, aggregate, systems, task_cov, coarse_inverse, pattern, lengthscales, noise],
         "invert",
         hbm=9,
@@ -697,8 +711,6 @@
             ],
             cells + [pack, extra],
             name,
-            far_outs=1,
-            scratch=[pltpu.VMEM((blocks, deep, BS), f32), pltpu.SemaphoreType.DMA((blocks,))],
             flops=10**9,
         )
 
@@ -715,8 +727,15 @@
         flops=10**9,
     )
     d1_l, d1_r = both_sides(d1)
-    (early,) = call(
-        early_moments_kernel, [shape(rows, lanes)], [pack, d1, v0], "early", flops=10**9
+    cells = [own_hi, own_lo, own_sim, halo_hi, halo_lo, halo_sim]
+    early, *stashed = call(
+        early_moments_kernel,
+        [shape(rows, lanes)] + [shape(*a.shape, kind=a.dtype) for a in cells],
+        [pack, systems, d1, v0] + cells,
+        "early",
+        far_outs=len(cells),
+        scratch=[pltpu.SemaphoreType.DMA((len(cells),))],
+        flops=10**9,
     )
     v1, d2 = call(
         second_kernel,
@@ -744,11 +763,10 @@
         flops=10**9,
     )
     gram = lax.all_to_all(gram, "pts", 0, 0, tiled=True)
-    stored = [pack, pack_l, pack_r, d1, d1_l, d1_r, d2, d2_l, d2_r]
-    stored += [own_hi, own_lo, own_sim, halo_hi, halo_lo, halo_sim]
+    stored = [systems, pack, pack_l, pack_r, d1, d1_l, d1_r, d2, d2_l, d2_r] + stashed
     answer, grads = call(
         functools.partial(final_kernel, sides=sides * count, points=ranks * width),
-        [shape(count, width), shape(ranks * sides, TASKS, LANES)],
+        [shape(count, width), shape(ranks * sides, FEAT, LANES)],
         [probe, gram] + stored,
         "final",
         smem=1,
@@ -759,8 +777,10 @@
         limit=32,
     )
     grads = lax.all_to_all(grads, ("pts", "probe"), 0, 0, tiled=True)
-    grads = jnp.sum(grads, axis=0)
-    return answer, grads[:FEAT, TASKS], grads[:, :TASKS]
+    lengths, tasks = call(
+        tail_kernel, [shape(FEAT, 1), shape(TASKS, TASKS)], [grads], "tail", flops=10**5
+    )
+    return answer, lengths[:, 0], tasks
 
 
 def solution(mesh):

time: 96 us -> 94.7 us (0.986)
  Pallas kernels: 38.7 us -> 42.9 us
  waiting for transfers between devices: 19.7 us -> 16.2 us
  local copies, waits for them, and re-layouts: 3.19 us -> 1.59 us
  blocking collectives: 10.5 us -> 9.48 us
    pallas_call x9 -> x10, Pallas kernels: 38.7 us -> 42.9 us  [call(): pl.pallas_call(body, out_shape=outs, in_specs=[sm] * smem + [vm] * (len(a...]
    ppermute x6, waiting for transfers between devices: 12.2 us -> 8.68 us  [both_sides(): return (lax.ppermute(cells, 'pts', up), lax.ppermute(cells, 'pts', down))]
    all_to_all x1, blocking collectives: 10.5 us -> 9.48 us  [shards(): grads = lax.all_to_all(grads, ('pts', 'probe'), 0, 0, tiled=True)]
    unnamed x36 -> x26, local copies, waits for them, and re-layouts: 2.5 us -> 1.59 us
  transfers between devices with their start and end apart: 7 -> 7, of which waited for: 5 -> 4; matrix products, arithmetic and copies ran while one was open for 0% -> 0% of each run, Pallas kernels for 3% -> 7%
where the time goes in v5:
time: 94.7 us; the launch traced here: 94.2 us
  Pallas kernels  42.9 us (45%)
  starting transfers between devices  22.5 us (24%)
  waiting for transfers between devices  16.2 us (17%)
  blocking collectives  9.48 us (10%)
  local copies, waits for them, and re-layouts  1.59 us (2%)
    pallas_call x10, Pallas kernels, call(): pl.pallas_call(body, out_shape=outs, in_specs=[sm] * smem + [vm] * (len(a...  42.9 us
    ppermute x6, starting transfers between devices, both_sides(): return (lax.ppermute(cells, 'pts', up), lax.ppermute(cells, 'pts', down))  17.4 us
    all_to_all x1, blocking collectives, shards(): grads = lax.all_to_all(grads, ('pts', 'probe'), 0, 0, tiled=True)  9.48 us
    ppermute x6, waiting for transfers between devices, both_sides(): return (lax.ppermute(cells, 'pts', up), lax.ppermute(cells, 'pts', down))  8.68 us
    all_to_all x1, waiting for transfers between devices, shards(): gram = lax.all_to_all(gram, 'pts', 0, 0, tiled=True)  7.56 us
    all_to_all x1, starting transfers between devices, shards(): gram = lax.all_to_all(gram, 'pts', 0, 0, tiled=True)  5.09 us
  transfers between devices with their start and end apart: 7, of which 4 were waited for; matrix products, arithmetic and copies ran while one was open for 0% of the time, Pallas kernels for 7%

profile of v5, /device:TPU:0, one launch (start us, length us, event | category | flops | bytes accessed | tf_op | source)
XLA Modules:
  0.0 94.2 jit_solution(17132864202384512213)
XLA Ops:
  0.6 17.1 %invert.1 = (bf16[3,3,256,256]{3,2,1,0:T(8,128)(2,1)S(1)}, f32[32,768]{1,0:T(8,128)S(1)}, f32[24,768]{1,0:T(8,128)S(1)}) custom-call(f32[8,768]{1,0:T(8,128)} %feat_hbm.1, s32[768]{0:T(1024)} %ids_hbm.1, s32[768]{0:T(1024)} %agg_hbm.1, f32[16,768]{1,0:T(8,128)} %refs_0_.1, f32[16,16]{1,0:T(8,128)} %cov_hbm.1, f32[3,24]{1,0:T(4,128)} %coarse_hbm.1, ...), custom_call_target="tpu_custom_call" | custom-call | flops 10000000000 | bytes 1048576 | tf_op jit(solution)/shard_map/invert/pallas_call | solution.py:647
  17.8 4.9 %collective-permute-start = (f32[32,768]{1,0:T(8,128)S(1)}, f32[32,768]{1,0:T(8,128)S(1)}, u32[]{:S(2)}, u32[]{:S(2)}) collective-permute-start(f32[32,768]{1,0:T(8,128)S(1)} %get-tuple-element.28.refs_0_.refs_1_.refs_2_.own_ref), channel_id=1, source_target_pairs={{0,2},{2,4},{4,6},{6,8},{8,10},{10,12},{12,14},{1,3},{3,5},{5,7},{... | collective-permute-start | bytes 294920 | tf_op jit(solution)/shard_map/ppermute | solution.py:663
  22.7 1.3 %collective-permute-start.1 = (f32[32,768]{1,0:T(8,128)S(1)}, f32[32,768]{1,0:T(8,128)S(1)}, u32[]{:S(2)}, u32[]{:S(2)}) collective-permute-start(f32[32,768]{1,0:T(8,128)S(1)} %get-tuple-element.28.refs_0_.refs_1_.refs_2_.own_ref), channel_id=1, source_target_pairs={{2,0},{4,2},{6,4},{8,6},{10,8},{12,10},{14,12},{3,1},{5,3},{7,5},{... | collective-permute-start | bytes 294920 | tf_op jit(solution)/shard_map/ppermute | solution.py:663
  24.0 1.0 %build_own.1 = (bf16[3,768,256]{2,1,0:T(8,128)(2,1)S(1)}, bf16[3,768,256]{2,1,0:T(8,128)(2,1)S(1)}, f32[3,768,256]{2,1,0:T(8,128)S(1)}) custom-call(f32[32,768]{1,0:T(8,128)S(1)} %get-tuple-element.28.refs_0_.refs_1_.refs_2_.own_ref, f32[32,768]{1,0:T(8,128)S(1)} %get-tuple-element.28.refs_0_.refs_1_.refs_2_.own_ref, ...), custom_call_target="tpu_custom_call" | custom-call | flops 1000000000 | bytes 1048576 | tf_op jit(solution)/shard_map/build_own/pallas_call | solution.py:647
  25.0 0.0 collective-permute-done.refs_0_.left_ref.refs_2_
  25.0 4.2 %collective-permute-done.1.refs_1_.right_ref.refs_3_ = f32[32,768]{1,0:T(8,128)S(1)} collective-permute-done((f32[32,768]{1,0:T(8,128)S(1)}, f32[32,768]{1,0:T(8,128)S(1)}, u32[]{:S(2)}, u32[]{:S(2)}) %collective-permute-start.1) | collective-permute-done | bytes 98336 | tf_op jit(solution)/shard_map/ppermute | solution.py:663
  29.2 1.4 %build_halo.1 = (bf16[3,1024,256]{2,1,0:T(8,128)(2,1)S(1)}, bf16[3,1024,256]{2,1,0:T(8,128)(2,1)S(1)}, f32[3,1024,256]{2,1,0:T(8,128)S(1)}) custom-call(f32[32,768]{1,0:T(8,128)S(1)} %collective-permute-done.refs_0_.left_ref.refs_2_, f32[32,768]{1,0:T(8,128)S(1)} %collective-permute-done.1.refs_1_.right_ref.refs_3_, ...), custom_call_target="tpu_custom_call" | custom-call | flops 1000000000 | bytes 1048576 | tf_op jit(solution)/shard_map/build_halo/pallas_call | solution.py:647
  30.6 0.0 copy-start.10
  30.6 1.2 %first.1 = (f32[40,768]{1,0:T(8,128)S(1)}, f32[40,768]{1,0:T(8,128)S(1)}) custom-call(f32[32,768]{1,0:T(8,128)S(1)} %get-tuple-element.28.refs_0_.refs_1_.refs_2_.own_ref, f32[32,768]{1,0:T(8,128)S(1)} %collective-permute-done.refs_0_.left_ref.refs_2_, f32[32,768]{1,0:T(8,128)S(1)} %collective-permute-done.1.refs_1_.right_ref.refs_3_, ...), custom_call_target="tpu_custom_call" | custom-call | flops 1000000000 | bytes 1048576 | tf_op jit(solution)/shard_map/first/pallas_call | solution.py:647
  31.8 0.0 copy-start.4
  31.8 4.3 %collective-permute-start.2 = (f32[40,768]{1,0:T(8,128)S(1)}, f32[40,768]{1,0:T(8,128)S(1)}, u32[]{:S(2)}, u32[]{:S(2)}) collective-permute-start(f32[40,768]{1,0:T(8,128)S(1)} %get-tuple-element.34.d1_ref.vec_ref.refs_4_), channel_id=1, source_target_pairs={{0,2},{2,4},{4,6},{6,8},{8,10},{10,12},{12,14},{1,3},{3,5},{5,7},{... | collective-permute-start | bytes 368648 | tf_op jit(solution)/shard_map/ppermute | solution.py:663
  36.2 1.5 %collective-permute-start.3 = (f32[40,768]{1,0:T(8,128)S(1)}, f32[40,768]{1,0:T(8,128)S(1)}, u32[]{:S(2)}, u32[]{:S(2)}) collective-permute-start(f32[40,768]{1,0:T(8,128)S(1)} %get-tuple-element.34.d1_ref.vec_ref.refs_4_), channel_id=1, source_target_pairs={{2,0},{4,2},{6,4},{8,6},{10,8},{12,10},{14,12},{3,1},{5,3},{7,5},{... | collective-permute-start | bytes 368648 | tf_op jit(solution)/shard_map/ppermute | solution.py:663
  37.7 4.1 %early.1 = (f32[40,128]{1,0:T(8,128)S(1)}, bf16[3,768,256]{2,1,0:T(8,128)(2,1)}, bf16[3,768,256]{2,1,0:T(8,128)(2,1)}, f32[3,768,256]{2,1,0:T(8,128)}, bf16[3,10...) custom-call(f32[32,768]{1,0:T(8,128)S(1)} %get-tuple-element.28.refs_0_.refs_1_.refs_2_.own_ref, ...), custom_call_target="tpu_custom_call" | custom-call | flops 1000000000 | bytes 1048576 | tf_op jit(solution)/shard_map/early/pallas_call | solution.py:647
  41.8 0.0 collective-permute-done.2.left_ref.refs_5_
  41.9 1.1 %collective-permute-done.3.right_ref.refs_6_ = f32[40,768]{1,0:T(8,128)S(1)} collective-permute-done((f32[40,768]{1,0:T(8,128)S(1)}, f32[40,768]{1,0:T(8,128)S(1)}, u32[]{:S(2)}, u32[]{:S(2)}) %collective-permute-start.3) | collective-permute-done | bytes 122912 | tf_op jit(solution)/shard_map/ppermute | solution.py:663
  43.0 1.9 %second.1 = (f32[40,768]{1,0:T(8,128)S(1)}, f32[40,768]{1,0:T(8,128)}) custom-call(f32[24,768]{1,0:T(8,128)S(1)} %get-tuple-element.27.refs_2_.refs_3_.extra_ref, f32[40,768]{1,0:T(8,128)S(1)} %get-tuple-element.34.d1_ref.vec_ref.refs_4_, f32[40,768]{1,0:T(8,128)S(1)} %collective-permute-done.2.left_ref.refs_5_, ...), custom_call_target="tpu_custom_call" | custom-call | flops 1000000000 | bytes 1048576 | tf_op jit(solution)/shard_map/second/pallas_call | solution.py:647
  44.8 0.7 copy-done.11
  45.5 4.1 %collective-permute-start.4 = (f32[40,768]{1,0:T(8,128)}, f32[40,768]{1,0:T(8,128)}, u32[]{:S(2)}, u32[]{:S(2)}) collective-permute-start(f32[40,768]{1,0:T(8,128)} %get-tuple-element.39.d2_ref.vec_ref.refs_7_), channel_id=1, source_target_pairs={{0,2},{2,4},{4,6},{6,8},{8,10},{10,12},{12,14},{1,3},{3,5},{5,7},{... | collective-permute-start | bytes 368648 | tf_op jit(solution)/shard_map/ppermute | solution.py:663
  49.6 1.3 %collective-permute-start.5 = (f32[40,768]{1,0:T(8,128)}, f32[40,768]{1,0:T(8,128)}, u32[]{:S(2)}, u32[]{:S(2)}) collective-permute-start(f32[40,768]{1,0:T(8,128)} %get-tuple-element.39.d2_ref.vec_ref.refs_7_), channel_id=1, source_target_pairs={{2,0},{4,2},{6,4},{8,6},{10,8},{12,10},{14,12},{3,1},{5,3},{7,5},{... | collective-permute-start | bytes 368648 | tf_op jit(solution)/shard_map/ppermute | solution.py:663
  50.9 0.0 copy-done.4
  50.9 0.0 copy-start.12
  50.9 0.9 copy-done.12
  51.8 1.4 %late.1.before_ref = f32[40,128]{1,0:T(8,128)S(1)} custom-call(f32[40,128]{1,0:T(8,128)S(1)} %get-tuple-element.38.early_ref.before_ref, f32[40,768]{1,0:T(8,128)S(1)} %get-tuple-element.34.d1_ref.vec_ref.refs_4_, f32[40,768]{1,0:T(8,128)} %get-tuple-element.39.d2_ref.vec_ref.refs_7_, f32[40,768]{1,0:T(8,128)S(1)} %copy-done.12), custom_call_target="tpu_custom_call" | custom-call | flops 1000000000 | bytes 1048576 | tf_op jit(solution)/shard_map/late/pallas_call | solution.py:647
  53.3 0.0 collective-permute-done.4.left_ref.refs_8_
  53.3 3.4 %collective-permute-done.5.right_ref.refs_9_ = f32[40,768]{1,0:T(8,128)} collective-permute-done((f32[40,768]{1,0:T(8,128)}, f32[40,768]{1,0:T(8,128)}, u32[]{:S(2)}, u32[]{:S(2)}) %collective-permute-start.5) | collective-permute-done | bytes 122912 | tf_op jit(solution)/shard_map/ppermute | solution.py:663
  56.7 3.0 %third.1 = f32[8,40,128]{2,1,0:T(8,128)} custom-call(s32[1]{0:T(128)} %bitcast.1.place_ref, f32[24,768]{1,0:T(8,128)S(1)} %get-tuple-element.27.refs_2_.refs_3_.extra_ref, f32[40,128]{1,0:T(8,128)S(1)} %late.1.before_ref, f32[40,768]{1,0:T(8,128)} %get-tuple-element.39.d2_ref.vec_ref.refs_7_, f32[40,768]{1,0:T(8,128)} %collective-permute-done.4.left_ref.refs_8_, ...), custom_call_target="tpu_custom_call" | custom-call | flops 1000000000 | bytes 1048576 | tf_op jit(solution)/shard_map/third/pallas_call | solution.py:647
  59.7 5.1 %all-to-all-start = ((f32[8,40,128]{2,1,0:T(8,128)}), f32[8,40,128]{2,1,0:T(8,128)S(1)}, u32[]{:S(2)}, u32[]{:S(2)}) async-start(f32[8,40,128]{2,1,0:T(8,128)} %third.1), calls=%async_computation | async-start | bytes 327680 | tf_op jit(solution)/shard_map/all_to_all | solution.py:765
  64.8 7.6 %all-to-all-done.gram_ref = f32[8,40,128]{2,1,0:T(8,128)S(1)} async-done(((f32[8,40,128]{2,1,0:T(8,128)}), f32[8,40,128]{2,1,0:T(8,128)S(1)}, u32[]{:S(2)}, u32[]{:S(2)}) %all-to-all-start) | async-done | bytes 163872 | tf_op jit(solution)/shard_map/all_to_all | solution.py:765
  72.3 11.1 %final.1 = (f32[16,768]{1,0:T(8,128)}, f32[16,8,128]{2,1,0:T(8,128)S(1)}) custom-call(s32[1]{0:T(128)} %bitcast.probe_ref, f32[8,40,128]{2,1,0:T(8,128)S(1)} %all-to-all-done.gram_ref, f32[16,768]{1,0:T(8,128)} %refs_0_.1, f32[32,768]{1,0:T(8,128)} %copy-done.5, f32[32,768]{1,0:T(8,128)} %copy-done.8, f32[32,768]{1,0:T(8,128)} %copy-done.9, ...), custom_call_target="tpu_custom_call" | custom-call | flops 1000000000 | bytes 1048576 | tf_op jit(solution)/shard_map/final/pallas_call | solution.py:647
  83.4 9.5 %all_to_all.10.parts_ref = f32[16,8,128]{2,1,0:T(8,128)S(1)} all-to-all(f32[16,8,128]{2,1,0:T(8,128)S(1)} %get-tuple-element.48), channel_id=1, replica_groups=mesh['groups'=2,'pts'=8,'probe'=2] {'pts','probe'}, dimensions={0} | all-to-all | bytes 131072 | tf_op jit(solution)/shard_map/all_to_all | solution.py:779
  92.9 0.7 tail.1
  93.6 0.6 reduce
  (20 shorter events, 0.0 us)
Async XLA Ops:
  17.8 19.9 %copy-start.5 = (f32[32,768]{1,0:T(8,128)}, f32[32,768]{1,0:T(8,128)S(1)}, u32[]{:S(2)}) copy-start(f32[32,768]{1,0:T(8,128)S(1)} %get-tuple-element.28.refs_0_.refs_1_.refs_2_.own_ref) | copy-start | bytes 294916
  17.8 7.2 %collective-permute-start = (f32[32,768]{1,0:T(8,128)S(1)}, f32[32,768]{1,0:T(8,128)S(1)}, u32[]{:S(2)}, u32[]{:S(2)}) collective-permute-start(f32[32,768]{1,0:T(8,128)S(1)} %get-tuple-element.28.refs_0_.refs_1_.refs_2_.own_ref), channel_id=1, source_target_pairs={{0,2},{2,4},{4,6},{6,8},{8,10},{10,12},{12,14},{1,3},{3,5},{5,7},{... | collective-permute-start | bytes 294920 | tf_op jit(solution)/shard_map/ppermute | solution.py:663
  22.7 6.5 %collective-permute-start.1 = (f32[32,768]{1,0:T(8,128)S(1)}, f32[32,768]{1,0:T(8,128)S(1)}, u32[]{:S(2)}, u32[]{:S(2)}) collective-permute-start(f32[32,768]{1,0:T(8,128)S(1)} %get-tuple-element.28.refs_0_.refs_1_.refs_2_.own_ref), channel_id=1, source_target_pairs={{2,0},{4,2},{6,4},{8,6},{10,8},{12,10},{14,12},{3,1},{5,3},{7,5},{... | collective-permute-start | bytes 294920 | tf_op jit(solution)/shard_map/ppermute | solution.py:663
  25.0 18.0 %copy-start = (bf16[3,768,256]{2,1,0:T(8,128)(2,1)}, bf16[3,768,256]{2,1,0:T(8,128)(2,1)S(1)}, u32[]{:S(2)}) copy-start(bf16[3,768,256]{2,1,0:T(8,128)(2,1)S(1)} %get-tuple-element.29.refs_0_) | copy-start | bytes 3538948
  25.0 18.0 %copy-start.2 = (bf16[3,768,256]{2,1,0:T(8,128)(2,1)}, bf16[3,768,256]{2,1,0:T(8,128)(2,1)S(1)}, u32[]{:S(2)}) copy-start(bf16[3,768,256]{2,1,0:T(8,128)(2,1)S(1)} %get-tuple-element.30.refs_1_) | copy-start | bytes 3538948
  25.0 5.6 %copy-start.8 = (f32[32,768]{1,0:T(8,128)}, f32[32,768]{1,0:T(8,128)S(1)}, u32[]{:S(2)}) copy-start(f32[32,768]{1,0:T(8,128)S(1)} %collective-permute-done.refs_0_.left_ref.refs_2_) | copy-start | bytes 294916
  29.2 1.4 %copy-start.9 = (f32[32,768]{1,0:T(8,128)}, f32[32,768]{1,0:T(8,128)S(1)}, u32[]{:S(2)}) copy-start(f32[32,768]{1,0:T(8,128)S(1)} %collective-permute-done.1.refs_1_.right_ref.refs_3_) | copy-start | bytes 294916
  30.6 7.1 %copy-start.10 = (f32[16,768]{1,0:T(8,128)S(1)}, f32[16,768]{1,0:T(8,128)}, u32[]{:S(2)}) copy-start(f32[16,768]{1,0:T(8,128)} %refs_0_.1) | copy-start | bytes 147460
  31.8 19.1 %copy-start.4 = (f32[40,768]{1,0:T(8,128)}, f32[40,768]{1,0:T(8,128)S(1)}, u32[]{:S(2)}) copy-start(f32[40,768]{1,0:T(8,128)S(1)} %get-tuple-element.34.d1_ref.vec_ref.refs_4_) | copy-start | bytes 368644
  31.8 10.0 %collective-permute-start.2 = (f32[40,768]{1,0:T(8,128)S(1)}, f32[40,768]{1,0:T(8,128)S(1)}, u32[]{:S(2)}, u32[]{:S(2)}) collective-permute-start(f32[40,768]{1,0:T(8,128)S(1)} %get-tuple-element.34.d1_ref.vec_ref.refs_4_), channel_id=1, source_target_pairs={{0,2},{2,4},{4,6},{6,8},{8,10},{10,12},{12,14},{1,3},{3,5},{5,7},{... | collective-permute-start | bytes 368648 | tf_op jit(solution)/shard_map/ppermute | solution.py:663
  36.2 6.8 %collective-permute-start.3 = (f32[40,768]{1,0:T(8,128)S(1)}, f32[40,768]{1,0:T(8,128)S(1)}, u32[]{:S(2)}, u32[]{:S(2)}) collective-permute-start(f32[40,768]{1,0:T(8,128)S(1)} %get-tuple-element.34.d1_ref.vec_ref.refs_4_), channel_id=1, source_target_pairs={{2,0},{4,2},{6,4},{8,6},{10,8},{12,10},{14,12},{3,1},{5,3},{7,5},{... | collective-permute-start | bytes 368648 | tf_op jit(solution)/shard_map/ppermute | solution.py:663
  41.9 3.0 %copy-start.6 = (f32[40,768]{1,0:T(8,128)}, f32[40,768]{1,0:T(8,128)S(1)}, u32[]{:S(2)}) copy-start(f32[40,768]{1,0:T(8,128)S(1)} %collective-permute-done.2.left_ref.refs_5_) | copy-start | bytes 368644
  43.0 1.9 %copy-start.7 = (f32[40,768]{1,0:T(8,128)}, f32[40,768]{1,0:T(8,128)S(1)}, u32[]{:S(2)}) copy-start(f32[40,768]{1,0:T(8,128)S(1)} %collective-permute-done.3.right_ref.refs_6_) | copy-start | bytes 368644
  44.8 0.7 copy-start.11
  45.5 7.8 %collective-permute-start.4 = (f32[40,768]{1,0:T(8,128)}, f32[40,768]{1,0:T(8,128)}, u32[]{:S(2)}, u32[]{:S(2)}) collective-permute-start(f32[40,768]{1,0:T(8,128)} %get-tuple-element.39.d2_ref.vec_ref.refs_7_), channel_id=1, source_target_pairs={{0,2},{2,4},{4,6},{6,8},{8,10},{10,12},{12,14},{1,3},{3,5},{5,7},{... | collective-permute-start | bytes 368648 | tf_op jit(solution)/shard_map/ppermute | solution.py:663
  49.6 7.1 %collective-permute-start.5 = (f32[40,768]{1,0:T(8,128)}, f32[40,768]{1,0:T(8,128)}, u32[]{:S(2)}, u32[]{:S(2)}) collective-permute-start(f32[40,768]{1,0:T(8,128)} %get-tuple-element.39.d2_ref.vec_ref.refs_7_), channel_id=1, source_target_pairs={{2,0},{4,2},{6,4},{8,6},{10,8},{12,10},{14,12},{3,1},{5,3},{7,5},{... | collective-permute-start | bytes 368648 | tf_op jit(solution)/shard_map/ppermute | solution.py:663
  50.9 0.9 copy-start.12
  51.8 4.9 %copy-start.1 = (bf16[3,768,256]{2,1,0:T(8,128)(2,1)S(1)}, bf16[3,768,256]{2,1,0:T(8,128)(2,1)}, u32[]{:S(2)}) copy-start(bf16[3,768,256]{2,1,0:T(8,128)(2,1)} %copy-done) | copy-start | bytes 3538948
  51.8 4.9 %copy-start.3 = (bf16[3,768,256]{2,1,0:T(8,128)(2,1)S(1)}, bf16[3,768,256]{2,1,0:T(8,128)(2,1)}, u32[]{:S(2)}) copy-start(bf16[3,768,256]{2,1,0:T(8,128)(2,1)} %copy-done.2) | copy-start | bytes 3538948
  59.7 12.7 %all-to-all-start = ((f32[8,40,128]{2,1,0:T(8,128)}), f32[8,40,128]{2,1,0:T(8,128)S(1)}, u32[]{:S(2)}, u32[]{:S(2)}) async-start(f32[8,40,128]{2,1,0:T(8,128)} %third.1), calls=%async_computation | async-start | bytes 327680 | tf_op jit(solution)/shard_map/all_to_all | solution.py:765

commit v6 on v5

--- a/solution.py
+++ b/solution.py
@@ -133,30 +133,49 @@
     return out
 
 
+def with_rows(cells, first, rows):
+    top = first - first % 8
+    part = cells[top : top + 8]
+    sub = iota((8, 1), 0)
+    for t, row in enumerate(rows):
+        part = jnp.where(sub == first - top + t, row, part)
+    pieces = [cells[:top], part, cells[top + 8 :]]
+    return jnp.concatenate([p for p in pieces if p.shape[0]], axis=0)
+
+
 def sweep_base(cells):
     lane = iota((BASE, LANES), 1)
     start = lane - lane % BASE
     inner = iota((1, LANES), 1) % BASE
-    sub = iota((BASE, 1), 0)
-    for g in range(BASE // GROUP):
-        first = g * GROUP
-        cols = [
+
+    def columns(first):
+        return [
             jnp.take_along_axis(cells, start + (first + t), axis=1, mode="promise_in_bounds")
             for t in range(GROUP)
         ]
-        rows = [cells[first + t : first + t + 1, :] for t in range(GROUP)]
+
+    cols = columns(0)
+    for first in range(0, BASE, GROUP):
+        ahead = columns(first + GROUP) if first + GROUP < BASE else []
         pivots = [[cols[u][first + t : first + t + 1, :] for u in range(GROUP)] for t in range(GROUP)]
         inv = small_inverse(pivots)
-        rows = [jnp.where(inner == first + t, -1.0, rows[t]) for t in range(GROUP)]
+        coming = []
+        for col in ahead:
+            head = [col[first + t : first + t + 1, :] for t in range(GROUP)]
+            factor = [sum(inv[t][u] * head[u] for u in range(GROUP)) for t in range(GROUP)]
+            for t in range(GROUP):
+                col = col - cols[t] * factor[t]
+            coming.append(with_rows(col, first, factor))
+        rows = [cells[first + t : first + t + 1, :] for t in range(GROUP)]
         group = (inner >= first) & (inner < first + GROUP)
         for t in range(GROUP):
-            rows[t] = jnp.where(group & (inner != first + t), 0.0, rows[t])
+            rows[t] = jnp.where(inner == first + t, -1.0, jnp.where(group, 0.0, rows[t]))
         new = [sum(inv[t][u] * rows[u] for u in range(GROUP)) for t in range(GROUP)]
         cells = jnp.where(group, 0.0, cells)
         for t in range(GROUP):
             cells = cells - cols[t] * new[t]
-        for t in range(GROUP):
-            cells = jnp.where(sub == first + t, new[t], cells)
+        cells = with_rows(cells, first, new)
+        cols = coming
     return cells
 
 
@@ -219,10 +238,10 @@
     seg = iota((BASE, LANES), 1) // BASE
     wide = iota((BASE, BS), 1)
     deep = iota((BASE, BS), 0)
+    strips = [work[m, 0:BASE, :] for m in range(blocks)]
     for k in range(BS // BASE):
         first = k * BASE
         tile, inside = first // LANES, first % LANES
-        strips = [work[m, first : first + BASE, :] for m in range(blocks)]
         cells = jnp.where(iota((BASE, LANES), 1) % BASE == iota((BASE, LANES), 0), 1.0, 0.0)
         for m in range(blocks):
             piece = strips[m][:, tile * LANES : (tile + 1) * LANES]
@@ -241,20 +260,23 @@
         spread = jnp.concatenate([jnp.where(seg == m, inv, 0.0) for m in range(blocks)], axis=0)
         new = dot(spread, stack, precision=highest)
         gone = (iota((1, BS), 1) >= first) & (iota((1, BS), 1) < first + BASE)
+        coming = []
         for m in range(blocks):
             row = new[m * BASE : (m + 1) * BASE, :]
             r0, r1, r2 = split(strips[m], 3)
             p0, p1, p2 = split(row, 3)
             a = jnp.concatenate([r0, r0, r1, r1, r0, r2], axis=0).astype(bf16)
             b = jnp.concatenate([p0, p1, p0, p1, p2, p0], axis=0).astype(bf16)
-            work[m] = jnp.where(gone, 0.0, work[m]) - dot(a, b, TN)
+            value = jnp.where(gone, 0.0, work[m]) - dot(a, b, TN)
+            coming.append(value[first + BASE : first + 2 * BASE])
+            work[m] = value
             work[m, first : first + BASE, :] = row
+        strips = coming
     for m in range(blocks):
-        at = slice(m * BS, (m + 1) * BS)
         inv = -work[m]
         for i, part in enumerate(split(inv, 3)):
             jac_ref[i, m] = part.astype(bf16)
-        pack_ref[SYS:, at] = dot(sys_ref[:, at], inv, precision=highest)
+    pack_ref[SYS:, :] = smooth(sys_ref[...], jac_ref)
 
 
 def own_places(m):
@@ -422,7 +444,8 @@
 def third_kernel(
     place_ref, extra_ref, before_ref, vec_ref, left_ref, right_ref, *refs, count, held
 ):
-    kernel, out_ref = refs[:4], refs[4]
+    kernel, others, (out_ref, *stashes), sems = refs[:4], refs[4:10], refs[10:20], refs[20]
+    copies = fetch(list(zip([*others, vec_ref, left_ref, right_ref], stashes)), sems)
     coarse = vec_ref.shape[0] - count
     lanes = out_ref.shape[2]
     pitch = pitch_of(coarse)
@@ -441,6 +464,8 @@
     for c in range(out_ref.shape[0]):
         out_ref[c, 0:count, :] = top
         out_ref[c, count:, :] = bottom
+    for copy in copies:
+        copy.wait()
 
 
 def final_kernel(
@@ -614,8 +639,8 @@
         [
             task_total[:half],
             task_total[half:],
-            length_total,
-            jnp.zeros((half, LANES - 2 * TASKS - 1), f32),
+            jnp.where(iota((half, FEAT), 0) == iota((half, FEAT), 1), length_total, 0.0),
+            jnp.zeros((half, LANES - 2 * TASKS - FEAT), f32),
         ],
         axis=1,
     )
@@ -630,7 +655,7 @@
     half = TASKS // 2
     task_ref[0:half, :] = total[:, :TASKS]
     task_ref[half:, :] = total[:, TASKS : 2 * TASKS]
-    length_ref[...] = total[:, 2 * TASKS : 2 * TASKS + 1]
+    length_ref[...] = jnp.sum(total[:, 2 * TASKS : 2 * TASKS + FEAT], axis=0)
 
 
 MIB = 1024 * 1024
@@ -754,16 +779,19 @@
     )
     place = lax.axis_index("pts").astype(jnp.int32)[None]
     probe = lax.axis_index("probe").astype(jnp.int32)[None]
-    (gram,) = call(
+    others = [pack, pack_l, pack_r, d1, d1_l, d1_r]
+    gram, *vectors = call(
         functools.partial(third_kernel, count=count, held=coarse_inverse.shape[0]),
-        [shape(ranks, rows, lanes)],
-        [place, extra, late, d2, d2_l, d2_r] + kernel,
+        [shape(ranks, rows, lanes)] + [shape(*a.shape) for a in others + [d2] * 3],
+        [place, extra, late, d2, d2_l, d2_r] + kernel + others,
         "third",
         smem=1,
+        far_outs=9,
+        scratch=[pltpu.SemaphoreType.DMA((9,))],
         flops=10**9,
     )
     gram = lax.all_to_all(gram, "pts", 0, 0, tiled=True)
-    stored = [systems, pack, pack_l, pack_r, d1, d1_l, d1_r, d2, d2_l, d2_r] + stashed
+    stored = [systems] + vectors + stashed
     answer, grads = call(
         functools.partial(final_kernel, sides=sides * count, points=ranks * width),
         [shape(count, width), shape(ranks * sides, FEAT, LANES)],
@@ -778,9 +806,9 @@
     )
     grads = lax.all_to_all(grads, ("pts", "probe"), 0, 0, tiled=True)
     lengths, tasks = call(
-        tail_kernel, [shape(FEAT, 1), shape(TASKS, TASKS)], [grads], "tail", flops=10**5
-    )
-    return answer, lengths[:, 0], tasks
+        tail_kernel, [shape(FEAT), shape(TASKS, TASKS)], [grads], "tail", flops=10**5
+    )
+    return answer, lengths, tasks
 
 
 def solution(mesh):

time: 94.7 us -> 90.7 us (0.958)
  Pallas kernels: 42.9 us -> 39 us
  local copies, waits for them, and re-layouts: 1.59 us -> 2.97 us
    pallas_call x10, Pallas kernels: 42.9 us -> 39 us  [call(): pl.pallas_call(body, out_shape=outs, in_specs=[sm] * smem + [vm] * (len(a...]
    unnamed x26 -> x32, local copies, waits for them, and re-layouts: 1.59 us -> 2.97 us
where the time goes in v6:
time: 90.7 us; the launch traced here: 90.2 us
  Pallas kernels  39 us (43%)
  starting transfers between devices  22.3 us (25%)
  waiting for transfers between devices  15.5 us (17%)
  blocking collectives  9.48 us (10%)
  local copies, waits for them, and re-layouts  2.97 us (3%)
    pallas_call x10, Pallas kernels, call(): pl.pallas_call(body, out_shape=outs, in_specs=[sm] * smem + [vm] * (len(a...  39 us
    ppermute x6, starting transfers between devices, both_sides(): return (lax.ppermute(cells, 'pts', up), lax.ppermute(cells, 'pts', down))  17.3 us
    all_to_all x1, blocking collectives, shards(): grads = lax.all_to_all(grads, ('pts', 'probe'), 0, 0, tiled=True)  9.48 us
    ppermute x6, waiting for transfers between devices, both_sides(): return (lax.ppermute(cells, 'pts', up), lax.ppermute(cells, 'pts', down))  7.95 us
    all_to_all x1, waiting for transfers between devices, shards(): gram = lax.all_to_all(gram, 'pts', 0, 0, tiled=True)  7.56 us
    all_to_all x1, starting transfers between devices, shards(): gram = lax.all_to_all(gram, 'pts', 0, 0, tiled=True)  4.98 us
    unnamed x32, local copies, waits for them, and re-layouts  2.97 us
  transfers between devices with their start and end apart: 7, of which 4 were waited for; matrix products, arithmetic and copies ran while one was open for 0% of the time, Pallas kernels for 7%

profile of v6, /device:TPU:0, one launch (start us, length us, event | category | flops | bytes accessed | tf_op | source)
XLA Modules:
  0.0 90.2 jit_solution(15055497302765867439)
XLA Ops:
  0.6 13.1 %invert.1 = (bf16[3,3,256,256]{3,2,1,0:T(8,128)(2,1)S(1)}, f32[32,768]{1,0:T(8,128)S(1)}, f32[24,768]{1,0:T(8,128)S(1)}) custom-call(f32[8,768]{1,0:T(8,128)} %feat_hbm.1, s32[768]{0:T(1024)} %ids_hbm.1, s32[768]{0:T(1024)} %agg_hbm.1, f32[16,768]{1,0:T(8,128)} %refs_0_.1, f32[16,16]{1,0:T(8,128)} %cov_hbm.1, f32[3,24]{1,0:T(4,128)} %coarse_hbm.1, ...), custom_call_target="tpu_custom_call" | custom-call | flops 10000000000 | bytes 1048576 | tf_op jit(solution)/shard_map/invert/pallas_call | solution.py:672
  13.7 4.9 %collective-permute-start = (f32[32,768]{1,0:T(8,128)S(1)}, f32[32,768]{1,0:T(8,128)S(1)}, u32[]{:S(2)}, u32[]{:S(2)}) collective-permute-start(f32[32,768]{1,0:T(8,128)S(1)} %get-tuple-element.38.refs_0_.refs_1_.refs_2_.own_ref.refs_4_), channel_id=1, source_target_pairs={{0,2},{2,4},{4,6},{6,8},{8,10},{10,12},{12,14},{1,3},{3,5},{5,7},{... | collective-permute-start | bytes 294920 | tf_op jit(solution)/shard_map/ppermute | solution.py:688
  18.6 1.5 %collective-permute-start.1 = (f32[32,768]{1,0:T(8,128)S(1)}, f32[32,768]{1,0:T(8,128)S(1)}, u32[]{:S(2)}, u32[]{:S(2)}) collective-permute-start(f32[32,768]{1,0:T(8,128)S(1)} %get-tuple-element.38.refs_0_.refs_1_.refs_2_.own_ref.refs_4_), channel_id=1, source_target_pairs={{2,0},{4,2},{6,4},{8,6},{10,8},{12,10},{14,12},{3,1},{5,3},{7,5},{... | collective-permute-start | bytes 294920 | tf_op jit(solution)/shard_map/ppermute | solution.py:688
  20.1 1.0 %build_own.1 = (bf16[3,768,256]{2,1,0:T(8,128)(2,1)S(1)}, bf16[3,768,256]{2,1,0:T(8,128)(2,1)S(1)}, f32[3,768,256]{2,1,0:T(8,128)S(1)}) custom-call(f32[32,768]{1,0:T(8,128)S(1)} %get-tuple-element.38.refs_0_.refs_1_.refs_2_.own_ref.refs_4_, f32[32,768]{1,0:T(8,128)S(1)} %get-tuple-element.38.refs_0_.refs_1_.refs_2_.own_ref.refs_4_, ...), custom_call_target="tpu_custom_call" | custom-call | flops 1000000000 | bytes 1048576 | tf_op jit(solution)/shard_map/build_own/pallas_call | solution.py:672
  21.1 0.0 collective-permute-done.refs_0_.left_ref.refs_5_
  21.1 4.0 %collective-permute-done.1.refs_1_.right_ref.refs_6_ = f32[32,768]{1,0:T(8,128)S(1)} collective-permute-done((f32[32,768]{1,0:T(8,128)S(1)}, f32[32,768]{1,0:T(8,128)S(1)}, u32[]{:S(2)}, u32[]{:S(2)}) %collective-permute-start.1) | collective-permute-done | bytes 98336 | tf_op jit(solution)/shard_map/ppermute | solution.py:688
  25.1 1.4 %build_halo.1 = (bf16[3,1024,256]{2,1,0:T(8,128)(2,1)S(1)}, bf16[3,1024,256]{2,1,0:T(8,128)(2,1)S(1)}, f32[3,1024,256]{2,1,0:T(8,128)S(1)}) custom-call(f32[32,768]{1,0:T(8,128)S(1)} %collective-permute-done.refs_0_.left_ref.refs_5_, f32[32,768]{1,0:T(8,128)S(1)} %collective-permute-done.1.refs_1_.right_ref.refs_6_, ...), custom_call_target="tpu_custom_call" | custom-call | flops 1000000000 | bytes 1048576 | tf_op jit(solution)/shard_map/build_halo/pallas_call | solution.py:672
  26.5 0.0 copy-start.10
  26.5 1.2 %first.1 = (f32[40,768]{1,0:T(8,128)S(1)}, f32[40,768]{1,0:T(8,128)S(1)}) custom-call(f32[32,768]{1,0:T(8,128)S(1)} %get-tuple-element.38.refs_0_.refs_1_.refs_2_.own_ref.refs_4_, f32[32,768]{1,0:T(8,128)S(1)} %collective-permute-done.refs_0_.left_ref.refs_5_, f32[32,768]{1,0:T(8,128)S(1)} %collective-permute-done.1.refs_1_.right_ref.refs_6_, ...), custom_call_target="tpu_custom_call" | custom-call | flops 1000000000 | bytes 1048576 | tf_op jit(solution)/shard_map/first/pallas_call | solution.py:672
  27.8 4.3 %collective-permute-start.2 = (f32[40,768]{1,0:T(8,128)S(1)}, f32[40,768]{1,0:T(8,128)S(1)}, u32[]{:S(2)}, u32[]{:S(2)}) collective-permute-start(f32[40,768]{1,0:T(8,128)S(1)} %get-tuple-element.44.d1_ref.vec_ref.refs_7_), channel_id=1, source_target_pairs={{0,2},{2,4},{4,6},{6,8},{8,10},{10,12},{12,14},{1,3},{3,5},{5,7},{... | collective-permute-start | bytes 368648 | tf_op jit(solution)/shard_map/ppermute | solution.py:688
  32.1 1.3 %collective-permute-start.3 = (f32[40,768]{1,0:T(8,128)S(1)}, f32[40,768]{1,0:T(8,128)S(1)}, u32[]{:S(2)}, u32[]{:S(2)}) collective-permute-start(f32[40,768]{1,0:T(8,128)S(1)} %get-tuple-element.44.d1_ref.vec_ref.refs_7_), channel_id=1, source_target_pairs={{2,0},{4,2},{6,4},{8,6},{10,8},{12,10},{14,12},{3,1},{5,3},{7,5},{... | collective-permute-start | bytes 368648 | tf_op jit(solution)/shard_map/ppermute | solution.py:688
  33.4 4.1 %early.1 = (f32[40,128]{1,0:T(8,128)S(1)}, bf16[3,768,256]{2,1,0:T(8,128)(2,1)}, bf16[3,768,256]{2,1,0:T(8,128)(2,1)}, f32[3,768,256]{2,1,0:T(8,128)}, bf16[3,10...) custom-call(f32[32,768]{1,0:T(8,128)S(1)} %get-tuple-element.38.refs_0_.refs_1_.refs_2_.own_ref.refs_4_,, ...), custom_call_target="tpu_custom_call" | custom-call | flops 1000000000 | bytes 1048576 | tf_op jit(solution)/shard_map/early/pallas_call | solution.py:672
  37.6 0.0 copy-start.12
  37.6 0.0 collective-permute-done.2.left_ref.refs_8_
  37.6 1.3 %collective-permute-done.3.right_ref.refs_9_ = f32[40,768]{1,0:T(8,128)S(1)} collective-permute-done((f32[40,768]{1,0:T(8,128)S(1)}, f32[40,768]{1,0:T(8,128)S(1)}, u32[]{:S(2)}, u32[]{:S(2)}) %collective-permute-start.3) | collective-permute-done | bytes 122912 | tf_op jit(solution)/shard_map/ppermute | solution.py:688
  38.9 1.8 %second.1 = (f32[40,768]{1,0:T(8,128)S(1)}, f32[40,768]{1,0:T(8,128)}) custom-call(f32[24,768]{1,0:T(8,128)S(1)} %get-tuple-element.37.refs_2_.refs_3_.extra_ref, f32[40,768]{1,0:T(8,128)S(1)} %get-tuple-element.44.d1_ref.vec_ref.refs_7_, f32[40,768]{1,0:T(8,128)S(1)} %collective-permute-done.2.left_ref.refs_8_, ...), custom_call_target="tpu_custom_call" | custom-call | flops 1000000000 | bytes 1048576 | tf_op jit(solution)/shard_map/second/pallas_call | solution.py:672
  40.7 0.6 copy-done.14
  41.4 4.1 %collective-permute-start.4 = (f32[40,768]{1,0:T(8,128)}, f32[40,768]{1,0:T(8,128)}, u32[]{:S(2)}, u32[]{:S(2)}) collective-permute-start(f32[40,768]{1,0:T(8,128)} %get-tuple-element.49.d2_ref.vec_ref), channel_id=1, source_target_pairs={{0,2},{2,4},{4,6},{6,8},{8,10},{10,12},{12,14},{1,3},{3,5},{5,7},{... | collective-permute-start | bytes 368648 | tf_op jit(solution)/shard_map/ppermute | solution.py:688
  45.4 1.3 %collective-permute-start.5 = (f32[40,768]{1,0:T(8,128)}, f32[40,768]{1,0:T(8,128)}, u32[]{:S(2)}, u32[]{:S(2)}) collective-permute-start(f32[40,768]{1,0:T(8,128)} %get-tuple-element.49.d2_ref.vec_ref), channel_id=1, source_target_pairs={{2,0},{4,2},{6,4},{8,6},{10,8},{12,10},{14,12},{3,1},{5,3},{7,5},{... | collective-permute-start | bytes 368648 | tf_op jit(solution)/shard_map/ppermute | solution.py:688
  46.7 0.0 copy-start.13
  46.7 0.7 copy-done.13
  47.5 0.9 copy-done.15
  48.4 1.4 %late.1.before_ref = f32[40,128]{1,0:T(8,128)S(1)} custom-call(f32[40,128]{1,0:T(8,128)S(1)} %copy-done.13, f32[40,768]{1,0:T(8,128)S(1)} %get-tuple-element.44.d1_ref.vec_ref.refs_7_, f32[40,768]{1,0:T(8,128)} %get-tuple-element.49.d2_ref.vec_ref, f32[40,768]{1,0:T(8,128)S(1)} %copy-done.15), custom_call_target="tpu_custom_call" | custom-call | flops 1000000000 | bytes 1048576 | tf_op jit(solution)/shard_map/late/pallas_call | solution.py:672
  49.8 0.0 collective-permute-done.4.left_ref
  49.8 2.7 %collective-permute-done.5.right_ref = f32[40,768]{1,0:T(8,128)} collective-permute-done((f32[40,768]{1,0:T(8,128)}, f32[40,768]{1,0:T(8,128)}, u32[]{:S(2)}, u32[]{:S(2)}) %collective-permute-start.5) | collective-permute-done | bytes 122912 | tf_op jit(solution)/shard_map/ppermute | solution.py:688
  52.5 3.1 %third.1 = (f32[8,40,128]{2,1,0:T(8,128)S(1)}, f32[32,768]{1,0:T(8,128)}, f32[32,768]{1,0:T(8,128)}, f32[32,768]{1,0:T(8,128)}, f32[40,768]{1,0:T(8,128)}, /*ind...) custom-call(s32[1]{0:T(128)} %bitcast.1.place_ref, ...), custom_call_target="tpu_custom_call" | custom-call | flops 1000000000 | bytes 1048576 | tf_op jit(solution)/shard_map/third/pallas_call | solution.py:672
  55.7 0.7 copy-done.11
  56.4 5.0 %all-to-all-start = ((f32[8,40,128]{2,1,0:T(8,128)}), f32[8,40,128]{2,1,0:T(8,128)S(1)}, u32[]{:S(2)}, u32[]{:S(2)}) async-start(f32[8,40,128]{2,1,0:T(8,128)} %copy-done.11), calls=%async_computation | async-start | bytes 327680 | tf_op jit(solution)/shard_map/all_to_all | solution.py:793
  61.3 7.6 %all-to-all-done.gram_ref = f32[8,40,128]{2,1,0:T(8,128)S(1)} async-done(((f32[8,40,128]{2,1,0:T(8,128)}), f32[8,40,128]{2,1,0:T(8,128)S(1)}, u32[]{:S(2)}, u32[]{:S(2)}) %all-to-all-start) | async-done | bytes 163872 | tf_op jit(solution)/shard_map/all_to_all | solution.py:793
  68.9 11.1 %final.1 = (f32[16,768]{1,0:T(8,128)}, f32[16,8,128]{2,1,0:T(8,128)S(1)}) custom-call(s32[1]{0:T(128)} %bitcast.probe_ref, f32[8,40,128]{2,1,0:T(8,128)S(1)} %all-to-all-done.gram_ref, f32[16,768]{1,0:T(8,128)} %refs_0_.1, f32[32,768]{1,0:T(8,128)} %get-tuple-element.52.refs_1_, f32[32,768]{1,0:T(8,128)} %get-tuple-element.53.refs_2_, ...), custom_call_target="tpu_custom_call" | custom-call | flops 1000000000 | bytes 1048576 | tf_op jit(solution)/shard_map/final/pallas_call | solution.py:672
  80.0 9.5 %all_to_all.10.parts_ref = f32[16,8,128]{2,1,0:T(8,128)S(1)} all-to-all(f32[16,8,128]{2,1,0:T(8,128)S(1)} %get-tuple-element.68), channel_id=1, replica_groups=mesh['groups'=2,'pts'=8,'probe'=2] {'pts','probe'}, dimensions={0} | all-to-all | bytes 131072 | tf_op jit(solution)/shard_map/all_to_all | solution.py:807
  89.5 0.7 tail.1
  (25 shorter events, 0.0 us)
Async XLA Ops:
  13.7 7.4 %collective-permute-start = (f32[32,768]{1,0:T(8,128)S(1)}, f32[32,768]{1,0:T(8,128)S(1)}, u32[]{:S(2)}, u32[]{:S(2)}) collective-permute-start(f32[32,768]{1,0:T(8,128)S(1)} %get-tuple-element.38.refs_0_.refs_1_.refs_2_.own_ref.refs_4_), channel_id=1, source_target_pairs={{0,2},{2,4},{4,6},{6,8},{8,10},{10,12},{12,14},{1,3},{3,5},{5,7},{... | collective-permute-start | bytes 294920 | tf_op jit(solution)/shard_map/ppermute | solution.py:688
  18.6 6.5 %collective-permute-start.1 = (f32[32,768]{1,0:T(8,128)S(1)}, f32[32,768]{1,0:T(8,128)S(1)}, u32[]{:S(2)}, u32[]{:S(2)}) collective-permute-start(f32[32,768]{1,0:T(8,128)S(1)} %get-tuple-element.38.refs_0_.refs_1_.refs_2_.own_ref.refs_4_), channel_id=1, source_target_pairs={{2,0},{4,2},{6,4},{8,6},{10,8},{12,10},{14,12},{3,1},{5,3},{7,5},{... | collective-permute-start | bytes 294920 | tf_op jit(solution)/shard_map/ppermute | solution.py:688
  21.1 17.8 %copy-start = (bf16[3,768,256]{2,1,0:T(8,128)(2,1)}, bf16[3,768,256]{2,1,0:T(8,128)(2,1)S(1)}, u32[]{:S(2)}) copy-start(bf16[3,768,256]{2,1,0:T(8,128)(2,1)S(1)} %get-tuple-element.39.refs_0_) | copy-start | bytes 3538948
  21.1 17.8 %copy-start.2 = (bf16[3,768,256]{2,1,0:T(8,128)(2,1)}, bf16[3,768,256]{2,1,0:T(8,128)(2,1)S(1)}, u32[]{:S(2)}) copy-start(bf16[3,768,256]{2,1,0:T(8,128)(2,1)S(1)} %get-tuple-element.40.refs_1_) | copy-start | bytes 3538948
  25.1 1.4 %copy-start.8 = (f32[32,768]{1,0:T(8,128)}, f32[32,768]{1,0:T(8,128)S(1)}, u32[]{:S(2)}) copy-start(f32[32,768]{1,0:T(8,128)S(1)} %collective-permute-done.1.refs_1_.right_ref.refs_6_) | copy-start | bytes 294916
  26.5 6.9 %copy-start.10 = (f32[16,768]{1,0:T(8,128)S(1)}, f32[16,768]{1,0:T(8,128)}, u32[]{:S(2)}) copy-start(f32[16,768]{1,0:T(8,128)} %refs_0_.1) | copy-start | bytes 147460
  27.8 9.8 %collective-permute-start.2 = (f32[40,768]{1,0:T(8,128)S(1)}, f32[40,768]{1,0:T(8,128)S(1)}, u32[]{:S(2)}, u32[]{:S(2)}) collective-permute-start(f32[40,768]{1,0:T(8,128)S(1)} %get-tuple-element.44.d1_ref.vec_ref.refs_7_), channel_id=1, source_target_pairs={{0,2},{2,4},{4,6},{6,8},{8,10},{10,12},{12,14},{1,3},{3,5},{5,7},{... | collective-permute-start | bytes 368648 | tf_op jit(solution)/shard_map/ppermute | solution.py:688
  32.1 6.8 %collective-permute-start.3 = (f32[40,768]{1,0:T(8,128)S(1)}, f32[40,768]{1,0:T(8,128)S(1)}, u32[]{:S(2)}, u32[]{:S(2)}) collective-permute-start(f32[40,768]{1,0:T(8,128)S(1)} %get-tuple-element.44.d1_ref.vec_ref.refs_7_), channel_id=1, source_target_pairs={{2,0},{4,2},{6,4},{8,6},{10,8},{12,10},{14,12},{3,1},{5,3},{7,5},{... | collective-permute-start | bytes 368648 | tf_op jit(solution)/shard_map/ppermute | solution.py:688
  37.6 3.2 %copy-start.12 = (f32[40,128]{1,0:T(8,128)}, f32[40,128]{1,0:T(8,128)S(1)}, u32[]{:S(2)}) copy-start(f32[40,128]{1,0:T(8,128)S(1)} %get-tuple-element.48.early_ref.before_ref) | copy-start | bytes 61444
  37.6 3.1 %copy-start.4 = (f32[40,768]{1,0:T(8,128)}, f32[40,768]{1,0:T(8,128)S(1)}, u32[]{:S(2)}) copy-start(f32[40,768]{1,0:T(8,128)S(1)} %collective-permute-done.2.left_ref.refs_8_) | copy-start | bytes 368644
  38.9 1.9 %copy-start.6 = (f32[40,768]{1,0:T(8,128)}, f32[40,768]{1,0:T(8,128)S(1)}, u32[]{:S(2)}) copy-start(f32[40,768]{1,0:T(8,128)S(1)} %collective-permute-done.3.right_ref.refs_9_) | copy-start | bytes 368644
  40.7 0.6 copy-start.14
  41.4 8.5 %collective-permute-start.4 = (f32[40,768]{1,0:T(8,128)}, f32[40,768]{1,0:T(8,128)}, u32[]{:S(2)}, u32[]{:S(2)}) collective-permute-start(f32[40,768]{1,0:T(8,128)} %get-tuple-element.49.d2_ref.vec_ref), channel_id=1, source_target_pairs={{0,2},{2,4},{4,6},{6,8},{8,10},{10,12},{12,14},{1,3},{3,5},{5,7},{... | collective-permute-start | bytes 368648 | tf_op jit(solution)/shard_map/ppermute | solution.py:688
  45.4 7.1 %collective-permute-start.5 = (f32[40,768]{1,0:T(8,128)}, f32[40,768]{1,0:T(8,128)}, u32[]{:S(2)}, u32[]{:S(2)}) collective-permute-start(f32[40,768]{1,0:T(8,128)} %get-tuple-element.49.d2_ref.vec_ref), channel_id=1, source_target_pairs={{2,0},{4,2},{6,4},{8,6},{10,8},{12,10},{14,12},{3,1},{5,3},{7,5},{... | collective-permute-start | bytes 368648 | tf_op jit(solution)/shard_map/ppermute | solution.py:688
  46.7 0.7 copy-start.13
  47.5 0.9 copy-start.15
  48.4 4.2 %copy-start.1 = (bf16[3,768,256]{2,1,0:T(8,128)(2,1)S(1)}, bf16[3,768,256]{2,1,0:T(8,128)(2,1)}, u32[]{:S(2)}) copy-start(bf16[3,768,256]{2,1,0:T(8,128)(2,1)} %copy-done) | copy-start | bytes 3538948
  48.4 4.2 %copy-start.3 = (bf16[3,768,256]{2,1,0:T(8,128)(2,1)S(1)}, bf16[3,768,256]{2,1,0:T(8,128)(2,1)}, u32[]{:S(2)}) copy-start(bf16[3,768,256]{2,1,0:T(8,128)(2,1)} %copy-done.2) | copy-start | bytes 3538948
  48.4 4.2 %copy-start.5 = (f32[40,768]{1,0:T(8,128)S(1)}, f32[40,768]{1,0:T(8,128)}, u32[]{:S(2)}) copy-start(f32[40,768]{1,0:T(8,128)} %copy-done.4) | copy-start | bytes 368644
  48.4 4.2 %copy-start.7 = (f32[40,768]{1,0:T(8,128)S(1)}, f32[40,768]{1,0:T(8,128)}, u32[]{:S(2)}) copy-start(f32[40,768]{1,0:T(8,128)} %copy-done.6) | copy-start | bytes 368644
  48.4 4.2 %copy-start.9 = (f32[32,768]{1,0:T(8,128)S(1)}, f32[32,768]{1,0:T(8,128)}, u32[]{:S(2)}) copy-start(f32[32,768]{1,0:T(8,128)} %copy-done.8) | copy-start | bytes 294916
  55.7 0.7 copy-start.11
  56.4 12.5 %all-to-all-start = ((f32[8,40,128]{2,1,0:T(8,128)}), f32[8,40,128]{2,1,0:T(8,128)S(1)}, u32[]{:S(2)}, u32[]{:S(2)}) async-start(f32[8,40,128]{2,1,0:T(8,128)} %copy-done.11), calls=%async_computation | async-start | bytes 327680 | tf_op jit(solution)/shard_map/all_to_all | solution.py:793

commit v7 on v6

--- a/solution.py
+++ b/solution.py
@@ -187,7 +187,7 @@
 
 
 def invert_kernel(
-    feat_hbm, ids_hbm, agg_hbm, sys_hbm, cov_hbm, coarse_hbm, pat_hbm, len_hbm, noise_hbm,
+    place_ref, probe_ref, feat_hbm, ids_hbm, agg_hbm, sys_hbm, cov_hbm, coarse_hbm, pat_hbm, len_hbm, noise_hbm,
     jac_ref, pack_ref, extra_ref,
     work, feat_ref, ids_ref, agg_ref, sys_ref, cov_ref, coarse_ref, pat_ref, len_ref, noise_ref, sems,
 ):
@@ -216,7 +216,9 @@
             weights = jnp.where(places == m * SLOTS + o, weight(pat_ref, m, o), weights)
     pack_ref[0:FEAT, :] = scaled
     pack_ref[FEAT : 2 * FEAT, :] = jnp.where(
-        rows == 0, ids, jnp.where(rows == 1, which, 0.0)
+        rows == 0,
+        ids,
+        jnp.where(rows == 1, which, jnp.where(rows == 2, probe_ref[0].astype(f32), 0.0)),
     )
     extra_ref[0:TASKS, :] = picked
     tail = jnp.where(rows == 0, noise, jnp.where(rows == 1, weights, 0.0))
@@ -224,8 +226,9 @@
     inverse = jnp.concatenate(
         [coarse_ref[...], jnp.zeros((held, width - coarse_ref.shape[1]), f32)], axis=1
     )
+    tail = jnp.where(rows == 2, place_ref[0].astype(f32), tail)
     for r in range(held):
-        tail = jnp.where(rows == 2 + r, inverse[r : r + 1], tail)
+        tail = jnp.where(rows == 3 + r, inverse[r : r + 1], tail)
     extra_ref[TASKS : TASKS + FEAT, :] = tail
     near = near_stack(scaled, table)
     mates, norm = own_stack(scaled, picked)
@@ -442,34 +445,35 @@
 
 
 def third_kernel(
-    place_ref, extra_ref, before_ref, vec_ref, left_ref, right_ref, *refs, count, held
+    extra_ref, before_ref, vec_ref, left_ref, right_ref, *refs, count, held
 ):
-    kernel, others, (out_ref, *stashes), sems = refs[:4], refs[4:10], refs[10:20], refs[20]
+    kernel, others, (out_hbm, *stashes) = refs[:4], refs[4:10], refs[10:20]
+    out_ref, sems, out_sems = refs[20:]
     copies = fetch(list(zip([*others, vec_ref, left_ref, right_ref], stashes)), sems)
     coarse = vec_ref.shape[0] - count
-    lanes = out_ref.shape[2]
+    lanes = out_ref.shape[1]
     pitch = pitch_of(coarse)
     d2 = vec_ref[...]
     noise = extra_ref[TASKS : TASKS + 1, :]
     v2 = operate(d2, left_ref[...], right_ref[...], noise, *kernel)
     m4 = moment(d2[count:], v2, d2[:count] * v2[:count])
-    row = iota((coarse, 1), 0)
-    start = place_ref[0] * held
+    row = iota((coarse, 1), 0).astype(f32)
+    start = extra_ref[TASKS + 2 : TASKS + 3, 0:1] * held
     inverse = jnp.zeros((coarse, pitch), f32)
     for r in range(held):
-        line = extra_ref[TASKS + 2 + r : TASKS + 3 + r, 0:pitch]
+        line = extra_ref[TASKS + 3 + r : TASKS + 4 + r, 0:pitch]
         inverse = jnp.where(row == start + r, line, inverse)
     top = before_ref[0:count, :] + spread_out({4: m4[:count]}, lanes)
     bottom = before_ref[count:, :] + spread_out({2: m4[count:], 4: inverse}, lanes)
-    for c in range(out_ref.shape[0]):
-        out_ref[c, 0:count, :] = top
-        out_ref[c, count:, :] = bottom
-    for copy in copies:
+    out_ref[0:count, :] = top
+    out_ref[count:, :] = bottom
+    pairs = [(out_ref, out_hbm.at[c]) for c in range(out_hbm.shape[0])]
+    for copy in copies + fetch(pairs, out_sems):
         copy.wait()
 
 
 def final_kernel(
-    probe_ref, gram_ref, *refs, sides, points,
+    gram_ref, *refs, sides, points,
 ):
     far, (sol_ref, grad_ref), near_refs, sems = refs[:16], refs[16:18], refs[18:34], refs[34]
     copies = fetch(list(zip(far, near_refs)), sems)
@@ -587,7 +591,8 @@
     mine = slice(REACH * BS, REACH * BS + width)
     sol_ref[...] = x[:, mine]
 
-    line = iota((count, 1), 0) + probe_ref[0] * count
+    probe = own_ref[FEAT + 2 : FEAT + 3, 0:1]
+    line = iota((count, 1), 0).astype(f32) + probe * count
     right = jnp.where(line == 0, x[:, mine], sys_ref[...])
     coef = jnp.where(line == 0, 0.5 / points, -0.5 / (sides - 1) / points)
     r0, r1 = split(right, 2)
@@ -697,6 +702,8 @@
     rows = count + coarse
     lanes = lanes_of(coarse)
     assert blocks == REACH
+    place = lax.axis_index("pts").astype(jnp.int32)[None]
+    probe = lax.axis_index("probe").astype(jnp.int32)[None]
     ranks = lax.axis_size("pts")
     sides = lax.axis_size("probe")
 
@@ -706,8 +713,9 @@
     jac, pack, extra = call(
         invert_kernel,
         [shape(3, blocks, BS, BS, kind=bf16), shape(SYS + count, width), shape(TASKS + FEAT, width)],
-        [features, task_ids, aggregate, systems, task_cov, coarse_inverse, pattern, lengthscales, noise],
+        [place, probe, features, task_ids, aggregate, systems, task_cov, coarse_inverse, pattern, lengthscales, noise],
         "invert",
+        smem=2,
         hbm=9,
         scratch=[
             pltpu.VMEM((blocks, BS, BS), f32),
@@ -777,17 +785,18 @@
         "late",
         flops=10**9,
     )
-    place = lax.axis_index("pts").astype(jnp.int32)[None]
-    probe = lax.axis_index("probe").astype(jnp.int32)[None]
     others = [pack, pack_l, pack_r, d1, d1_l, d1_r]
     gram, *vectors = call(
         functools.partial(third_kernel, count=count, held=coarse_inverse.shape[0]),
         [shape(ranks, rows, lanes)] + [shape(*a.shape) for a in others + [d2] * 3],
-        [place, extra, late, d2, d2_l, d2_r] + kernel + others,
+        [extra, late, d2, d2_l, d2_r] + kernel + others,
         "third",
-        smem=1,
-        far_outs=9,
-        scratch=[pltpu.SemaphoreType.DMA((9,))],
+        far_outs=10,
+        scratch=[
+            pltpu.VMEM((rows, lanes), f32),
+            pltpu.SemaphoreType.DMA((9,)),
+            pltpu.SemaphoreType.DMA((ranks,)),
+        ],
         flops=10**9,
     )
     gram = lax.all_to_all(gram, "pts", 0, 0, tiled=True)
@@ -795,9 +804,8 @@
     answer, grads = call(
         functools.partial(final_kernel, sides=sides * count, points=ranks * width),
         [shape(count, width), shape(ranks * sides, FEAT, LANES)],
-        [probe, gram] + stored,
+        [gram] + stored,
         "final",
-        smem=1,
         hbm=len(stored),
         scratch=[pltpu.VMEM(a.shape, a.dtype) for a in stored]
         + [pltpu.SemaphoreType.DMA((len(stored),))],

time: 90.7 us -> 87.4 us (0.964)
  blocking collectives: 9.48 us -> 22.6 us
  starting transfers between devices: 22.3 us -> 16.7 us
  waiting for transfers between devices: 15.5 us -> 10.4 us
  local copies, waits for them, and re-layouts: 2.97 us -> 0.01 us
  Pallas kernels: 39 us -> 36.5 us
    all_to_all x0 -> x1, blocking collectives: none -> 13.1 us  [shards(): gram = lax.all_to_all(gram, 'pts', 0, 0, tiled=True)]
    all_to_all x1 -> x0, waiting for transfers between devices: 7.56 us -> none  [shards(): gram = lax.all_to_all(gram, 'pts', 0, 0, tiled=True)]
    all_to_all x1 -> x0, starting transfers between devices: 4.98 us -> none  [shards(): gram = lax.all_to_all(gram, 'pts', 0, 0, tiled=True)]
    unnamed x32 -> x2, local copies, waits for them, and re-layouts: 2.97 us -> 0.01 us
    pallas_call x10, Pallas kernels: 39 us -> 36.5 us  [call(): pl.pallas_call(body, out_shape=outs, in_specs=[sm] * smem + [vm] * (len(a...]
    ppermute x6, waiting for transfers between devices: 7.95 us -> 10.4 us  [both_sides(): return (lax.ppermute(cells, 'pts', up), lax.ppermute(cells, 'pts', down))]
  transfers between devices with their start and end apart: 7 -> 6, of which waited for: 4 -> 4; matrix products, arithmetic and copies ran while one was open for 0% -> 0% of each run, Pallas kernels for 7% -> 6%
where the time goes in v7:
time: 87.4 us; the launch traced here: 87 us
  Pallas kernels  36.5 us (42%)
  blocking collectives  22.6 us (26%)
  starting transfers between devices  16.7 us (19%)
  waiting for transfers between devices  10.4 us (12%)
    pallas_call x10, Pallas kernels, call(): pl.pallas_call(body, out_shape=outs, in_specs=[sm] * smem + [vm] * (len(a...  36.5 us
    ppermute x6, starting transfers between devices, both_sides(): return (lax.ppermute(cells, 'pts', up), lax.ppermute(cells, 'pts', down))  16.7 us
    all_to_all x1, blocking collectives, shards(): gram = lax.all_to_all(gram, 'pts', 0, 0, tiled=True)  13.1 us
    ppermute x6, waiting for transfers between devices, both_sides(): return (lax.ppermute(cells, 'pts', up), lax.ppermute(cells, 'pts', down))  10.4 us
    all_to_all x1, blocking collectives, shards(): grads = lax.all_to_all(grads, ('pts', 'probe'), 0, 0, tiled=True)  9.48 us
  transfers between devices with their start and end apart: 6, of which 4 were waited for; matrix products, arithmetic and copies ran while one was open for 0% of the time, Pallas kernels for 6%

profile of v7, /device:TPU:0, one launch (start us, length us, event | category | flops | bytes accessed | tf_op | source)
XLA Modules:
  0.0 87.0 jit_solution(2271302674526378662)
XLA Ops:
  0.6 13.1 %invert.1 = (bf16[3,3,256,256]{3,2,1,0:T(8,128)(2,1)S(1)}, f32[32,768]{1,0:T(8,128)S(1)}, f32[24,768]{1,0:T(8,128)S(1)}) custom-call(s32[1]{0:T(128)} %bitcast.place_ref, s32[1]{0:T(128)} %bitcast.1.probe_ref, f32[8,768]{1,0:T(8,128)} %feat_hbm.1, s32[768]{0:T(1024)} %ids_hbm.1, s32[768]{0:T(1024)} %agg_hbm.1, f32[16,768]{1,0:T(8,128)} %refs_0_.1, ...), custom_call_target="tpu_custom_call" | custom-call | flops 10000000000 | bytes 1048576 | tf_op jit(solution)/shard_map/invert/pallas_call | solution.py:677
  13.7 4.9 %collective-permute-start = (f32[32,768]{1,0:T(8,128)S(1)}, f32[32,768]{1,0:T(8,128)S(1)}, u32[]{:S(2)}, u32[]{:S(2)}) collective-permute-start(f32[32,768]{1,0:T(8,128)S(1)} %get-tuple-element.38.refs_0_.refs_1_.refs_2_.own_ref.refs_4_), channel_id=1, source_target_pairs={{0,2},{2,4},{4,6},{6,8},{8,10},{10,12},{12,14},{1,3},{3,5},{5,7},{... | collective-permute-start | bytes 294920 | tf_op jit(solution)/shard_map/ppermute | solution.py:693
  18.6 1.5 %collective-permute-start.1 = (f32[32,768]{1,0:T(8,128)S(1)}, f32[32,768]{1,0:T(8,128)S(1)}, u32[]{:S(2)}, u32[]{:S(2)}) collective-permute-start(f32[32,768]{1,0:T(8,128)S(1)} %get-tuple-element.38.refs_0_.refs_1_.refs_2_.own_ref.refs_4_), channel_id=1, source_target_pairs={{2,0},{4,2},{6,4},{8,6},{10,8},{12,10},{14,12},{3,1},{5,3},{7,5},{... | collective-permute-start | bytes 294920 | tf_op jit(solution)/shard_map/ppermute | solution.py:693
  20.1 1.0 %build_own.1 = (bf16[3,768,256]{2,1,0:T(8,128)(2,1)S(1)}, bf16[3,768,256]{2,1,0:T(8,128)(2,1)S(1)}, f32[3,768,256]{2,1,0:T(8,128)S(1)}) custom-call(f32[32,768]{1,0:T(8,128)S(1)} %get-tuple-element.38.refs_0_.refs_1_.refs_2_.own_ref.refs_4_, f32[32,768]{1,0:T(8,128)S(1)} %get-tuple-element.38.refs_0_.refs_1_.refs_2_.own_ref.refs_4_, ...), custom_call_target="tpu_custom_call" | custom-call | flops 1000000000 | bytes 1048576 | tf_op jit(solution)/shard_map/build_own/pallas_call | solution.py:677
  21.1 0.0 collective-permute-done.refs_0_.left_ref.refs_5_
  21.1 4.0 %collective-permute-done.1.refs_1_.right_ref.refs_6_ = f32[32,768]{1,0:T(8,128)S(1)} collective-permute-done((f32[32,768]{1,0:T(8,128)S(1)}, f32[32,768]{1,0:T(8,128)S(1)}, u32[]{:S(2)}, u32[]{:S(2)}) %collective-permute-start.1) | collective-permute-done | bytes 98336 | tf_op jit(solution)/shard_map/ppermute | solution.py:693
  25.1 1.4 %build_halo.1 = (bf16[3,1024,256]{2,1,0:T(8,128)(2,1)S(1)}, bf16[3,1024,256]{2,1,0:T(8,128)(2,1)S(1)}, f32[3,1024,256]{2,1,0:T(8,128)S(1)}) custom-call(f32[32,768]{1,0:T(8,128)S(1)} %collective-permute-done.refs_0_.left_ref.refs_5_, f32[32,768]{1,0:T(8,128)S(1)} %collective-permute-done.1.refs_1_.right_ref.refs_6_, ...), custom_call_target="tpu_custom_call" | custom-call | flops 1000000000 | bytes 1048576 | tf_op jit(solution)/shard_map/build_halo/pallas_call | solution.py:677
  26.5 0.0 copy-start
  26.5 1.2 %first.1 = (f32[40,768]{1,0:T(8,128)S(1)}, f32[40,768]{1,0:T(8,128)S(1)}) custom-call(f32[32,768]{1,0:T(8,128)S(1)} %get-tuple-element.38.refs_0_.refs_1_.refs_2_.own_ref.refs_4_, f32[32,768]{1,0:T(8,128)S(1)} %collective-permute-done.refs_0_.left_ref.refs_5_, f32[32,768]{1,0:T(8,128)S(1)} %collective-permute-done.1.refs_1_.right_ref.refs_6_, ...), custom_call_target="tpu_custom_call" | custom-call | flops 1000000000 | bytes 1048576 | tf_op jit(solution)/shard_map/first/pallas_call | solution.py:677
  27.7 4.3 %collective-permute-start.2 = (f32[40,768]{1,0:T(8,128)S(1)}, f32[40,768]{1,0:T(8,128)S(1)}, u32[]{:S(2)}, u32[]{:S(2)}) collective-permute-start(f32[40,768]{1,0:T(8,128)S(1)} %get-tuple-element.44.d1_ref.vec_ref.refs_7_), channel_id=1, source_target_pairs={{0,2},{2,4},{4,6},{6,8},{8,10},{10,12},{12,14},{1,3},{3,5},{5,7},{... | collective-permute-start | bytes 368648 | tf_op jit(solution)/shard_map/ppermute | solution.py:693
  32.1 1.3 %collective-permute-start.3 = (f32[40,768]{1,0:T(8,128)S(1)}, f32[40,768]{1,0:T(8,128)S(1)}, u32[]{:S(2)}, u32[]{:S(2)}) collective-permute-start(f32[40,768]{1,0:T(8,128)S(1)} %get-tuple-element.44.d1_ref.vec_ref.refs_7_), channel_id=1, source_target_pairs={{2,0},{4,2},{6,4},{8,6},{10,8},{12,10},{14,12},{3,1},{5,3},{7,5},{... | collective-permute-start | bytes 368648 | tf_op jit(solution)/shard_map/ppermute | solution.py:693
  33.4 0.0 copy-done
  33.4 4.1 %early.1 = (f32[40,128]{1,0:T(8,128)S(1)}, bf16[3,768,256]{2,1,0:T(8,128)(2,1)}, bf16[3,768,256]{2,1,0:T(8,128)(2,1)}, f32[3,768,256]{2,1,0:T(8,128)}, bf16[3,10...) custom-call(f32[32,768]{1,0:T(8,128)S(1)} %get-tuple-element.38.refs_0_.refs_1_.refs_2_.own_ref.refs_4_,, ...), custom_call_target="tpu_custom_call" | custom-call | flops 1000000000 | bytes 1048576 | tf_op jit(solution)/shard_map/early/pallas_call | solution.py:677
  37.5 0.0 collective-permute-done.2.left_ref.refs_8_
  37.5 1.3 %collective-permute-done.3.right_ref.refs_9_ = f32[40,768]{1,0:T(8,128)S(1)} collective-permute-done((f32[40,768]{1,0:T(8,128)S(1)}, f32[40,768]{1,0:T(8,128)S(1)}, u32[]{:S(2)}, u32[]{:S(2)}) %collective-permute-start.3) | collective-permute-done | bytes 122912 | tf_op jit(solution)/shard_map/ppermute | solution.py:693
  38.9 1.2 %second.1 = (f32[40,768]{1,0:T(8,128)S(1)}, f32[40,768]{1,0:T(8,128)S(1)}) custom-call(f32[24,768]{1,0:T(8,128)S(1)} %get-tuple-element.37.refs_2_.refs_3_.extra_ref, f32[40,768]{1,0:T(8,128)S(1)} %get-tuple-element.44.d1_ref.vec_ref.refs_7_, f32[40,768]{1,0:T(8,128)S(1)} %collective-permute-done.2.left_ref.refs_8_, ...), custom_call_target="tpu_custom_call" | custom-call | flops 1000000000 | bytes 1048576 | tf_op jit(solution)/shard_map/second/pallas_call | solution.py:677
  40.1 3.4 %collective-permute-start.4 = (f32[40,768]{1,0:T(8,128)S(1)}, f32[40,768]{1,0:T(8,128)S(1)}, u32[]{:S(2)}, u32[]{:S(2)}) collective-permute-start(f32[40,768]{1,0:T(8,128)S(1)} %get-tuple-element.49.d2_ref.vec_ref), channel_id=1, source_target_pairs={{0,2},{2,4},{4,6},{6,8},{8,10},{10,12},{12,14},{1,3},{3,5},{5,7},{... | collective-permute-start | bytes 368648 | tf_op jit(solution)/shard_map/ppermute | solution.py:693
  43.5 1.3 %collective-permute-start.5 = (f32[40,768]{1,0:T(8,128)S(1)}, f32[40,768]{1,0:T(8,128)S(1)}, u32[]{:S(2)}, u32[]{:S(2)}) collective-permute-start(f32[40,768]{1,0:T(8,128)S(1)} %get-tuple-element.49.d2_ref.vec_ref), channel_id=1, source_target_pairs={{2,0},{4,2},{6,4},{8,6},{10,8},{12,10},{14,12},{3,1},{5,3},{7,5},{... | collective-permute-start | bytes 368648 | tf_op jit(solution)/shard_map/ppermute | solution.py:693
  44.8 0.4 late.1.before_ref
  45.2 2.0 %collective-permute-done.4.left_ref = f32[40,768]{1,0:T(8,128)S(1)} collective-permute-done((f32[40,768]{1,0:T(8,128)S(1)}, f32[40,768]{1,0:T(8,128)S(1)}, u32[]{:S(2)}, u32[]{:S(2)}) %collective-permute-start.4) | collective-permute-done | bytes 122912 | tf_op jit(solution)/shard_map/ppermute | solution.py:693
  47.2 3.0 %collective-permute-done.5.right_ref = f32[40,768]{1,0:T(8,128)S(1)} collective-permute-done((f32[40,768]{1,0:T(8,128)S(1)}, f32[40,768]{1,0:T(8,128)S(1)}, u32[]{:S(2)}, u32[]{:S(2)}) %collective-permute-start.5) | collective-permute-done | bytes 122912 | tf_op jit(solution)/shard_map/ppermute | solution.py:693
  50.3 2.3 %third.1 = (f32[8,40,128]{2,1,0:T(8,128)}, f32[32,768]{1,0:T(8,128)}, f32[32,768]{1,0:T(8,128)}, f32[32,768]{1,0:T(8,128)}, f32[40,768]{1,0:T(8,128)}, /*index=5...) custom-call(f32[24,768]{1,0:T(8,128)S(1)} %get-tuple-element.37.refs_2_.refs_3_., ...), custom_call_target="tpu_custom_call" | custom-call | flops 1000000000 | bytes 1048576 | tf_op jit(solution)/shard_map/third/pallas_call | solution.py:677
  52.6 13.1 %all_to_all.10.gram_ref = f32[8,40,128]{2,1,0:T(8,128)S(1)} all-to-all(f32[8,40,128]{2,1,0:T(8,128)} %get-tuple-element.51), channel_id=1, replica_groups=mesh['groups'=2,'pts'=8,'probe'=2] {'pts'}, dimensions={0} | all-to-all | bytes 327680 | tf_op jit(solution)/shard_map/all_to_all | solution.py:802
  65.7 11.1 %final.1 = (f32[16,768]{1,0:T(8,128)}, f32[16,8,128]{2,1,0:T(8,128)S(1)}) custom-call(f32[8,40,128]{2,1,0:T(8,128)S(1)} %all_to_all.10.gram_ref, f32[16,768]{1,0:T(8,128)} %refs_0_.1, f32[32,768]{1,0:T(8,128)} %get-tuple-element.52.refs_1_, f32[32,768]{1,0:T(8,128)} %get-tuple-element.53.refs_2_, f32[32,768]{1,0:T(8,128)} %get-tuple-element.54.refs_3_, ...), custom_call_target="tpu_custom_call" | custom-call | flops 1000000000 | bytes 1048576 | tf_op jit(solution)/shard_map/final/pallas_call | solution.py:677
  76.8 9.5 %all_to_all.11.parts_ref = f32[16,8,128]{2,1,0:T(8,128)S(1)} all-to-all(f32[16,8,128]{2,1,0:T(8,128)S(1)} %get-tuple-element.68), channel_id=1, replica_groups=mesh['groups'=2,'pts'=8,'probe'=2] {'pts','probe'}, dimensions={0} | all-to-all | bytes 131072 | tf_op jit(solution)/shard_map/all_to_all | solution.py:815
  86.3 0.7 tail.1
Async XLA Ops:
  13.7 7.4 %collective-permute-start = (f32[32,768]{1,0:T(8,128)S(1)}, f32[32,768]{1,0:T(8,128)S(1)}, u32[]{:S(2)}, u32[]{:S(2)}) collective-permute-start(f32[32,768]{1,0:T(8,128)S(1)} %get-tuple-element.38.refs_0_.refs_1_.refs_2_.own_ref.refs_4_), channel_id=1, source_target_pairs={{0,2},{2,4},{4,6},{6,8},{8,10},{10,12},{12,14},{1,3},{3,5},{5,7},{... | collective-permute-start | bytes 294920 | tf_op jit(solution)/shard_map/ppermute | solution.py:693
  18.6 6.5 %collective-permute-start.1 = (f32[32,768]{1,0:T(8,128)S(1)}, f32[32,768]{1,0:T(8,128)S(1)}, u32[]{:S(2)}, u32[]{:S(2)}) collective-permute-start(f32[32,768]{1,0:T(8,128)S(1)} %get-tuple-element.38.refs_0_.refs_1_.refs_2_.own_ref.refs_4_), channel_id=1, source_target_pairs={{2,0},{4,2},{6,4},{8,6},{10,8},{12,10},{14,12},{3,1},{5,3},{7,5},{... | collective-permute-start | bytes 294920 | tf_op jit(solution)/shard_map/ppermute | solution.py:693
  26.5 6.9 %copy-start = (f32[16,768]{1,0:T(8,128)S(1)}, f32[16,768]{1,0:T(8,128)}, u32[]{:S(2)}) copy-start(f32[16,768]{1,0:T(8,128)} %refs_0_.1) | copy-start | bytes 147460
  27.7 9.8 %collective-permute-start.2 = (f32[40,768]{1,0:T(8,128)S(1)}, f32[40,768]{1,0:T(8,128)S(1)}, u32[]{:S(2)}, u32[]{:S(2)}) collective-permute-start(f32[40,768]{1,0:T(8,128)S(1)} %get-tuple-element.44.d1_ref.vec_ref.refs_7_), channel_id=1, source_target_pairs={{0,2},{2,4},{4,6},{6,8},{8,10},{10,12},{12,14},{1,3},{3,5},{5,7},{... | collective-permute-start | bytes 368648 | tf_op jit(solution)/shard_map/ppermute | solution.py:693
  32.1 6.8 %collective-permute-start.3 = (f32[40,768]{1,0:T(8,128)S(1)}, f32[40,768]{1,0:T(8,128)S(1)}, u32[]{:S(2)}, u32[]{:S(2)}) collective-permute-start(f32[40,768]{1,0:T(8,128)S(1)} %get-tuple-element.44.d1_ref.vec_ref.refs_7_), channel_id=1, source_target_pairs={{2,0},{4,2},{6,4},{8,6},{10,8},{12,10},{14,12},{3,1},{5,3},{7,5},{... | collective-permute-start | bytes 368648 | tf_op jit(solution)/shard_map/ppermute | solution.py:693
  40.1 7.2 %collective-permute-start.4 = (f32[40,768]{1,0:T(8,128)S(1)}, f32[40,768]{1,0:T(8,128)S(1)}, u32[]{:S(2)}, u32[]{:S(2)}) collective-permute-start(f32[40,768]{1,0:T(8,128)S(1)} %get-tuple-element.49.d2_ref.vec_ref), channel_id=1, source_target_pairs={{0,2},{2,4},{4,6},{6,8},{8,10},{10,12},{12,14},{1,3},{3,5},{5,7},{... | collective-permute-start | bytes 368648 | tf_op jit(solution)/shard_map/ppermute | solution.py:693
  43.5 6.8 %collective-permute-start.5 = (f32[40,768]{1,0:T(8,128)S(1)}, f32[40,768]{1,0:T(8,128)S(1)}, u32[]{:S(2)}, u32[]{:S(2)}) collective-permute-start(f32[40,768]{1,0:T(8,128)S(1)} %get-tuple-element.49.d2_ref.vec_ref), channel_id=1, source_target_pairs={{2,0},{4,2},{6,4},{8,6},{10,8},{12,10},{14,12},{3,1},{5,3},{7,5},{... | collective-permute-start | bytes 368648 | tf_op jit(solution)/shard_map/ppermute | solution.py:693

commit v8 on v7

--- a/solution.py
+++ b/solution.py
@@ -410,9 +410,7 @@
     return low, high
 
 
-def early_moments_kernel(own_ref, sys_ref, d1_ref, v0_ref, *refs):
-    sources, (out_ref, *stashes), sems = refs[:6], refs[6:13], refs[13]
-    copies = fetch(list(zip(sources, stashes)), sems)
+def early_moments_kernel(own_ref, sys_ref, d1_ref, v0_ref, out_ref):
     count = own_ref.shape[0] - SYS
     coarse = d1_ref.shape[0] - count
     lanes = out_ref.shape[1]
@@ -429,8 +427,6 @@
         start = jnp.concatenate([start, jnp.zeros((coarse - count, pitch), f32)], axis=0)
     fold = folded(m0[count:, :coarse], m1[count:, :coarse])
     out_ref[count:, :] = spread_out({0: fold, 3: start}, lanes)
-    for copy in copies:
-        copy.wait()
 
 
 def late_moments_kernel(before_ref, d1_ref, d2_ref, v1_ref, out_ref, *, count):
@@ -447,11 +443,9 @@
 def third_kernel(
     extra_ref, before_ref, vec_ref, left_ref, right_ref, *refs, count, held
 ):
-    kernel, others, (out_hbm, *stashes) = refs[:4], refs[4:10], refs[10:20]
-    out_ref, sems, out_sems = refs[20:]
-    copies = fetch(list(zip([*others, vec_ref, left_ref, right_ref], stashes)), sems)
+    kernel, out_ref = refs[:4], refs[4]
     coarse = vec_ref.shape[0] - count
-    lanes = out_ref.shape[1]
+    lanes = out_ref.shape[2]
     pitch = pitch_of(coarse)
     d2 = vec_ref[...]
     noise = extra_ref[TASKS : TASKS + 1, :]
@@ -465,22 +459,16 @@
         inverse = jnp.where(row == start + r, line, inverse)
     top = before_ref[0:count, :] + spread_out({4: m4[:count]}, lanes)
     bottom = before_ref[count:, :] + spread_out({2: m4[count:], 4: inverse}, lanes)
-    out_ref[0:count, :] = top
-    out_ref[count:, :] = bottom
-    pairs = [(out_ref, out_hbm.at[c]) for c in range(out_hbm.shape[0])]
-    for copy in copies + fetch(pairs, out_sems):
-        copy.wait()
+    for c in range(out_ref.shape[0]):
+        out_ref[c, 0:count, :] = top
+        out_ref[c, count:, :] = bottom
 
 
 def final_kernel(
-    gram_ref, *refs, sides, points,
+    gram_ref, sys_ref, own_ref, left_ref, right_ref, d1_ref, d1l_ref, d1r_ref, d2_ref, d2l_ref,
+    d2r_ref, *refs, sides, points,
 ):
-    far, (sol_ref, grad_ref), near_refs, sems = refs[:16], refs[16:18], refs[18:34], refs[34]
-    copies = fetch(list(zip(far, near_refs)), sems)
-    (
-        sys_ref, own_ref, left_ref, right_ref, d1_ref, d1l_ref, d1r_ref, d2_ref, d2l_ref, d2r_ref,
-        *kernel_refs,
-    ) = near_refs
+    kernel_refs, (sol_ref, grad_ref) = refs[:6], refs[6:]
     width = own_ref.shape[1]
     count = own_ref.shape[0] - SYS
     rows = d1_ref.shape[0]
@@ -561,8 +549,6 @@
             direction = pre + (gamma_new / gamma) * direction
             gamma = gamma_new
 
-    for copy in copies[:10]:
-        copy.wait()
     pack = jnp.concatenate(
         [left_ref[:, edge:], own_ref[...], right_ref[:, : width - edge]], axis=1
     )
@@ -610,8 +596,6 @@
     heads = jnp.concatenate([t0, pad8], axis=0).astype(bf16)
     tables = table.astype(bf16)
     high = 32
-    for copy in copies[10:]:
-        copy.wait()
     length_total = jnp.zeros((FEAT, 1), f32)
     task_total = jnp.zeros((TASKS, TASKS), f32)
     for m in range(blocks):
@@ -760,15 +744,8 @@
         flops=10**9,
     )
     d1_l, d1_r = both_sides(d1)
-    cells = [own_hi, own_lo, own_sim, halo_hi, halo_lo, halo_sim]
-    early, *stashed = call(
-        early_moments_kernel,
-        [shape(rows, lanes)] + [shape(*a.shape, kind=a.dtype) for a in cells],
-        [pack, systems, d1, v0] + cells,
-        "early",
-        far_outs=len(cells),
-        scratch=[pltpu.SemaphoreType.DMA((len(cells),))],
-        flops=10**9,
+    (early,) = call(
+        early_moments_kernel, [shape(rows, lanes)], [pack, systems, d1, v0], "early", flops=10**9
     )
     v1, d2 = call(
         second_kernel,
@@ -785,32 +762,21 @@
         "late",
         flops=10**9,
     )
-    others = [pack, pack_l, pack_r, d1, d1_l, d1_r]
-    gram, *vectors = call(
+    (gram,) = call(
         functools.partial(third_kernel, count=count, held=coarse_inverse.shape[0]),
-        [shape(ranks, rows, lanes)] + [shape(*a.shape) for a in others + [d2] * 3],
-        [extra, late, d2, d2_l, d2_r] + kernel + others,
+        [shape(ranks, rows, lanes)],
+        [extra, late, d2, d2_l, d2_r] + kernel,
         "third",
-        far_outs=10,
-        scratch=[
-            pltpu.VMEM((rows, lanes), f32),
-            pltpu.SemaphoreType.DMA((9,)),
-            pltpu.SemaphoreType.DMA((ranks,)),
-        ],
         flops=10**9,
     )
     gram = lax.all_to_all(gram, "pts", 0, 0, tiled=True)
-    stored = [systems] + vectors + stashed
+    cells = [own_hi, own_lo, own_sim, halo_hi, halo_lo, halo_sim]
     answer, grads = call(
         functools.partial(final_kernel, sides=sides * count, points=ranks * width),
         [shape(count, width), shape(ranks * sides, FEAT, LANES)],
-        [gram] + stored,
+        [gram, systems, pack, pack_l, pack_r, d1, d1_l, d1_r, d2, d2_l, d2_r] + cells,
         "final",
-        hbm=len(stored),
-        scratch=[pltpu.VMEM(a.shape, a.dtype) for a in stored]
-        + [pltpu.SemaphoreType.DMA((len(stored),))],
         flops=10**9,
-        limit=32,
     )
     grads = lax.all_to_all(grads, ("pts", "probe"), 0, 0, tiled=True)
     lengths, tasks = call(

time: 87.4 us -> 81.2 us (0.929)
  Pallas kernels: 36.5 us -> 27.7 us
  starting transfers between devices: 16.7 us -> 19.6 us
    pallas_call x10, Pallas kernels: 36.5 us -> 27.7 us  [call(): pl.pallas_call(body, out_shape=outs, in_specs=[sm] * smem + [vm] * (len(a...]
    ppermute x6, starting transfers between devices: 16.7 us -> 19.6 us  [both_sides(): return (lax.ppermute(cells, 'pts', up), lax.ppermute(cells, 'pts', down))]
  transfers between devices with their start and end apart: 6 -> 6, of which waited for: 4 -> 5; matrix products, arithmetic and copies ran while one was open for 0% -> 0% of each run, Pallas kernels for 6% -> 2%
where the time goes in v8:
time: 81.2 us; the launch traced here: 80.8 us
  Pallas kernels  27.7 us (34%)
  blocking collectives  22.9 us (28%)
  starting transfers between devices  19.6 us (24%)
  waiting for transfers between devices  9.8 us (12%)
    pallas_call x10, Pallas kernels, call(): pl.pallas_call(body, out_shape=outs, in_specs=[sm] * smem + [vm] * (len(a...  27.7 us
    ppermute x6, starting transfers between devices, both_sides(): return (lax.ppermute(cells, 'pts', up), lax.ppermute(cells, 'pts', down))  19.6 us
    all_to_all x1, blocking collectives, shards(): gram = lax.all_to_all(gram, 'pts', 0, 0, tiled=True)  13.4 us
    ppermute x6, waiting for transfers between devices, both_sides(): return (lax.ppermute(cells, 'pts', up), lax.ppermute(cells, 'pts', down))  9.8 us
    all_to_all x1, blocking collectives, shards(): grads = lax.all_to_all(grads, ('pts', 'probe'), 0, 0, tiled=True)  9.53 us
  transfers between devices with their start and end apart: 6, of which 5 were waited for; matrix products, arithmetic and copies ran while one was open for 0% of the time, Pallas kernels for 2%

profile of v8, /device:TPU:0, one launch (start us, length us, event | category | flops | bytes accessed | tf_op | source)
XLA Modules:
  0.0 80.8 jit_solution(7606360760565259363)
XLA Ops:
  0.6 13.1 %invert.1 = (bf16[3,3,256,256]{3,2,1,0:T(8,128)(2,1)S(1)}, f32[32,768]{1,0:T(8,128)S(1)}, f32[24,768]{1,0:T(8,128)S(1)}) custom-call(s32[1]{0:T(128)} %bitcast.place_ref, s32[1]{0:T(128)} %bitcast.1.probe_ref, f32[8,768]{1,0:T(8,128)} %feat_hbm.1, s32[768]{0:T(1024)} %ids_hbm.1, s32[768]{0:T(1024)} %agg_hbm.1, f32[16,768]{1,0:T(8,128)} %sys_ref.3, ...), custom_call_target="tpu_custom_call" | custom-call | flops 10000000000 | bytes 1048576 | tf_op jit(solution)/shard_map/invert/pallas_call | solution.py:661
  13.7 1.3 %collective-permute-start.1 = (f32[32,768]{1,0:T(8,128)S(1)}, f32[32,768]{1,0:T(8,128)S(1)}, u32[]{:S(2)}, u32[]{:S(2)}) collective-permute-start(f32[32,768]{1,0:T(8,128)S(1)} %get-tuple-element.21.refs_0_.refs_1_.refs_2_.own_ref), channel_id=1, source_target_pairs={{2,0},{4,2},{6,4},{8,6},{10,8},{12,10},{14,12},{3,1},{5,3},{7,5},{... | collective-permute-start | bytes 294920 | tf_op jit(solution)/shard_map/ppermute | solution.py:677
  15.0 5.7 %collective-permute-start = (f32[32,768]{1,0:T(8,128)S(1)}, f32[32,768]{1,0:T(8,128)S(1)}, u32[]{:S(2)}, u32[]{:S(2)}) collective-permute-start(f32[32,768]{1,0:T(8,128)S(1)} %get-tuple-element.21.refs_0_.refs_1_.refs_2_.own_ref), channel_id=1, source_target_pairs={{0,2},{2,4},{4,6},{6,8},{8,10},{10,12},{12,14},{1,3},{3,5},{5,7},{... | collective-permute-start | bytes 294920 | tf_op jit(solution)/shard_map/ppermute | solution.py:677
  20.7 1.0 %build_own.1 = (bf16[3,768,256]{2,1,0:T(8,128)(2,1)S(1)}, bf16[3,768,256]{2,1,0:T(8,128)(2,1)S(1)}, f32[3,768,256]{2,1,0:T(8,128)S(1)}) custom-call(f32[32,768]{1,0:T(8,128)S(1)} %get-tuple-element.21.refs_0_.refs_1_.refs_2_.own_ref, f32[32,768]{1,0:T(8,128)S(1)} %get-tuple-element.21.refs_0_.refs_1_.refs_2_.own_ref, ...), custom_call_target="tpu_custom_call" | custom-call | flops 1000000000 | bytes 1048576 | tf_op jit(solution)/shard_map/build_own/pallas_call | solution.py:661
  21.7 0.0 collective-permute-done.1.refs_1_.right_ref
  21.7 1.9 %collective-permute-done.refs_0_.left_ref = f32[32,768]{1,0:T(8,128)S(1)} collective-permute-done((f32[32,768]{1,0:T(8,128)S(1)}, f32[32,768]{1,0:T(8,128)S(1)}, u32[]{:S(2)}, u32[]{:S(2)}) %collective-permute-start) | collective-permute-done | bytes 98336 | tf_op jit(solution)/shard_map/ppermute | solution.py:677
  23.6 1.4 %build_halo.1 = (bf16[3,1024,256]{2,1,0:T(8,128)(2,1)S(1)}, bf16[3,1024,256]{2,1,0:T(8,128)(2,1)S(1)}, f32[3,1024,256]{2,1,0:T(8,128)S(1)}) custom-call(f32[32,768]{1,0:T(8,128)S(1)} %collective-permute-done.refs_0_.left_ref, f32[32,768]{1,0:T(8,128)S(1)} %collective-permute-done.1.refs_1_.right_ref, ...), custom_call_target="tpu_custom_call" | custom-call | flops 1000000000 | bytes 1048576 | tf_op jit(solution)/shard_map/build_halo/pallas_call | solution.py:661
  25.0 0.0 copy-start
  25.1 1.2 %first.1 = (f32[40,768]{1,0:T(8,128)S(1)}, f32[40,768]{1,0:T(8,128)S(1)}) custom-call(f32[32,768]{1,0:T(8,128)S(1)} %get-tuple-element.21.refs_0_.refs_1_.refs_2_.own_ref, f32[32,768]{1,0:T(8,128)S(1)} %collective-permute-done.refs_0_.left_ref, f32[32,768]{1,0:T(8,128)S(1)} %collective-permute-done.1.refs_1_.right_ref, ...), custom_call_target="tpu_custom_call" | custom-call | flops 1000000000 | bytes 1048576 | tf_op jit(solution)/shard_map/first/pallas_call | solution.py:661
  26.3 1.3 %collective-permute-start.3 = (f32[40,768]{1,0:T(8,128)S(1)}, f32[40,768]{1,0:T(8,128)S(1)}, u32[]{:S(2)}, u32[]{:S(2)}) collective-permute-start(f32[40,768]{1,0:T(8,128)S(1)} %get-tuple-element.27.d1_ref.vec_ref), channel_id=1, source_target_pairs={{2,0},{4,2},{6,4},{8,6},{10,8},{12,10},{14,12},{3,1},{5,3},{7,5},{... | collective-permute-start | bytes 368648 | tf_op jit(solution)/shard_map/ppermute | solution.py:677
  27.6 5.0 %collective-permute-start.2 = (f32[40,768]{1,0:T(8,128)S(1)}, f32[40,768]{1,0:T(8,128)S(1)}, u32[]{:S(2)}, u32[]{:S(2)}) collective-permute-start(f32[40,768]{1,0:T(8,128)S(1)} %get-tuple-element.27.d1_ref.vec_ref), channel_id=1, source_target_pairs={{0,2},{2,4},{4,6},{6,8},{8,10},{10,12},{12,14},{1,3},{3,5},{5,7},{... | collective-permute-start | bytes 368648 | tf_op jit(solution)/shard_map/ppermute | solution.py:677
  32.6 0.0 copy-done
  32.6 0.4 early.1.early_ref.before_ref
  33.0 1.1 %collective-permute-done.3.right_ref.d1r_ref = f32[40,768]{1,0:T(8,128)S(1)} collective-permute-done((f32[40,768]{1,0:T(8,128)S(1)}, f32[40,768]{1,0:T(8,128)S(1)}, u32[]{:S(2)}, u32[]{:S(2)}) %collective-permute-start.3) | collective-permute-done | bytes 122912 | tf_op jit(solution)/shard_map/ppermute | solution.py:677
  34.1 2.8 %collective-permute-done.2.left_ref.d1l_ref = f32[40,768]{1,0:T(8,128)S(1)} collective-permute-done((f32[40,768]{1,0:T(8,128)S(1)}, f32[40,768]{1,0:T(8,128)S(1)}, u32[]{:S(2)}, u32[]{:S(2)}) %collective-permute-start.2) | collective-permute-done | bytes 122912 | tf_op jit(solution)/shard_map/ppermute | solution.py:677
  36.9 1.2 %second.1 = (f32[40,768]{1,0:T(8,128)S(1)}, f32[40,768]{1,0:T(8,128)S(1)}) custom-call(f32[24,768]{1,0:T(8,128)S(1)} %get-tuple-element.20.refs_2_.refs_3_.extra_ref, f32[40,768]{1,0:T(8,128)S(1)} %get-tuple-element.27.d1_ref.vec_ref, f32[40,768]{1,0:T(8,128)S(1)} %collective-permute-done.2.left_ref.d1l_ref, ...), custom_call_target="tpu_custom_call" | custom-call | flops 1000000000 | bytes 1048576 | tf_op jit(solution)/shard_map/second/pallas_call | solution.py:661
  38.1 1.3 %collective-permute-start.5 = (f32[40,768]{1,0:T(8,128)S(1)}, f32[40,768]{1,0:T(8,128)S(1)}, u32[]{:S(2)}, u32[]{:S(2)}) collective-permute-start(f32[40,768]{1,0:T(8,128)S(1)} %get-tuple-element.29.d2_ref.vec_ref), channel_id=1, source_target_pairs={{2,0},{4,2},{6,4},{8,6},{10,8},{12,10},{14,12},{3,1},{5,3},{7,5},{... | collective-permute-start | bytes 368648 | tf_op jit(solution)/shard_map/ppermute | solution.py:677
  39.4 5.0 %collective-permute-start.4 = (f32[40,768]{1,0:T(8,128)S(1)}, f32[40,768]{1,0:T(8,128)S(1)}, u32[]{:S(2)}, u32[]{:S(2)}) collective-permute-start(f32[40,768]{1,0:T(8,128)S(1)} %get-tuple-element.29.d2_ref.vec_ref), channel_id=1, source_target_pairs={{0,2},{2,4},{4,6},{6,8},{8,10},{10,12},{12,14},{1,3},{3,5},{5,7},{... | collective-permute-start | bytes 368648 | tf_op jit(solution)/shard_map/ppermute | solution.py:677
  44.4 0.4 late.1.before_ref
  44.8 1.2 %collective-permute-done.5.right_ref.d2r_ref = f32[40,768]{1,0:T(8,128)S(1)} collective-permute-done((f32[40,768]{1,0:T(8,128)S(1)}, f32[40,768]{1,0:T(8,128)S(1)}, u32[]{:S(2)}, u32[]{:S(2)}) %collective-permute-start.5) | collective-permute-done | bytes 122912 | tf_op jit(solution)/shard_map/ppermute | solution.py:677
  46.0 2.8 %collective-permute-done.4.left_ref.d2l_ref = f32[40,768]{1,0:T(8,128)S(1)} collective-permute-done((f32[40,768]{1,0:T(8,128)S(1)}, f32[40,768]{1,0:T(8,128)S(1)}, u32[]{:S(2)}, u32[]{:S(2)}) %collective-permute-start.4) | collective-permute-done | bytes 122912 | tf_op jit(solution)/shard_map/ppermute | solution.py:677
  48.8 1.3 %third.1 = f32[8,40,128]{2,1,0:T(8,128)S(1)} custom-call(f32[24,768]{1,0:T(8,128)S(1)} %get-tuple-element.20.refs_2_.refs_3_.extra_ref, f32[40,128]{1,0:T(8,128)S(1)} %late.1.before_ref, f32[40,768]{1,0:T(8,128)S(1)} %get-tuple-element.29.d2_ref.vec_ref, f32[40,768]{1,0:T(8,128)S(1)} %collective-permute-done.4.left_ref.d2l_ref, ...), custom_call_target="tpu_custom_call" | custom-call | flops 1000000000 | bytes 1048576 | tf_op jit(solution)/shard_map/third/pallas_call | solution.py:661
  50.1 13.4 %all_to_all.10.gram_ref = f32[8,40,128]{2,1,0:T(8,128)S(1)} all-to-all(f32[8,40,128]{2,1,0:T(8,128)S(1)} %third.1), channel_id=1, replica_groups=mesh['groups'=2,'pts'=8,'probe'=2] {'pts'}, dimensions={0} | all-to-all | bytes 327680 | tf_op jit(solution)/shard_map/all_to_all | solution.py:772
  63.4 7.1 %final.1 = (f32[16,768]{1,0:T(8,128)}, f32[16,8,128]{2,1,0:T(8,128)S(1)}) custom-call(f32[8,40,128]{2,1,0:T(8,128)S(1)} %all_to_all.10.gram_ref, f32[16,768]{1,0:T(8,128)S(1)} %copy-done, f32[32,768]{1,0:T(8,128)S(1)} %get-tuple-element.21.refs_0_.refs_1_.refs_2_.own_ref, f32[32,768]{1,0:T(8,128)S(1)} %collective-permute-done.refs_0_.left_ref, ...), custom_call_target="tpu_custom_call" | custom-call | flops 1000000000 | bytes 1048576 | tf_op jit(solution)/shard_map/final/pallas_call | solution.py:661
  70.6 9.5 %all_to_all.11.parts_ref = f32[16,8,128]{2,1,0:T(8,128)S(1)} all-to-all(f32[16,8,128]{2,1,0:T(8,128)S(1)} %get-tuple-element.34), channel_id=1, replica_groups=mesh['groups'=2,'pts'=8,'probe'=2] {'pts','probe'}, dimensions={0} | all-to-all | bytes 131072 | tf_op jit(solution)/shard_map/all_to_all | solution.py:781
  80.1 0.7 tail.1
Async XLA Ops:
  13.7 8.0 %collective-permute-start.1 = (f32[32,768]{1,0:T(8,128)S(1)}, f32[32,768]{1,0:T(8,128)S(1)}, u32[]{:S(2)}, u32[]{:S(2)}) collective-permute-start(f32[32,768]{1,0:T(8,128)S(1)} %get-tuple-element.21.refs_0_.refs_1_.refs_2_.own_ref), channel_id=1, source_target_pairs={{2,0},{4,2},{6,4},{8,6},{10,8},{12,10},{14,12},{3,1},{5,3},{7,5},{... | collective-permute-start | bytes 294920 | tf_op jit(solution)/shard_map/ppermute | solution.py:677
  15.0 8.6 %collective-permute-start = (f32[32,768]{1,0:T(8,128)S(1)}, f32[32,768]{1,0:T(8,128)S(1)}, u32[]{:S(2)}, u32[]{:S(2)}) collective-permute-start(f32[32,768]{1,0:T(8,128)S(1)} %get-tuple-element.21.refs_0_.refs_1_.refs_2_.own_ref), channel_id=1, source_target_pairs={{0,2},{2,4},{4,6},{6,8},{8,10},{10,12},{12,14},{1,3},{3,5},{5,7},{... | collective-permute-start | bytes 294920 | tf_op jit(solution)/shard_map/ppermute | solution.py:677
  25.0 7.6 %copy-start = (f32[16,768]{1,0:T(8,128)S(1)}, f32[16,768]{1,0:T(8,128)}, u32[]{:S(2)}) copy-start(f32[16,768]{1,0:T(8,128)} %sys_ref.3) | copy-start | bytes 147460
  26.3 7.9 %collective-permute-start.3 = (f32[40,768]{1,0:T(8,128)S(1)}, f32[40,768]{1,0:T(8,128)S(1)}, u32[]{:S(2)}, u32[]{:S(2)}) collective-permute-start(f32[40,768]{1,0:T(8,128)S(1)} %get-tuple-element.27.d1_ref.vec_ref), channel_id=1, source_target_pairs={{2,0},{4,2},{6,4},{8,6},{10,8},{12,10},{14,12},{3,1},{5,3},{7,5},{... | collective-permute-start | bytes 368648 | tf_op jit(solution)/shard_map/ppermute | solution.py:677
  27.6 9.3 %collective-permute-start.2 = (f32[40,768]{1,0:T(8,128)S(1)}, f32[40,768]{1,0:T(8,128)S(1)}, u32[]{:S(2)}, u32[]{:S(2)}) collective-permute-start(f32[40,768]{1,0:T(8,128)S(1)} %get-tuple-element.27.d1_ref.vec_ref), channel_id=1, source_target_pairs={{0,2},{2,4},{4,6},{6,8},{8,10},{10,12},{12,14},{1,3},{3,5},{5,7},{... | collective-permute-start | bytes 368648 | tf_op jit(solution)/shard_map/ppermute | solution.py:677
  38.1 7.9 %collective-permute-start.5 = (f32[40,768]{1,0:T(8,128)S(1)}, f32[40,768]{1,0:T(8,128)S(1)}, u32[]{:S(2)}, u32[]{:S(2)}) collective-permute-start(f32[40,768]{1,0:T(8,128)S(1)} %get-tuple-element.29.d2_ref.vec_ref), channel_id=1, source_target_pairs={{2,0},{4,2},{6,4},{8,6},{10,8},{12,10},{14,12},{3,1},{5,3},{7,5},{... | collective-permute-start | bytes 368648 | tf_op jit(solution)/shard_map/ppermute | solution.py:677
  39.4 9.4 %collective-permute-start.4 = (f32[40,768]{1,0:T(8,128)S(1)}, f32[40,768]{1,0:T(8,128)S(1)}, u32[]{:S(2)}, u32[]{:S(2)}) collective-permute-start(f32[40,768]{1,0:T(8,128)S(1)} %get-tuple-element.29.d2_ref.vec_ref), channel_id=1, source_target_pairs={{0,2},{2,4},{4,6},{6,8},{8,10},{10,12},{12,14},{1,3},{3,5},{5,7},{... | collective-permute-start | bytes 368648 | tf_op jit(solution)/shard_map/ppermute | solution.py:677

commit v9 on v8

--- a/solution.py
+++ b/solution.py
@@ -310,27 +310,44 @@
             kernel = similar * both[:, BS:]
             head = kernel.astype(bf16)
             rows = slice(row * BS, (row + 1) * BS)
-            sim_ref[m, rows, :] = similar
+            if o <= REACH or sides == 1:
+                sim_ref[m, rows, :] = similar
             hi_ref[m, rows, :] = head
             lo_ref[m, rows, :] = (kernel - head.astype(f32)).astype(bf16)
 
 
+def pieces(vectors):
+    return jnp.concatenate(split(vectors, 2), axis=0).astype(bf16)
+
+
+def apply(cells, hi, lo):
+    rows = cells.shape[0] // 2
+    first = dot(cells, hi)
+    return first[:rows] + first[rows:] + dot(cells[:rows], lo)
+
+
+def operate_own(own, noise, own_hi, own_lo):
+    mine = pieces(own)
+    out = [apply(mine, own_hi[m], own_lo[m]) for m in range(REACH)]
+    return jnp.concatenate(out, axis=1) + noise * own
+
+
+def operate_left(left, halo_hi, halo_lo):
+    cells = pieces(left)
+    out = []
+    for m in range(REACH):
+        part = slice(0, (REACH - m) * BS)
+        out.append(apply(cells[:, m * BS :], halo_hi[m, part, :], halo_lo[m, part, :]))
+    return jnp.concatenate(out, axis=1)
+
+
 def operate(own, left, right, noise, own_hi, own_lo, halo_hi, halo_lo):
-    rows = own.shape[0]
-    width = own.shape[1]
-
-    def pieces(vectors):
-        head, tail = split(vectors, 2)
-        return jnp.concatenate([head, tail], axis=0).astype(bf16)
-
-    mine, lefts, rights = pieces(own), pieces(left), pieces(right)
+    lefts, rights = pieces(left), pieces(right)
     out = []
     for m in range(REACH):
         beyond = jnp.concatenate([lefts[:, m * BS :], rights[:, : (m + 1) * BS]], axis=1)
-        first = dot(mine, own_hi[m]) + dot(beyond, halo_hi[m])
-        second = dot(mine[:rows], own_lo[m]) + dot(beyond[:rows], halo_lo[m])
-        out.append(first[:rows] + first[rows:] + second)
-    return jnp.concatenate(out, axis=1) + noise * own
+        out.append(apply(beyond, halo_hi[m], halo_lo[m]))
+    return operate_own(own, noise, own_hi, own_lo) + jnp.concatenate(out, axis=1)
 
 
 def smooth(image, jac_ref):
@@ -360,12 +377,14 @@
     next_ref[...] = smooth(image, jac_ref)
 
 
-def second_kernel(extra_ref, vec_ref, left_ref, right_ref, early_ref, *refs):
-    kernel, (jac_ref, image_ref, next_ref) = refs[:4], refs[4:]
+def second_kernel(extra_ref, vec_ref, left_ref, right_ref, early_ref, sys_ref, *refs):
+    kernel, (jac_ref, image_ref, cargo_ref) = refs[:4], refs[4:]
+    rows = vec_ref.shape[0]
     noise = extra_ref[TASKS : TASKS + 1, :]
     image = operate(vec_ref[...], left_ref[...], right_ref[...], noise, *kernel)
     image_ref[...] = image
-    next_ref[...] = smooth(image, jac_ref)
+    cargo_ref[0:rows, :] = smooth(image, jac_ref)
+    cargo_ref[rows:, :] = sys_ref[...]
 
 
 def pitch_of(coarse):
@@ -429,9 +448,9 @@
     out_ref[count:, :] = spread_out({0: fold, 3: start}, lanes)
 
 
-def late_moments_kernel(before_ref, d1_ref, d2_ref, v1_ref, out_ref, *, count):
+def late_moments_kernel(before_ref, d1_ref, cargo_ref, v1_ref, out_ref, *, count):
     lanes = out_ref.shape[1]
-    d1, d2, v1 = d1_ref[...], d2_ref[...], v1_ref[...]
+    d1, d2, v1 = d1_ref[...], cargo_ref[0 : d1_ref.shape[0], :], v1_ref[...]
     coarse = d1.shape[0] - count
     m2 = moment(d1[count:], v1, d1[:count] * v1[:count])
     m3 = moment(d2[count:], v1, d2[:count] * v1[:count])
@@ -441,16 +460,20 @@
 
 
 def third_kernel(
-    extra_ref, before_ref, vec_ref, left_ref, right_ref, *refs, count, held
+    extra_ref, before_ref, cargo_ref, left_ref, *refs, count, held
 ):
     kernel, out_ref = refs[:4], refs[4]
-    coarse = vec_ref.shape[0] - count
+    rows = cargo_ref.shape[0] - count
+    coarse = rows - count
     lanes = out_ref.shape[2]
     pitch = pitch_of(coarse)
-    d2 = vec_ref[...]
+    d2 = cargo_ref[0:rows, :]
     noise = extra_ref[TASKS : TASKS + 1, :]
-    v2 = operate(d2, left_ref[...], right_ref[...], noise, *kernel)
-    m4 = moment(d2[count:], v2, d2[:count] * v2[:count])
+    inner = operate_own(d2, noise, *kernel[:2])
+    cross = operate_left(left_ref[0:rows, :], *kernel[2:])
+    m4 = moment(d2[count:], inner + cross, d2[:count] * (inner + 2.0 * cross)[:count])
+    mirror = dot(d2, cross[count:], NT, lax.Precision.HIGH)
+    m4 = m4 + jnp.concatenate([mirror, jnp.zeros((rows, 1), f32)], axis=1)
     row = iota((coarse, 1), 0).astype(f32)
     start = extra_ref[TASKS + 2 : TASKS + 3, 0:1] * held
     inverse = jnp.zeros((coarse, pitch), f32)
@@ -465,8 +488,7 @@
 
 
 def final_kernel(
-    gram_ref, sys_ref, own_ref, left_ref, right_ref, d1_ref, d1l_ref, d1r_ref, d2_ref, d2l_ref,
-    d2r_ref, *refs, sides, points,
+    gram_ref, own_ref, left_ref, d1_ref, d1l_ref, cargo_ref, cargol_ref, *refs, sides, points,
 ):
     kernel_refs, (sol_ref, grad_ref) = refs[:6], refs[6:]
     width = own_ref.shape[1]
@@ -476,7 +498,6 @@
     pitch = pitch_of(coarse)
     wide = -(-3 * pitch // LANES) * LANES
     blocks = width // BS
-    edge = width - REACH * BS
     gram = gram_ref[0]
     for c in range(1, gram_ref.shape[0]):
         gram = gram + gram_ref[c]
@@ -549,13 +570,12 @@
             direction = pre + (gamma_new / gamma) * direction
             gamma = gamma_new
 
-    pack = jnp.concatenate(
-        [left_ref[:, edge:], own_ref[...], right_ref[:, : width - edge]], axis=1
-    )
+    pack = jnp.concatenate([left_ref[...], own_ref[...]], axis=1)
     z = one_hot(pack[FEAT + 1 : FEAT + 2], coarse)
     q0 = pack[SYS:]
-    d1 = jnp.concatenate([d1l_ref[:, edge:], d1_ref[...], d1r_ref[:, : width - edge]], axis=1)
-    d2 = jnp.concatenate([d2l_ref[:, edge:], d2_ref[...], d2r_ref[:, : width - edge]], axis=1)
+    d1 = jnp.concatenate([d1l_ref[...], d1_ref[...]], axis=1)
+    cargo = jnp.concatenate([cargol_ref[...], cargo_ref[...]], axis=1)
+    d2 = cargo[:rows]
     span = q0.shape[1]
     step = -(-coarse // FEAT) * FEAT
     deep = -(-3 * step // LANES) * LANES
@@ -574,18 +594,25 @@
     )
     x = x + scalars(answer, 0) * q0 + scalars(answer, 1) * d1[:count]
     x = x + scalars(answer, 2) * d2[:count]
-    mine = slice(REACH * BS, REACH * BS + width)
+    mine = slice(width, 2 * width)
     sol_ref[...] = x[:, mine]
 
     probe = own_ref[FEAT + 2 : FEAT + 3, 0:1]
     line = iota((count, 1), 0).astype(f32) + probe * count
-    right = jnp.where(line == 0, x[:, mine], sys_ref[...])
+    right = jnp.where(line == 0, x, cargo[rows:])
     coef = jnp.where(line == 0, 0.5 / points, -0.5 / (sides - 1) / points)
     r0, r1 = split(right, 2)
     w0, w1 = split(x * coef, 2)
-    rest = LANES - 3 * count
-    near = jnp.concatenate([w0, w1, w0, jnp.zeros((rest, span), f32)], axis=0).T.astype(bf16)
-    mate = jnp.concatenate([r0, r0, r1, jnp.zeros((rest, width), f32)], axis=0).astype(bf16)
+    rest = jnp.zeros((LANES - 6 * count, span), f32)
+    near = jnp.concatenate([w0, w1, w0, r0, r1, r0, rest], axis=0).T.astype(bf16)
+    none = jnp.zeros((3 * count, width), f32)
+    rest = rest[:, mine]
+    ahead = jnp.concatenate([r0, r0, r1], axis=0)[:, mine]
+    back = jnp.concatenate([w0, w0, w1], axis=0)[:, mine]
+    mates = [
+        jnp.concatenate([ahead, none, rest], axis=0).astype(bf16),
+        jnp.concatenate([none, back, rest], axis=0).astype(bf16),
+    ]
     scaled = pack[0:FEAT]
     table = one_hot(pack[FEAT : FEAT + 1], TASKS)
     ones = jnp.ones((8, span), f32)
@@ -601,28 +628,30 @@
     for m in range(blocks):
         at = slice(m * BS, (m + 1) * BS)
         sums = jnp.zeros((high, BS), f32)
-        held_sums = jnp.zeros((TASKS, BS), f32)
-        places = [(0, row, j + REACH) for row, j, _ in own_places(m)]
-        places += [(1, row, j if j < REACH else j + REACH) for row, j, _ in halo_places(m)]
-        for side, row, block in places:
-            hi_ref, lo_ref, sim_ref = kernel_refs[3 * side : 3 * side + 3]
+        held_sums = [jnp.zeros((TASKS, BS), f32) for _ in mates]
+        places = [(1, row, j + REACH) for row, j, _ in own_places(m)]
+        places += [(2, row, j) for row, j, _ in halo_places(m) if j < REACH]
+        for orders, row, block in places:
+            hi_ref, lo_ref, sim_ref = kernel_refs[3 * orders - 3 : 3 * orders]
             j = slice(block * BS, (block + 1) * BS)
             rows_at = slice(row * BS, (row + 1) * BS)
-            outer = dot(near[j], mate[:, at])
+            outers = [dot(near[j], mate[:, at]) for mate in mates[:orders]]
             kernel = hi_ref[m, rows_at, :].astype(f32) + lo_ref[m, rows_at, :].astype(f32)
-            energy = outer * kernel
-            held = outer * sim_ref[m, rows_at, :]
+            similar = sim_ref[m, rows_at, :]
+            energy = sum(outers) * kernel
             e0, e1 = (part.astype(bf16) for part in split(energy, 2))
-            h0, h1 = (part.astype(bf16) for part in split(held, 2))
             first = dot(both[:, j], e0)
             sums = sums + first[:high] + first[high:] + dot(heads[:, j], e1)
-            held_sums = held_sums + dot(tables[:, j], h0) + dot(tables[:, j], h1)
-        mid = slice((REACH + m) * BS, (REACH + m + 1) * BS)
+            for k in range(orders):
+                h0, h1 = (part.astype(bf16) for part in split(outers[k] * similar, 2))
+                held_sums[k] = held_sums[k] + dot(tables[:, j], h0) + dot(tables[:, j], h1)
+        mid = slice(width + m * BS, width + (m + 1) * BS)
         left = scaled[:, mid]
         value = left * left * sums[FEAT : FEAT + 1] + sums[2 * FEAT : 3 * FEAT]
         value = value - 2.0 * left * sums[:FEAT]
         length_total = length_total + jnp.sum(value, axis=1, keepdims=True)
-        task_total = task_total + dot(held_sums, table[:, mid], NT, highest)
+        task_total = task_total + dot(held_sums[0], table[:, mid], NT, highest)
+        task_total = task_total + dot(table[:, mid], held_sums[1], NT, highest)
     half = TASKS // 2
     value = jnp.concatenate(
         [
@@ -675,6 +704,11 @@
     up = [(i, i + 1) for i in range(count - 1)]
     down = [(i + 1, i) for i in range(count - 1)]
     return lax.ppermute(cells, "pts", up), lax.ppermute(cells, "pts", down)
+
+
+def from_left(cells):
+    count = lax.axis_size("pts")
+    return lax.ppermute(cells, "pts", [(i, i + 1) for i in range(count - 1)])
 
 
 def shards(
@@ -747,25 +781,25 @@
     (early,) = call(
         early_moments_kernel, [shape(rows, lanes)], [pack, systems, d1, v0], "early", flops=10**9
     )
-    v1, d2 = call(
+    v1, cargo = call(
         second_kernel,
-        [shape(rows, width), shape(rows, width)],
-        [extra, d1, d1_l, d1_r, early] + kernel + [jac],
+        [shape(rows, width), shape(rows + count, width)],
+        [extra, d1, d1_l, d1_r, early, systems] + kernel + [jac],
         "second",
         flops=10**9,
     )
-    d2_l, d2_r = both_sides(d2)
+    cargo_l = from_left(cargo)
     (late,) = call(
         functools.partial(late_moments_kernel, count=count),
         [shape(rows, lanes)],
-        [early, d1, d2, v1],
+        [early, d1, cargo, v1],
         "late",
         flops=10**9,
     )
     (gram,) = call(
         functools.partial(third_kernel, count=count, held=coarse_inverse.shape[0]),
         [shape(ranks, rows, lanes)],
-        [extra, late, d2, d2_l, d2_r] + kernel,
+        [extra, late, cargo, cargo_l] + kernel,
         "third",
         flops=10**9,
     )
@@ -774,7 +808,7 @@
     answer, grads = call(
         functools.partial(final_kernel, sides=sides * count, points=ranks * width),
         [shape(count, width), shape(ranks * sides, FEAT, LANES)],
-        [gram, systems, pack, pack_l, pack_r, d1, d1_l, d1_r, d2, d2_l, d2_r] + cells,
+        [gram, pack, pack_l, d1, d1_l, cargo, cargo_l] + cells,
         "final",
         flops=10**9,
     )

time: 81.2 us -> 78 us (0.961)
  starting transfers between devices: 19.6 us -> 17.7 us
  Pallas kernels: 27.7 us -> 26.8 us
    ppermute x6 -> x4, starting transfers between devices: 19.6 us -> 13.3 us  [both_sides(): return (lax.ppermute(cells, 'pts', up), lax.ppermute(cells, 'pts', down))]
    ppermute x0 -> x1, starting transfers between devices: none -> 4.4 us  [from_left(): return lax.ppermute(cells, 'pts', [(i, i + 1) for i in range(count - 1)])]
    ppermute x6 -> x4, waiting for transfers between devices: 9.8 us -> 5.84 us  [both_sides(): return (lax.ppermute(cells, 'pts', up), lax.ppermute(cells, 'pts', down))]
    ppermute x0 -> x1, waiting for transfers between devices: none -> 3.4 us  [from_left(): return lax.ppermute(cells, 'pts', [(i, i + 1) for i in range(count - 1)])]
    pallas_call x10, Pallas kernels: 27.7 us -> 26.8 us  [call(): pl.pallas_call(body, out_shape=outs, in_specs=[sm] * smem + [vm] * (len(a...]
  transfers between devices with their start and end apart: 6 -> 5, of which waited for: 5 -> 4; matrix products, arithmetic and copies ran while one was open for 0% -> 0% of each run, Pallas kernels for 2% -> 2%
where the time goes in v9:
time: 78 us; the launch traced here: 77.7 us
  Pallas kernels  26.8 us (34%)
  blocking collectives  23.2 us (30%)
  starting transfers between devices  17.7 us (23%)
  waiting for transfers between devices  9.24 us (12%)
    pallas_call x10, Pallas kernels, call(): pl.pallas_call(body, out_shape=outs, in_specs=[sm] * smem + [vm] * (len(a...  26.8 us
    all_to_all x1, blocking collectives, shards(): gram = lax.all_to_all(gram, 'pts', 0, 0, tiled=True)  13.6 us
    ppermute x4, starting transfers between devices, both_sides(): return (lax.ppermute(cells, 'pts', up), lax.ppermute(cells, 'pts', down))  13.3 us
    all_to_all x1, blocking collectives, shards(): grads = lax.all_to_all(grads, ('pts', 'probe'), 0, 0, tiled=True)  9.53 us
    ppermute x4, waiting for transfers between devices, both_sides(): return (lax.ppermute(cells, 'pts', up), lax.ppermute(cells, 'pts', down))  5.84 us
    ppermute x1, starting transfers between devices, from_left(): return lax.ppermute(cells, 'pts', [(i, i + 1) for i in range(count - 1)])  4.4 us
    ppermute x1, waiting for transfers between devices, from_left(): return lax.ppermute(cells, 'pts', [(i, i + 1) for i in range(count - 1)])  3.4 us
  transfers between devices with their start and end apart: 5, of which 4 were waited for; matrix products, arithmetic and copies ran while one was open for 0% of the time, Pallas kernels for 2%

profile of v9, /device:TPU:0, one launch (start us, length us, event | category | flops | bytes accessed | tf_op | source)
XLA Modules:
  0.0 77.7 jit_solution(5543350528157778227)
XLA Ops:
  0.6 13.1 %invert.1 = (bf16[3,3,256,256]{3,2,1,0:T(8,128)(2,1)S(1)}, f32[32,768]{1,0:T(8,128)S(1)}, f32[24,768]{1,0:T(8,128)S(1)}) custom-call(s32[1]{0:T(128)} %bitcast.place_ref, s32[1]{0:T(128)} %bitcast.1.probe_ref, f32[8,768]{1,0:T(8,128)} %feat_hbm.1, s32[768]{0:T(1024)} %ids_hbm.1, s32[768]{0:T(1024)} %agg_hbm.1, f32[16,768]{1,0:T(8,128)} %sys_ref.3, ...), custom_call_target="tpu_custom_call" | custom-call | flops 10000000000 | bytes 1048576 | tf_op jit(solution)/shard_map/invert/pallas_call | solution.py:690
  13.7 1.3 %collective-permute-start.1 = (f32[32,768]{1,0:T(8,128)S(1)}, f32[32,768]{1,0:T(8,128)S(1)}, u32[]{:S(2)}, u32[]{:S(2)}) collective-permute-start(f32[32,768]{1,0:T(8,128)S(1)} %get-tuple-element.21.refs_0_.refs_1_.refs_2_.own_ref), channel_id=1, source_target_pairs={{2,0},{4,2},{6,4},{8,6},{10,8},{12,10},{14,12},{3,1},{5,3},{7,5},{... | collective-permute-start | bytes 294920 | tf_op jit(solution)/shard_map/ppermute | solution.py:706
  15.0 5.7 %collective-permute-start = (f32[32,768]{1,0:T(8,128)S(1)}, f32[32,768]{1,0:T(8,128)S(1)}, u32[]{:S(2)}, u32[]{:S(2)}) collective-permute-start(f32[32,768]{1,0:T(8,128)S(1)} %get-tuple-element.21.refs_0_.refs_1_.refs_2_.own_ref), channel_id=1, source_target_pairs={{0,2},{2,4},{4,6},{6,8},{8,10},{10,12},{12,14},{1,3},{3,5},{5,7},{... | collective-permute-start | bytes 294920 | tf_op jit(solution)/shard_map/ppermute | solution.py:706
  20.7 1.0 %build_own.1 = (bf16[3,768,256]{2,1,0:T(8,128)(2,1)S(1)}, bf16[3,768,256]{2,1,0:T(8,128)(2,1)S(1)}, f32[3,768,256]{2,1,0:T(8,128)S(1)}) custom-call(f32[32,768]{1,0:T(8,128)S(1)} %get-tuple-element.21.refs_0_.refs_1_.refs_2_.own_ref, f32[32,768]{1,0:T(8,128)S(1)} %get-tuple-element.21.refs_0_.refs_1_.refs_2_.own_ref, ...), custom_call_target="tpu_custom_call" | custom-call | flops 1000000000 | bytes 1048576 | tf_op jit(solution)/shard_map/build_own/pallas_call | solution.py:690
  21.7 0.0 collective-permute-done.1.refs_1_.right_ref
  21.7 1.9 %collective-permute-done.refs_0_.left_ref = f32[32,768]{1,0:T(8,128)S(1)} collective-permute-done((f32[32,768]{1,0:T(8,128)S(1)}, f32[32,768]{1,0:T(8,128)S(1)}, u32[]{:S(2)}, u32[]{:S(2)}) %collective-permute-start) | collective-permute-done | bytes 98336 | tf_op jit(solution)/shard_map/ppermute | solution.py:706
  23.6 1.4 %build_halo.1 = (bf16[3,1024,256]{2,1,0:T(8,128)(2,1)S(1)}, bf16[3,1024,256]{2,1,0:T(8,128)(2,1)S(1)}, f32[3,1024,256]{2,1,0:T(8,128)S(1)}) custom-call(f32[32,768]{1,0:T(8,128)S(1)} %collective-permute-done.refs_0_.left_ref, f32[32,768]{1,0:T(8,128)S(1)} %collective-permute-done.1.refs_1_.right_ref, ...), custom_call_target="tpu_custom_call" | custom-call | flops 1000000000 | bytes 1048576 | tf_op jit(solution)/shard_map/build_halo/pallas_call | solution.py:690
  25.0 0.0 copy-start
  25.1 1.2 %first.1 = (f32[40,768]{1,0:T(8,128)S(1)}, f32[40,768]{1,0:T(8,128)S(1)}) custom-call(f32[32,768]{1,0:T(8,128)S(1)} %get-tuple-element.21.refs_0_.refs_1_.refs_2_.own_ref, f32[32,768]{1,0:T(8,128)S(1)} %collective-permute-done.refs_0_.left_ref, f32[32,768]{1,0:T(8,128)S(1)} %collective-permute-done.1.refs_1_.right_ref, ...), custom_call_target="tpu_custom_call" | custom-call | flops 1000000000 | bytes 1048576 | tf_op jit(solution)/shard_map/first/pallas_call | solution.py:690
  26.3 1.3 %collective-permute-start.3 = (f32[40,768]{1,0:T(8,128)S(1)}, f32[40,768]{1,0:T(8,128)S(1)}, u32[]{:S(2)}, u32[]{:S(2)}) collective-permute-start(f32[40,768]{1,0:T(8,128)S(1)} %get-tuple-element.27.d1_ref.vec_ref), channel_id=1, source_target_pairs={{2,0},{4,2},{6,4},{8,6},{10,8},{12,10},{14,12},{3,1},{5,3},{7,5},{... | collective-permute-start | bytes 368648 | tf_op jit(solution)/shard_map/ppermute | solution.py:706
  27.6 5.0 %collective-permute-start.2 = (f32[40,768]{1,0:T(8,128)S(1)}, f32[40,768]{1,0:T(8,128)S(1)}, u32[]{:S(2)}, u32[]{:S(2)}) collective-permute-start(f32[40,768]{1,0:T(8,128)S(1)} %get-tuple-element.27.d1_ref.vec_ref), channel_id=1, source_target_pairs={{0,2},{2,4},{4,6},{6,8},{8,10},{10,12},{12,14},{1,3},{3,5},{5,7},{... | collective-permute-start | bytes 368648 | tf_op jit(solution)/shard_map/ppermute | solution.py:706
  32.6 0.0 copy-done
  32.6 0.4 early.1.early_ref.before_ref
  33.0 1.1 %collective-permute-done.3.right_ref = f32[40,768]{1,0:T(8,128)S(1)} collective-permute-done((f32[40,768]{1,0:T(8,128)S(1)}, f32[40,768]{1,0:T(8,128)S(1)}, u32[]{:S(2)}, u32[]{:S(2)}) %collective-permute-start.3) | collective-permute-done | bytes 122912 | tf_op jit(solution)/shard_map/ppermute | solution.py:706
  34.1 2.8 %collective-permute-done.2.left_ref.d1l_ref = f32[40,768]{1,0:T(8,128)S(1)} collective-permute-done((f32[40,768]{1,0:T(8,128)S(1)}, f32[40,768]{1,0:T(8,128)S(1)}, u32[]{:S(2)}, u32[]{:S(2)}) %collective-permute-start.2) | collective-permute-done | bytes 122912 | tf_op jit(solution)/shard_map/ppermute | solution.py:706
  36.9 1.2 %second.1 = (f32[40,768]{1,0:T(8,128)S(1)}, f32[56,768]{1,0:T(8,128)S(1)}) custom-call(f32[24,768]{1,0:T(8,128)S(1)} %get-tuple-element.20.refs_2_.refs_3_.extra_ref, f32[40,768]{1,0:T(8,128)S(1)} %get-tuple-element.27.d1_ref.vec_ref, f32[40,768]{1,0:T(8,128)S(1)} %collective-permute-done.2.left_ref.d1l_ref, f32[40,768]{1,0:T(8,128)S(1)} %collective-permute-done.3.right_ref, ...), custom_call_target="tpu_custom_call" | custom-call | flops 1000000000 | bytes 1048576 | tf_op jit(solution)/shard_map/second/pallas_call | solution.py:690
  38.1 4.4 %collective-permute-start.4 = (f32[56,768]{1,0:T(8,128)S(1)}, f32[56,768]{1,0:T(8,128)S(1)}, u32[]{:S(2)}, u32[]{:S(2)}) collective-permute-start(f32[56,768]{1,0:T(8,128)S(1)} %get-tuple-element.29.cargo_ref), channel_id=1, source_target_pairs={{0,2},{2,4},{4,6},{6,8},{8,10},{10,12},{12,14},{1,3},{3,5},{5,7},{... | collective-permute-start | bytes 516104 | tf_op jit(solution)/shard_map/ppermute | solution.py:711
  42.5 0.4 late.1.before_ref
  42.9 3.4 %collective-permute-done.4.left_ref.cargol_ref = f32[56,768]{1,0:T(8,128)S(1)} collective-permute-done((f32[56,768]{1,0:T(8,128)S(1)}, f32[56,768]{1,0:T(8,128)S(1)}, u32[]{:S(2)}, u32[]{:S(2)}) %collective-permute-start.4) | collective-permute-done | bytes 172064 | tf_op jit(solution)/shard_map/ppermute | solution.py:711
  46.3 1.0 %third.1 = f32[8,40,128]{2,1,0:T(8,128)S(1)} custom-call(f32[24,768]{1,0:T(8,128)S(1)} %get-tuple-element.20.refs_2_.refs_3_.extra_ref, f32[40,128]{1,0:T(8,128)S(1)} %late.1.before_ref, f32[56,768]{1,0:T(8,128)S(1)} %get-tuple-element.29.cargo_ref, f32[56,768]{1,0:T(8,128)S(1)} %collective-permute-done.4.left_ref.cargol_ref, ...), custom_call_target="tpu_custom_call" | custom-call | flops 1000000000 | bytes 1048576 | tf_op jit(solution)/shard_map/third/pallas_call | solution.py:690
  47.3 13.6 %all_to_all.10.gram_ref = f32[8,40,128]{2,1,0:T(8,128)S(1)} all-to-all(f32[8,40,128]{2,1,0:T(8,128)S(1)} %third.1), channel_id=1, replica_groups=mesh['groups'=2,'pts'=8,'probe'=2] {'pts'}, dimensions={0} | all-to-all | bytes 327680 | tf_op jit(solution)/shard_map/all_to_all | solution.py:806
  61.0 6.5 %final.1 = (f32[16,768]{1,0:T(8,128)}, f32[16,8,128]{2,1,0:T(8,128)S(1)}) custom-call(f32[8,40,128]{2,1,0:T(8,128)S(1)} %all_to_all.10.gram_ref, f32[32,768]{1,0:T(8,128)S(1)} %get-tuple-element.21.refs_0_.refs_1_.refs_2_.own_ref, f32[32,768]{1,0:T(8,128)S(1)} %collective-permute-done.refs_0_.left_ref, f32[40,768]{1,0:T(8,128)S(1)} %get-tuple-element.27.d1_ref.vec_ref, ...), custom_call_target="tpu_custom_call" | custom-call | flops 1000000000 | bytes 1048576 | tf_op jit(solution)/shard_map/final/pallas_call | solution.py:690
  67.5 9.5 %all_to_all.11.parts_ref = f32[16,8,128]{2,1,0:T(8,128)S(1)} all-to-all(f32[16,8,128]{2,1,0:T(8,128)S(1)} %get-tuple-element.34), channel_id=1, replica_groups=mesh['groups'=2,'pts'=8,'probe'=2] {'pts','probe'}, dimensions={0} | all-to-all | bytes 131072 | tf_op jit(solution)/shard_map/all_to_all | solution.py:815
  77.0 0.7 tail.1
Async XLA Ops:
  13.7 8.0 %collective-permute-start.1 = (f32[32,768]{1,0:T(8,128)S(1)}, f32[32,768]{1,0:T(8,128)S(1)}, u32[]{:S(2)}, u32[]{:S(2)}) collective-permute-start(f32[32,768]{1,0:T(8,128)S(1)} %get-tuple-element.21.refs_0_.refs_1_.refs_2_.own_ref), channel_id=1, source_target_pairs={{2,0},{4,2},{6,4},{8,6},{10,8},{12,10},{14,12},{3,1},{5,3},{7,5},{... | collective-permute-start | bytes 294920 | tf_op jit(solution)/shard_map/ppermute | solution.py:706
  15.0 8.6 %collective-permute-start = (f32[32,768]{1,0:T(8,128)S(1)}, f32[32,768]{1,0:T(8,128)S(1)}, u32[]{:S(2)}, u32[]{:S(2)}) collective-permute-start(f32[32,768]{1,0:T(8,128)S(1)} %get-tuple-element.21.refs_0_.refs_1_.refs_2_.own_ref), channel_id=1, source_target_pairs={{0,2},{2,4},{4,6},{6,8},{8,10},{10,12},{12,14},{1,3},{3,5},{5,7},{... | collective-permute-start | bytes 294920 | tf_op jit(solution)/shard_map/ppermute | solution.py:706
  25.0 7.6 %copy-start = (f32[16,768]{1,0:T(8,128)S(1)}, f32[16,768]{1,0:T(8,128)}, u32[]{:S(2)}) copy-start(f32[16,768]{1,0:T(8,128)} %sys_ref.3) | copy-start | bytes 147460
  26.3 7.9 %collective-permute-start.3 = (f32[40,768]{1,0:T(8,128)S(1)}, f32[40,768]{1,0:T(8,128)S(1)}, u32[]{:S(2)}, u32[]{:S(2)}) collective-permute-start(f32[40,768]{1,0:T(8,128)S(1)} %get-tuple-element.27.d1_ref.vec_ref), channel_id=1, source_target_pairs={{2,0},{4,2},{6,4},{8,6},{10,8},{12,10},{14,12},{3,1},{5,3},{7,5},{... | collective-permute-start | bytes 368648 | tf_op jit(solution)/shard_map/ppermute | solution.py:706
  27.6 9.3 %collective-permute-start.2 = (f32[40,768]{1,0:T(8,128)S(1)}, f32[40,768]{1,0:T(8,128)S(1)}, u32[]{:S(2)}, u32[]{:S(2)}) collective-permute-start(f32[40,768]{1,0:T(8,128)S(1)} %get-tuple-element.27.d1_ref.vec_ref), channel_id=1, source_target_pairs={{0,2},{2,4},{4,6},{6,8},{8,10},{10,12},{12,14},{1,3},{3,5},{5,7},{... | collective-permute-start | bytes 368648 | tf_op jit(solution)/shard_map/ppermute | solution.py:706
  38.1 8.2 %collective-permute-start.4 = (f32[56,768]{1,0:T(8,128)S(1)}, f32[56,768]{1,0:T(8,128)S(1)}, u32[]{:S(2)}, u32[]{:S(2)}) collective-permute-start(f32[56,768]{1,0:T(8,128)S(1)} %get-tuple-element.29.cargo_ref), channel_id=1, source_target_pairs={{0,2},{2,4},{4,6},{6,8},{8,10},{10,12},{12,14},{1,3},{3,5},{5,7},{... | collective-permute-start | bytes 516104 | tf_op jit(solution)/shard_map/ppermute | solution.py:711

commit v10 on v9

--- a/solution.py
+++ b/solution.py
@@ -106,10 +106,10 @@
 def small_inverse(p):
     n = len(p)
     if n == 1:
-        return [[1.0 / p[0][0]]]
+        return [[pltpu.reciprocal(p[0][0], approx=True)]]
     if n == 2:
         a, b, d = p[0][0], p[0][1], p[1][1]
-        r = 1.0 / (a * d - b * b)
+        r = pltpu.reciprocal(a * d - b * b, approx=True)
         off = -b * r
         return [[d * r, off], [off, a * r]]
     h = n // 2
@@ -241,18 +241,33 @@
     seg = iota((BASE, LANES), 1) // BASE
     wide = iota((BASE, BS), 1)
     deep = iota((BASE, BS), 0)
-    strips = [work[m, 0:BASE, :] for m in range(blocks)]
-    for k in range(BS // BASE):
-        first = k * BASE
+
+    def packed(strips, first):
         tile, inside = first // LANES, first % LANES
-        cells = jnp.where(iota((BASE, LANES), 1) % BASE == iota((BASE, LANES), 0), 1.0, 0.0)
+        cells = jnp.zeros((BASE, LANES), f32)
         for m in range(blocks):
             piece = strips[m][:, tile * LANES : (tile + 1) * LANES]
             shift = (BASE * m - inside) % LANES
             if shift:
                 piece = pltpu.roll(piece, shift, axis=1)
             cells = jnp.where(seg == m, piece, cells)
+        return cells
+
+    def diagonal(cells):
+        parts = [jnp.where(seg == m, cells, 0.0) for m in range(LANES // BASE)]
+        return jnp.concatenate(parts, axis=0)
+
+    eye = jnp.where(iota((BASE, LANES), 1) % BASE == iota((BASE, LANES), 0), 1.0, 0.0)
+    strips = [work[m, 0:BASE, :] for m in range(blocks)]
+    after = [work[m, BASE : 2 * BASE, :] for m in range(blocks)]
+    cells = jnp.where(seg < blocks, packed(strips, 0), eye)
+    for k in range(BS // BASE):
+        first = k * BASE
         inv = -sweep_base(cells)
+        if first + BASE < BS:
+            half = dot(inv, diagonal(packed(strips, first + BASE)), precision=highest)
+            drop = dot(packed(after, first), diagonal(half), precision=highest)
+            cells = jnp.where(seg < blocks, packed(after, first + BASE) - drop, eye)
         held = (wide >= first) & (wide < first + BASE)
         minus = jnp.where(wide - first == deep, -1.0, 0.0)
         stack = jnp.concatenate(
@@ -263,7 +278,7 @@
         spread = jnp.concatenate([jnp.where(seg == m, inv, 0.0) for m in range(blocks)], axis=0)
         new = dot(spread, stack, precision=highest)
         gone = (iota((1, BS), 1) >= first) & (iota((1, BS), 1) < first + BASE)
-        coming = []
+        coming, then = [], []
         for m in range(blocks):
             row = new[m * BASE : (m + 1) * BASE, :]
             r0, r1, r2 = split(strips[m], 3)
@@ -272,9 +287,10 @@
             b = jnp.concatenate([p0, p1, p0, p1, p2, p0], axis=0).astype(bf16)
             value = jnp.where(gone, 0.0, work[m]) - dot(a, b, TN)
             coming.append(value[first + BASE : first + 2 * BASE])
+            then.append(value[first + 2 * BASE : first + 3 * BASE])
             work[m] = value
             work[m, first : first + BASE, :] = row
-        strips = coming
+        strips, after = coming, then
     for m in range(blocks):
         inv = -work[m]
         for i, part in enumerate(split(inv, 3)):

time: 78 us -> 77.7 us (level)
  no operation moved by 1% of the time
where the time goes in v10:
time: 77.7 us; the launch traced here: 77.4 us
  Pallas kernels  26.5 us (34%)
  blocking collectives  23.2 us (30%)
  starting transfers between devices  17.7 us (23%)
  waiting for transfers between devices  9.24 us (12%)
    pallas_call x10, Pallas kernels, call(): pl.pallas_call(body, out_shape=outs, in_specs=[sm] * smem + [vm] * (len(a...  26.5 us
    all_to_all x1, blocking collectives, shards(): gram = lax.all_to_all(gram, 'pts', 0, 0, tiled=True)  13.6 us
    ppermute x4, starting transfers between devices, both_sides(): return (lax.ppermute(cells, 'pts', up), lax.ppermute(cells, 'pts', down))  13.3 us
    all_to_all x1, blocking collectives, shards(): grads = lax.all_to_all(grads, ('pts', 'probe'), 0, 0, tiled=True)  9.53 us
    ppermute x4, waiting for transfers between devices, both_sides(): return (lax.ppermute(cells, 'pts', up), lax.ppermute(cells, 'pts', down))  5.83 us
    ppermute x1, starting transfers between devices, from_left(): return lax.ppermute(cells, 'pts', [(i, i + 1) for i in range(count - 1)])  4.4 us
    ppermute x1, waiting for transfers between devices, from_left(): return lax.ppermute(cells, 'pts', [(i, i + 1) for i in range(count - 1)])  3.4 us
  transfers between devices with their start and end apart: 5, of which 4 were waited for; matrix products, arithmetic and copies ran while one was open for 0% of the time, Pallas kernels for 2%

profile of v10, /device:TPU:0, one launch (start us, length us, event | category | flops | bytes accessed | tf_op | source)
XLA Modules:
  0.0 77.4 jit_solution(4271549001889893449)
XLA Ops:
  0.6 12.8 %invert.1 = (bf16[3,3,256,256]{3,2,1,0:T(8,128)(2,1)S(1)}, f32[32,768]{1,0:T(8,128)S(1)}, f32[24,768]{1,0:T(8,128)S(1)}) custom-call(s32[1]{0:T(128)} %bitcast.place_ref, s32[1]{0:T(128)} %bitcast.1.probe_ref, f32[8,768]{1,0:T(8,128)} %feat_hbm.1, s32[768]{0:T(1024)} %ids_hbm.1, s32[768]{0:T(1024)} %agg_hbm.1, f32[16,768]{1,0:T(8,128)} %sys_ref.3, ...), custom_call_target="tpu_custom_call" | custom-call | flops 10000000000 | bytes 1048576 | tf_op jit(solution)/shard_map/invert/pallas_call | solution.py:706
  13.4 1.3 %collective-permute-start.1 = (f32[32,768]{1,0:T(8,128)S(1)}, f32[32,768]{1,0:T(8,128)S(1)}, u32[]{:S(2)}, u32[]{:S(2)}) collective-permute-start(f32[32,768]{1,0:T(8,128)S(1)} %get-tuple-element.21.refs_0_.refs_1_.refs_2_.own_ref), channel_id=1, source_target_pairs={{2,0},{4,2},{6,4},{8,6},{10,8},{12,10},{14,12},{3,1},{5,3},{7,5},{... | collective-permute-start | bytes 294920 | tf_op jit(solution)/shard_map/ppermute | solution.py:722
  14.7 5.7 %collective-permute-start = (f32[32,768]{1,0:T(8,128)S(1)}, f32[32,768]{1,0:T(8,128)S(1)}, u32[]{:S(2)}, u32[]{:S(2)}) collective-permute-start(f32[32,768]{1,0:T(8,128)S(1)} %get-tuple-element.21.refs_0_.refs_1_.refs_2_.own_ref), channel_id=1, source_target_pairs={{0,2},{2,4},{4,6},{6,8},{8,10},{10,12},{12,14},{1,3},{3,5},{5,7},{... | collective-permute-start | bytes 294920 | tf_op jit(solution)/shard_map/ppermute | solution.py:722
  20.4 1.0 %build_own.1 = (bf16[3,768,256]{2,1,0:T(8,128)(2,1)S(1)}, bf16[3,768,256]{2,1,0:T(8,128)(2,1)S(1)}, f32[3,768,256]{2,1,0:T(8,128)S(1)}) custom-call(f32[32,768]{1,0:T(8,128)S(1)} %get-tuple-element.21.refs_0_.refs_1_.refs_2_.own_ref, f32[32,768]{1,0:T(8,128)S(1)} %get-tuple-element.21.refs_0_.refs_1_.refs_2_.own_ref, ...), custom_call_target="tpu_custom_call" | custom-call | flops 1000000000 | bytes 1048576 | tf_op jit(solution)/shard_map/build_own/pallas_call | solution.py:706
  21.4 0.0 collective-permute-done.1.refs_1_.right_ref
  21.4 1.9 %collective-permute-done.refs_0_.left_ref = f32[32,768]{1,0:T(8,128)S(1)} collective-permute-done((f32[32,768]{1,0:T(8,128)S(1)}, f32[32,768]{1,0:T(8,128)S(1)}, u32[]{:S(2)}, u32[]{:S(2)}) %collective-permute-start) | collective-permute-done | bytes 98336 | tf_op jit(solution)/shard_map/ppermute | solution.py:722
  23.3 1.4 %build_halo.1 = (bf16[3,1024,256]{2,1,0:T(8,128)(2,1)S(1)}, bf16[3,1024,256]{2,1,0:T(8,128)(2,1)S(1)}, f32[3,1024,256]{2,1,0:T(8,128)S(1)}) custom-call(f32[32,768]{1,0:T(8,128)S(1)} %collective-permute-done.refs_0_.left_ref, f32[32,768]{1,0:T(8,128)S(1)} %collective-permute-done.1.refs_1_.right_ref, ...), custom_call_target="tpu_custom_call" | custom-call | flops 1000000000 | bytes 1048576 | tf_op jit(solution)/shard_map/build_halo/pallas_call | solution.py:706
  24.7 0.0 copy-start
  24.8 1.2 %first.1 = (f32[40,768]{1,0:T(8,128)S(1)}, f32[40,768]{1,0:T(8,128)S(1)}) custom-call(f32[32,768]{1,0:T(8,128)S(1)} %get-tuple-element.21.refs_0_.refs_1_.refs_2_.own_ref, f32[32,768]{1,0:T(8,128)S(1)} %collective-permute-done.refs_0_.left_ref, f32[32,768]{1,0:T(8,128)S(1)} %collective-permute-done.1.refs_1_.right_ref, ...), custom_call_target="tpu_custom_call" | custom-call | flops 1000000000 | bytes 1048576 | tf_op jit(solution)/shard_map/first/pallas_call | solution.py:706
  26.0 1.3 %collective-permute-start.3 = (f32[40,768]{1,0:T(8,128)S(1)}, f32[40,768]{1,0:T(8,128)S(1)}, u32[]{:S(2)}, u32[]{:S(2)}) collective-permute-start(f32[40,768]{1,0:T(8,128)S(1)} %get-tuple-element.27.d1_ref.vec_ref), channel_id=1, source_target_pairs={{2,0},{4,2},{6,4},{8,6},{10,8},{12,10},{14,12},{3,1},{5,3},{7,5},{... | collective-permute-start | bytes 368648 | tf_op jit(solution)/shard_map/ppermute | solution.py:722
  27.3 5.0 %collective-permute-start.2 = (f32[40,768]{1,0:T(8,128)S(1)}, f32[40,768]{1,0:T(8,128)S(1)}, u32[]{:S(2)}, u32[]{:S(2)}) collective-permute-start(f32[40,768]{1,0:T(8,128)S(1)} %get-tuple-element.27.d1_ref.vec_ref), channel_id=1, source_target_pairs={{0,2},{2,4},{4,6},{6,8},{8,10},{10,12},{12,14},{1,3},{3,5},{5,7},{... | collective-permute-start | bytes 368648 | tf_op jit(solution)/shard_map/ppermute | solution.py:722
  32.3 0.0 copy-done
  32.3 0.4 early.1.early_ref.before_ref
  32.7 1.1 %collective-permute-done.3.right_ref = f32[40,768]{1,0:T(8,128)S(1)} collective-permute-done((f32[40,768]{1,0:T(8,128)S(1)}, f32[40,768]{1,0:T(8,128)S(1)}, u32[]{:S(2)}, u32[]{:S(2)}) %collective-permute-start.3) | collective-permute-done | bytes 122912 | tf_op jit(solution)/shard_map/ppermute | solution.py:722
  33.8 2.8 %collective-permute-done.2.left_ref.d1l_ref = f32[40,768]{1,0:T(8,128)S(1)} collective-permute-done((f32[40,768]{1,0:T(8,128)S(1)}, f32[40,768]{1,0:T(8,128)S(1)}, u32[]{:S(2)}, u32[]{:S(2)}) %collective-permute-start.2) | collective-permute-done | bytes 122912 | tf_op jit(solution)/shard_map/ppermute | solution.py:722
  36.6 1.2 %second.1 = (f32[40,768]{1,0:T(8,128)S(1)}, f32[56,768]{1,0:T(8,128)S(1)}) custom-call(f32[24,768]{1,0:T(8,128)S(1)} %get-tuple-element.20.refs_2_.refs_3_.extra_ref, f32[40,768]{1,0:T(8,128)S(1)} %get-tuple-element.27.d1_ref.vec_ref, f32[40,768]{1,0:T(8,128)S(1)} %collective-permute-done.2.left_ref.d1l_ref, f32[40,768]{1,0:T(8,128)S(1)} %collective-permute-done.3.right_ref, ...), custom_call_target="tpu_custom_call" | custom-call | flops 1000000000 | bytes 1048576 | tf_op jit(solution)/shard_map/second/pallas_call | solution.py:706
  37.8 4.4 %collective-permute-start.4 = (f32[56,768]{1,0:T(8,128)S(1)}, f32[56,768]{1,0:T(8,128)S(1)}, u32[]{:S(2)}, u32[]{:S(2)}) collective-permute-start(f32[56,768]{1,0:T(8,128)S(1)} %get-tuple-element.29.cargo_ref), channel_id=1, source_target_pairs={{0,2},{2,4},{4,6},{6,8},{8,10},{10,12},{12,14},{1,3},{3,5},{5,7},{... | collective-permute-start | bytes 516104 | tf_op jit(solution)/shard_map/ppermute | solution.py:727
  42.2 0.4 late.1.before_ref
  42.6 3.4 %collective-permute-done.4.left_ref.cargol_ref = f32[56,768]{1,0:T(8,128)S(1)} collective-permute-done((f32[56,768]{1,0:T(8,128)S(1)}, f32[56,768]{1,0:T(8,128)S(1)}, u32[]{:S(2)}, u32[]{:S(2)}) %collective-permute-start.4) | collective-permute-done | bytes 172064 | tf_op jit(solution)/shard_map/ppermute | solution.py:727
  46.0 1.0 %third.1 = f32[8,40,128]{2,1,0:T(8,128)S(1)} custom-call(f32[24,768]{1,0:T(8,128)S(1)} %get-tuple-element.20.refs_2_.refs_3_.extra_ref, f32[40,128]{1,0:T(8,128)S(1)} %late.1.before_ref, f32[56,768]{1,0:T(8,128)S(1)} %get-tuple-element.29.cargo_ref, f32[56,768]{1,0:T(8,128)S(1)} %collective-permute-done.4.left_ref.cargol_ref, ...), custom_call_target="tpu_custom_call" | custom-call | flops 1000000000 | bytes 1048576 | tf_op jit(solution)/shard_map/third/pallas_call | solution.py:706
  47.0 13.6 %all_to_all.10.gram_ref = f32[8,40,128]{2,1,0:T(8,128)S(1)} all-to-all(f32[8,40,128]{2,1,0:T(8,128)S(1)} %third.1), channel_id=1, replica_groups=mesh['groups'=2,'pts'=8,'probe'=2] {'pts'}, dimensions={0} | all-to-all | bytes 327680 | tf_op jit(solution)/shard_map/all_to_all | solution.py:822
  60.7 6.5 %final.1 = (f32[16,768]{1,0:T(8,128)}, f32[16,8,128]{2,1,0:T(8,128)S(1)}) custom-call(f32[8,40,128]{2,1,0:T(8,128)S(1)} %all_to_all.10.gram_ref, f32[32,768]{1,0:T(8,128)S(1)} %get-tuple-element.21.refs_0_.refs_1_.refs_2_.own_ref, f32[32,768]{1,0:T(8,128)S(1)} %collective-permute-done.refs_0_.left_ref, f32[40,768]{1,0:T(8,128)S(1)} %get-tuple-element.27.d1_ref.vec_ref, ...), custom_call_target="tpu_custom_call" | custom-call | flops 1000000000 | bytes 1048576 | tf_op jit(solution)/shard_map/final/pallas_call | solution.py:706
  67.2 9.5 %all_to_all.11.parts_ref = f32[16,8,128]{2,1,0:T(8,128)S(1)} all-to-all(f32[16,8,128]{2,1,0:T(8,128)S(1)} %get-tuple-element.34), channel_id=1, replica_groups=mesh['groups'=2,'pts'=8,'probe'=2] {'pts','probe'}, dimensions={0} | all-to-all | bytes 131072 | tf_op jit(solution)/shard_map/all_to_all | solution.py:831
  76.7 0.7 tail.1
Async XLA Ops:
  13.4 8.0 %collective-permute-start.1 = (f32[32,768]{1,0:T(8,128)S(1)}, f32[32,768]{1,0:T(8,128)S(1)}, u32[]{:S(2)}, u32[]{:S(2)}) collective-permute-start(f32[32,768]{1,0:T(8,128)S(1)} %get-tuple-element.21.refs_0_.refs_1_.refs_2_.own_ref), channel_id=1, source_target_pairs={{2,0},{4,2},{6,4},{8,6},{10,8},{12,10},{14,12},{3,1},{5,3},{7,5},{... | collective-permute-start | bytes 294920 | tf_op jit(solution)/shard_map/ppermute | solution.py:722
  14.7 8.6 %collective-permute-start = (f32[32,768]{1,0:T(8,128)S(1)}, f32[32,768]{1,0:T(8,128)S(1)}, u32[]{:S(2)}, u32[]{:S(2)}) collective-permute-start(f32[32,768]{1,0:T(8,128)S(1)} %get-tuple-element.21.refs_0_.refs_1_.refs_2_.own_ref), channel_id=1, source_target_pairs={{0,2},{2,4},{4,6},{6,8},{8,10},{10,12},{12,14},{1,3},{3,5},{5,7},{... | collective-permute-start | bytes 294920 | tf_op jit(solution)/shard_map/ppermute | solution.py:722
  24.7 7.6 %copy-start = (f32[16,768]{1,0:T(8,128)S(1)}, f32[16,768]{1,0:T(8,128)}, u32[]{:S(2)}) copy-start(f32[16,768]{1,0:T(8,128)} %sys_ref.3) | copy-start | bytes 147460
  26.0 7.9 %collective-permute-start.3 = (f32[40,768]{1,0:T(8,128)S(1)}, f32[40,768]{1,0:T(8,128)S(1)}, u32[]{:S(2)}, u32[]{:S(2)}) collective-permute-start(f32[40,768]{1,0:T(8,128)S(1)} %get-tuple-element.27.d1_ref.vec_ref), channel_id=1, source_target_pairs={{2,0},{4,2},{6,4},{8,6},{10,8},{12,10},{14,12},{3,1},{5,3},{7,5},{... | collective-permute-start | bytes 368648 | tf_op jit(solution)/shard_map/ppermute | solution.py:722
  27.3 9.3 %collective-permute-start.2 = (f32[40,768]{1,0:T(8,128)S(1)}, f32[40,768]{1,0:T(8,128)S(1)}, u32[]{:S(2)}, u32[]{:S(2)}) collective-permute-start(f32[40,768]{1,0:T(8,128)S(1)} %get-tuple-element.27.d1_ref.vec_ref), channel_id=1, source_target_pairs={{0,2},{2,4},{4,6},{6,8},{8,10},{10,12},{12,14},{1,3},{3,5},{5,7},{... | collective-permute-start | bytes 368648 | tf_op jit(solution)/shard_map/ppermute | solution.py:722
  37.8 8.2 %collective-permute-start.4 = (f32[56,768]{1,0:T(8,128)S(1)}, f32[56,768]{1,0:T(8,128)S(1)}, u32[]{:S(2)}, u32[]{:S(2)}) collective-permute-start(f32[56,768]{1,0:T(8,128)S(1)} %get-tuple-element.29.cargo_ref), channel_id=1, source_target_pairs={{0,2},{2,4},{4,6},{6,8},{8,10},{10,12},{12,14},{1,3},{3,5},{5,7},{... | collective-permute-start | bytes 516104 | tf_op jit(solution)/shard_map/ppermute | solution.py:727

commit v11 on v10

--- a/solution.py
+++ b/solution.py
@@ -143,7 +143,7 @@
     return jnp.concatenate([p for p in pieces if p.shape[0]], axis=0)
 
 
-def sweep_base(cells):
+def sweep_base(cells, beside):
     lane = iota((BASE, LANES), 1)
     start = lane - lane % BASE
     inner = iota((1, LANES), 1) % BASE
@@ -176,6 +176,9 @@
             cells = cells - cols[t] * new[t]
         cells = with_rows(cells, first, new)
         cols = coming
+        if beside:
+            beside.pop(0)()
+    assert not beside
     return cells
 
 
@@ -258,39 +261,57 @@
         return jnp.concatenate(parts, axis=0)
 
     eye = jnp.where(iota((BASE, LANES), 1) % BASE == iota((BASE, LANES), 0), 1.0, 0.0)
-    strips = [work[m, 0:BASE, :] for m in range(blocks)]
-    after = [work[m, BASE : 2 * BASE, :] for m in range(blocks)]
-    cells = jnp.where(seg < blocks, packed(strips, 0), eye)
-    for k in range(BS // BASE):
-        first = k * BASE
-        inv = -sweep_base(cells)
+
+    def updates(first, inv, strips):
+        state = {}
+
+        def product():
+            held = (wide >= first) & (wide < first + BASE)
+            minus = jnp.where(wide - first == deep, -1.0, 0.0)
+            stack = jnp.concatenate(
+                [jnp.where(held, minus, s) for s in strips]
+                + [jnp.zeros((LANES - blocks * BASE, BS), f32)],
+                axis=0,
+            )
+            spread = diagonal(inv)[: blocks * BASE]
+            new = dot(spread, stack, precision=highest)
+            for m in range(blocks):
+                state[m] = new[m * BASE : (m + 1) * BASE, :]
+
+        def rows_of(m, low, high):
+            def piece():
+                r0, r1, r2 = split(strips[m][:, low:high], 3)
+                p0, p1, p2 = split(state[m], 3)
+                a = jnp.concatenate([r0, r0, r1, r1, r0, r2], axis=0).astype(bf16)
+                b = jnp.concatenate([p0, p1, p0, p1, p2, p0], axis=0).astype(bf16)
+                gone = (iota((1, BS), 1) >= first) & (iota((1, BS), 1) < first + BASE)
+                work[m, low:high, :] = jnp.where(gone, 0.0, work[m, low:high, :]) - dot(a, b, TN)
+                if low <= first < high:
+                    work[m, first : first + BASE, :] = state[m]
+
+            return piece
+
+        half = BS // 2
+        return [product] + [
+            rows_of(m, low, low + half) for m in range(blocks) for low in range(0, BS, half)
+        ]
+
+    def strips_at(first):
+        return [work[m, first : first + BASE, :] for m in range(blocks)]
+
+    cells = jnp.where(seg < blocks, packed(strips_at(0), 0), eye)
+    pending = []
+    for first in range(0, BS, BASE):
+        inv = -sweep_base(cells, pending)
+        strips = strips_at(first)
         if first + BASE < BS:
+            after = strips_at(first + BASE)
             half = dot(inv, diagonal(packed(strips, first + BASE)), precision=highest)
             drop = dot(packed(after, first), diagonal(half), precision=highest)
             cells = jnp.where(seg < blocks, packed(after, first + BASE) - drop, eye)
-        held = (wide >= first) & (wide < first + BASE)
-        minus = jnp.where(wide - first == deep, -1.0, 0.0)
-        stack = jnp.concatenate(
-            [jnp.where(held, minus, s) for s in strips]
-            + [jnp.zeros((LANES - blocks * BASE, BS), f32)],
-            axis=0,
-        )
-        spread = jnp.concatenate([jnp.where(seg == m, inv, 0.0) for m in range(blocks)], axis=0)
-        new = dot(spread, stack, precision=highest)
-        gone = (iota((1, BS), 1) >= first) & (iota((1, BS), 1) < first + BASE)
-        coming, then = [], []
-        for m in range(blocks):
-            row = new[m * BASE : (m + 1) * BASE, :]
-            r0, r1, r2 = split(strips[m], 3)
-            p0, p1, p2 = split(row, 3)
-            a = jnp.concatenate([r0, r0, r1, r1, r0, r2], axis=0).astype(bf16)
-            b = jnp.concatenate([p0, p1, p0, p1, p2, p0], axis=0).astype(bf16)
-            value = jnp.where(gone, 0.0, work[m]) - dot(a, b, TN)
-            coming.append(value[first + BASE : first + 2 * BASE])
-            then.append(value[first + 2 * BASE : first + 3 * BASE])
-            work[m] = value
-            work[m, first : first + BASE, :] = row
-        strips, after = coming, then
+        pending = updates(first, inv, strips)
+    for piece in pending:
+        piece()
     for m in range(blocks):
         inv = -work[m]
         for i, part in enumerate(split(inv, 3)):

time: 77.7 us -> 77.8 us (level)
  no operation moved by 1% of the time
where the time goes in v11:
time: 77.8 us; the launch traced here: 77.5 us
  Pallas kernels  26.6 us (34%)
  blocking collectives  23.2 us (30%)
  starting transfers between devices  17.7 us (23%)
  waiting for transfers between devices  9.24 us (12%)
    pallas_call x10, Pallas kernels, call(): pl.pallas_call(body, out_shape=outs, in_specs=[sm] * smem + [vm] * (len(a...  26.6 us
    all_to_all x1, blocking collectives, shards(): gram = lax.all_to_all(gram, 'pts', 0, 0, tiled=True)  13.6 us
    ppermute x4, starting transfers between devices, both_sides(): return (lax.ppermute(cells, 'pts', up), lax.ppermute(cells, 'pts', down))  13.3 us
    all_to_all x1, blocking collectives, shards(): grads = lax.all_to_all(grads, ('pts', 'probe'), 0, 0, tiled=True)  9.53 us
    ppermute x4, waiting for transfers between devices, both_sides(): return (lax.ppermute(cells, 'pts', up), lax.ppermute(cells, 'pts', down))  5.84 us
    ppermute x1, starting transfers between devices, from_left(): return lax.ppermute(cells, 'pts', [(i, i + 1) for i in range(count - 1)])  4.4 us
    ppermute x1, waiting for transfers between devices, from_left(): return lax.ppermute(cells, 'pts', [(i, i + 1) for i in range(count - 1)])  3.4 us
  transfers between devices with their start and end apart: 5, of which 4 were waited for; matrix products, arithmetic and copies ran while one was open for 0% of the time, Pallas kernels for 2%

profile of v11, /device:TPU:0, one launch (start us, length us, event | category | flops | bytes accessed | tf_op | source)
XLA Modules:
  0.0 77.5 jit_solution(1279157499750789795)
XLA Ops:
  0.6 12.9 %invert.1 = (bf16[3,3,256,256]{3,2,1,0:T(8,128)(2,1)S(1)}, f32[32,768]{1,0:T(8,128)S(1)}, f32[24,768]{1,0:T(8,128)S(1)}) custom-call(s32[1]{0:T(128)} %bitcast.place_ref, s32[1]{0:T(128)} %bitcast.1.probe_ref, f32[8,768]{1,0:T(8,128)} %feat_hbm.1, s32[768]{0:T(1024)} %ids_hbm.1, s32[768]{0:T(1024)} %agg_hbm.1, f32[16,768]{1,0:T(8,128)} %sys_ref.3, ...), custom_call_target="tpu_custom_call" | custom-call | flops 10000000000 | bytes 1048576 | tf_op jit(solution)/shard_map/invert/pallas_call | solution.py:727
  13.5 1.3 %collective-permute-start.1 = (f32[32,768]{1,0:T(8,128)S(1)}, f32[32,768]{1,0:T(8,128)S(1)}, u32[]{:S(2)}, u32[]{:S(2)}) collective-permute-start(f32[32,768]{1,0:T(8,128)S(1)} %get-tuple-element.21.refs_0_.refs_1_.refs_2_.own_ref), channel_id=1, source_target_pairs={{2,0},{4,2},{6,4},{8,6},{10,8},{12,10},{14,12},{3,1},{5,3},{7,5},{... | collective-permute-start | bytes 294920 | tf_op jit(solution)/shard_map/ppermute | solution.py:743
  14.8 5.7 %collective-permute-start = (f32[32,768]{1,0:T(8,128)S(1)}, f32[32,768]{1,0:T(8,128)S(1)}, u32[]{:S(2)}, u32[]{:S(2)}) collective-permute-start(f32[32,768]{1,0:T(8,128)S(1)} %get-tuple-element.21.refs_0_.refs_1_.refs_2_.own_ref), channel_id=1, source_target_pairs={{0,2},{2,4},{4,6},{6,8},{8,10},{10,12},{12,14},{1,3},{3,5},{5,7},{... | collective-permute-start | bytes 294920 | tf_op jit(solution)/shard_map/ppermute | solution.py:743
  20.5 1.0 %build_own.1 = (bf16[3,768,256]{2,1,0:T(8,128)(2,1)S(1)}, bf16[3,768,256]{2,1,0:T(8,128)(2,1)S(1)}, f32[3,768,256]{2,1,0:T(8,128)S(1)}) custom-call(f32[32,768]{1,0:T(8,128)S(1)} %get-tuple-element.21.refs_0_.refs_1_.refs_2_.own_ref, f32[32,768]{1,0:T(8,128)S(1)} %get-tuple-element.21.refs_0_.refs_1_.refs_2_.own_ref, ...), custom_call_target="tpu_custom_call" | custom-call | flops 1000000000 | bytes 1048576 | tf_op jit(solution)/shard_map/build_own/pallas_call | solution.py:727
  21.5 0.0 collective-permute-done.1.refs_1_.right_ref
  21.5 1.9 %collective-permute-done.refs_0_.left_ref = f32[32,768]{1,0:T(8,128)S(1)} collective-permute-done((f32[32,768]{1,0:T(8,128)S(1)}, f32[32,768]{1,0:T(8,128)S(1)}, u32[]{:S(2)}, u32[]{:S(2)}) %collective-permute-start) | collective-permute-done | bytes 98336 | tf_op jit(solution)/shard_map/ppermute | solution.py:743
  23.5 1.4 %build_halo.1 = (bf16[3,1024,256]{2,1,0:T(8,128)(2,1)S(1)}, bf16[3,1024,256]{2,1,0:T(8,128)(2,1)S(1)}, f32[3,1024,256]{2,1,0:T(8,128)S(1)}) custom-call(f32[32,768]{1,0:T(8,128)S(1)} %collective-permute-done.refs_0_.left_ref, f32[32,768]{1,0:T(8,128)S(1)} %collective-permute-done.1.refs_1_.right_ref, ...), custom_call_target="tpu_custom_call" | custom-call | flops 1000000000 | bytes 1048576 | tf_op jit(solution)/shard_map/build_halo/pallas_call | solution.py:727
  24.9 0.0 copy-start
  24.9 1.2 %first.1 = (f32[40,768]{1,0:T(8,128)S(1)}, f32[40,768]{1,0:T(8,128)S(1)}) custom-call(f32[32,768]{1,0:T(8,128)S(1)} %get-tuple-element.21.refs_0_.refs_1_.refs_2_.own_ref, f32[32,768]{1,0:T(8,128)S(1)} %collective-permute-done.refs_0_.left_ref, f32[32,768]{1,0:T(8,128)S(1)} %collective-permute-done.1.refs_1_.right_ref, ...), custom_call_target="tpu_custom_call" | custom-call | flops 1000000000 | bytes 1048576 | tf_op jit(solution)/shard_map/first/pallas_call | solution.py:727
  26.1 1.3 %collective-permute-start.3 = (f32[40,768]{1,0:T(8,128)S(1)}, f32[40,768]{1,0:T(8,128)S(1)}, u32[]{:S(2)}, u32[]{:S(2)}) collective-permute-start(f32[40,768]{1,0:T(8,128)S(1)} %get-tuple-element.27.d1_ref.vec_ref), channel_id=1, source_target_pairs={{2,0},{4,2},{6,4},{8,6},{10,8},{12,10},{14,12},{3,1},{5,3},{7,5},{... | collective-permute-start | bytes 368648 | tf_op jit(solution)/shard_map/ppermute | solution.py:743
  27.4 5.0 %collective-permute-start.2 = (f32[40,768]{1,0:T(8,128)S(1)}, f32[40,768]{1,0:T(8,128)S(1)}, u32[]{:S(2)}, u32[]{:S(2)}) collective-permute-start(f32[40,768]{1,0:T(8,128)S(1)} %get-tuple-element.27.d1_ref.vec_ref), channel_id=1, source_target_pairs={{0,2},{2,4},{4,6},{6,8},{8,10},{10,12},{12,14},{1,3},{3,5},{5,7},{... | collective-permute-start | bytes 368648 | tf_op jit(solution)/shard_map/ppermute | solution.py:743
  32.4 0.0 copy-done
  32.4 0.4 early.1.early_ref.before_ref
  32.8 1.1 %collective-permute-done.3.right_ref = f32[40,768]{1,0:T(8,128)S(1)} collective-permute-done((f32[40,768]{1,0:T(8,128)S(1)}, f32[40,768]{1,0:T(8,128)S(1)}, u32[]{:S(2)}, u32[]{:S(2)}) %collective-permute-start.3) | collective-permute-done | bytes 122912 | tf_op jit(solution)/shard_map/ppermute | solution.py:743
  33.9 2.8 %collective-permute-done.2.left_ref.d1l_ref = f32[40,768]{1,0:T(8,128)S(1)} collective-permute-done((f32[40,768]{1,0:T(8,128)S(1)}, f32[40,768]{1,0:T(8,128)S(1)}, u32[]{:S(2)}, u32[]{:S(2)}) %collective-permute-start.2) | collective-permute-done | bytes 122912 | tf_op jit(solution)/shard_map/ppermute | solution.py:743
  36.7 1.2 %second.1 = (f32[40,768]{1,0:T(8,128)S(1)}, f32[56,768]{1,0:T(8,128)S(1)}) custom-call(f32[24,768]{1,0:T(8,128)S(1)} %get-tuple-element.20.refs_2_.refs_3_.extra_ref, f32[40,768]{1,0:T(8,128)S(1)} %get-tuple-element.27.d1_ref.vec_ref, f32[40,768]{1,0:T(8,128)S(1)} %collective-permute-done.2.left_ref.d1l_ref, f32[40,768]{1,0:T(8,128)S(1)} %collective-permute-done.3.right_ref, ...), custom_call_target="tpu_custom_call" | custom-call | flops 1000000000 | bytes 1048576 | tf_op jit(solution)/shard_map/second/pallas_call | solution.py:727
  37.9 4.4 %collective-permute-start.4 = (f32[56,768]{1,0:T(8,128)S(1)}, f32[56,768]{1,0:T(8,128)S(1)}, u32[]{:S(2)}, u32[]{:S(2)}) collective-permute-start(f32[56,768]{1,0:T(8,128)S(1)} %get-tuple-element.29.cargo_ref), channel_id=1, source_target_pairs={{0,2},{2,4},{4,6},{6,8},{8,10},{10,12},{12,14},{1,3},{3,5},{5,7},{... | collective-permute-start | bytes 516104 | tf_op jit(solution)/shard_map/ppermute | solution.py:748
  42.3 0.4 late.1.before_ref
  42.7 3.4 %collective-permute-done.4.left_ref.cargol_ref = f32[56,768]{1,0:T(8,128)S(1)} collective-permute-done((f32[56,768]{1,0:T(8,128)S(1)}, f32[56,768]{1,0:T(8,128)S(1)}, u32[]{:S(2)}, u32[]{:S(2)}) %collective-permute-start.4) | collective-permute-done | bytes 172064 | tf_op jit(solution)/shard_map/ppermute | solution.py:748
  46.1 1.0 %third.1 = f32[8,40,128]{2,1,0:T(8,128)S(1)} custom-call(f32[24,768]{1,0:T(8,128)S(1)} %get-tuple-element.20.refs_2_.refs_3_.extra_ref, f32[40,128]{1,0:T(8,128)S(1)} %late.1.before_ref, f32[56,768]{1,0:T(8,128)S(1)} %get-tuple-element.29.cargo_ref, f32[56,768]{1,0:T(8,128)S(1)} %collective-permute-done.4.left_ref.cargol_ref, ...), custom_call_target="tpu_custom_call" | custom-call | flops 1000000000 | bytes 1048576 | tf_op jit(solution)/shard_map/third/pallas_call | solution.py:727
  47.1 13.6 %all_to_all.10.gram_ref = f32[8,40,128]{2,1,0:T(8,128)S(1)} all-to-all(f32[8,40,128]{2,1,0:T(8,128)S(1)} %third.1), channel_id=1, replica_groups=mesh['groups'=2,'pts'=8,'probe'=2] {'pts'}, dimensions={0} | all-to-all | bytes 327680 | tf_op jit(solution)/shard_map/all_to_all | solution.py:843
  60.8 6.5 %final.1 = (f32[16,768]{1,0:T(8,128)}, f32[16,8,128]{2,1,0:T(8,128)S(1)}) custom-call(f32[8,40,128]{2,1,0:T(8,128)S(1)} %all_to_all.10.gram_ref, f32[32,768]{1,0:T(8,128)S(1)} %get-tuple-element.21.refs_0_.refs_1_.refs_2_.own_ref, f32[32,768]{1,0:T(8,128)S(1)} %collective-permute-done.refs_0_.left_ref, f32[40,768]{1,0:T(8,128)S(1)} %get-tuple-element.27.d1_ref.vec_ref, ...), custom_call_target="tpu_custom_call" | custom-call | flops 1000000000 | bytes 1048576 | tf_op jit(solution)/shard_map/final/pallas_call | solution.py:727
  67.3 9.5 %all_to_all.11.parts_ref = f32[16,8,128]{2,1,0:T(8,128)S(1)} all-to-all(f32[16,8,128]{2,1,0:T(8,128)S(1)} %get-tuple-element.34), channel_id=1, replica_groups=mesh['groups'=2,'pts'=8,'probe'=2] {'pts','probe'}, dimensions={0} | all-to-all | bytes 131072 | tf_op jit(solution)/shard_map/all_to_all | solution.py:852
  76.8 0.7 tail.1
Async XLA Ops:
  13.5 8.0 %collective-permute-start.1 = (f32[32,768]{1,0:T(8,128)S(1)}, f32[32,768]{1,0:T(8,128)S(1)}, u32[]{:S(2)}, u32[]{:S(2)}) collective-permute-start(f32[32,768]{1,0:T(8,128)S(1)} %get-tuple-element.21.refs_0_.refs_1_.refs_2_.own_ref), channel_id=1, source_target_pairs={{2,0},{4,2},{6,4},{8,6},{10,8},{12,10},{14,12},{3,1},{5,3},{7,5},{... | collective-permute-start | bytes 294920 | tf_op jit(solution)/shard_map/ppermute | solution.py:743
  14.8 8.6 %collective-permute-start = (f32[32,768]{1,0:T(8,128)S(1)}, f32[32,768]{1,0:T(8,128)S(1)}, u32[]{:S(2)}, u32[]{:S(2)}) collective-permute-start(f32[32,768]{1,0:T(8,128)S(1)} %get-tuple-element.21.refs_0_.refs_1_.refs_2_.own_ref), channel_id=1, source_target_pairs={{0,2},{2,4},{4,6},{6,8},{8,10},{10,12},{12,14},{1,3},{3,5},{5,7},{... | collective-permute-start | bytes 294920 | tf_op jit(solution)/shard_map/ppermute | solution.py:743
  24.9 7.6 %copy-start = (f32[16,768]{1,0:T(8,128)S(1)}, f32[16,768]{1,0:T(8,128)}, u32[]{:S(2)}) copy-start(f32[16,768]{1,0:T(8,128)} %sys_ref.3) | copy-start | bytes 147460
  26.1 7.8 %collective-permute-start.3 = (f32[40,768]{1,0:T(8,128)S(1)}, f32[40,768]{1,0:T(8,128)S(1)}, u32[]{:S(2)}, u32[]{:S(2)}) collective-permute-start(f32[40,768]{1,0:T(8,128)S(1)} %get-tuple-element.27.d1_ref.vec_ref), channel_id=1, source_target_pairs={{2,0},{4,2},{6,4},{8,6},{10,8},{12,10},{14,12},{3,1},{5,3},{7,5},{... | collective-permute-start | bytes 368648 | tf_op jit(solution)/shard_map/ppermute | solution.py:743
  27.4 9.3 %collective-permute-start.2 = (f32[40,768]{1,0:T(8,128)S(1)}, f32[40,768]{1,0:T(8,128)S(1)}, u32[]{:S(2)}, u32[]{:S(2)}) collective-permute-start(f32[40,768]{1,0:T(8,128)S(1)} %get-tuple-element.27.d1_ref.vec_ref), channel_id=1, source_target_pairs={{0,2},{2,4},{4,6},{6,8},{8,10},{10,12},{12,14},{1,3},{3,5},{5,7},{... | collective-permute-start | bytes 368648 | tf_op jit(solution)/shard_map/ppermute | solution.py:743
  37.9 8.2 %collective-permute-start.4 = (f32[56,768]{1,0:T(8,128)S(1)}, f32[56,768]{1,0:T(8,128)S(1)}, u32[]{:S(2)}, u32[]{:S(2)}) collective-permute-start(f32[56,768]{1,0:T(8,128)S(1)} %get-tuple-element.29.cargo_ref), channel_id=1, source_target_pairs={{0,2},{2,4},{4,6},{6,8},{8,10},{10,12},{12,14},{1,3},{3,5},{5,7},{... | collective-permute-start | bytes 516104 | tf_op jit(solution)/shard_map/ppermute | solution.py:748

commit v12 on v11

--- a/solution.py
+++ b/solution.py
@@ -133,53 +133,68 @@
     return out
 
 
-def with_rows(cells, first, rows):
-    top = first - first % 8
-    part = cells[top : top + 8]
-    sub = iota((8, 1), 0)
-    for t, row in enumerate(rows):
-        part = jnp.where(sub == first - top + t, row, part)
-    pieces = [cells[:top], part, cells[top + 8 :]]
-    return jnp.concatenate([p for p in pieces if p.shape[0]], axis=0)
-
-
 def sweep_base(cells, beside):
-    lane = iota((BASE, LANES), 1)
+    tall = range(BASE // 8)
+    tiles = [cells[8 * i : 8 * i + 8] for i in tall]
+    lane = iota((8, LANES), 1)
     start = lane - lane % BASE
-    inner = iota((1, LANES), 1) % BASE
+    inner = lane % BASE
+    sub = iota((8, LANES), 0)
 
     def columns(first):
         return [
-            jnp.take_along_axis(cells, start + (first + t), axis=1, mode="promise_in_bounds")
+            [
+                jnp.take_along_axis(tile, start + (first + t), axis=1, mode="promise_in_bounds")
+                for tile in tiles
+            ]
             for t in range(GROUP)
         ]
+
+    def row(parts, r):
+        return jnp.broadcast_to(parts[r // 8][r % 8 : r % 8 + 1, :], (8, LANES))
+
+    def with_rows(parts, first, rows):
+        part = parts[first // 8]
+        for t, value in enumerate(rows):
+            part = jnp.where(sub == first % 8 + t, value, part)
+        return [part if i == first // 8 else parts[i] for i in tall]
+
+    def less(parts, factor):
+        out = []
+        for i in tall:
+            part = parts[i]
+            for t in range(GROUP):
+                part = part - cols[t][i] * factor[t]
+            out.append(part)
+        return out
 
     cols = columns(0)
     for first in range(0, BASE, GROUP):
         ahead = columns(first + GROUP) if first + GROUP < BASE else []
-        pivots = [[cols[u][first + t : first + t + 1, :] for u in range(GROUP)] for t in range(GROUP)]
+        pivots = [[None] * GROUP for _ in range(GROUP)]
+        for t in range(GROUP):
+            for u in range(t, GROUP):
+                pivots[t][u] = pivots[u][t] = row(cols[u], first + t)
         inv = small_inverse(pivots)
         coming = []
         for col in ahead:
-            head = [col[first + t : first + t + 1, :] for t in range(GROUP)]
+            head = [row(col, first + t) for t in range(GROUP)]
             factor = [sum(inv[t][u] * head[u] for u in range(GROUP)) for t in range(GROUP)]
-            for t in range(GROUP):
-                col = col - cols[t] * factor[t]
-            coming.append(with_rows(col, first, factor))
-        rows = [cells[first + t : first + t + 1, :] for t in range(GROUP)]
+            coming.append(with_rows(less(col, factor), first, factor))
         group = (inner >= first) & (inner < first + GROUP)
+        rows = []
         for t in range(GROUP):
-            rows[t] = jnp.where(inner == first + t, -1.0, jnp.where(group, 0.0, rows[t]))
+            value = jnp.where(group, 0.0, row(tiles, first + t))
+            rows.append(jnp.where(inner == first + t, -1.0, value))
         new = [sum(inv[t][u] * rows[u] for u in range(GROUP)) for t in range(GROUP)]
-        cells = jnp.where(group, 0.0, cells)
-        for t in range(GROUP):
-            cells = cells - cols[t] * new[t]
-        cells = with_rows(cells, first, new)
+        tiles = [jnp.where(group, 0.0, tile) for tile in tiles]
+        tiles = with_rows(less(tiles, new), first, new)
         cols = coming
         if beside:
             beside.pop(0)()
-    assert not beside
-    return cells
+    while beside:
+        beside.pop(0)()
+    return jnp.concatenate(tiles, axis=0)
 
 
 def fetch(pairs, sems):

time: 77.8 us -> 77 us (0.990)
  Pallas kernels: 26.6 us -> 25.8 us
    pallas_call x10, Pallas kernels: 26.6 us -> 25.8 us  [call(): pl.pallas_call(body, out_shape=outs, in_specs=[sm] * smem + [vm] * (len(a...]
where the time goes in v12:
time: 77 us; the launch traced here: 76.6 us
  Pallas kernels  25.8 us (34%)
  blocking collectives  23.2 us (30%)
  starting transfers between devices  17.7 us (23%)
  waiting for transfers between devices  9.23 us (12%)
  between operations  0.77 us (1%)
    pallas_call x10, Pallas kernels, call(): pl.pallas_call(body, out_shape=outs, in_specs=[sm] * smem + [vm] * (len(a...  25.8 us
    all_to_all x1, blocking collectives, shards(): gram = lax.all_to_all(gram, 'pts', 0, 0, tiled=True)  13.7 us
    ppermute x4, starting transfers between devices, both_sides(): return (lax.ppermute(cells, 'pts', up), lax.ppermute(cells, 'pts', down))  13.3 us
    all_to_all x1, blocking collectives, shards(): grads = lax.all_to_all(grads, ('pts', 'probe'), 0, 0, tiled=True)  9.53 us
    ppermute x4, waiting for transfers between devices, both_sides(): return (lax.ppermute(cells, 'pts', up), lax.ppermute(cells, 'pts', down))  5.83 us
    ppermute x1, starting transfers between devices, from_left(): return lax.ppermute(cells, 'pts', [(i, i + 1) for i in range(count - 1)])  4.4 us
    ppermute x1, waiting for transfers between devices, from_left(): return lax.ppermute(cells, 'pts', [(i, i + 1) for i in range(count - 1)])  3.4 us
  transfers between devices with their start and end apart: 5, of which 4 were waited for; matrix products, arithmetic and copies ran while one was open for 0% of the time, Pallas kernels for 2%

profile of v12, /device:TPU:0, one launch (start us, length us, event | category | flops | bytes accessed | tf_op | source)
XLA Modules:
  0.0 76.6 jit_solution(4020342656922398938)
XLA Ops:
  0.6 12.0 %invert.1 = (bf16[3,3,256,256]{3,2,1,0:T(8,128)(2,1)S(1)}, f32[32,768]{1,0:T(8,128)S(1)}, f32[24,768]{1,0:T(8,128)S(1)}) custom-call(s32[1]{0:T(128)} %bitcast.place_ref, s32[1]{0:T(128)} %bitcast.1.probe_ref, f32[8,768]{1,0:T(8,128)} %feat_hbm.1, s32[768]{0:T(1024)} %ids_hbm.1, s32[768]{0:T(1024)} %agg_hbm.1, f32[16,768]{1,0:T(8,128)} %sys_ref.3, ...), custom_call_target="tpu_custom_call" | custom-call | flops 10000000000 | bytes 1048576 | tf_op jit(solution)/shard_map/invert/pallas_call | solution.py:742
  12.7 1.3 %collective-permute-start.1 = (f32[32,768]{1,0:T(8,128)S(1)}, f32[32,768]{1,0:T(8,128)S(1)}, u32[]{:S(2)}, u32[]{:S(2)}) collective-permute-start(f32[32,768]{1,0:T(8,128)S(1)} %get-tuple-element.21.refs_0_.refs_1_.refs_2_.own_ref), channel_id=1, source_target_pairs={{2,0},{4,2},{6,4},{8,6},{10,8},{12,10},{14,12},{3,1},{5,3},{7,5},{... | collective-permute-start | bytes 294920 | tf_op jit(solution)/shard_map/ppermute | solution.py:758
  14.0 5.7 %collective-permute-start = (f32[32,768]{1,0:T(8,128)S(1)}, f32[32,768]{1,0:T(8,128)S(1)}, u32[]{:S(2)}, u32[]{:S(2)}) collective-permute-start(f32[32,768]{1,0:T(8,128)S(1)} %get-tuple-element.21.refs_0_.refs_1_.refs_2_.own_ref), channel_id=1, source_target_pairs={{0,2},{2,4},{4,6},{6,8},{8,10},{10,12},{12,14},{1,3},{3,5},{5,7},{... | collective-permute-start | bytes 294920 | tf_op jit(solution)/shard_map/ppermute | solution.py:758
  19.7 1.0 %build_own.1 = (bf16[3,768,256]{2,1,0:T(8,128)(2,1)S(1)}, bf16[3,768,256]{2,1,0:T(8,128)(2,1)S(1)}, f32[3,768,256]{2,1,0:T(8,128)S(1)}) custom-call(f32[32,768]{1,0:T(8,128)S(1)} %get-tuple-element.21.refs_0_.refs_1_.refs_2_.own_ref, f32[32,768]{1,0:T(8,128)S(1)} %get-tuple-element.21.refs_0_.refs_1_.refs_2_.own_ref, ...), custom_call_target="tpu_custom_call" | custom-call | flops 1000000000 | bytes 1048576 | tf_op jit(solution)/shard_map/build_own/pallas_call | solution.py:742
  20.7 0.0 collective-permute-done.1.refs_1_.right_ref
  20.7 1.9 %collective-permute-done.refs_0_.left_ref = f32[32,768]{1,0:T(8,128)S(1)} collective-permute-done((f32[32,768]{1,0:T(8,128)S(1)}, f32[32,768]{1,0:T(8,128)S(1)}, u32[]{:S(2)}, u32[]{:S(2)}) %collective-permute-start) | collective-permute-done | bytes 98336 | tf_op jit(solution)/shard_map/ppermute | solution.py:758
  22.6 1.4 %build_halo.1 = (bf16[3,1024,256]{2,1,0:T(8,128)(2,1)S(1)}, bf16[3,1024,256]{2,1,0:T(8,128)(2,1)S(1)}, f32[3,1024,256]{2,1,0:T(8,128)S(1)}) custom-call(f32[32,768]{1,0:T(8,128)S(1)} %collective-permute-done.refs_0_.left_ref, f32[32,768]{1,0:T(8,128)S(1)} %collective-permute-done.1.refs_1_.right_ref, ...), custom_call_target="tpu_custom_call" | custom-call | flops 1000000000 | bytes 1048576 | tf_op jit(solution)/shard_map/build_halo/pallas_call | solution.py:742
  24.0 0.0 copy-start
  24.0 1.2 %first.1 = (f32[40,768]{1,0:T(8,128)S(1)}, f32[40,768]{1,0:T(8,128)S(1)}) custom-call(f32[32,768]{1,0:T(8,128)S(1)} %get-tuple-element.21.refs_0_.refs_1_.refs_2_.own_ref, f32[32,768]{1,0:T(8,128)S(1)} %collective-permute-done.refs_0_.left_ref, f32[32,768]{1,0:T(8,128)S(1)} %collective-permute-done.1.refs_1_.right_ref, ...), custom_call_target="tpu_custom_call" | custom-call | flops 1000000000 | bytes 1048576 | tf_op jit(solution)/shard_map/first/pallas_call | solution.py:742
  25.2 1.3 %collective-permute-start.3 = (f32[40,768]{1,0:T(8,128)S(1)}, f32[40,768]{1,0:T(8,128)S(1)}, u32[]{:S(2)}, u32[]{:S(2)}) collective-permute-start(f32[40,768]{1,0:T(8,128)S(1)} %get-tuple-element.27.d1_ref.vec_ref), channel_id=1, source_target_pairs={{2,0},{4,2},{6,4},{8,6},{10,8},{12,10},{14,12},{3,1},{5,3},{7,5},{... | collective-permute-start | bytes 368648 | tf_op jit(solution)/shard_map/ppermute | solution.py:758
  26.5 5.0 %collective-permute-start.2 = (f32[40,768]{1,0:T(8,128)S(1)}, f32[40,768]{1,0:T(8,128)S(1)}, u32[]{:S(2)}, u32[]{:S(2)}) collective-permute-start(f32[40,768]{1,0:T(8,128)S(1)} %get-tuple-element.27.d1_ref.vec_ref), channel_id=1, source_target_pairs={{0,2},{2,4},{4,6},{6,8},{8,10},{10,12},{12,14},{1,3},{3,5},{5,7},{... | collective-permute-start | bytes 368648 | tf_op jit(solution)/shard_map/ppermute | solution.py:758
  31.5 0.0 copy-done
  31.6 0.4 early.1.early_ref.before_ref
  31.9 1.1 %collective-permute-done.3.right_ref = f32[40,768]{1,0:T(8,128)S(1)} collective-permute-done((f32[40,768]{1,0:T(8,128)S(1)}, f32[40,768]{1,0:T(8,128)S(1)}, u32[]{:S(2)}, u32[]{:S(2)}) %collective-permute-start.3) | collective-permute-done | bytes 122912 | tf_op jit(solution)/shard_map/ppermute | solution.py:758
  33.1 2.8 %collective-permute-done.2.left_ref.d1l_ref = f32[40,768]{1,0:T(8,128)S(1)} collective-permute-done((f32[40,768]{1,0:T(8,128)S(1)}, f32[40,768]{1,0:T(8,128)S(1)}, u32[]{:S(2)}, u32[]{:S(2)}) %collective-permute-start.2) | collective-permute-done | bytes 122912 | tf_op jit(solution)/shard_map/ppermute | solution.py:758
  35.8 1.2 %second.1 = (f32[40,768]{1,0:T(8,128)S(1)}, f32[56,768]{1,0:T(8,128)S(1)}) custom-call(f32[24,768]{1,0:T(8,128)S(1)} %get-tuple-element.20.refs_2_.refs_3_.extra_ref, f32[40,768]{1,0:T(8,128)S(1)} %get-tuple-element.27.d1_ref.vec_ref, f32[40,768]{1,0:T(8,128)S(1)} %collective-permute-done.2.left_ref.d1l_ref, f32[40,768]{1,0:T(8,128)S(1)} %collective-permute-done.3.right_ref, ...), custom_call_target="tpu_custom_call" | custom-call | flops 1000000000 | bytes 1048576 | tf_op jit(solution)/shard_map/second/pallas_call | solution.py:742
  37.1 4.4 %collective-permute-start.4 = (f32[56,768]{1,0:T(8,128)S(1)}, f32[56,768]{1,0:T(8,128)S(1)}, u32[]{:S(2)}, u32[]{:S(2)}) collective-permute-start(f32[56,768]{1,0:T(8,128)S(1)} %get-tuple-element.29.cargo_ref), channel_id=1, source_target_pairs={{0,2},{2,4},{4,6},{6,8},{8,10},{10,12},{12,14},{1,3},{3,5},{5,7},{... | collective-permute-start | bytes 516104 | tf_op jit(solution)/shard_map/ppermute | solution.py:763
  41.5 0.4 late.1.before_ref
  41.9 3.4 %collective-permute-done.4.left_ref.cargol_ref = f32[56,768]{1,0:T(8,128)S(1)} collective-permute-done((f32[56,768]{1,0:T(8,128)S(1)}, f32[56,768]{1,0:T(8,128)S(1)}, u32[]{:S(2)}, u32[]{:S(2)}) %collective-permute-start.4) | collective-permute-done | bytes 172064 | tf_op jit(solution)/shard_map/ppermute | solution.py:763
  45.3 1.0 %third.1 = f32[8,40,128]{2,1,0:T(8,128)S(1)} custom-call(f32[24,768]{1,0:T(8,128)S(1)} %get-tuple-element.20.refs_2_.refs_3_.extra_ref, f32[40,128]{1,0:T(8,128)S(1)} %late.1.before_ref, f32[56,768]{1,0:T(8,128)S(1)} %get-tuple-element.29.cargo_ref, f32[56,768]{1,0:T(8,128)S(1)} %collective-permute-done.4.left_ref.cargol_ref, ...), custom_call_target="tpu_custom_call" | custom-call | flops 1000000000 | bytes 1048576 | tf_op jit(solution)/shard_map/third/pallas_call | solution.py:742
  46.3 13.7 %all_to_all.10.gram_ref = f32[8,40,128]{2,1,0:T(8,128)S(1)} all-to-all(f32[8,40,128]{2,1,0:T(8,128)S(1)} %third.1), channel_id=1, replica_groups=mesh['groups'=2,'pts'=8,'probe'=2] {'pts'}, dimensions={0} | all-to-all | bytes 327680 | tf_op jit(solution)/shard_map/all_to_all | solution.py:858
  59.9 6.5 %final.1 = (f32[16,768]{1,0:T(8,128)}, f32[16,8,128]{2,1,0:T(8,128)S(1)}) custom-call(f32[8,40,128]{2,1,0:T(8,128)S(1)} %all_to_all.10.gram_ref, f32[32,768]{1,0:T(8,128)S(1)} %get-tuple-element.21.refs_0_.refs_1_.refs_2_.own_ref, f32[32,768]{1,0:T(8,128)S(1)} %collective-permute-done.refs_0_.left_ref, f32[40,768]{1,0:T(8,128)S(1)} %get-tuple-element.27.d1_ref.vec_ref, ...), custom_call_target="tpu_custom_call" | custom-call | flops 1000000000 | bytes 1048576 | tf_op jit(solution)/shard_map/final/pallas_call | solution.py:742
  66.4 9.5 %all_to_all.11.parts_ref = f32[16,8,128]{2,1,0:T(8,128)S(1)} all-to-all(f32[16,8,128]{2,1,0:T(8,128)S(1)} %get-tuple-element.34), channel_id=1, replica_groups=mesh['groups'=2,'pts'=8,'probe'=2] {'pts','probe'}, dimensions={0} | all-to-all | bytes 131072 | tf_op jit(solution)/shard_map/all_to_all | solution.py:867
  76.0 0.7 tail.1
Async XLA Ops:
  12.7 8.0 %collective-permute-start.1 = (f32[32,768]{1,0:T(8,128)S(1)}, f32[32,768]{1,0:T(8,128)S(1)}, u32[]{:S(2)}, u32[]{:S(2)}) collective-permute-start(f32[32,768]{1,0:T(8,128)S(1)} %get-tuple-element.21.refs_0_.refs_1_.refs_2_.own_ref), channel_id=1, source_target_pairs={{2,0},{4,2},{6,4},{8,6},{10,8},{12,10},{14,12},{3,1},{5,3},{7,5},{... | collective-permute-start | bytes 294920 | tf_op jit(solution)/shard_map/ppermute | solution.py:758
  14.0 8.6 %collective-permute-start = (f32[32,768]{1,0:T(8,128)S(1)}, f32[32,768]{1,0:T(8,128)S(1)}, u32[]{:S(2)}, u32[]{:S(2)}) collective-permute-start(f32[32,768]{1,0:T(8,128)S(1)} %get-tuple-element.21.refs_0_.refs_1_.refs_2_.own_ref), channel_id=1, source_target_pairs={{0,2},{2,4},{4,6},{6,8},{8,10},{10,12},{12,14},{1,3},{3,5},{5,7},{... | collective-permute-start | bytes 294920 | tf_op jit(solution)/shard_map/ppermute | solution.py:758
  24.0 7.6 %copy-start = (f32[16,768]{1,0:T(8,128)S(1)}, f32[16,768]{1,0:T(8,128)}, u32[]{:S(2)}) copy-start(f32[16,768]{1,0:T(8,128)} %sys_ref.3) | copy-start | bytes 147460
  25.2 7.8 %collective-permute-start.3 = (f32[40,768]{1,0:T(8,128)S(1)}, f32[40,768]{1,0:T(8,128)S(1)}, u32[]{:S(2)}, u32[]{:S(2)}) collective-permute-start(f32[40,768]{1,0:T(8,128)S(1)} %get-tuple-element.27.d1_ref.vec_ref), channel_id=1, source_target_pairs={{2,0},{4,2},{6,4},{8,6},{10,8},{12,10},{14,12},{3,1},{5,3},{7,5},{... | collective-permute-start | bytes 368648 | tf_op jit(solution)/shard_map/ppermute | solution.py:758
  26.5 9.3 %collective-permute-start.2 = (f32[40,768]{1,0:T(8,128)S(1)}, f32[40,768]{1,0:T(8,128)S(1)}, u32[]{:S(2)}, u32[]{:S(2)}) collective-permute-start(f32[40,768]{1,0:T(8,128)S(1)} %get-tuple-element.27.d1_ref.vec_ref), channel_id=1, source_target_pairs={{0,2},{2,4},{4,6},{6,8},{8,10},{10,12},{12,14},{1,3},{3,5},{5,7},{... | collective-permute-start | bytes 368648 | tf_op jit(solution)/shard_map/ppermute | solution.py:758
  37.1 8.2 %collective-permute-start.4 = (f32[56,768]{1,0:T(8,128)S(1)}, f32[56,768]{1,0:T(8,128)S(1)}, u32[]{:S(2)}, u32[]{:S(2)}) collective-permute-start(f32[56,768]{1,0:T(8,128)S(1)} %get-tuple-element.29.cargo_ref), channel_id=1, source_target_pairs={{0,2},{2,4},{4,6},{6,8},{8,10},{10,12},{12,14},{1,3},{3,5},{5,7},{... | collective-permute-start | bytes 516104 | tf_op jit(solution)/shard_map/ppermute | solution.py:763

commit v13 on v12

--- a/solution.py
+++ b/solution.py
@@ -15,7 +15,7 @@
 SLOTS = 2 * REACH + 1
 BAND = SLOTS * BS
 BASE = 32
-GROUP = 4
+GROUP = 2
 LANES = 128
 SYS = 2 * FEAT
 

time: 77 us -> 78.3 us (1.017)
  Pallas kernels: 25.8 us -> 27.1 us
    pallas_call x10, Pallas kernels: 25.8 us -> 27.1 us  [call(): pl.pallas_call(body, out_shape=outs, in_specs=[sm] * smem + [vm] * (len(a...]
where the time goes in v13:
time: 78.3 us; the launch traced here: 78 us
  Pallas kernels  27.1 us (35%)
  blocking collectives  23.2 us (30%)
  starting transfers between devices  17.7 us (23%)
  waiting for transfers between devices  9.23 us (12%)
    pallas_call x10, Pallas kernels, call(): pl.pallas_call(body, out_shape=outs, in_specs=[sm] * smem + [vm] * (len(a...  27.1 us
    all_to_all x1, blocking collectives, shards(): gram = lax.all_to_all(gram, 'pts', 0, 0, tiled=True)  13.6 us
    ppermute x4, starting transfers between devices, both_sides(): return (lax.ppermute(cells, 'pts', up), lax.ppermute(cells, 'pts', down))  13.3 us
    all_to_all x1, blocking collectives, shards(): grads = lax.all_to_all(grads, ('pts', 'probe'), 0, 0, tiled=True)  9.53 us
    ppermute x4, waiting for transfers between devices, both_sides(): return (lax.ppermute(cells, 'pts', up), lax.ppermute(cells, 'pts', down))  5.83 us
    ppermute x1, starting transfers between devices, from_left(): return lax.ppermute(cells, 'pts', [(i, i + 1) for i in range(count - 1)])  4.4 us
    ppermute x1, waiting for transfers between devices, from_left(): return lax.ppermute(cells, 'pts', [(i, i + 1) for i in range(count - 1)])  3.4 us
  transfers between devices with their start and end apart: 5, of which 4 were waited for; matrix products, arithmetic and copies ran while one was open for 0% of the time, Pallas kernels for 2%

profile of v13, /device:TPU:0, one launch (start us, length us, event | category | flops | bytes accessed | tf_op | source)
XLA Modules:
  0.0 78.0 jit_solution(6186571684727803421)
XLA Ops:
  0.6 13.4 %invert.1 = (bf16[3,3,256,256]{3,2,1,0:T(8,128)(2,1)S(1)}, f32[32,768]{1,0:T(8,128)S(1)}, f32[24,768]{1,0:T(8,128)S(1)}) custom-call(s32[1]{0:T(128)} %bitcast.place_ref, s32[1]{0:T(128)} %bitcast.1.probe_ref, f32[8,768]{1,0:T(8,128)} %feat_hbm.1, s32[768]{0:T(1024)} %ids_hbm.1, s32[768]{0:T(1024)} %agg_hbm.1, f32[16,768]{1,0:T(8,128)} %sys_ref.3, ...), custom_call_target="tpu_custom_call" | custom-call | flops 10000000000 | bytes 1048576 | tf_op jit(solution)/shard_map/invert/pallas_call | solution.py:742
  14.0 1.3 %collective-permute-start.1 = (f32[32,768]{1,0:T(8,128)S(1)}, f32[32,768]{1,0:T(8,128)S(1)}, u32[]{:S(2)}, u32[]{:S(2)}) collective-permute-start(f32[32,768]{1,0:T(8,128)S(1)} %get-tuple-element.21.refs_0_.refs_1_.refs_2_.own_ref), channel_id=1, source_target_pairs={{2,0},{4,2},{6,4},{8,6},{10,8},{12,10},{14,12},{3,1},{5,3},{7,5},{... | collective-permute-start | bytes 294920 | tf_op jit(solution)/shard_map/ppermute | solution.py:758
  15.3 5.5 %collective-permute-start = (f32[32,768]{1,0:T(8,128)S(1)}, f32[32,768]{1,0:T(8,128)S(1)}, u32[]{:S(2)}, u32[]{:S(2)}) collective-permute-start(f32[32,768]{1,0:T(8,128)S(1)} %get-tuple-element.21.refs_0_.refs_1_.refs_2_.own_ref), channel_id=1, source_target_pairs={{0,2},{2,4},{4,6},{6,8},{8,10},{10,12},{12,14},{1,3},{3,5},{5,7},{... | collective-permute-start | bytes 294920 | tf_op jit(solution)/shard_map/ppermute | solution.py:758
  20.9 1.0 %build_own.1 = (bf16[3,768,256]{2,1,0:T(8,128)(2,1)S(1)}, bf16[3,768,256]{2,1,0:T(8,128)(2,1)S(1)}, f32[3,768,256]{2,1,0:T(8,128)S(1)}) custom-call(f32[32,768]{1,0:T(8,128)S(1)} %get-tuple-element.21.refs_0_.refs_1_.refs_2_.own_ref, f32[32,768]{1,0:T(8,128)S(1)} %get-tuple-element.21.refs_0_.refs_1_.refs_2_.own_ref, ...), custom_call_target="tpu_custom_call" | custom-call | flops 1000000000 | bytes 1048576 | tf_op jit(solution)/shard_map/build_own/pallas_call | solution.py:742
  21.9 0.0 collective-permute-done.1.refs_1_.right_ref
  21.9 2.1 %collective-permute-done.refs_0_.left_ref = f32[32,768]{1,0:T(8,128)S(1)} collective-permute-done((f32[32,768]{1,0:T(8,128)S(1)}, f32[32,768]{1,0:T(8,128)S(1)}, u32[]{:S(2)}, u32[]{:S(2)}) %collective-permute-start) | collective-permute-done | bytes 98336 | tf_op jit(solution)/shard_map/ppermute | solution.py:758
  24.0 1.4 %build_halo.1 = (bf16[3,1024,256]{2,1,0:T(8,128)(2,1)S(1)}, bf16[3,1024,256]{2,1,0:T(8,128)(2,1)S(1)}, f32[3,1024,256]{2,1,0:T(8,128)S(1)}) custom-call(f32[32,768]{1,0:T(8,128)S(1)} %collective-permute-done.refs_0_.left_ref, f32[32,768]{1,0:T(8,128)S(1)} %collective-permute-done.1.refs_1_.right_ref, ...), custom_call_target="tpu_custom_call" | custom-call | flops 1000000000 | bytes 1048576 | tf_op jit(solution)/shard_map/build_halo/pallas_call | solution.py:742
  25.4 0.0 copy-start
  25.4 1.2 %first.1 = (f32[40,768]{1,0:T(8,128)S(1)}, f32[40,768]{1,0:T(8,128)S(1)}) custom-call(f32[32,768]{1,0:T(8,128)S(1)} %get-tuple-element.21.refs_0_.refs_1_.refs_2_.own_ref, f32[32,768]{1,0:T(8,128)S(1)} %collective-permute-done.refs_0_.left_ref, f32[32,768]{1,0:T(8,128)S(1)} %collective-permute-done.1.refs_1_.right_ref, ...), custom_call_target="tpu_custom_call" | custom-call | flops 1000000000 | bytes 1048576 | tf_op jit(solution)/shard_map/first/pallas_call | solution.py:742
  26.6 1.3 %collective-permute-start.3 = (f32[40,768]{1,0:T(8,128)S(1)}, f32[40,768]{1,0:T(8,128)S(1)}, u32[]{:S(2)}, u32[]{:S(2)}) collective-permute-start(f32[40,768]{1,0:T(8,128)S(1)} %get-tuple-element.27.d1_ref.vec_ref), channel_id=1, source_target_pairs={{2,0},{4,2},{6,4},{8,6},{10,8},{12,10},{14,12},{3,1},{5,3},{7,5},{... | collective-permute-start | bytes 368648 | tf_op jit(solution)/shard_map/ppermute | solution.py:758
  27.9 5.2 %collective-permute-start.2 = (f32[40,768]{1,0:T(8,128)S(1)}, f32[40,768]{1,0:T(8,128)S(1)}, u32[]{:S(2)}, u32[]{:S(2)}) collective-permute-start(f32[40,768]{1,0:T(8,128)S(1)} %get-tuple-element.27.d1_ref.vec_ref), channel_id=1, source_target_pairs={{0,2},{2,4},{4,6},{6,8},{8,10},{10,12},{12,14},{1,3},{3,5},{5,7},{... | collective-permute-start | bytes 368648 | tf_op jit(solution)/shard_map/ppermute | solution.py:758
  33.1 0.0 copy-done
  33.1 0.4 early.1.early_ref.before_ref
  33.5 1.0 %collective-permute-done.3.right_ref = f32[40,768]{1,0:T(8,128)S(1)} collective-permute-done((f32[40,768]{1,0:T(8,128)S(1)}, f32[40,768]{1,0:T(8,128)S(1)}, u32[]{:S(2)}, u32[]{:S(2)}) %collective-permute-start.3) | collective-permute-done | bytes 122912 | tf_op jit(solution)/shard_map/ppermute | solution.py:758
  34.4 2.8 %collective-permute-done.2.left_ref.d1l_ref = f32[40,768]{1,0:T(8,128)S(1)} collective-permute-done((f32[40,768]{1,0:T(8,128)S(1)}, f32[40,768]{1,0:T(8,128)S(1)}, u32[]{:S(2)}, u32[]{:S(2)}) %collective-permute-start.2) | collective-permute-done | bytes 122912 | tf_op jit(solution)/shard_map/ppermute | solution.py:758
  37.2 1.2 %second.1 = (f32[40,768]{1,0:T(8,128)S(1)}, f32[56,768]{1,0:T(8,128)S(1)}) custom-call(f32[24,768]{1,0:T(8,128)S(1)} %get-tuple-element.20.refs_2_.refs_3_.extra_ref, f32[40,768]{1,0:T(8,128)S(1)} %get-tuple-element.27.d1_ref.vec_ref, f32[40,768]{1,0:T(8,128)S(1)} %collective-permute-done.2.left_ref.d1l_ref, f32[40,768]{1,0:T(8,128)S(1)} %collective-permute-done.3.right_ref, ...), custom_call_target="tpu_custom_call" | custom-call | flops 1000000000 | bytes 1048576 | tf_op jit(solution)/shard_map/second/pallas_call | solution.py:742
  38.4 4.4 %collective-permute-start.4 = (f32[56,768]{1,0:T(8,128)S(1)}, f32[56,768]{1,0:T(8,128)S(1)}, u32[]{:S(2)}, u32[]{:S(2)}) collective-permute-start(f32[56,768]{1,0:T(8,128)S(1)} %get-tuple-element.29.cargo_ref), channel_id=1, source_target_pairs={{0,2},{2,4},{4,6},{6,8},{8,10},{10,12},{12,14},{1,3},{3,5},{5,7},{... | collective-permute-start | bytes 516104 | tf_op jit(solution)/shard_map/ppermute | solution.py:763
  42.8 0.4 late.1.before_ref
  43.2 3.4 %collective-permute-done.4.left_ref.cargol_ref = f32[56,768]{1,0:T(8,128)S(1)} collective-permute-done((f32[56,768]{1,0:T(8,128)S(1)}, f32[56,768]{1,0:T(8,128)S(1)}, u32[]{:S(2)}, u32[]{:S(2)}) %collective-permute-start.4) | collective-permute-done | bytes 172064 | tf_op jit(solution)/shard_map/ppermute | solution.py:763
  46.6 1.0 %third.1 = f32[8,40,128]{2,1,0:T(8,128)S(1)} custom-call(f32[24,768]{1,0:T(8,128)S(1)} %get-tuple-element.20.refs_2_.refs_3_.extra_ref, f32[40,128]{1,0:T(8,128)S(1)} %late.1.before_ref, f32[56,768]{1,0:T(8,128)S(1)} %get-tuple-element.29.cargo_ref, f32[56,768]{1,0:T(8,128)S(1)} %collective-permute-done.4.left_ref.cargol_ref, ...), custom_call_target="tpu_custom_call" | custom-call | flops 1000000000 | bytes 1048576 | tf_op jit(solution)/shard_map/third/pallas_call | solution.py:742
  47.6 13.6 %all_to_all.10.gram_ref = f32[8,40,128]{2,1,0:T(8,128)S(1)} all-to-all(f32[8,40,128]{2,1,0:T(8,128)S(1)} %third.1), channel_id=1, replica_groups=mesh['groups'=2,'pts'=8,'probe'=2] {'pts'}, dimensions={0} | all-to-all | bytes 327680 | tf_op jit(solution)/shard_map/all_to_all | solution.py:858
  61.3 6.5 %final.1 = (f32[16,768]{1,0:T(8,128)}, f32[16,8,128]{2,1,0:T(8,128)S(1)}) custom-call(f32[8,40,128]{2,1,0:T(8,128)S(1)} %all_to_all.10.gram_ref, f32[32,768]{1,0:T(8,128)S(1)} %get-tuple-element.21.refs_0_.refs_1_.refs_2_.own_ref, f32[32,768]{1,0:T(8,128)S(1)} %collective-permute-done.refs_0_.left_ref, f32[40,768]{1,0:T(8,128)S(1)} %get-tuple-element.27.d1_ref.vec_ref, ...), custom_call_target="tpu_custom_call" | custom-call | flops 1000000000 | bytes 1048576 | tf_op jit(solution)/shard_map/final/pallas_call | solution.py:742
  67.8 9.5 %all_to_all.11.parts_ref = f32[16,8,128]{2,1,0:T(8,128)S(1)} all-to-all(f32[16,8,128]{2,1,0:T(8,128)S(1)} %get-tuple-element.34), channel_id=1, replica_groups=mesh['groups'=2,'pts'=8,'probe'=2] {'pts','probe'}, dimensions={0} | all-to-all | bytes 131072 | tf_op jit(solution)/shard_map/all_to_all | solution.py:867
  77.3 0.7 tail.1
Async XLA Ops:
  14.0 7.8 %collective-permute-start.1 = (f32[32,768]{1,0:T(8,128)S(1)}, f32[32,768]{1,0:T(8,128)S(1)}, u32[]{:S(2)}, u32[]{:S(2)}) collective-permute-start(f32[32,768]{1,0:T(8,128)S(1)} %get-tuple-element.21.refs_0_.refs_1_.refs_2_.own_ref), channel_id=1, source_target_pairs={{2,0},{4,2},{6,4},{8,6},{10,8},{12,10},{14,12},{3,1},{5,3},{7,5},{... | collective-permute-start | bytes 294920 | tf_op jit(solution)/shard_map/ppermute | solution.py:758
  15.3 8.6 %collective-permute-start = (f32[32,768]{1,0:T(8,128)S(1)}, f32[32,768]{1,0:T(8,128)S(1)}, u32[]{:S(2)}, u32[]{:S(2)}) collective-permute-start(f32[32,768]{1,0:T(8,128)S(1)} %get-tuple-element.21.refs_0_.refs_1_.refs_2_.own_ref), channel_id=1, source_target_pairs={{0,2},{2,4},{4,6},{6,8},{8,10},{10,12},{12,14},{1,3},{3,5},{5,7},{... | collective-permute-start | bytes 294920 | tf_op jit(solution)/shard_map/ppermute | solution.py:758
  25.4 7.7 %copy-start = (f32[16,768]{1,0:T(8,128)S(1)}, f32[16,768]{1,0:T(8,128)}, u32[]{:S(2)}) copy-start(f32[16,768]{1,0:T(8,128)} %sys_ref.3) | copy-start | bytes 147460
  26.6 7.9 %collective-permute-start.3 = (f32[40,768]{1,0:T(8,128)S(1)}, f32[40,768]{1,0:T(8,128)S(1)}, u32[]{:S(2)}, u32[]{:S(2)}) collective-permute-start(f32[40,768]{1,0:T(8,128)S(1)} %get-tuple-element.27.d1_ref.vec_ref), channel_id=1, source_target_pairs={{2,0},{4,2},{6,4},{8,6},{10,8},{12,10},{14,12},{3,1},{5,3},{7,5},{... | collective-permute-start | bytes 368648 | tf_op jit(solution)/shard_map/ppermute | solution.py:758
  27.9 9.3 %collective-permute-start.2 = (f32[40,768]{1,0:T(8,128)S(1)}, f32[40,768]{1,0:T(8,128)S(1)}, u32[]{:S(2)}, u32[]{:S(2)}) collective-permute-start(f32[40,768]{1,0:T(8,128)S(1)} %get-tuple-element.27.d1_ref.vec_ref), channel_id=1, source_target_pairs={{0,2},{2,4},{4,6},{6,8},{8,10},{10,12},{12,14},{1,3},{3,5},{5,7},{... | collective-permute-start | bytes 368648 | tf_op jit(solution)/shard_map/ppermute | solution.py:758
  38.4 8.2 %collective-permute-start.4 = (f32[56,768]{1,0:T(8,128)S(1)}, f32[56,768]{1,0:T(8,128)S(1)}, u32[]{:S(2)}, u32[]{:S(2)}) collective-permute-start(f32[56,768]{1,0:T(8,128)S(1)} %get-tuple-element.29.cargo_ref), channel_id=1, source_target_pairs={{0,2},{2,4},{4,6},{6,8},{8,10},{10,12},{12,14},{1,3},{3,5},{5,7},{... | collective-permute-start | bytes 516104 | tf_op jit(solution)/shard_map/ppermute | solution.py:763

commit v14 on v12

--- a/solution.py
+++ b/solution.py
@@ -159,7 +159,7 @@
             part = jnp.where(sub == first % 8 + t, value, part)
         return [part if i == first // 8 else parts[i] for i in tall]
 
-    def less(parts, factor):
+    def less(parts, cols, factor):
         out = []
         for i in tall:
             part = parts[i]
@@ -168,19 +168,33 @@
             out.append(part)
         return out
 
-    cols = columns(0)
-    for first in range(0, BASE, GROUP):
-        ahead = columns(first + GROUP) if first + GROUP < BASE else []
-        pivots = [[None] * GROUP for _ in range(GROUP)]
+    def symmetric(entry):
+        out = [[None] * GROUP for _ in range(GROUP)]
         for t in range(GROUP):
             for u in range(t, GROUP):
-                pivots[t][u] = pivots[u][t] = row(cols[u], first + t)
+                out[t][u] = out[u][t] = entry(t, u)
+        return out
+
+    cols, ahead = columns(0), columns(GROUP)
+    pivots = symmetric(lambda t, u: row(cols[u], t))
+    for first in range(0, BASE, GROUP):
+        then = first + GROUP
+        far = columns(first + 2 * GROUP) if first + 2 * GROUP < BASE else []
+        heads = [[row(col, first + t) for t in range(GROUP)] for col in ahead + far]
         inv = small_inverse(pivots)
-        coming = []
-        for col in ahead:
-            head = [row(col, first + t) for t in range(GROUP)]
-            factor = [sum(inv[t][u] * head[u] for u in range(GROUP)) for t in range(GROUP)]
-            coming.append(with_rows(less(col, factor), first, factor))
+        factors = [
+            [sum(inv[t][u] * head[u] for u in range(GROUP)) for t in range(GROUP)]
+            for head in heads
+        ]
+        if ahead:
+            pivots = symmetric(
+                lambda t, u: row(ahead[u], then + t)
+                - sum(heads[t][i] * factors[u][i] for i in range(GROUP))
+            )
+        coming = [
+            with_rows(less(col, cols, factor), first, factor)
+            for col, factor in zip(ahead + far, factors)
+        ]
         group = (inner >= first) & (inner < first + GROUP)
         rows = []
         for t in range(GROUP):
@@ -188,8 +202,8 @@
             rows.append(jnp.where(inner == first + t, -1.0, value))
         new = [sum(inv[t][u] * rows[u] for u in range(GROUP)) for t in range(GROUP)]
         tiles = [jnp.where(group, 0.0, tile) for tile in tiles]
-        tiles = with_rows(less(tiles, new), first, new)
-        cols = coming
+        tiles = with_rows(less(tiles, cols, new), first, new)
+        cols, ahead = coming[:GROUP], coming[GROUP:]
         if beside:
             beside.pop(0)()
     while beside:

time: 77 us -> 78.1 us (1.014)
  Pallas kernels: 25.8 us -> 26.9 us
    pallas_call x10, Pallas kernels: 25.8 us -> 26.9 us  [call(): pl.pallas_call(body, out_shape=outs, in_specs=[sm] * smem + [vm] * (len(a...]
where the time goes in v14:
time: 78.1 us; the launch traced here: 77.8 us
  Pallas kernels  26.9 us (34%)
  blocking collectives  23.2 us (30%)
  starting transfers between devices  17.7 us (23%)
  waiting for transfers between devices  9.24 us (12%)
    pallas_call x10, Pallas kernels, call(): pl.pallas_call(body, out_shape=outs, in_specs=[sm] * smem + [vm] * (len(a...  26.9 us
    all_to_all x1, blocking collectives, shards(): gram = lax.all_to_all(gram, 'pts', 0, 0, tiled=True)  13.6 us
    ppermute x4, starting transfers between devices, both_sides(): return (lax.ppermute(cells, 'pts', up), lax.ppermute(cells, 'pts', down))  13.3 us
    all_to_all x1, blocking collectives, shards(): grads = lax.all_to_all(grads, ('pts', 'probe'), 0, 0, tiled=True)  9.53 us
    ppermute x4, waiting for transfers between devices, both_sides(): return (lax.ppermute(cells, 'pts', up), lax.ppermute(cells, 'pts', down))  5.84 us
    ppermute x1, starting transfers between devices, from_left(): return lax.ppermute(cells, 'pts', [(i, i + 1) for i in range(count - 1)])  4.4 us
    ppermute x1, waiting for transfers between devices, from_left(): return lax.ppermute(cells, 'pts', [(i, i + 1) for i in range(count - 1)])  3.4 us
  transfers between devices with their start and end apart: 5, of which 4 were waited for; matrix products, arithmetic and copies ran while one was open for 0% of the time, Pallas kernels for 2%

profile of v14, /device:TPU:0, one launch (start us, length us, event | category | flops | bytes accessed | tf_op | source)
XLA Modules:
  0.0 77.8 jit_solution(2166602721824881596)
XLA Ops:
  0.6 13.2 %invert.1 = (bf16[3,3,256,256]{3,2,1,0:T(8,128)(2,1)S(1)}, f32[32,768]{1,0:T(8,128)S(1)}, f32[24,768]{1,0:T(8,128)S(1)}) custom-call(s32[1]{0:T(128)} %bitcast.place_ref, s32[1]{0:T(128)} %bitcast.1.probe_ref, f32[8,768]{1,0:T(8,128)} %feat_hbm.1, s32[768]{0:T(1024)} %ids_hbm.1, s32[768]{0:T(1024)} %agg_hbm.1, f32[16,768]{1,0:T(8,128)} %sys_ref.3, ...), custom_call_target="tpu_custom_call" | custom-call | flops 10000000000 | bytes 1048576 | tf_op jit(solution)/shard_map/invert/pallas_call | solution.py:756
  13.8 1.3 %collective-permute-start.1 = (f32[32,768]{1,0:T(8,128)S(1)}, f32[32,768]{1,0:T(8,128)S(1)}, u32[]{:S(2)}, u32[]{:S(2)}) collective-permute-start(f32[32,768]{1,0:T(8,128)S(1)} %get-tuple-element.21.refs_0_.refs_1_.refs_2_.own_ref), channel_id=1, source_target_pairs={{2,0},{4,2},{6,4},{8,6},{10,8},{12,10},{14,12},{3,1},{5,3},{7,5},{... | collective-permute-start | bytes 294920 | tf_op jit(solution)/shard_map/ppermute | solution.py:772
  15.1 5.7 %collective-permute-start = (f32[32,768]{1,0:T(8,128)S(1)}, f32[32,768]{1,0:T(8,128)S(1)}, u32[]{:S(2)}, u32[]{:S(2)}) collective-permute-start(f32[32,768]{1,0:T(8,128)S(1)} %get-tuple-element.21.refs_0_.refs_1_.refs_2_.own_ref), channel_id=1, source_target_pairs={{0,2},{2,4},{4,6},{6,8},{8,10},{10,12},{12,14},{1,3},{3,5},{5,7},{... | collective-permute-start | bytes 294920 | tf_op jit(solution)/shard_map/ppermute | solution.py:772
  20.8 1.0 %build_own.1 = (bf16[3,768,256]{2,1,0:T(8,128)(2,1)S(1)}, bf16[3,768,256]{2,1,0:T(8,128)(2,1)S(1)}, f32[3,768,256]{2,1,0:T(8,128)S(1)}) custom-call(f32[32,768]{1,0:T(8,128)S(1)} %get-tuple-element.21.refs_0_.refs_1_.refs_2_.own_ref, f32[32,768]{1,0:T(8,128)S(1)} %get-tuple-element.21.refs_0_.refs_1_.refs_2_.own_ref, ...), custom_call_target="tpu_custom_call" | custom-call | flops 1000000000 | bytes 1048576 | tf_op jit(solution)/shard_map/build_own/pallas_call | solution.py:756
  21.8 0.0 collective-permute-done.1.refs_1_.right_ref
  21.8 1.9 %collective-permute-done.refs_0_.left_ref = f32[32,768]{1,0:T(8,128)S(1)} collective-permute-done((f32[32,768]{1,0:T(8,128)S(1)}, f32[32,768]{1,0:T(8,128)S(1)}, u32[]{:S(2)}, u32[]{:S(2)}) %collective-permute-start) | collective-permute-done | bytes 98336 | tf_op jit(solution)/shard_map/ppermute | solution.py:772
  23.7 1.4 %build_halo.1 = (bf16[3,1024,256]{2,1,0:T(8,128)(2,1)S(1)}, bf16[3,1024,256]{2,1,0:T(8,128)(2,1)S(1)}, f32[3,1024,256]{2,1,0:T(8,128)S(1)}) custom-call(f32[32,768]{1,0:T(8,128)S(1)} %collective-permute-done.refs_0_.left_ref, f32[32,768]{1,0:T(8,128)S(1)} %collective-permute-done.1.refs_1_.right_ref, ...), custom_call_target="tpu_custom_call" | custom-call | flops 1000000000 | bytes 1048576 | tf_op jit(solution)/shard_map/build_halo/pallas_call | solution.py:756
  25.1 0.0 copy-start
  25.1 1.2 %first.1 = (f32[40,768]{1,0:T(8,128)S(1)}, f32[40,768]{1,0:T(8,128)S(1)}) custom-call(f32[32,768]{1,0:T(8,128)S(1)} %get-tuple-element.21.refs_0_.refs_1_.refs_2_.own_ref, f32[32,768]{1,0:T(8,128)S(1)} %collective-permute-done.refs_0_.left_ref, f32[32,768]{1,0:T(8,128)S(1)} %collective-permute-done.1.refs_1_.right_ref, ...), custom_call_target="tpu_custom_call" | custom-call | flops 1000000000 | bytes 1048576 | tf_op jit(solution)/shard_map/first/pallas_call | solution.py:756
  26.4 1.3 %collective-permute-start.3 = (f32[40,768]{1,0:T(8,128)S(1)}, f32[40,768]{1,0:T(8,128)S(1)}, u32[]{:S(2)}, u32[]{:S(2)}) collective-permute-start(f32[40,768]{1,0:T(8,128)S(1)} %get-tuple-element.27.d1_ref.vec_ref), channel_id=1, source_target_pairs={{2,0},{4,2},{6,4},{8,6},{10,8},{12,10},{14,12},{3,1},{5,3},{7,5},{... | collective-permute-start | bytes 368648 | tf_op jit(solution)/shard_map/ppermute | solution.py:772
  27.7 5.0 %collective-permute-start.2 = (f32[40,768]{1,0:T(8,128)S(1)}, f32[40,768]{1,0:T(8,128)S(1)}, u32[]{:S(2)}, u32[]{:S(2)}) collective-permute-start(f32[40,768]{1,0:T(8,128)S(1)} %get-tuple-element.27.d1_ref.vec_ref), channel_id=1, source_target_pairs={{0,2},{2,4},{4,6},{6,8},{8,10},{10,12},{12,14},{1,3},{3,5},{5,7},{... | collective-permute-start | bytes 368648 | tf_op jit(solution)/shard_map/ppermute | solution.py:772
  32.7 0.0 copy-done
  32.7 0.4 early.1.early_ref.before_ref
  33.1 1.1 %collective-permute-done.3.right_ref = f32[40,768]{1,0:T(8,128)S(1)} collective-permute-done((f32[40,768]{1,0:T(8,128)S(1)}, f32[40,768]{1,0:T(8,128)S(1)}, u32[]{:S(2)}, u32[]{:S(2)}) %collective-permute-start.3) | collective-permute-done | bytes 122912 | tf_op jit(solution)/shard_map/ppermute | solution.py:772
  34.2 2.8 %collective-permute-done.2.left_ref.d1l_ref = f32[40,768]{1,0:T(8,128)S(1)} collective-permute-done((f32[40,768]{1,0:T(8,128)S(1)}, f32[40,768]{1,0:T(8,128)S(1)}, u32[]{:S(2)}, u32[]{:S(2)}) %collective-permute-start.2) | collective-permute-done | bytes 122912 | tf_op jit(solution)/shard_map/ppermute | solution.py:772
  37.0 1.2 %second.1 = (f32[40,768]{1,0:T(8,128)S(1)}, f32[56,768]{1,0:T(8,128)S(1)}) custom-call(f32[24,768]{1,0:T(8,128)S(1)} %get-tuple-element.20.refs_2_.refs_3_.extra_ref, f32[40,768]{1,0:T(8,128)S(1)} %get-tuple-element.27.d1_ref.vec_ref, f32[40,768]{1,0:T(8,128)S(1)} %collective-permute-done.2.left_ref.d1l_ref, f32[40,768]{1,0:T(8,128)S(1)} %collective-permute-done.3.right_ref, ...), custom_call_target="tpu_custom_call" | custom-call | flops 1000000000 | bytes 1048576 | tf_op jit(solution)/shard_map/second/pallas_call | solution.py:756
  38.2 4.4 %collective-permute-start.4 = (f32[56,768]{1,0:T(8,128)S(1)}, f32[56,768]{1,0:T(8,128)S(1)}, u32[]{:S(2)}, u32[]{:S(2)}) collective-permute-start(f32[56,768]{1,0:T(8,128)S(1)} %get-tuple-element.29.cargo_ref), channel_id=1, source_target_pairs={{0,2},{2,4},{4,6},{6,8},{8,10},{10,12},{12,14},{1,3},{3,5},{5,7},{... | collective-permute-start | bytes 516104 | tf_op jit(solution)/shard_map/ppermute | solution.py:777
  42.6 0.4 late.1.before_ref
  43.0 3.4 %collective-permute-done.4.left_ref.cargol_ref = f32[56,768]{1,0:T(8,128)S(1)} collective-permute-done((f32[56,768]{1,0:T(8,128)S(1)}, f32[56,768]{1,0:T(8,128)S(1)}, u32[]{:S(2)}, u32[]{:S(2)}) %collective-permute-start.4) | collective-permute-done | bytes 172064 | tf_op jit(solution)/shard_map/ppermute | solution.py:777
  46.4 1.0 %third.1 = f32[8,40,128]{2,1,0:T(8,128)S(1)} custom-call(f32[24,768]{1,0:T(8,128)S(1)} %get-tuple-element.20.refs_2_.refs_3_.extra_ref, f32[40,128]{1,0:T(8,128)S(1)} %late.1.before_ref, f32[56,768]{1,0:T(8,128)S(1)} %get-tuple-element.29.cargo_ref, f32[56,768]{1,0:T(8,128)S(1)} %collective-permute-done.4.left_ref.cargol_ref, ...), custom_call_target="tpu_custom_call" | custom-call | flops 1000000000 | bytes 1048576 | tf_op jit(solution)/shard_map/third/pallas_call | solution.py:756
  47.4 13.6 %all_to_all.10.gram_ref = f32[8,40,128]{2,1,0:T(8,128)S(1)} all-to-all(f32[8,40,128]{2,1,0:T(8,128)S(1)} %third.1), channel_id=1, replica_groups=mesh['groups'=2,'pts'=8,'probe'=2] {'pts'}, dimensions={0} | all-to-all | bytes 327680 | tf_op jit(solution)/shard_map/all_to_all | solution.py:872
  61.1 6.5 %final.1 = (f32[16,768]{1,0:T(8,128)}, f32[16,8,128]{2,1,0:T(8,128)S(1)}) custom-call(f32[8,40,128]{2,1,0:T(8,128)S(1)} %all_to_all.10.gram_ref, f32[32,768]{1,0:T(8,128)S(1)} %get-tuple-element.21.refs_0_.refs_1_.refs_2_.own_ref, f32[32,768]{1,0:T(8,128)S(1)} %collective-permute-done.refs_0_.left_ref, f32[40,768]{1,0:T(8,128)S(1)} %get-tuple-element.27.d1_ref.vec_ref, ...), custom_call_target="tpu_custom_call" | custom-call | flops 1000000000 | bytes 1048576 | tf_op jit(solution)/shard_map/final/pallas_call | solution.py:756
  67.6 9.5 %all_to_all.11.parts_ref = f32[16,8,128]{2,1,0:T(8,128)S(1)} all-to-all(f32[16,8,128]{2,1,0:T(8,128)S(1)} %get-tuple-element.34), channel_id=1, replica_groups=mesh['groups'=2,'pts'=8,'probe'=2] {'pts','probe'}, dimensions={0} | all-to-all | bytes 131072 | tf_op jit(solution)/shard_map/all_to_all | solution.py:881
  77.1 0.7 tail.1
Async XLA Ops:
  13.8 8.0 %collective-permute-start.1 = (f32[32,768]{1,0:T(8,128)S(1)}, f32[32,768]{1,0:T(8,128)S(1)}, u32[]{:S(2)}, u32[]{:S(2)}) collective-permute-start(f32[32,768]{1,0:T(8,128)S(1)} %get-tuple-element.21.refs_0_.refs_1_.refs_2_.own_ref), channel_id=1, source_target_pairs={{2,0},{4,2},{6,4},{8,6},{10,8},{12,10},{14,12},{3,1},{5,3},{7,5},{... | collective-permute-start | bytes 294920 | tf_op jit(solution)/shard_map/ppermute | solution.py:772
  15.1 8.6 %collective-permute-start = (f32[32,768]{1,0:T(8,128)S(1)}, f32[32,768]{1,0:T(8,128)S(1)}, u32[]{:S(2)}, u32[]{:S(2)}) collective-permute-start(f32[32,768]{1,0:T(8,128)S(1)} %get-tuple-element.21.refs_0_.refs_1_.refs_2_.own_ref), channel_id=1, source_target_pairs={{0,2},{2,4},{4,6},{6,8},{8,10},{10,12},{12,14},{1,3},{3,5},{5,7},{... | collective-permute-start | bytes 294920 | tf_op jit(solution)/shard_map/ppermute | solution.py:772
  25.1 7.6 %copy-start = (f32[16,768]{1,0:T(8,128)S(1)}, f32[16,768]{1,0:T(8,128)}, u32[]{:S(2)}) copy-start(f32[16,768]{1,0:T(8,128)} %sys_ref.3) | copy-start | bytes 147460
  26.4 7.9 %collective-permute-start.3 = (f32[40,768]{1,0:T(8,128)S(1)}, f32[40,768]{1,0:T(8,128)S(1)}, u32[]{:S(2)}, u32[]{:S(2)}) collective-permute-start(f32[40,768]{1,0:T(8,128)S(1)} %get-tuple-element.27.d1_ref.vec_ref), channel_id=1, source_target_pairs={{2,0},{4,2},{6,4},{8,6},{10,8},{12,10},{14,12},{3,1},{5,3},{7,5},{... | collective-permute-start | bytes 368648 | tf_op jit(solution)/shard_map/ppermute | solution.py:772
  27.7 9.3 %collective-permute-start.2 = (f32[40,768]{1,0:T(8,128)S(1)}, f32[40,768]{1,0:T(8,128)S(1)}, u32[]{:S(2)}, u32[]{:S(2)}) collective-permute-start(f32[40,768]{1,0:T(8,128)S(1)} %get-tuple-element.27.d1_ref.vec_ref), channel_id=1, source_target_pairs={{0,2},{2,4},{4,6},{6,8},{8,10},{10,12},{12,14},{1,3},{3,5},{5,7},{... | collective-permute-start | bytes 368648 | tf_op jit(solution)/shard_map/ppermute | solution.py:772
  38.2 8.2 %collective-permute-start.4 = (f32[56,768]{1,0:T(8,128)S(1)}, f32[56,768]{1,0:T(8,128)S(1)}, u32[]{:S(2)}, u32[]{:S(2)}) collective-permute-start(f32[56,768]{1,0:T(8,128)S(1)} %get-tuple-element.29.cargo_ref), channel_id=1, source_target_pairs={{0,2},{2,4},{4,6},{6,8},{8,10},{10,12},{12,14},{1,3},{3,5},{5,7},{... | collective-permute-start | bytes 516104 | tf_op jit(solution)/shard_map/ppermute | solution.py:777

commit v15 on v12

--- a/solution.py
+++ b/solution.py
@@ -393,47 +393,61 @@
     return jnp.concatenate(out, axis=1)
 
 
-def operate(own, left, right, noise, own_hi, own_lo, halo_hi, halo_lo):
+def operate_halo(left, right, halo_hi, halo_lo):
     lefts, rights = pieces(left), pieces(right)
     out = []
     for m in range(REACH):
         beyond = jnp.concatenate([lefts[:, m * BS :], rights[:, : (m + 1) * BS]], axis=1)
         out.append(apply(beyond, halo_hi[m], halo_lo[m]))
-    return operate_own(own, noise, own_hi, own_lo) + jnp.concatenate(out, axis=1)
+    return jnp.concatenate(out, axis=1)
+
+
+def smooth_pieces(vectors, parts):
+    rows = vectors.shape[0]
+    cells = jnp.concatenate(split(vectors, 3), axis=0).astype(bf16)
+    a = dot(cells, parts[0])
+    b = dot(cells[: 2 * rows], parts[1])
+    c = dot(cells[:rows], parts[2])
+    return a[:rows] + (a[rows : 2 * rows] + b[:rows] + (a[2 * rows :] + b[rows:] + c))
 
 
 def smooth(image, jac_ref):
-    rows = image.shape[0]
-    out = []
-    for m in range(jac_ref.shape[1]):
-        pieces = jnp.concatenate(split(image[:, m * BS : (m + 1) * BS], 3), axis=0).astype(bf16)
-        a = dot(pieces, jac_ref[0, m])
-        b = dot(pieces[: 2 * rows], jac_ref[1, m])
-        c = dot(pieces[:rows], jac_ref[2, m])
-        out.append(a[:rows] + (a[rows : 2 * rows] + b[:rows] + (a[2 * rows :] + b[rows:] + c)))
-    return jnp.concatenate(out, axis=1)
-
-
-def first_kernel(own_ref, left_ref, right_ref, extra_ref, *refs):
-    kernel, (jac_ref, image_ref, next_ref) = refs[:4], refs[4:]
-    count = own_ref.shape[0] - SYS
-    coarse = image_ref.shape[0] - count
-
-    def basis(ref):
-        z = one_hot(ref[FEAT + 1 : FEAT + 2, :], coarse)
-        return jnp.concatenate([ref[SYS:, :], z], axis=0)
-
+    return jnp.concatenate(
+        [
+            smooth_pieces(image[:, m * BS : (m + 1) * BS], [jac_ref[i, m] for i in range(3)])
+            for m in range(REACH)
+        ],
+        axis=1,
+    )
+
+
+def basis(pack_ref, coarse):
+    z = one_hot(pack_ref[FEAT + 1 : FEAT + 2, :], coarse)
+    return jnp.concatenate([pack_ref[SYS:, :], z], axis=0)
+
+
+def build_own_kernel(own_ref, extra_ref, hi_ref, lo_ref, sim_ref, part_ref):
+    build_kernel(
+        own_ref, own_ref, extra_ref, hi_ref, lo_ref, sim_ref, places=own_places, sides=1
+    )
+    coarse = part_ref.shape[0] - (own_ref.shape[0] - SYS)
     noise = extra_ref[TASKS : TASKS + 1, :]
-    image = operate(basis(own_ref), basis(left_ref), basis(right_ref), noise, *kernel)
+    part_ref[...] = operate_own(basis(own_ref, coarse), noise, hi_ref, lo_ref)
+
+
+def first_kernel(part_ref, left_ref, right_ref, hi_ref, lo_ref, jac_ref, image_ref, next_ref):
+    coarse = part_ref.shape[0] - (left_ref.shape[0] - SYS)
+    ends = [basis(ref, coarse) for ref in (left_ref, right_ref)]
+    image = part_ref[...] + operate_halo(*ends, hi_ref, lo_ref)
     image_ref[...] = image
     next_ref[...] = smooth(image, jac_ref)
 
 
-def second_kernel(extra_ref, vec_ref, left_ref, right_ref, early_ref, sys_ref, *refs):
-    kernel, (jac_ref, image_ref, cargo_ref) = refs[:4], refs[4:]
-    rows = vec_ref.shape[0]
-    noise = extra_ref[TASKS : TASKS + 1, :]
-    image = operate(vec_ref[...], left_ref[...], right_ref[...], noise, *kernel)
+def second_kernel(
+    part_ref, left_ref, right_ref, sys_ref, hi_ref, lo_ref, jac_ref, image_ref, cargo_ref
+):
+    rows = part_ref.shape[0]
+    image = part_ref[...] + operate_halo(left_ref[...], right_ref[...], hi_ref, lo_ref)
     image_ref[...] = image
     cargo_ref[0:rows, :] = smooth(image, jac_ref)
     cargo_ref[rows:, :] = sys_ref[...]
@@ -481,7 +495,10 @@
     return low, high
 
 
-def early_moments_kernel(own_ref, sys_ref, d1_ref, v0_ref, out_ref):
+def early_moments_kernel(
+    own_ref, sys_ref, d1_ref, v0_ref, extra_ref, hi_ref, lo_ref, out_ref, part_ref
+):
+    part_ref[...] = operate_own(d1_ref[...], extra_ref[TASKS : TASKS + 1, :], hi_ref, lo_ref)
     count = own_ref.shape[0] - SYS
     coarse = d1_ref.shape[0] - count
     lanes = out_ref.shape[1]
@@ -500,9 +517,12 @@
     out_ref[count:, :] = spread_out({0: fold, 3: start}, lanes)
 
 
-def late_moments_kernel(before_ref, d1_ref, cargo_ref, v1_ref, out_ref, *, count):
+def late_moments_kernel(
+    before_ref, d1_ref, cargo_ref, v1_ref, extra_ref, hi_ref, lo_ref, out_ref, part_ref, *, count
+):
     lanes = out_ref.shape[1]
     d1, d2, v1 = d1_ref[...], cargo_ref[0 : d1_ref.shape[0], :], v1_ref[...]
+    part_ref[...] = operate_own(d2, extra_ref[TASKS : TASKS + 1, :], hi_ref, lo_ref)
     coarse = d1.shape[0] - count
     m2 = moment(d1[count:], v1, d1[:count] * v1[:count])
     m3 = moment(d2[count:], v1, d2[:count] * v1[:count])
@@ -512,17 +532,15 @@
 
 
 def third_kernel(
-    extra_ref, before_ref, cargo_ref, left_ref, *refs, count, held
+    extra_ref, before_ref, cargo_ref, left_ref, part_ref, hi_ref, lo_ref, out_ref, *, count, held
 ):
-    kernel, out_ref = refs[:4], refs[4]
     rows = cargo_ref.shape[0] - count
     coarse = rows - count
     lanes = out_ref.shape[2]
     pitch = pitch_of(coarse)
     d2 = cargo_ref[0:rows, :]
-    noise = extra_ref[TASKS : TASKS + 1, :]
-    inner = operate_own(d2, noise, *kernel[:2])
-    cross = operate_left(left_ref[0:rows, :], *kernel[2:])
+    inner = part_ref[...]
+    cross = operate_left(left_ref[0:rows, :], hi_ref, lo_ref)
     m4 = moment(d2[count:], inner + cross, d2[:count] * (inner + 2.0 * cross)[:count])
     mirror = dot(d2, cross[count:], NT, lax.Precision.HIGH)
     m4 = m4 + jnp.concatenate([mirror, jnp.zeros((rows, 1), f32)], axis=1)
@@ -631,19 +649,18 @@
     span = q0.shape[1]
     step = -(-coarse // FEAT) * FEAT
     deep = -(-3 * step // LANES) * LANES
-    parts, basis = [], []
+    parts, planes = [], []
     for i, rest in enumerate((z, d1[count:], d2[count:])):
         parts.append(answer[:, i * pitch : i * pitch + coarse])
-        basis.append(rest)
+        planes.append(rest)
         if step > coarse:
             parts.append(jnp.zeros((count, step - coarse), f32))
-            basis.append(jnp.zeros((step - coarse, span), f32))
+            planes.append(jnp.zeros((step - coarse, span), f32))
     if deep > 3 * step:
         parts.append(jnp.zeros((count, deep - 3 * step), f32))
-        basis.append(jnp.zeros((deep - 3 * step, span), f32))
-    x = dot(
-        jnp.concatenate(parts, axis=1), jnp.concatenate(basis, axis=0), precision=highest
-    )
+        planes.append(jnp.zeros((deep - 3 * step, span), f32))
+    planes = [plane.astype(bf16) for plane in split(jnp.concatenate(planes, axis=0), 3)]
+    x = smooth_pieces(jnp.concatenate(parts, axis=1), planes)
     x = x + scalars(answer, 0) * q0 + scalars(answer, 1) * d1[:count]
     x = x + scalars(answer, 2) * d2[:count]
     mine = slice(width, 2 * width)
@@ -804,54 +821,62 @@
     )
     pack_l, pack_r = both_sides(pack)
 
-    def build(places, deep, cells, name):
-        return call(
-            functools.partial(build_kernel, places=places, sides=len(cells)),
-            [
-                shape(blocks, deep, BS, kind=bf16),
-                shape(blocks, deep, BS, kind=bf16),
-                shape(blocks, deep, BS),
-            ],
-            cells + [pack, extra],
-            name,
-            flops=10**9,
-        )
-
-    own_hi, own_lo, own_sim = build(own_places, width, [pack], "build_own")
-    halo_hi, halo_lo, halo_sim = build(
-        halo_places, BAND - width, [pack_l, pack_r], "build_halo"
-    )
-    kernel = [own_hi, own_lo, halo_hi, halo_lo]
+    def cells_of(deep):
+        return [
+            shape(blocks, deep, BS, kind=bf16),
+            shape(blocks, deep, BS, kind=bf16),
+            shape(blocks, deep, BS),
+        ]
+
+    own_hi, own_lo, own_sim, part = call(
+        build_own_kernel,
+        cells_of(width) + [shape(rows, width)],
+        [pack, extra],
+        "build_own",
+        flops=10**9,
+    )
+    halo_hi, halo_lo, halo_sim = call(
+        functools.partial(build_kernel, places=halo_places, sides=2),
+        cells_of(BAND - width),
+        [pack_l, pack_r, pack, extra],
+        "build_halo",
+        flops=10**9,
+    )
+    own, halo = [own_hi, own_lo], [halo_hi, halo_lo]
     v0, d1 = call(
         first_kernel,
         [shape(rows, width), shape(rows, width)],
-        [pack, pack_l, pack_r, extra] + kernel + [jac],
+        [part, pack_l, pack_r] + halo + [jac],
         "first",
         flops=10**9,
     )
     d1_l, d1_r = both_sides(d1)
-    (early,) = call(
-        early_moments_kernel, [shape(rows, lanes)], [pack, systems, d1, v0], "early", flops=10**9
+    early, part = call(
+        early_moments_kernel,
+        [shape(rows, lanes), shape(rows, width)],
+        [pack, systems, d1, v0, extra] + own,
+        "early",
+        flops=10**9,
     )
     v1, cargo = call(
         second_kernel,
         [shape(rows, width), shape(rows + count, width)],
-        [extra, d1, d1_l, d1_r, early, systems] + kernel + [jac],
+        [part, d1_l, d1_r, systems] + halo + [jac],
         "second",
         flops=10**9,
     )
     cargo_l = from_left(cargo)
-    (late,) = call(
+    late, part = call(
         functools.partial(late_moments_kernel, count=count),
-        [shape(rows, lanes)],
-        [early, d1, cargo, v1],
+        [shape(rows, lanes), shape(rows, width)],
+        [early, d1, cargo, v1, extra] + own,
         "late",
         flops=10**9,
     )
     (gram,) = call(
         functools.partial(third_kernel, count=count, held=coarse_inverse.shape[0]),
         [shape(ranks, rows, lanes)],
-        [extra, late, cargo, cargo_l] + kernel,
+        [extra, late, cargo, cargo_l, part] + halo,
         "third",
         flops=10**9,
     )

time: 77 us -> 75.9 us (0.986)
  waiting for transfers between devices: 9.23 us -> 8.12 us
  transfers between devices with their start and end apart: 5 -> 5, of which waited for: 4 -> 4; matrix products, arithmetic and copies ran while one was open for 0% -> 0% of each run, Pallas kernels for 2% -> 4%
where the time goes in v15:
time: 75.9 us; the launch traced here: 75.5 us
  Pallas kernels  25.8 us (34%)
  blocking collectives  23.1 us (30%)
  starting transfers between devices  17.7 us (23%)
  waiting for transfers between devices  8.12 us (11%)
  between operations  0.76 us (1%)
    pallas_call x10, Pallas kernels, call(): pl.pallas_call(body, out_shape=outs, in_specs=[sm] * smem + [vm] * (len(a...  25.8 us
    all_to_all x1, blocking collectives, shards(): gram = lax.all_to_all(gram, 'pts', 0, 0, tiled=True)  13.7 us
    ppermute x4, starting transfers between devices, both_sides(): return (lax.ppermute(cells, 'pts', up), lax.ppermute(cells, 'pts', down))  13.3 us
    all_to_all x1, blocking collectives, shards(): grads = lax.all_to_all(grads, ('pts', 'probe'), 0, 0, tiled=True)  9.47 us
    ppermute x4, waiting for transfers between devices, both_sides(): return (lax.ppermute(cells, 'pts', up), lax.ppermute(cells, 'pts', down))  5.11 us
    ppermute x1, starting transfers between devices, from_left(): return lax.ppermute(cells, 'pts', [(i, i + 1) for i in range(count - 1)])  4.4 us
    ppermute x1, waiting for transfers between devices, from_left(): return lax.ppermute(cells, 'pts', [(i, i + 1) for i in range(count - 1)])  3.01 us
  transfers between devices with their start and end apart: 5, of which 4 were waited for; matrix products, arithmetic and copies ran while one was open for 0% of the time, Pallas kernels for 4%

profile of v15, /device:TPU:0, one launch (start us, length us, event | category | flops | bytes accessed | tf_op | source)
XLA Modules:
  0.0 75.5 jit_solution(17692164188562561272)
XLA Ops:
  0.6 12.0 %invert.1 = (bf16[3,3,256,256]{3,2,1,0:T(8,128)(2,1)S(1)}, f32[32,768]{1,0:T(8,128)S(1)}, f32[24,768]{1,0:T(8,128)S(1)}) custom-call(s32[1]{0:T(128)} %bitcast.place_ref, s32[1]{0:T(128)} %bitcast.1.probe_ref, f32[8,768]{1,0:T(8,128)} %feat_hbm.1, s32[768]{0:T(1024)} %ids_hbm.1, s32[768]{0:T(1024)} %agg_hbm.1, f32[16,768]{1,0:T(8,128)} %sys_ref.3, ...), custom_call_target="tpu_custom_call" | custom-call | flops 10000000000 | bytes 1048576 | tf_op jit(solution)/shard_map/invert/pallas_call | solution.py:759
  12.7 1.3 %collective-permute-start.1 = (f32[32,768]{1,0:T(8,128)S(1)}, f32[32,768]{1,0:T(8,128)S(1)}, u32[]{:S(2)}, u32[]{:S(2)}) collective-permute-start(f32[32,768]{1,0:T(8,128)S(1)} %get-tuple-element.26.own_ref.refs_2_), channel_id=1, source_target_pairs={{2,0},{4,2},{6,4},{8,6},{10,8},{12,10},{14,12},{3,1},{5,3},{7,5},{... | collective-permute-start | bytes 294920 | tf_op jit(solution)/shard_map/ppermute | solution.py:775
  14.0 5.7 %collective-permute-start = (f32[32,768]{1,0:T(8,128)S(1)}, f32[32,768]{1,0:T(8,128)S(1)}, u32[]{:S(2)}, u32[]{:S(2)}) collective-permute-start(f32[32,768]{1,0:T(8,128)S(1)} %get-tuple-element.26.own_ref.refs_2_), channel_id=1, source_target_pairs={{0,2},{2,4},{4,6},{6,8},{8,10},{10,12},{12,14},{1,3},{3,5},{5,7},{... | collective-permute-start | bytes 294920 | tf_op jit(solution)/shard_map/ppermute | solution.py:775
  19.7 1.4 %build_own.1 = (bf16[3,768,256]{2,1,0:T(8,128)(2,1)S(1)}, bf16[3,768,256]{2,1,0:T(8,128)(2,1)S(1)}, f32[3,768,256]{2,1,0:T(8,128)S(1)}, f32[40,768]{1,0:T(8,128)S(1)}) custom-call(f32[32,768]{1,0:T(8,128)S(1)} %get-tuple-element.26.own_ref.refs_2_, f32[24,768]{1,0:T(8,128)S(1)} %get-tuple-element.25.extra_ref.refs_3_), custom_call_target="tpu_custom_call" | custom-call | flops 1000000000 | bytes 1048576 | tf_op jit(solution)/shard_map/build_own/pallas_call | solution.py:759
  21.0 0.0 collective-permute-done.1.refs_1_.right_ref
  21.0 1.6 %collective-permute-done.refs_0_.left_ref = f32[32,768]{1,0:T(8,128)S(1)} collective-permute-done((f32[32,768]{1,0:T(8,128)S(1)}, f32[32,768]{1,0:T(8,128)S(1)}, u32[]{:S(2)}, u32[]{:S(2)}) %collective-permute-start) | collective-permute-done | bytes 98336 | tf_op jit(solution)/shard_map/ppermute | solution.py:775
  22.6 1.4 %build_halo.1 = (bf16[3,1024,256]{2,1,0:T(8,128)(2,1)S(1)}, bf16[3,1024,256]{2,1,0:T(8,128)(2,1)S(1)}, f32[3,1024,256]{2,1,0:T(8,128)S(1)}) custom-call(f32[32,768]{1,0:T(8,128)S(1)} %collective-permute-done.refs_0_.left_ref, f32[32,768]{1,0:T(8,128)S(1)} %collective-permute-done.1.refs_1_.right_ref, f32[32,768]{1,0:T(8,128)S(1)} %get-tuple-element.26.own_ref.refs_2_, ...), custom_call_target="tpu_custom_call" | custom-call | flops 1000000000 | bytes 1048576 | tf_op jit(solution)/shard_map/build_halo/pallas_call | solution.py:759
  24.0 0.0 copy-start
  24.0 0.8 %first.1 = (f32[40,768]{1,0:T(8,128)S(1)}, f32[40,768]{1,0:T(8,128)S(1)}) custom-call(f32[40,768]{1,0:T(8,128)S(1)} %get-tuple-element.27.part_ref, f32[32,768]{1,0:T(8,128)S(1)} %collective-permute-done.refs_0_.left_ref, f32[32,768]{1,0:T(8,128)S(1)} %collective-permute-done.1.refs_1_.right_ref, bf16[3,1024,256]{2,1,0:T(8,128)(2,1)S(1)} %get-tuple-element.28.hi_ref.refs_3_, ...), custom_call_target="tpu_custom_call" | custom-call | flops 1000000000 | bytes 1048576 | tf_op jit(solution)/shard_map/first/pallas_call | solution.py:759
  24.8 1.3 %collective-permute-start.3 = (f32[40,768]{1,0:T(8,128)S(1)}, f32[40,768]{1,0:T(8,128)S(1)}, u32[]{:S(2)}, u32[]{:S(2)}) collective-permute-start(f32[40,768]{1,0:T(8,128)S(1)} %get-tuple-element.31.d1_ref), channel_id=1, source_target_pairs={{2,0},{4,2},{6,4},{8,6},{10,8},{12,10},{14,12},{3,1},{5,3},{7,5},{... | collective-permute-start | bytes 368648 | tf_op jit(solution)/shard_map/ppermute | solution.py:775
  26.1 5.0 %collective-permute-start.2 = (f32[40,768]{1,0:T(8,128)S(1)}, f32[40,768]{1,0:T(8,128)S(1)}, u32[]{:S(2)}, u32[]{:S(2)}) collective-permute-start(f32[40,768]{1,0:T(8,128)S(1)} %get-tuple-element.31.d1_ref), channel_id=1, source_target_pairs={{0,2},{2,4},{4,6},{6,8},{8,10},{10,12},{12,14},{1,3},{3,5},{5,7},{... | collective-permute-start | bytes 368648 | tf_op jit(solution)/shard_map/ppermute | solution.py:775
  31.2 0.0 copy-done
  31.2 0.7 early.1
  31.9 0.8 %collective-permute-done.3.right_ref = f32[40,768]{1,0:T(8,128)S(1)} collective-permute-done((f32[40,768]{1,0:T(8,128)S(1)}, f32[40,768]{1,0:T(8,128)S(1)}, u32[]{:S(2)}, u32[]{:S(2)}) %collective-permute-start.3) | collective-permute-done | bytes 122912 | tf_op jit(solution)/shard_map/ppermute | solution.py:775
  32.7 2.8 %collective-permute-done.2.left_ref.d1l_ref = f32[40,768]{1,0:T(8,128)S(1)} collective-permute-done((f32[40,768]{1,0:T(8,128)S(1)}, f32[40,768]{1,0:T(8,128)S(1)}, u32[]{:S(2)}, u32[]{:S(2)}) %collective-permute-start.2) | collective-permute-done | bytes 122912 | tf_op jit(solution)/shard_map/ppermute | solution.py:775
  35.5 0.8 %second.1 = (f32[40,768]{1,0:T(8,128)S(1)}, f32[56,768]{1,0:T(8,128)S(1)}) custom-call(f32[40,768]{1,0:T(8,128)S(1)} %get-tuple-element.36.part_ref, f32[40,768]{1,0:T(8,128)S(1)} %collective-permute-done.2.left_ref.d1l_ref, f32[40,768]{1,0:T(8,128)S(1)} %collective-permute-done.3.right_ref, f32[16,768]{1,0:T(8,128)S(1)} %copy-done, ...), custom_call_target="tpu_custom_call" | custom-call | flops 1000000000 | bytes 1048576 | tf_op jit(solution)/shard_map/second/pallas_call | solution.py:759
  36.3 4.4 %collective-permute-start.4 = (f32[56,768]{1,0:T(8,128)S(1)}, f32[56,768]{1,0:T(8,128)S(1)}, u32[]{:S(2)}, u32[]{:S(2)}) collective-permute-start(f32[56,768]{1,0:T(8,128)S(1)} %get-tuple-element.37.cargo_ref), channel_id=1, source_target_pairs={{0,2},{2,4},{4,6},{6,8},{8,10},{10,12},{12,14},{1,3},{3,5},{5,7},{... | collective-permute-start | bytes 516104 | tf_op jit(solution)/shard_map/ppermute | solution.py:780
  40.7 0.8 %late.1 = (f32[40,128]{1,0:T(8,128)S(1)}, f32[40,768]{1,0:T(8,128)S(1)}) custom-call(f32[40,128]{1,0:T(8,128)S(1)} %get-tuple-element.35.before_ref, f32[40,768]{1,0:T(8,128)S(1)} %get-tuple-element.31.d1_ref, f32[56,768]{1,0:T(8,128)S(1)} %get-tuple-element.37.cargo_ref, f32[40,768]{1,0:T(8,128)S(1)} %get-tuple-element.38.v1_ref, ...), custom_call_target="tpu_custom_call" | custom-call | flops 1000000000 | bytes 1048576 | tf_op jit(solution)/shard_map/late/pallas_call | solution.py:759
  41.5 3.0 %collective-permute-done.4.left_ref.cargol_ref = f32[56,768]{1,0:T(8,128)S(1)} collective-permute-done((f32[56,768]{1,0:T(8,128)S(1)}, f32[56,768]{1,0:T(8,128)S(1)}, u32[]{:S(2)}, u32[]{:S(2)}) %collective-permute-start.4) | collective-permute-done | bytes 172064 | tf_op jit(solution)/shard_map/ppermute | solution.py:780
  44.5 0.6 third.1
  45.1 13.7 %all_to_all.10.gram_ref = f32[8,40,128]{2,1,0:T(8,128)S(1)} all-to-all(f32[8,40,128]{2,1,0:T(8,128)S(1)} %third.1), channel_id=1, replica_groups=mesh['groups'=2,'pts'=8,'probe'=2] {'pts'}, dimensions={0} | all-to-all | bytes 327680 | tf_op jit(solution)/shard_map/all_to_all | solution.py:883
  58.8 6.6 %final.1 = (f32[16,768]{1,0:T(8,128)}, f32[16,8,128]{2,1,0:T(8,128)S(1)}) custom-call(f32[8,40,128]{2,1,0:T(8,128)S(1)} %all_to_all.10.gram_ref, f32[32,768]{1,0:T(8,128)S(1)} %get-tuple-element.26.own_ref.refs_2_, f32[32,768]{1,0:T(8,128)S(1)} %collective-permute-done.refs_0_.left_ref, f32[40,768]{1,0:T(8,128)S(1)} %get-tuple-element.31.d1_ref, ...), custom_call_target="tpu_custom_call" | custom-call | flops 1000000000 | bytes 1048576 | tf_op jit(solution)/shard_map/final/pallas_call | solution.py:759
  65.4 9.5 %all_to_all.11.parts_ref = f32[16,8,128]{2,1,0:T(8,128)S(1)} all-to-all(f32[16,8,128]{2,1,0:T(8,128)S(1)} %get-tuple-element.44), channel_id=1, replica_groups=mesh['groups'=2,'pts'=8,'probe'=2] {'pts','probe'}, dimensions={0} | all-to-all | bytes 131072 | tf_op jit(solution)/shard_map/all_to_all | solution.py:892
  74.8 0.7 tail.1
Async XLA Ops:
  12.7 8.4 %collective-permute-start.1 = (f32[32,768]{1,0:T(8,128)S(1)}, f32[32,768]{1,0:T(8,128)S(1)}, u32[]{:S(2)}, u32[]{:S(2)}) collective-permute-start(f32[32,768]{1,0:T(8,128)S(1)} %get-tuple-element.26.own_ref.refs_2_), channel_id=1, source_target_pairs={{2,0},{4,2},{6,4},{8,6},{10,8},{12,10},{14,12},{3,1},{5,3},{7,5},{... | collective-permute-start | bytes 294920 | tf_op jit(solution)/shard_map/ppermute | solution.py:775
  14.0 8.6 %collective-permute-start = (f32[32,768]{1,0:T(8,128)S(1)}, f32[32,768]{1,0:T(8,128)S(1)}, u32[]{:S(2)}, u32[]{:S(2)}) collective-permute-start(f32[32,768]{1,0:T(8,128)S(1)} %get-tuple-element.26.own_ref.refs_2_), channel_id=1, source_target_pairs={{0,2},{2,4},{4,6},{6,8},{8,10},{10,12},{12,14},{1,3},{3,5},{5,7},{... | collective-permute-start | bytes 294920 | tf_op jit(solution)/shard_map/ppermute | solution.py:775
  24.0 7.2 %copy-start = (f32[16,768]{1,0:T(8,128)S(1)}, f32[16,768]{1,0:T(8,128)}, u32[]{:S(2)}) copy-start(f32[16,768]{1,0:T(8,128)} %sys_ref.3) | copy-start | bytes 147460
  24.8 7.8 %collective-permute-start.3 = (f32[40,768]{1,0:T(8,128)S(1)}, f32[40,768]{1,0:T(8,128)S(1)}, u32[]{:S(2)}, u32[]{:S(2)}) collective-permute-start(f32[40,768]{1,0:T(8,128)S(1)} %get-tuple-element.31.d1_ref), channel_id=1, source_target_pairs={{2,0},{4,2},{6,4},{8,6},{10,8},{12,10},{14,12},{3,1},{5,3},{7,5},{... | collective-permute-start | bytes 368648 | tf_op jit(solution)/shard_map/ppermute | solution.py:775
  26.1 9.3 %collective-permute-start.2 = (f32[40,768]{1,0:T(8,128)S(1)}, f32[40,768]{1,0:T(8,128)S(1)}, u32[]{:S(2)}, u32[]{:S(2)}) collective-permute-start(f32[40,768]{1,0:T(8,128)S(1)} %get-tuple-element.31.d1_ref), channel_id=1, source_target_pairs={{0,2},{2,4},{4,6},{6,8},{8,10},{10,12},{12,14},{1,3},{3,5},{5,7},{... | collective-permute-start | bytes 368648 | tf_op jit(solution)/shard_map/ppermute | solution.py:775
  36.3 8.2 %collective-permute-start.4 = (f32[56,768]{1,0:T(8,128)S(1)}, f32[56,768]{1,0:T(8,128)S(1)}, u32[]{:S(2)}, u32[]{:S(2)}) collective-permute-start(f32[56,768]{1,0:T(8,128)S(1)} %get-tuple-element.37.cargo_ref), channel_id=1, source_target_pairs={{0,2},{2,4},{4,6},{6,8},{8,10},{10,12},{12,14},{1,3},{3,5},{5,7},{... | collective-permute-start | bytes 516104 | tf_op jit(solution)/shard_map/ppermute | solution.py:780

commit v16 on v15

--- a/solution.py
+++ b/solution.py
@@ -295,10 +295,12 @@
 
         def rows_of(m, low, high):
             def piece():
-                r0, r1, r2 = split(strips[m][:, low:high], 3)
-                p0, p1, p2 = split(state[m], 3)
-                a = jnp.concatenate([r0, r0, r1, r1, r0, r2], axis=0).astype(bf16)
-                b = jnp.concatenate([p0, p1, p0, p1, p2, p0], axis=0).astype(bf16)
+                if (m, 0) not in state:
+                    r0, r1, r2 = (part.astype(bf16) for part in split(strips[m], 3))
+                    p0, p1, p2 = (part.astype(bf16) for part in split(state[m], 3))
+                    state[m, 0] = jnp.concatenate([r0, r0, r1, r1, r0, r2], axis=0)
+                    state[m, 1] = jnp.concatenate([p0, p1, p0, p1, p2, p0], axis=0)
+                a, b = state[m, 0][:, low:high], state[m, 1]
                 gone = (iota((1, BS), 1) >= first) & (iota((1, BS), 1) < first + BASE)
                 work[m, low:high, :] = jnp.where(gone, 0.0, work[m, low:high, :]) - dot(a, b, TN)
                 if low <= first < high:
@@ -443,14 +445,10 @@
     next_ref[...] = smooth(image, jac_ref)
 
 
-def second_kernel(
-    part_ref, left_ref, right_ref, sys_ref, hi_ref, lo_ref, jac_ref, image_ref, cargo_ref
-):
-    rows = part_ref.shape[0]
+def second_kernel(part_ref, left_ref, right_ref, hi_ref, lo_ref, jac_ref, image_ref, next_ref):
     image = part_ref[...] + operate_halo(left_ref[...], right_ref[...], hi_ref, lo_ref)
     image_ref[...] = image
-    cargo_ref[0:rows, :] = smooth(image, jac_ref)
-    cargo_ref[rows:, :] = sys_ref[...]
+    next_ref[...] = smooth(image, jac_ref)
 
 
 def pitch_of(coarse):
@@ -518,10 +516,13 @@
 
 
 def late_moments_kernel(
-    before_ref, d1_ref, cargo_ref, v1_ref, extra_ref, hi_ref, lo_ref, out_ref, part_ref, *, count
+    before_ref, d1_ref, d2_ref, v1_ref, sys_ref, extra_ref, hi_ref, lo_ref, out_ref, part_ref,
+    cargo_ref,
 ):
+    cargo_ref[...] = sys_ref[...]
+    count = sys_ref.shape[0]
     lanes = out_ref.shape[1]
-    d1, d2, v1 = d1_ref[...], cargo_ref[0 : d1_ref.shape[0], :], v1_ref[...]
+    d1, d2, v1 = d1_ref[...], d2_ref[...], v1_ref[...]
     part_ref[...] = operate_own(d2, extra_ref[TASKS : TASKS + 1, :], hi_ref, lo_ref)
     coarse = d1.shape[0] - count
     m2 = moment(d1[count:], v1, d1[:count] * v1[:count])
@@ -532,15 +533,15 @@
 
 
 def third_kernel(
-    extra_ref, before_ref, cargo_ref, left_ref, part_ref, hi_ref, lo_ref, out_ref, *, count, held
+    extra_ref, before_ref, vec_ref, left_ref, part_ref, hi_ref, lo_ref, out_ref, *, count, held
 ):
-    rows = cargo_ref.shape[0] - count
-    coarse = rows - count
+    coarse = vec_ref.shape[0] - count
     lanes = out_ref.shape[2]
     pitch = pitch_of(coarse)
-    d2 = cargo_ref[0:rows, :]
+    d2 = vec_ref[...]
+    rows = d2.shape[0]
     inner = part_ref[...]
-    cross = operate_left(left_ref[0:rows, :], hi_ref, lo_ref)
+    cross = operate_left(left_ref[...], hi_ref, lo_ref)
     m4 = moment(d2[count:], inner + cross, d2[:count] * (inner + 2.0 * cross)[:count])
     mirror = dot(d2, cross[count:], NT, lax.Precision.HIGH)
     m4 = m4 + jnp.concatenate([mirror, jnp.zeros((rows, 1), f32)], axis=1)
@@ -558,7 +559,8 @@
 
 
 def final_kernel(
-    gram_ref, own_ref, left_ref, d1_ref, d1l_ref, cargo_ref, cargol_ref, *refs, sides, points,
+    gram_ref, own_ref, left_ref, d1_ref, d1l_ref, d2_ref, d2l_ref, sys_ref, sysl_ref, *refs,
+    sides, points,
 ):
     kernel_refs, (sol_ref, grad_ref) = refs[:6], refs[6:]
     width = own_ref.shape[1]
@@ -644,8 +646,7 @@
     z = one_hot(pack[FEAT + 1 : FEAT + 2], coarse)
     q0 = pack[SYS:]
     d1 = jnp.concatenate([d1l_ref[...], d1_ref[...]], axis=1)
-    cargo = jnp.concatenate([cargol_ref[...], cargo_ref[...]], axis=1)
-    d2 = cargo[:rows]
+    d2 = jnp.concatenate([d2l_ref[...], d2_ref[...]], axis=1)
     span = q0.shape[1]
     step = -(-coarse // FEAT) * FEAT
     deep = -(-3 * step // LANES) * LANES
@@ -668,7 +669,8 @@
 
     probe = own_ref[FEAT + 2 : FEAT + 3, 0:1]
     line = iota((count, 1), 0).astype(f32) + probe * count
-    right = jnp.where(line == 0, x, cargo[rows:])
+    systems = jnp.concatenate([sysl_ref[...], sys_ref[...]], axis=1)
+    right = jnp.where(line == 0, x, systems)
     coef = jnp.where(line == 0, 0.5 / points, -0.5 / (sides - 1) / points)
     r0, r1 = split(right, 2)
     w0, w1 = split(x * coef, 2)
@@ -858,25 +860,26 @@
         "early",
         flops=10**9,
     )
-    v1, cargo = call(
+    v1, d2 = call(
         second_kernel,
-        [shape(rows, width), shape(rows + count, width)],
-        [part, d1_l, d1_r, systems] + halo + [jac],
+        [shape(rows, width), shape(rows, width)],
+        [part, d1_l, d1_r] + halo + [jac],
         "second",
         flops=10**9,
     )
-    cargo_l = from_left(cargo)
-    late, part = call(
-        functools.partial(late_moments_kernel, count=count),
-        [shape(rows, lanes), shape(rows, width)],
-        [early, d1, cargo, v1, extra] + own,
+    d2_l = from_left(d2)
+    late, part, cargo = call(
+        late_moments_kernel,
+        [shape(rows, lanes), shape(rows, width), shape(count, width)],
+        [early, d1, d2, v1, systems, extra] + own,
         "late",
         flops=10**9,
     )
+    cargo_l = from_left(cargo)
     (gram,) = call(
         functools.partial(third_kernel, count=count, held=coarse_inverse.shape[0]),
         [shape(ranks, rows, lanes)],
-        [extra, late, cargo, cargo_l, part] + halo,
+        [extra, late, d2, d2_l, part] + halo,
         "third",
         flops=10**9,
     )
@@ -885,7 +888,7 @@
     answer, grads = call(
         functools.partial(final_kernel, sides=sides * count, points=ranks * width),
         [shape(count, width), shape(ranks * sides, FEAT, LANES)],
-        [gram, pack, pack_l, d1, d1_l, cargo, cargo_l] + cells,
+        [gram, pack, pack_l, d1, d1_l, d2, d2_l, cargo, cargo_l] + cells,
         "final",
         flops=10**9,
     )

time: 75.9 us -> 93 us (1.23)
  local copies, waits for them, and re-layouts: 0.01 us -> 15.6 us
  starting transfers between devices: 17.7 us -> 29 us
  blocking collectives: 23.1 us -> 12 us
    unnamed x2 -> x42, local copies, waits for them, and re-layouts: 0.01 us -> 15.6 us
    all_to_all x1 -> x0, blocking collectives: 13.7 us -> none  [shards(): gram = lax.all_to_all(gram, 'pts', 0, 0, tiled=True)]
    all_to_all x0 -> x1, starting transfers between devices: none -> 7.08 us  [shards(): gram = lax.all_to_all(gram, 'pts', 0, 0, tiled=True)]
    ppermute x1 -> x2, starting transfers between devices: 4.4 us -> 8.31 us  [from_left(): return lax.ppermute(cells, 'pts', [(i, i + 1) for i in range(count - 1)])]
    all_to_all x1, blocking collectives: 9.47 us -> 12 us  [shards(): grads = lax.all_to_all(grads, ('pts', 'probe'), 0, 0, tiled=True)]
    ppermute x4, waiting for transfers between devices: 5.11 us -> 3.33 us  [both_sides(): return (lax.ppermute(cells, 'pts', up), lax.ppermute(cells, 'pts', down))]
    all_to_all x0 -> x1, waiting for transfers between devices: none -> 0.98 us  [shards(): gram = lax.all_to_all(gram, 'pts', 0, 0, tiled=True)]
    ppermute x1 -> x2, waiting for transfers between devices: 3.01 us -> 3.94 us  [from_left(): return lax.ppermute(cells, 'pts', [(i, i + 1) for i in range(count - 1)])]
  transfers between devices with their start and end apart: 5 -> 7, of which waited for: 4 -> 6; matrix products, arithmetic and copies ran while one was open for 0% -> 0% of each run, Pallas kernels for 4% -> 3%
where the time goes in v16:
time: 93 us; the launch traced here: 92.2 us
  starting transfers between devices  29 us (31%)
  Pallas kernels  26.4 us (28%)
  local copies, waits for them, and re-layouts  15.6 us (17%)
  blocking collectives  12 us (13%)
  waiting for transfers between devices  8.26 us (9%)
    pallas_call x10, Pallas kernels, call(): pl.pallas_call(body, out_shape=outs, in_specs=[sm] * smem + [vm] * (len(a...  26.4 us
    unnamed x42, local copies, waits for them, and re-layouts  15.6 us
    ppermute x4, starting transfers between devices, both_sides(): return (lax.ppermute(cells, 'pts', up), lax.ppermute(cells, 'pts', down))  13.6 us
    all_to_all x1, blocking collectives, shards(): grads = lax.all_to_all(grads, ('pts', 'probe'), 0, 0, tiled=True)  12 us
    ppermute x2, starting transfers between devices, from_left(): return lax.ppermute(cells, 'pts', [(i, i + 1) for i in range(count - 1)])  8.31 us
    all_to_all x1, starting transfers between devices, shards(): gram = lax.all_to_all(gram, 'pts', 0, 0, tiled=True)  7.08 us
    ppermute x2, waiting for transfers between devices, from_left(): return lax.ppermute(cells, 'pts', [(i, i + 1) for i in range(count - 1)])  3.94 us
    ppermute x4, waiting for transfers between devices, both_sides(): return (lax.ppermute(cells, 'pts', up), lax.ppermute(cells, 'pts', down))  3.33 us
  transfers between devices with their start and end apart: 7, of which 6 were waited for; matrix products, arithmetic and copies ran while one was open for 0% of the time, Pallas kernels for 3%

profile of v16, /device:TPU:0, one launch (start us, length us, event | category | flops | bytes accessed | tf_op | source)
XLA Modules:
  0.0 92.2 jit_solution(7691259292619197402)
XLA Ops:
  0.6 12.0 %invert.1 = (bf16[3,3,256,256]{3,2,1,0:T(8,128)(2,1)S(1)}, f32[32,768]{1,0:T(8,128)S(1)}, f32[24,768]{1,0:T(8,128)S(1)}) custom-call(s32[1]{0:T(128)} %bitcast.place_ref, s32[1]{0:T(128)} %bitcast.1.probe_ref, f32[8,768]{1,0:T(8,128)} %feat_hbm.1, s32[768]{0:T(1024)} %ids_hbm.1, s32[768]{0:T(1024)} %agg_hbm.1, f32[16,768]{1,0:T(8,128)} %sys_ref.3, ...), custom_call_target="tpu_custom_call" | custom-call | flops 10000000000 | bytes 1048576 | tf_op jit(solution)/shard_map/invert/pallas_call | solution.py:761
  12.7 1.3 %collective-permute-start.1 = (f32[32,768]{1,0:T(8,128)S(1)}, f32[32,768]{1,0:T(8,128)S(1)}, u32[]{:S(2)}, u32[]{:S(2)}) collective-permute-start(f32[32,768]{1,0:T(8,128)S(1)} %get-tuple-element.27.own_ref.refs_2_), channel_id=1, source_target_pairs={{2,0},{4,2},{6,4},{8,6},{10,8},{12,10},{14,12},{3,1},{5,3},{7,5},{... | collective-permute-start | bytes 294920 | tf_op jit(solution)/shard_map/ppermute | solution.py:777
  14.0 5.7 %collective-permute-start = (f32[32,768]{1,0:T(8,128)S(1)}, f32[32,768]{1,0:T(8,128)S(1)}, u32[]{:S(2)}, u32[]{:S(2)}) collective-permute-start(f32[32,768]{1,0:T(8,128)S(1)} %get-tuple-element.27.own_ref.refs_2_), channel_id=1, source_target_pairs={{0,2},{2,4},{4,6},{6,8},{8,10},{10,12},{12,14},{1,3},{3,5},{5,7},{... | collective-permute-start | bytes 294920 | tf_op jit(solution)/shard_map/ppermute | solution.py:777
  19.7 1.4 %build_own.1 = (bf16[3,768,256]{2,1,0:T(8,128)(2,1)S(1)}, bf16[3,768,256]{2,1,0:T(8,128)(2,1)S(1)}, f32[3,768,256]{2,1,0:T(8,128)S(1)}, f32[40,768]{1,0:T(8,128)S(1)}) custom-call(f32[32,768]{1,0:T(8,128)S(1)} %get-tuple-element.27.own_ref.refs_2_, f32[24,768]{1,0:T(8,128)S(1)} %get-tuple-element.26.extra_ref.refs_3_), custom_call_target="tpu_custom_call" | custom-call | flops 1000000000 | bytes 1048576 | tf_op jit(solution)/shard_map/build_own/pallas_call | solution.py:761
  21.1 1.4 %copy-done.2 = f32[3,768,256]{2,1,0:T(8,128)} copy-done((f32[3,768,256]{2,1,0:T(8,128)}, f32[3,768,256]{2,1,0:T(8,128)S(1)}, u32[]{:S(2)}) %copy-start.2) | copy-done | bytes 2359320
  22.6 1.4 %build_halo.1 = (bf16[3,1024,256]{2,1,0:T(8,128)(2,1)S(1)}, bf16[3,1024,256]{2,1,0:T(8,128)(2,1)S(1)}, f32[3,1024,256]{2,1,0:T(8,128)S(1)}) custom-call(f32[32,768]{1,0:T(8,128)S(1)} %collective-permute-done.refs_0_.left_ref, f32[32,768]{1,0:T(8,128)S(1)} %collective-permute-done.1.refs_1_.right_ref, f32[32,768]{1,0:T(8,128)S(1)} %get-tuple-element.27.own_ref.refs_2_, ...), custom_call_target="tpu_custom_call" | custom-call | flops 1000000000 | bytes 1048576 | tf_op jit(solution)/shard_map/build_halo/pallas_call | solution.py:761
  24.0 1.6 %copy-done = f32[3,1024,256]{2,1,0:T(8,128)} copy-done((f32[3,1024,256]{2,1,0:T(8,128)}, f32[3,1024,256]{2,1,0:T(8,128)S(1)}, u32[]{:S(2)}) %copy-start) | copy-done | bytes 3145752
  25.6 0.8 first.1
  26.5 1.3 %collective-permute-start.3 = (f32[40,768]{1,0:T(8,128)S(1)}, f32[40,768]{1,0:T(8,128)S(1)}, u32[]{:S(2)}, u32[]{:S(2)}) collective-permute-start(f32[40,768]{1,0:T(8,128)S(1)} %get-tuple-element.32.d1_ref), channel_id=1, source_target_pairs={{2,0},{4,2},{6,4},{8,6},{10,8},{12,10},{14,12},{3,1},{5,3},{7,5},{... | collective-permute-start | bytes 368648 | tf_op jit(solution)/shard_map/ppermute | solution.py:777
  27.8 5.4 %collective-permute-start.2 = (f32[40,768]{1,0:T(8,128)S(1)}, f32[40,768]{1,0:T(8,128)S(1)}, u32[]{:S(2)}, u32[]{:S(2)}) collective-permute-start(f32[40,768]{1,0:T(8,128)S(1)} %get-tuple-element.32.d1_ref), channel_id=1, source_target_pairs={{0,2},{2,4},{4,6},{6,8},{8,10},{10,12},{12,14},{1,3},{3,5},{5,7},{... | collective-permute-start | bytes 368648 | tf_op jit(solution)/shard_map/ppermute | solution.py:777
  34.3 2.8 %collective-permute-done.2.left_ref.d1l_ref = f32[40,768]{1,0:T(8,128)S(1)} collective-permute-done((f32[40,768]{1,0:T(8,128)S(1)}, f32[40,768]{1,0:T(8,128)S(1)}, u32[]{:S(2)}, u32[]{:S(2)}) %collective-permute-start.2) | collective-permute-done | bytes 122912 | tf_op jit(solution)/shard_map/ppermute | solution.py:777
  37.1 0.8 second.1
  37.9 4.4 %collective-permute-start.4 = (f32[40,768]{1,0:T(8,128)S(1)}, f32[40,768]{1,0:T(8,128)S(1)}, u32[]{:S(2)}, u32[]{:S(2)}) collective-permute-start(f32[40,768]{1,0:T(8,128)S(1)} %get-tuple-element.38.d2_ref.vec_ref), channel_id=1, source_target_pairs={{0,2},{2,4},{4,6},{6,8},{8,10},{10,12},{12,14},{1,3},{3,5},{5,7},{... | collective-permute-start | bytes 368648 | tf_op jit(solution)/shard_map/ppermute | solution.py:782
  42.4 0.8 late.1
  43.2 1.9 %collective-permute-done.4.left_ref.d2l_ref = f32[40,768]{1,0:T(8,128)S(1)} collective-permute-done((f32[40,768]{1,0:T(8,128)S(1)}, f32[40,768]{1,0:T(8,128)S(1)}, u32[]{:S(2)}, u32[]{:S(2)}) %collective-permute-start.4) | collective-permute-done | bytes 122912 | tf_op jit(solution)/shard_map/ppermute | solution.py:782
  45.1 1.3 %third.1 = f32[8,40,128]{2,1,0:T(8,128)} custom-call(f32[24,768]{1,0:T(8,128)S(1)} %get-tuple-element.26.extra_ref.refs_3_, f32[40,128]{1,0:T(8,128)S(1)} %get-tuple-element.40.before_ref, f32[40,768]{1,0:T(8,128)S(1)} %get-tuple-element.38.d2_ref.vec_ref, f32[40,768]{1,0:T(8,128)S(1)} %collective-permute-done.4.left_ref.d2l_ref, ...), custom_call_target="tpu_custom_call" | custom-call | flops 1000000000 | bytes 1048576 | tf_op jit(solution)/shard_map/third/pallas_call | solution.py:761
  47.0 7.1 %all-to-all-start = ((f32[8,40,128]{2,1,0:T(8,128)}), f32[8,40,128]{2,1,0:T(8,128)S(1)}, u32[]{:S(2)}, u32[]{:S(2)}) async-start(f32[8,40,128]{2,1,0:T(8,128)} %third.1), calls=%async_computation | async-start | bytes 327680 | tf_op jit(solution)/shard_map/all_to_all | solution.py:886
  54.1 3.9 %collective-permute-start.5 = (f32[16,768]{1,0:T(8,128)}, f32[16,768]{1,0:T(8,128)S(1)}, u32[]{:S(2)}, u32[]{:S(2)}) collective-permute-start(f32[16,768]{1,0:T(8,128)} %copy-done.16), channel_id=1, source_target_pairs={{0,2},{2,4},{4,6},{6,8},{8,10},{10,12},{12,14},{1,3},{3,5},{5,7},{... | collective-permute-start | bytes 147464 | tf_op jit(solution)/shard_map/ppermute | solution.py:782
  58.0 2.0 %collective-permute-done.5.sysl_ref = f32[16,768]{1,0:T(8,128)S(1)} collective-permute-done((f32[16,768]{1,0:T(8,128)}, f32[16,768]{1,0:T(8,128)S(1)}, u32[]{:S(2)}, u32[]{:S(2)}) %collective-permute-start.5) | collective-permute-done | bytes 49184 | tf_op jit(solution)/shard_map/ppermute | solution.py:782
  60.7 1.0 %all-to-all-done.gram_ref = f32[8,40,128]{2,1,0:T(8,128)S(1)} async-done(((f32[8,40,128]{2,1,0:T(8,128)}), f32[8,40,128]{2,1,0:T(8,128)S(1)}, u32[]{:S(2)}, u32[]{:S(2)}) %all-to-all-start) | async-done | bytes 163872 | tf_op jit(solution)/shard_map/all_to_all | solution.py:886
  61.6 1.9 %copy-done.1 = f32[3,1024,256]{2,1,0:T(8,128)S(1)} copy-done((f32[3,1024,256]{2,1,0:T(8,128)S(1)}, f32[3,1024,256]{2,1,0:T(8,128)}, u32[]{:S(2)}) %copy-start.1) | copy-done | bytes 3145752
  63.5 1.7 %copy-done.3 = f32[3,768,256]{2,1,0:T(8,128)S(1)} copy-done((f32[3,768,256]{2,1,0:T(8,128)S(1)}, f32[3,768,256]{2,1,0:T(8,128)}, u32[]{:S(2)}) %copy-start.3) | copy-done | bytes 2359320
  65.2 1.3 %copy-done.5 = bf16[3,768,256]{2,1,0:T(8,128)(2,1)S(1)} copy-done((bf16[3,768,256]{2,1,0:T(8,128)(2,1)S(1)}, bf16[3,768,256]{2,1,0:T(8,128)(2,1)}, u32[]{:S(2)}) %copy-start.5) | copy-done | bytes 1179672
  66.5 1.3 %copy-done.7 = bf16[3,768,256]{2,1,0:T(8,128)(2,1)S(1)} copy-done((bf16[3,768,256]{2,1,0:T(8,128)(2,1)S(1)}, bf16[3,768,256]{2,1,0:T(8,128)(2,1)}, u32[]{:S(2)}) %copy-start.7) | copy-done | bytes 1179672
  67.7 0.9 copy-done.9
  68.6 0.9 copy-done.11
  69.5 0.9 copy-done.13
  70.4 0.9 copy-done.15
  71.3 0.8 copy-done.17
  72.1 0.8 copy-done.19
  72.9 6.5 %final.1 = (f32[16,768]{1,0:T(8,128)}, f32[16,8,128]{2,1,0:T(8,128)S(1)}) custom-call(f32[8,40,128]{2,1,0:T(8,128)S(1)} %all-to-all-done.gram_ref, f32[32,768]{1,0:T(8,128)S(1)} %copy-done.15, f32[32,768]{1,0:T(8,128)S(1)} %copy-done.11, f32[40,768]{1,0:T(8,128)S(1)} %copy-done.13, f32[40,768]{1,0:T(8,128)S(1)} %collective-permute-done.2.left_ref.d1l_ref, ...), custom_call_target="tpu_custom_call" | custom-call | flops 1000000000 | bytes 1048576 | tf_op jit(solution)/shard_map/final/pallas_call | solution.py:761
  79.5 12.0 %all_to_all.10.parts_ref = f32[16,8,128]{2,1,0:T(8,128)S(1)} all-to-all(f32[16,8,128]{2,1,0:T(8,128)S(1)} %get-tuple-element.46), channel_id=1, replica_groups=mesh['groups'=2,'pts'=8,'probe'=2] {'pts','probe'}, dimensions={0} | all-to-all | bytes 131072 | tf_op jit(solution)/shard_map/all_to_all | solution.py:895
  (35 shorter events, 3.3 us)
Async XLA Ops:
  12.7 20.5 %copy-start.14 = (f32[32,768]{1,0:T(8,128)}, f32[32,768]{1,0:T(8,128)S(1)}, u32[]{:S(2)}) copy-start(f32[32,768]{1,0:T(8,128)S(1)} %get-tuple-element.27.own_ref.refs_2_) | copy-start | bytes 294916
  12.7 9.8 %collective-permute-start.1 = (f32[32,768]{1,0:T(8,128)S(1)}, f32[32,768]{1,0:T(8,128)S(1)}, u32[]{:S(2)}, u32[]{:S(2)}) collective-permute-start(f32[32,768]{1,0:T(8,128)S(1)} %get-tuple-element.27.own_ref.refs_2_), channel_id=1, source_target_pairs={{2,0},{4,2},{6,4},{8,6},{10,8},{12,10},{14,12},{3,1},{5,3},{7,5},{... | collective-permute-start | bytes 294920 | tf_op jit(solution)/shard_map/ppermute | solution.py:777
  14.0 8.6 %collective-permute-start = (f32[32,768]{1,0:T(8,128)S(1)}, f32[32,768]{1,0:T(8,128)S(1)}, u32[]{:S(2)}, u32[]{:S(2)}) collective-permute-start(f32[32,768]{1,0:T(8,128)S(1)} %get-tuple-element.27.own_ref.refs_2_), channel_id=1, source_target_pairs={{0,2},{2,4},{4,6},{6,8},{8,10},{10,12},{12,14},{1,3},{3,5},{5,7},{... | collective-permute-start | bytes 294920 | tf_op jit(solution)/shard_map/ppermute | solution.py:777
  21.0 1.4 %copy-start.2 = (f32[3,768,256]{2,1,0:T(8,128)}, f32[3,768,256]{2,1,0:T(8,128)S(1)}, u32[]{:S(2)}) copy-start(f32[3,768,256]{2,1,0:T(8,128)S(1)} %get-tuple-element.43.refs_2_) | copy-start | bytes 7077892
  22.5 19.9 %copy-start.4 = (bf16[3,768,256]{2,1,0:T(8,128)(2,1)}, bf16[3,768,256]{2,1,0:T(8,128)(2,1)S(1)}, u32[]{:S(2)}) copy-start(bf16[3,768,256]{2,1,0:T(8,128)(2,1)S(1)} %get-tuple-element.34.hi_ref.refs_0_) | copy-start | bytes 3538948
  22.5 19.9 %copy-start.6 = (bf16[3,768,256]{2,1,0:T(8,128)(2,1)}, bf16[3,768,256]{2,1,0:T(8,128)(2,1)S(1)}, u32[]{:S(2)}) copy-start(bf16[3,768,256]{2,1,0:T(8,128)(2,1)S(1)} %get-tuple-element.35.lo_ref.refs_1_) | copy-start | bytes 3538948
  22.6 3.0 %copy-start.10 = (f32[32,768]{1,0:T(8,128)}, f32[32,768]{1,0:T(8,128)S(1)}, u32[]{:S(2)}) copy-start(f32[32,768]{1,0:T(8,128)S(1)} %collective-permute-done.refs_0_.left_ref) | copy-start | bytes 294916
  24.0 1.6 %copy-start = (f32[3,1024,256]{2,1,0:T(8,128)}, f32[3,1024,256]{2,1,0:T(8,128)S(1)}, u32[]{:S(2)}) copy-start(f32[3,1024,256]{2,1,0:T(8,128)S(1)} %get-tuple-element.44.refs_5_) | copy-start | bytes 9437188
  25.6 7.5 %copy-start.20 = (f32[16,768]{1,0:T(8,128)S(1)}, f32[16,768]{1,0:T(8,128)}, u32[]{:S(2)}) copy-start(f32[16,768]{1,0:T(8,128)} %sys_ref.3) | copy-start | bytes 147460
  26.5 15.9 %copy-start.12 = (f32[40,768]{1,0:T(8,128)}, f32[40,768]{1,0:T(8,128)S(1)}, u32[]{:S(2)}) copy-start(f32[40,768]{1,0:T(8,128)S(1)} %get-tuple-element.32.d1_ref) | copy-start | bytes 368644
  26.5 7.8 %collective-permute-start.3 = (f32[40,768]{1,0:T(8,128)S(1)}, f32[40,768]{1,0:T(8,128)S(1)}, u32[]{:S(2)}, u32[]{:S(2)}) collective-permute-start(f32[40,768]{1,0:T(8,128)S(1)} %get-tuple-element.32.d1_ref), channel_id=1, source_target_pairs={{2,0},{4,2},{6,4},{8,6},{10,8},{12,10},{14,12},{3,1},{5,3},{7,5},{... | collective-permute-start | bytes 368648 | tf_op jit(solution)/shard_map/ppermute | solution.py:777
  27.8 9.3 %collective-permute-start.2 = (f32[40,768]{1,0:T(8,128)S(1)}, f32[40,768]{1,0:T(8,128)S(1)}, u32[]{:S(2)}, u32[]{:S(2)}) collective-permute-start(f32[40,768]{1,0:T(8,128)S(1)} %get-tuple-element.32.d1_ref), channel_id=1, source_target_pairs={{0,2},{2,4},{4,6},{6,8},{8,10},{10,12},{12,14},{1,3},{3,5},{5,7},{... | collective-permute-start | bytes 368648 | tf_op jit(solution)/shard_map/ppermute | solution.py:777
  37.9 7.1 %collective-permute-start.4 = (f32[40,768]{1,0:T(8,128)S(1)}, f32[40,768]{1,0:T(8,128)S(1)}, u32[]{:S(2)}, u32[]{:S(2)}) collective-permute-start(f32[40,768]{1,0:T(8,128)S(1)} %get-tuple-element.38.d2_ref.vec_ref), channel_id=1, source_target_pairs={{0,2},{2,4},{4,6},{6,8},{8,10},{10,12},{12,14},{1,3},{3,5},{5,7},{... | collective-permute-start | bytes 368648 | tf_op jit(solution)/shard_map/ppermute | solution.py:782
  43.2 1.9 %copy-start.16 = (f32[16,768]{1,0:T(8,128)}, f32[16,768]{1,0:T(8,128)S(1)}, u32[]{:S(2)}) copy-start(f32[16,768]{1,0:T(8,128)S(1)} %get-tuple-element.42.sys_ref) | copy-start | bytes 147460
  46.4 0.6 copy-start.8
  47.0 14.6 %all-to-all-start = ((f32[8,40,128]{2,1,0:T(8,128)}), f32[8,40,128]{2,1,0:T(8,128)S(1)}, u32[]{:S(2)}, u32[]{:S(2)}) async-start(f32[8,40,128]{2,1,0:T(8,128)} %third.1), calls=%async_computation | async-start | bytes 327680 | tf_op jit(solution)/shard_map/all_to_all | solution.py:886
  54.1 6.0 %collective-permute-start.5 = (f32[16,768]{1,0:T(8,128)}, f32[16,768]{1,0:T(8,128)S(1)}, u32[]{:S(2)}, u32[]{:S(2)}) collective-permute-start(f32[16,768]{1,0:T(8,128)} %copy-done.16), channel_id=1, source_target_pairs={{0,2},{2,4},{4,6},{6,8},{8,10},{10,12},{12,14},{1,3},{3,5},{5,7},{... | collective-permute-start | bytes 147464 | tf_op jit(solution)/shard_map/ppermute | solution.py:782
  60.1 0.6 copy-start.18
  61.6 1.9 %copy-start.1 = (f32[3,1024,256]{2,1,0:T(8,128)S(1)}, f32[3,1024,256]{2,1,0:T(8,128)}, u32[]{:S(2)}) copy-start(f32[3,1024,256]{2,1,0:T(8,128)} %copy-done) | copy-start | bytes 9437188
  63.5 1.7 %copy-start.3 = (f32[3,768,256]{2,1,0:T(8,128)S(1)}, f32[3,768,256]{2,1,0:T(8,128)}, u32[]{:S(2)}) copy-start(f32[3,768,256]{2,1,0:T(8,128)} %copy-done.2) | copy-start | bytes 7077892
  65.2 1.3 %copy-start.5 = (bf16[3,768,256]{2,1,0:T(8,128)(2,1)S(1)}, bf16[3,768,256]{2,1,0:T(8,128)(2,1)}, u32[]{:S(2)}) copy-start(bf16[3,768,256]{2,1,0:T(8,128)(2,1)} %copy-done.4) | copy-start | bytes 3538948
  66.5 1.3 %copy-start.7 = (bf16[3,768,256]{2,1,0:T(8,128)(2,1)S(1)}, bf16[3,768,256]{2,1,0:T(8,128)(2,1)}, u32[]{:S(2)}) copy-start(bf16[3,768,256]{2,1,0:T(8,128)(2,1)} %copy-done.6) | copy-start | bytes 3538948
  67.7 0.9 copy-start.9
  68.6 0.9 copy-start.11
  69.5 0.9 copy-start.13
  70.4 0.9 copy-start.15
  71.3 0.8 copy-start.17
  72.1 0.8 copy-start.19

commit v17 on v15

--- a/solution.py
+++ b/solution.py
@@ -168,19 +168,32 @@
             out.append(part)
         return out
 
-    cols = columns(0)
-    for first in range(0, BASE, GROUP):
-        ahead = columns(first + GROUP) if first + GROUP < BASE else []
-        pivots = [[None] * GROUP for _ in range(GROUP)]
+    def symmetric(entry):
+        out = [[None] * GROUP for _ in range(GROUP)]
         for t in range(GROUP):
             for u in range(t, GROUP):
-                pivots[t][u] = pivots[u][t] = row(cols[u], first + t)
+                out[t][u] = out[u][t] = entry(t, u)
+        return out
+
+    cols = columns(0)
+    pivots = symmetric(lambda t, u: row(cols[u], t))
+    for first in range(0, BASE, GROUP):
+        then = first + GROUP
+        ahead = columns(then) if then < BASE else []
+        heads = [[row(col, first + t) for t in range(GROUP)] for col in ahead]
         inv = small_inverse(pivots)
-        coming = []
-        for col in ahead:
-            head = [row(col, first + t) for t in range(GROUP)]
-            factor = [sum(inv[t][u] * head[u] for u in range(GROUP)) for t in range(GROUP)]
-            coming.append(with_rows(less(col, factor), first, factor))
+        factors = [
+            [sum(inv[t][u] * head[u] for u in range(GROUP)) for t in range(GROUP)]
+            for head in heads
+        ]
+        if ahead:
+            pivots = symmetric(
+                lambda t, u: row(ahead[u], then + t)
+                - sum(heads[t][i] * factors[u][i] for i in range(GROUP))
+            )
+        coming = [
+            with_rows(less(col, factor), first, factor) for col, factor in zip(ahead, factors)
+        ]
         group = (inner >= first) & (inner < first + GROUP)
         rows = []
         for t in range(GROUP):

time: 75.9 us -> 76 us (level)
  no operation moved by 1% of the time
where the time goes in v17:
time: 76 us; the launch traced here: 75.6 us
  Pallas kernels  25.9 us (34%)
  blocking collectives  23.1 us (30%)
  starting transfers between devices  17.7 us (23%)
  waiting for transfers between devices  8.11 us (11%)
  between operations  0.76 us (1%)
    pallas_call x10, Pallas kernels, call(): pl.pallas_call(body, out_shape=outs, in_specs=[sm] * smem + [vm] * (len(a...  25.9 us
    all_to_all x1, blocking collectives, shards(): gram = lax.all_to_all(gram, 'pts', 0, 0, tiled=True)  13.7 us
    ppermute x4, starting transfers between devices, both_sides(): return (lax.ppermute(cells, 'pts', up), lax.ppermute(cells, 'pts', down))  13.3 us
    all_to_all x1, blocking collectives, shards(): grads = lax.all_to_all(grads, ('pts', 'probe'), 0, 0, tiled=True)  9.47 us
    ppermute x4, waiting for transfers between devices, both_sides(): return (lax.ppermute(cells, 'pts', up), lax.ppermute(cells, 'pts', down))  5.1 us
    ppermute x1, starting transfers between devices, from_left(): return lax.ppermute(cells, 'pts', [(i, i + 1) for i in range(count - 1)])  4.4 us
    ppermute x1, waiting for transfers between devices, from_left(): return lax.ppermute(cells, 'pts', [(i, i + 1) for i in range(count - 1)])  3.01 us
  transfers between devices with their start and end apart: 5, of which 4 were waited for; matrix products, arithmetic and copies ran while one was open for 0% of the time, Pallas kernels for 4%

profile of v17, /device:TPU:0, one launch (start us, length us, event | category | flops | bytes accessed | tf_op | source)
XLA Modules:
  0.0 75.6 jit_solution(14743154070630855184)
XLA Ops:
  0.6 12.2 %invert.1 = (bf16[3,3,256,256]{3,2,1,0:T(8,128)(2,1)S(1)}, f32[32,768]{1,0:T(8,128)S(1)}, f32[24,768]{1,0:T(8,128)S(1)}) custom-call(s32[1]{0:T(128)} %bitcast.place_ref, s32[1]{0:T(128)} %bitcast.1.probe_ref, f32[8,768]{1,0:T(8,128)} %feat_hbm.1, s32[768]{0:T(1024)} %ids_hbm.1, s32[768]{0:T(1024)} %agg_hbm.1, f32[16,768]{1,0:T(8,128)} %sys_ref.3, ...), custom_call_target="tpu_custom_call" | custom-call | flops 10000000000 | bytes 1048576 | tf_op jit(solution)/shard_map/invert/pallas_call | solution.py:772
  12.8 1.3 %collective-permute-start.1 = (f32[32,768]{1,0:T(8,128)S(1)}, f32[32,768]{1,0:T(8,128)S(1)}, u32[]{:S(2)}, u32[]{:S(2)}) collective-permute-start(f32[32,768]{1,0:T(8,128)S(1)} %get-tuple-element.26.own_ref.refs_2_), channel_id=1, source_target_pairs={{2,0},{4,2},{6,4},{8,6},{10,8},{12,10},{14,12},{3,1},{5,3},{7,5},{... | collective-permute-start | bytes 294920 | tf_op jit(solution)/shard_map/ppermute | solution.py:788
  14.1 5.7 %collective-permute-start = (f32[32,768]{1,0:T(8,128)S(1)}, f32[32,768]{1,0:T(8,128)S(1)}, u32[]{:S(2)}, u32[]{:S(2)}) collective-permute-start(f32[32,768]{1,0:T(8,128)S(1)} %get-tuple-element.26.own_ref.refs_2_), channel_id=1, source_target_pairs={{0,2},{2,4},{4,6},{6,8},{8,10},{10,12},{12,14},{1,3},{3,5},{5,7},{... | collective-permute-start | bytes 294920 | tf_op jit(solution)/shard_map/ppermute | solution.py:788
  19.8 1.4 %build_own.1 = (bf16[3,768,256]{2,1,0:T(8,128)(2,1)S(1)}, bf16[3,768,256]{2,1,0:T(8,128)(2,1)S(1)}, f32[3,768,256]{2,1,0:T(8,128)S(1)}, f32[40,768]{1,0:T(8,128)S(1)}) custom-call(f32[32,768]{1,0:T(8,128)S(1)} %get-tuple-element.26.own_ref.refs_2_, f32[24,768]{1,0:T(8,128)S(1)} %get-tuple-element.25.extra_ref.refs_3_), custom_call_target="tpu_custom_call" | custom-call | flops 1000000000 | bytes 1048576 | tf_op jit(solution)/shard_map/build_own/pallas_call | solution.py:772
  21.2 0.0 collective-permute-done.1.refs_1_.right_ref
  21.2 1.6 %collective-permute-done.refs_0_.left_ref = f32[32,768]{1,0:T(8,128)S(1)} collective-permute-done((f32[32,768]{1,0:T(8,128)S(1)}, f32[32,768]{1,0:T(8,128)S(1)}, u32[]{:S(2)}, u32[]{:S(2)}) %collective-permute-start) | collective-permute-done | bytes 98336 | tf_op jit(solution)/shard_map/ppermute | solution.py:788
  22.7 1.4 %build_halo.1 = (bf16[3,1024,256]{2,1,0:T(8,128)(2,1)S(1)}, bf16[3,1024,256]{2,1,0:T(8,128)(2,1)S(1)}, f32[3,1024,256]{2,1,0:T(8,128)S(1)}) custom-call(f32[32,768]{1,0:T(8,128)S(1)} %collective-permute-done.refs_0_.left_ref, f32[32,768]{1,0:T(8,128)S(1)} %collective-permute-done.1.refs_1_.right_ref, f32[32,768]{1,0:T(8,128)S(1)} %get-tuple-element.26.own_ref.refs_2_, ...), custom_call_target="tpu_custom_call" | custom-call | flops 1000000000 | bytes 1048576 | tf_op jit(solution)/shard_map/build_halo/pallas_call | solution.py:772
  24.1 0.0 copy-start
  24.1 0.8 %first.1 = (f32[40,768]{1,0:T(8,128)S(1)}, f32[40,768]{1,0:T(8,128)S(1)}) custom-call(f32[40,768]{1,0:T(8,128)S(1)} %get-tuple-element.27.part_ref, f32[32,768]{1,0:T(8,128)S(1)} %collective-permute-done.refs_0_.left_ref, f32[32,768]{1,0:T(8,128)S(1)} %collective-permute-done.1.refs_1_.right_ref, bf16[3,1024,256]{2,1,0:T(8,128)(2,1)S(1)} %get-tuple-element.28.hi_ref.refs_3_, ...), custom_call_target="tpu_custom_call" | custom-call | flops 1000000000 | bytes 1048576 | tf_op jit(solution)/shard_map/first/pallas_call | solution.py:772
  25.0 1.3 %collective-permute-start.3 = (f32[40,768]{1,0:T(8,128)S(1)}, f32[40,768]{1,0:T(8,128)S(1)}, u32[]{:S(2)}, u32[]{:S(2)}) collective-permute-start(f32[40,768]{1,0:T(8,128)S(1)} %get-tuple-element.31.d1_ref), channel_id=1, source_target_pairs={{2,0},{4,2},{6,4},{8,6},{10,8},{12,10},{14,12},{3,1},{5,3},{7,5},{... | collective-permute-start | bytes 368648 | tf_op jit(solution)/shard_map/ppermute | solution.py:788
  26.3 5.0 %collective-permute-start.2 = (f32[40,768]{1,0:T(8,128)S(1)}, f32[40,768]{1,0:T(8,128)S(1)}, u32[]{:S(2)}, u32[]{:S(2)}) collective-permute-start(f32[40,768]{1,0:T(8,128)S(1)} %get-tuple-element.31.d1_ref), channel_id=1, source_target_pairs={{0,2},{2,4},{4,6},{6,8},{8,10},{10,12},{12,14},{1,3},{3,5},{5,7},{... | collective-permute-start | bytes 368648 | tf_op jit(solution)/shard_map/ppermute | solution.py:788
  31.3 0.0 copy-done
  31.3 0.7 early.1
  32.0 0.8 %collective-permute-done.3.right_ref = f32[40,768]{1,0:T(8,128)S(1)} collective-permute-done((f32[40,768]{1,0:T(8,128)S(1)}, f32[40,768]{1,0:T(8,128)S(1)}, u32[]{:S(2)}, u32[]{:S(2)}) %collective-permute-start.3) | collective-permute-done | bytes 122912 | tf_op jit(solution)/shard_map/ppermute | solution.py:788
  32.8 2.8 %collective-permute-done.2.left_ref.d1l_ref = f32[40,768]{1,0:T(8,128)S(1)} collective-permute-done((f32[40,768]{1,0:T(8,128)S(1)}, f32[40,768]{1,0:T(8,128)S(1)}, u32[]{:S(2)}, u32[]{:S(2)}) %collective-permute-start.2) | collective-permute-done | bytes 122912 | tf_op jit(solution)/shard_map/ppermute | solution.py:788
  35.6 0.8 %second.1 = (f32[40,768]{1,0:T(8,128)S(1)}, f32[56,768]{1,0:T(8,128)S(1)}) custom-call(f32[40,768]{1,0:T(8,128)S(1)} %get-tuple-element.36.part_ref, f32[40,768]{1,0:T(8,128)S(1)} %collective-permute-done.2.left_ref.d1l_ref, f32[40,768]{1,0:T(8,128)S(1)} %collective-permute-done.3.right_ref, f32[16,768]{1,0:T(8,128)S(1)} %copy-done, ...), custom_call_target="tpu_custom_call" | custom-call | flops 1000000000 | bytes 1048576 | tf_op jit(solution)/shard_map/second/pallas_call | solution.py:772
  36.4 4.4 %collective-permute-start.4 = (f32[56,768]{1,0:T(8,128)S(1)}, f32[56,768]{1,0:T(8,128)S(1)}, u32[]{:S(2)}, u32[]{:S(2)}) collective-permute-start(f32[56,768]{1,0:T(8,128)S(1)} %get-tuple-element.37.cargo_ref), channel_id=1, source_target_pairs={{0,2},{2,4},{4,6},{6,8},{8,10},{10,12},{12,14},{1,3},{3,5},{5,7},{... | collective-permute-start | bytes 516104 | tf_op jit(solution)/shard_map/ppermute | solution.py:793
  40.8 0.8 %late.1 = (f32[40,128]{1,0:T(8,128)S(1)}, f32[40,768]{1,0:T(8,128)S(1)}) custom-call(f32[40,128]{1,0:T(8,128)S(1)} %get-tuple-element.35.before_ref, f32[40,768]{1,0:T(8,128)S(1)} %get-tuple-element.31.d1_ref, f32[56,768]{1,0:T(8,128)S(1)} %get-tuple-element.37.cargo_ref, f32[40,768]{1,0:T(8,128)S(1)} %get-tuple-element.38.v1_ref, ...), custom_call_target="tpu_custom_call" | custom-call | flops 1000000000 | bytes 1048576 | tf_op jit(solution)/shard_map/late/pallas_call | solution.py:772
  41.6 3.0 %collective-permute-done.4.left_ref.cargol_ref = f32[56,768]{1,0:T(8,128)S(1)} collective-permute-done((f32[56,768]{1,0:T(8,128)S(1)}, f32[56,768]{1,0:T(8,128)S(1)}, u32[]{:S(2)}, u32[]{:S(2)}) %collective-permute-start.4) | collective-permute-done | bytes 172064 | tf_op jit(solution)/shard_map/ppermute | solution.py:793
  44.6 0.6 third.1
  45.2 13.7 %all_to_all.10.gram_ref = f32[8,40,128]{2,1,0:T(8,128)S(1)} all-to-all(f32[8,40,128]{2,1,0:T(8,128)S(1)} %third.1), channel_id=1, replica_groups=mesh['groups'=2,'pts'=8,'probe'=2] {'pts'}, dimensions={0} | all-to-all | bytes 327680 | tf_op jit(solution)/shard_map/all_to_all | solution.py:896
  58.9 6.6 %final.1 = (f32[16,768]{1,0:T(8,128)}, f32[16,8,128]{2,1,0:T(8,128)S(1)}) custom-call(f32[8,40,128]{2,1,0:T(8,128)S(1)} %all_to_all.10.gram_ref, f32[32,768]{1,0:T(8,128)S(1)} %get-tuple-element.26.own_ref.refs_2_, f32[32,768]{1,0:T(8,128)S(1)} %collective-permute-done.refs_0_.left_ref, f32[40,768]{1,0:T(8,128)S(1)} %get-tuple-element.31.d1_ref, ...), custom_call_target="tpu_custom_call" | custom-call | flops 1000000000 | bytes 1048576 | tf_op jit(solution)/shard_map/final/pallas_call | solution.py:772
  65.5 9.5 %all_to_all.11.parts_ref = f32[16,8,128]{2,1,0:T(8,128)S(1)} all-to-all(f32[16,8,128]{2,1,0:T(8,128)S(1)} %get-tuple-element.44), channel_id=1, replica_groups=mesh['groups'=2,'pts'=8,'probe'=2] {'pts','probe'}, dimensions={0} | all-to-all | bytes 131072 | tf_op jit(solution)/shard_map/all_to_all | solution.py:905
  75.0 0.7 tail.1
Async XLA Ops:
  12.8 8.4 %collective-permute-start.1 = (f32[32,768]{1,0:T(8,128)S(1)}, f32[32,768]{1,0:T(8,128)S(1)}, u32[]{:S(2)}, u32[]{:S(2)}) collective-permute-start(f32[32,768]{1,0:T(8,128)S(1)} %get-tuple-element.26.own_ref.refs_2_), channel_id=1, source_target_pairs={{2,0},{4,2},{6,4},{8,6},{10,8},{12,10},{14,12},{3,1},{5,3},{7,5},{... | collective-permute-start | bytes 294920 | tf_op jit(solution)/shard_map/ppermute | solution.py:788
  14.1 8.6 %collective-permute-start = (f32[32,768]{1,0:T(8,128)S(1)}, f32[32,768]{1,0:T(8,128)S(1)}, u32[]{:S(2)}, u32[]{:S(2)}) collective-permute-start(f32[32,768]{1,0:T(8,128)S(1)} %get-tuple-element.26.own_ref.refs_2_), channel_id=1, source_target_pairs={{0,2},{2,4},{4,6},{6,8},{8,10},{10,12},{12,14},{1,3},{3,5},{5,7},{... | collective-permute-start | bytes 294920 | tf_op jit(solution)/shard_map/ppermute | solution.py:788
  24.1 7.2 %copy-start = (f32[16,768]{1,0:T(8,128)S(1)}, f32[16,768]{1,0:T(8,128)}, u32[]{:S(2)}) copy-start(f32[16,768]{1,0:T(8,128)} %sys_ref.3) | copy-start | bytes 147460
  25.0 7.8 %collective-permute-start.3 = (f32[40,768]{1,0:T(8,128)S(1)}, f32[40,768]{1,0:T(8,128)S(1)}, u32[]{:S(2)}, u32[]{:S(2)}) collective-permute-start(f32[40,768]{1,0:T(8,128)S(1)} %get-tuple-element.31.d1_ref), channel_id=1, source_target_pairs={{2,0},{4,2},{6,4},{8,6},{10,8},{12,10},{14,12},{3,1},{5,3},{7,5},{... | collective-permute-start | bytes 368648 | tf_op jit(solution)/shard_map/ppermute | solution.py:788
  26.3 9.3 %collective-permute-start.2 = (f32[40,768]{1,0:T(8,128)S(1)}, f32[40,768]{1,0:T(8,128)S(1)}, u32[]{:S(2)}, u32[]{:S(2)}) collective-permute-start(f32[40,768]{1,0:T(8,128)S(1)} %get-tuple-element.31.d1_ref), channel_id=1, source_target_pairs={{0,2},{2,4},{4,6},{6,8},{8,10},{10,12},{12,14},{1,3},{3,5},{5,7},{... | collective-permute-start | bytes 368648 | tf_op jit(solution)/shard_map/ppermute | solution.py:788
  36.4 8.2 %collective-permute-start.4 = (f32[56,768]{1,0:T(8,128)S(1)}, f32[56,768]{1,0:T(8,128)S(1)}, u32[]{:S(2)}, u32[]{:S(2)}) collective-permute-start(f32[56,768]{1,0:T(8,128)S(1)} %get-tuple-element.37.cargo_ref), channel_id=1, source_target_pairs={{0,2},{2,4},{4,6},{6,8},{8,10},{10,12},{12,14},{1,3},{3,5},{5,7},{... | collective-permute-start | bytes 516104 | tf_op jit(solution)/shard_map/ppermute | solution.py:793

commit v18 on v15

--- a/solution.py
+++ b/solution.py
@@ -216,7 +216,8 @@
         (pat_hbm, pat_ref), (len_hbm, len_ref), (noise_hbm, noise_ref), (coarse_hbm, coarse_ref),
         (sys_hbm, sys_ref),
     ]
-    for copy in fetch(pairs, sems):
+    copies = fetch(pairs, sems)
+    for copy in copies[:-1]:
         copy.wait()
     scaled = feat_ref[...] / column(len_ref, FEAT)
     ids = ids_ref[...].astype(f32).reshape(1, width)
@@ -331,6 +332,7 @@
         inv = -work[m]
         for i, part in enumerate(split(inv, 3)):
             jac_ref[i, m] = part.astype(bf16)
+    copies[-1].wait()
     pack_ref[SYS:, :] = smooth(sys_ref[...], jac_ref)
 
 
@@ -560,7 +562,7 @@
 def final_kernel(
     gram_ref, own_ref, left_ref, d1_ref, d1l_ref, cargo_ref, cargol_ref, *refs, sides, points,
 ):
-    kernel_refs, (sol_ref, grad_ref) = refs[:6], refs[6:]
+    kernel_refs, (grad_ref, sol_hbm, sol_ref, sem) = refs[:6], refs[6:]
     width = own_ref.shape[1]
     count = own_ref.shape[0] - SYS
     rows = d1_ref.shape[0]
@@ -608,36 +610,45 @@
     def total(x):
         return jnp.sum(x, axis=1, keepdims=True)
 
-    def scalars(u, i):
-        return total(jnp.where(lane == i * pitch + coarse, u, 0.0))
-
-    def metric(u):
-        out = dot(jnp.where(is_vec, u, 0.0), hankel, precision=highest)
+    def metric(u, chain):
+        vec = dot(jnp.where(is_vec, u, 0.0), hankel, precision=highest)
         for j in range(3):
-            out = out + scalars(u, j) * own[j]
-        out = jnp.where(is_vec, out, 0.0)
+            vec = vec + chain[j] * own[j]
+        vec = jnp.where(is_vec, vec, 0.0)
+        picked = [total(u * own[i]) for i in range(3)]
+        out = vec
         for i in range(3):
-            out = jnp.where(lane == i * pitch + coarse, total(u * own[i]), out)
-        return out
+            out = jnp.where(lane == i * pitch + coarse, picked[i], out)
+        curve = total(u * vec)
+        for i in range(3):
+            curve = curve + chain[i] * picked[i]
+        return out, curve
 
     def corrected(w):
         return dot(jnp.where(lane < coarse, w, 0.0), inverse, precision=highest)
 
+    one, zero = jnp.ones((count, 1), f32), jnp.zeros((count, 1), f32)
     pre = corrected(against) + jnp.where(lane == coarse, 1.0, 0.0)
-    direction = pre
+    pre_chain = [one, zero, zero]
+    direction, chain = pre, pre_chain
     gamma = total(pre * against)
     answer = jnp.zeros_like(pre)
+    answer_chain = [zero] * 3
     image_sum = jnp.zeros_like(pre)
     for step in range(ITERS):
-        image = metric(direction)
-        alpha = gamma / total(direction * image)
+        image, curve = metric(direction, chain)
+        alpha = gamma / curve
         answer = answer + alpha * direction
+        answer_chain = [a + alpha * c for a, c in zip(answer_chain, chain)]
         if step + 1 < ITERS:
             image_sum = image_sum + alpha * image
             moved_on = jnp.where(live & (slot > 0), pltpu.roll(direction, pitch, axis=1), 0.0)
             pre = pre - alpha * (moved_on + corrected(image))
+            pre_chain = [p - alpha * c for p, c in zip(pre_chain, [zero] + chain[:2])]
             gamma_new = total(pre * (against - image_sum))
-            direction = pre + (gamma_new / gamma) * direction
+            beta = gamma_new / gamma
+            direction = pre + beta * direction
+            chain = [p + beta * c for p, c in zip(pre_chain, chain)]
             gamma = gamma_new
 
     pack = jnp.concatenate([left_ref[...], own_ref[...]], axis=1)
@@ -661,10 +672,11 @@
         planes.append(jnp.zeros((deep - 3 * step, span), f32))
     planes = [plane.astype(bf16) for plane in split(jnp.concatenate(planes, axis=0), 3)]
     x = smooth_pieces(jnp.concatenate(parts, axis=1), planes)
-    x = x + scalars(answer, 0) * q0 + scalars(answer, 1) * d1[:count]
-    x = x + scalars(answer, 2) * d2[:count]
+    x = x + answer_chain[0] * q0 + answer_chain[1] * d1[:count] + answer_chain[2] * d2[:count]
     mine = slice(width, 2 * width)
     sol_ref[...] = x[:, mine]
+    leave = pltpu.make_async_copy(sol_ref, sol_hbm, sem)
+    leave.start()
 
     probe = own_ref[FEAT + 2 : FEAT + 3, 0:1]
     line = iota((count, 1), 0).astype(f32) + probe * count
@@ -733,6 +745,7 @@
     )
     for c in range(grad_ref.shape[0]):
         grad_ref[c] = value
+    leave.wait()
 
 
 def tail_kernel(parts_ref, length_ref, task_ref):
@@ -882,11 +895,13 @@
     )
     gram = lax.all_to_all(gram, "pts", 0, 0, tiled=True)
     cells = [own_hi, own_lo, own_sim, halo_hi, halo_lo, halo_sim]
-    answer, grads = call(
+    grads, answer = call(
         functools.partial(final_kernel, sides=sides * count, points=ranks * width),
-        [shape(count, width), shape(ranks * sides, FEAT, LANES)],
+        [shape(ranks * sides, FEAT, LANES), shape(count, width)],
         [gram, pack, pack_l, d1, d1_l, cargo, cargo_l] + cells,
         "final",
+        far_outs=1,
+        scratch=[pltpu.VMEM((count, width), f32), pltpu.SemaphoreType.DMA],
         flops=10**9,
     )
     grads = lax.all_to_all(grads, ("pts", "probe"), 0, 0, tiled=True)

time: 75.9 us -> 75.9 us (level)
  no operation moved by 1% of the time
where the time goes in v18:
time: 75.9 us; the launch traced here: 75.6 us
  Pallas kernels  25.9 us (34%)
  blocking collectives  23.1 us (30%)
  starting transfers between devices  17.7 us (23%)
  waiting for transfers between devices  8.14 us (11%)
  between operations  0.77 us (1%)
    pallas_call x10, Pallas kernels, call(): pl.pallas_call(body, out_shape=outs, in_specs=[sm] * smem + [vm] * (len(a...  25.9 us
    all_to_all x1, blocking collectives, shards(): gram = lax.all_to_all(gram, 'pts', 0, 0, tiled=True)  13.6 us
    ppermute x4, starting transfers between devices, both_sides(): return (lax.ppermute(cells, 'pts', up), lax.ppermute(cells, 'pts', down))  13.3 us
    all_to_all x1, blocking collectives, shards(): grads = lax.all_to_all(grads, ('pts', 'probe'), 0, 0, tiled=True)  9.48 us
    ppermute x4, waiting for transfers between devices, both_sides(): return (lax.ppermute(cells, 'pts', up), lax.ppermute(cells, 'pts', down))  5.12 us
    ppermute x1, starting transfers between devices, from_left(): return lax.ppermute(cells, 'pts', [(i, i + 1) for i in range(count - 1)])  4.4 us
    ppermute x1, waiting for transfers between devices, from_left(): return lax.ppermute(cells, 'pts', [(i, i + 1) for i in range(count - 1)])  3.02 us
  transfers between devices with their start and end apart: 5, of which 4 were waited for; matrix products, arithmetic and copies ran while one was open for 0% of the time, Pallas kernels for 4%

profile of v18, /device:TPU:0, one launch (start us, length us, event | category | flops | bytes accessed | tf_op | source)
XLA Modules:
  0.0 75.6 jit_solution(9102804395232952959)
XLA Ops:
  0.6 12.1 %invert.1 = (bf16[3,3,256,256]{3,2,1,0:T(8,128)(2,1)S(1)}, f32[32,768]{1,0:T(8,128)S(1)}, f32[24,768]{1,0:T(8,128)S(1)}) custom-call(s32[1]{0:T(128)} %bitcast.place_ref, s32[1]{0:T(128)} %bitcast.1.probe_ref, f32[8,768]{1,0:T(8,128)} %feat_hbm.1, s32[768]{0:T(1024)} %ids_hbm.1, s32[768]{0:T(1024)} %agg_hbm.1, f32[16,768]{1,0:T(8,128)} %sys_ref.3, ...), custom_call_target="tpu_custom_call" | custom-call | flops 10000000000 | bytes 1048576 | tf_op jit(solution)/shard_map/invert/pallas_call | solution.py:772
  12.7 1.3 %collective-permute-start.1 = (f32[32,768]{1,0:T(8,128)S(1)}, f32[32,768]{1,0:T(8,128)S(1)}, u32[]{:S(2)}, u32[]{:S(2)}) collective-permute-start(f32[32,768]{1,0:T(8,128)S(1)} %get-tuple-element.26.own_ref.refs_2_), channel_id=1, source_target_pairs={{2,0},{4,2},{6,4},{8,6},{10,8},{12,10},{14,12},{3,1},{5,3},{7,5},{... | collective-permute-start | bytes 294920 | tf_op jit(solution)/shard_map/ppermute | solution.py:788
  14.0 5.7 %collective-permute-start = (f32[32,768]{1,0:T(8,128)S(1)}, f32[32,768]{1,0:T(8,128)S(1)}, u32[]{:S(2)}, u32[]{:S(2)}) collective-permute-start(f32[32,768]{1,0:T(8,128)S(1)} %get-tuple-element.26.own_ref.refs_2_), channel_id=1, source_target_pairs={{0,2},{2,4},{4,6},{6,8},{8,10},{10,12},{12,14},{1,3},{3,5},{5,7},{... | collective-permute-start | bytes 294920 | tf_op jit(solution)/shard_map/ppermute | solution.py:788
  19.7 1.4 %build_own.1 = (bf16[3,768,256]{2,1,0:T(8,128)(2,1)S(1)}, bf16[3,768,256]{2,1,0:T(8,128)(2,1)S(1)}, f32[3,768,256]{2,1,0:T(8,128)S(1)}, f32[40,768]{1,0:T(8,128)S(1)}) custom-call(f32[32,768]{1,0:T(8,128)S(1)} %get-tuple-element.26.own_ref.refs_2_, f32[24,768]{1,0:T(8,128)S(1)} %get-tuple-element.25.extra_ref.refs_3_), custom_call_target="tpu_custom_call" | custom-call | flops 1000000000 | bytes 1048576 | tf_op jit(solution)/shard_map/build_own/pallas_call | solution.py:772
  21.1 0.0 collective-permute-done.1.refs_1_.right_ref
  21.1 1.6 %collective-permute-done.refs_0_.left_ref = f32[32,768]{1,0:T(8,128)S(1)} collective-permute-done((f32[32,768]{1,0:T(8,128)S(1)}, f32[32,768]{1,0:T(8,128)S(1)}, u32[]{:S(2)}, u32[]{:S(2)}) %collective-permute-start) | collective-permute-done | bytes 98336 | tf_op jit(solution)/shard_map/ppermute | solution.py:788
  22.7 1.4 %build_halo.1 = (bf16[3,1024,256]{2,1,0:T(8,128)(2,1)S(1)}, bf16[3,1024,256]{2,1,0:T(8,128)(2,1)S(1)}, f32[3,1024,256]{2,1,0:T(8,128)S(1)}) custom-call(f32[32,768]{1,0:T(8,128)S(1)} %collective-permute-done.refs_0_.left_ref, f32[32,768]{1,0:T(8,128)S(1)} %collective-permute-done.1.refs_1_.right_ref, f32[32,768]{1,0:T(8,128)S(1)} %get-tuple-element.26.own_ref.refs_2_, ...), custom_call_target="tpu_custom_call" | custom-call | flops 1000000000 | bytes 1048576 | tf_op jit(solution)/shard_map/build_halo/pallas_call | solution.py:772
  24.1 0.0 copy-start
  24.1 0.8 %first.1 = (f32[40,768]{1,0:T(8,128)S(1)}, f32[40,768]{1,0:T(8,128)S(1)}) custom-call(f32[40,768]{1,0:T(8,128)S(1)} %get-tuple-element.27.part_ref, f32[32,768]{1,0:T(8,128)S(1)} %collective-permute-done.refs_0_.left_ref, f32[32,768]{1,0:T(8,128)S(1)} %collective-permute-done.1.refs_1_.right_ref, bf16[3,1024,256]{2,1,0:T(8,128)(2,1)S(1)} %get-tuple-element.28.hi_ref.refs_3_, ...), custom_call_target="tpu_custom_call" | custom-call | flops 1000000000 | bytes 1048576 | tf_op jit(solution)/shard_map/first/pallas_call | solution.py:772
  24.9 1.3 %collective-permute-start.3 = (f32[40,768]{1,0:T(8,128)S(1)}, f32[40,768]{1,0:T(8,128)S(1)}, u32[]{:S(2)}, u32[]{:S(2)}) collective-permute-start(f32[40,768]{1,0:T(8,128)S(1)} %get-tuple-element.31.d1_ref), channel_id=1, source_target_pairs={{2,0},{4,2},{6,4},{8,6},{10,8},{12,10},{14,12},{3,1},{5,3},{7,5},{... | collective-permute-start | bytes 368648 | tf_op jit(solution)/shard_map/ppermute | solution.py:788
  26.2 5.0 %collective-permute-start.2 = (f32[40,768]{1,0:T(8,128)S(1)}, f32[40,768]{1,0:T(8,128)S(1)}, u32[]{:S(2)}, u32[]{:S(2)}) collective-permute-start(f32[40,768]{1,0:T(8,128)S(1)} %get-tuple-element.31.d1_ref), channel_id=1, source_target_pairs={{0,2},{2,4},{4,6},{6,8},{8,10},{10,12},{12,14},{1,3},{3,5},{5,7},{... | collective-permute-start | bytes 368648 | tf_op jit(solution)/shard_map/ppermute | solution.py:788
  31.2 0.0 copy-done
  31.2 0.7 early.1
  32.0 0.8 %collective-permute-done.3.right_ref = f32[40,768]{1,0:T(8,128)S(1)} collective-permute-done((f32[40,768]{1,0:T(8,128)S(1)}, f32[40,768]{1,0:T(8,128)S(1)}, u32[]{:S(2)}, u32[]{:S(2)}) %collective-permute-start.3) | collective-permute-done | bytes 122912 | tf_op jit(solution)/shard_map/ppermute | solution.py:788
  32.8 2.8 %collective-permute-done.2.left_ref.d1l_ref = f32[40,768]{1,0:T(8,128)S(1)} collective-permute-done((f32[40,768]{1,0:T(8,128)S(1)}, f32[40,768]{1,0:T(8,128)S(1)}, u32[]{:S(2)}, u32[]{:S(2)}) %collective-permute-start.2) | collective-permute-done | bytes 122912 | tf_op jit(solution)/shard_map/ppermute | solution.py:788
  35.6 0.8 %second.1 = (f32[40,768]{1,0:T(8,128)S(1)}, f32[56,768]{1,0:T(8,128)S(1)}) custom-call(f32[40,768]{1,0:T(8,128)S(1)} %get-tuple-element.36.part_ref, f32[40,768]{1,0:T(8,128)S(1)} %collective-permute-done.2.left_ref.d1l_ref, f32[40,768]{1,0:T(8,128)S(1)} %collective-permute-done.3.right_ref, f32[16,768]{1,0:T(8,128)S(1)} %copy-done, ...), custom_call_target="tpu_custom_call" | custom-call | flops 1000000000 | bytes 1048576 | tf_op jit(solution)/shard_map/second/pallas_call | solution.py:772
  36.4 4.4 %collective-permute-start.4 = (f32[56,768]{1,0:T(8,128)S(1)}, f32[56,768]{1,0:T(8,128)S(1)}, u32[]{:S(2)}, u32[]{:S(2)}) collective-permute-start(f32[56,768]{1,0:T(8,128)S(1)} %get-tuple-element.37.cargo_ref), channel_id=1, source_target_pairs={{0,2},{2,4},{4,6},{6,8},{8,10},{10,12},{12,14},{1,3},{3,5},{5,7},{... | collective-permute-start | bytes 516104 | tf_op jit(solution)/shard_map/ppermute | solution.py:793
  40.8 0.8 %late.1 = (f32[40,128]{1,0:T(8,128)S(1)}, f32[40,768]{1,0:T(8,128)S(1)}) custom-call(f32[40,128]{1,0:T(8,128)S(1)} %get-tuple-element.35.before_ref, f32[40,768]{1,0:T(8,128)S(1)} %get-tuple-element.31.d1_ref, f32[56,768]{1,0:T(8,128)S(1)} %get-tuple-element.37.cargo_ref, f32[40,768]{1,0:T(8,128)S(1)} %get-tuple-element.38.v1_ref, ...), custom_call_target="tpu_custom_call" | custom-call | flops 1000000000 | bytes 1048576 | tf_op jit(solution)/shard_map/late/pallas_call | solution.py:772
  41.6 3.0 %collective-permute-done.4.left_ref.cargol_ref = f32[56,768]{1,0:T(8,128)S(1)} collective-permute-done((f32[56,768]{1,0:T(8,128)S(1)}, f32[56,768]{1,0:T(8,128)S(1)}, u32[]{:S(2)}, u32[]{:S(2)}) %collective-permute-start.4) | collective-permute-done | bytes 172064 | tf_op jit(solution)/shard_map/ppermute | solution.py:793
  44.6 0.6 third.1
  45.2 13.6 %all_to_all.10.gram_ref = f32[8,40,128]{2,1,0:T(8,128)S(1)} all-to-all(f32[8,40,128]{2,1,0:T(8,128)S(1)} %third.1), channel_id=1, replica_groups=mesh['groups'=2,'pts'=8,'probe'=2] {'pts'}, dimensions={0} | all-to-all | bytes 327680 | tf_op jit(solution)/shard_map/all_to_all | solution.py:896
  58.9 6.6 %final.1 = (f32[16,8,128]{2,1,0:T(8,128)S(1)}, f32[16,768]{1,0:T(8,128)}) custom-call(f32[8,40,128]{2,1,0:T(8,128)S(1)} %all_to_all.10.gram_ref, f32[32,768]{1,0:T(8,128)S(1)} %get-tuple-element.26.own_ref.refs_2_, f32[32,768]{1,0:T(8,128)S(1)} %collective-permute-done.refs_0_.left_ref, f32[40,768]{1,0:T(8,128)S(1)} %get-tuple-element.31.d1_ref, ...), custom_call_target="tpu_custom_call" | custom-call | flops 1000000000 | bytes 1048576 | tf_op jit(solution)/shard_map/final/pallas_call | solution.py:772
  65.4 9.5 %all_to_all.11.parts_ref = f32[16,8,128]{2,1,0:T(8,128)S(1)} all-to-all(f32[16,8,128]{2,1,0:T(8,128)S(1)} %get-tuple-element.44), channel_id=1, replica_groups=mesh['groups'=2,'pts'=8,'probe'=2] {'pts','probe'}, dimensions={0} | all-to-all | bytes 131072 | tf_op jit(solution)/shard_map/all_to_all | solution.py:907
  74.9 0.7 tail.1
Async XLA Ops:
  12.7 8.4 %collective-permute-start.1 = (f32[32,768]{1,0:T(8,128)S(1)}, f32[32,768]{1,0:T(8,128)S(1)}, u32[]{:S(2)}, u32[]{:S(2)}) collective-permute-start(f32[32,768]{1,0:T(8,128)S(1)} %get-tuple-element.26.own_ref.refs_2_), channel_id=1, source_target_pairs={{2,0},{4,2},{6,4},{8,6},{10,8},{12,10},{14,12},{3,1},{5,3},{7,5},{... | collective-permute-start | bytes 294920 | tf_op jit(solution)/shard_map/ppermute | solution.py:788
  14.0 8.6 %collective-permute-start = (f32[32,768]{1,0:T(8,128)S(1)}, f32[32,768]{1,0:T(8,128)S(1)}, u32[]{:S(2)}, u32[]{:S(2)}) collective-permute-start(f32[32,768]{1,0:T(8,128)S(1)} %get-tuple-element.26.own_ref.refs_2_), channel_id=1, source_target_pairs={{0,2},{2,4},{4,6},{6,8},{8,10},{10,12},{12,14},{1,3},{3,5},{5,7},{... | collective-permute-start | bytes 294920 | tf_op jit(solution)/shard_map/ppermute | solution.py:788
  24.1 7.2 %copy-start = (f32[16,768]{1,0:T(8,128)S(1)}, f32[16,768]{1,0:T(8,128)}, u32[]{:S(2)}) copy-start(f32[16,768]{1,0:T(8,128)} %sys_ref.3) | copy-start | bytes 147460
  24.9 7.9 %collective-permute-start.3 = (f32[40,768]{1,0:T(8,128)S(1)}, f32[40,768]{1,0:T(8,128)S(1)}, u32[]{:S(2)}, u32[]{:S(2)}) collective-permute-start(f32[40,768]{1,0:T(8,128)S(1)} %get-tuple-element.31.d1_ref), channel_id=1, source_target_pairs={{2,0},{4,2},{6,4},{8,6},{10,8},{12,10},{14,12},{3,1},{5,3},{7,5},{... | collective-permute-start | bytes 368648 | tf_op jit(solution)/shard_map/ppermute | solution.py:788
  26.2 9.3 %collective-permute-start.2 = (f32[40,768]{1,0:T(8,128)S(1)}, f32[40,768]{1,0:T(8,128)S(1)}, u32[]{:S(2)}, u32[]{:S(2)}) collective-permute-start(f32[40,768]{1,0:T(8,128)S(1)} %get-tuple-element.31.d1_ref), channel_id=1, source_target_pairs={{0,2},{2,4},{4,6},{6,8},{8,10},{10,12},{12,14},{1,3},{3,5},{5,7},{... | collective-permute-start | bytes 368648 | tf_op jit(solution)/shard_map/ppermute | solution.py:788
  36.4 8.2 %collective-permute-start.4 = (f32[56,768]{1,0:T(8,128)S(1)}, f32[56,768]{1,0:T(8,128)S(1)}, u32[]{:S(2)}, u32[]{:S(2)}) collective-permute-start(f32[56,768]{1,0:T(8,128)S(1)} %get-tuple-element.37.cargo_ref), channel_id=1, source_target_pairs={{0,2},{2,4},{4,6},{6,8},{8,10},{10,12},{12,14},{1,3},{3,5},{5,7},{... | collective-permute-start | bytes 516104 | tf_op jit(solution)/shard_map/ppermute | solution.py:793

commit v19 on v15

--- a/solution.py
+++ b/solution.py
@@ -43,6 +43,14 @@
         x = x - head
     out.append(x.astype(bf16).astype(f32))
     return out
+
+
+def halves(x, parts):
+    out = []
+    for _ in range(parts - 1):
+        out.append(x.astype(bf16))
+        x = x - out[-1].astype(f32)
+    return out + [x.astype(bf16)]
 
 
 def column(ref, size):
@@ -295,10 +303,12 @@
 
         def rows_of(m, low, high):
             def piece():
-                r0, r1, r2 = split(strips[m][:, low:high], 3)
-                p0, p1, p2 = split(state[m], 3)
-                a = jnp.concatenate([r0, r0, r1, r1, r0, r2], axis=0).astype(bf16)
-                b = jnp.concatenate([p0, p1, p0, p1, p2, p0], axis=0).astype(bf16)
+                if (m, 0) not in state:
+                    r0, r1, r2 = halves(strips[m], 3)
+                    p0, p1, p2 = halves(state[m], 3)
+                    state[m, 0] = jnp.concatenate([r0, r0, r1, r1, r0, r2], axis=0)
+                    state[m, 1] = jnp.concatenate([p0, p1, p0, p1, p2, p0], axis=0)
+                a, b = state[m, 0][:, low:high], state[m, 1]
                 gone = (iota((1, BS), 1) >= first) & (iota((1, BS), 1) < first + BASE)
                 work[m, low:high, :] = jnp.where(gone, 0.0, work[m, low:high, :]) - dot(a, b, TN)
                 if low <= first < high:
@@ -329,8 +339,8 @@
         piece()
     for m in range(blocks):
         inv = -work[m]
-        for i, part in enumerate(split(inv, 3)):
-            jac_ref[i, m] = part.astype(bf16)
+        for i, part in enumerate(halves(inv, 3)):
+            jac_ref[i, m] = part
     pack_ref[SYS:, :] = smooth(sys_ref[...], jac_ref)
 
 
@@ -345,7 +355,7 @@
 
 def build_kernel(*refs, places, sides):
     cells, (own_ref, extra_ref) = refs[:sides], refs[sides : sides + 2]
-    hi_ref, lo_ref, sim_ref = refs[sides + 2 :]
+    hi_ref, lo_ref, sim_ref, full_ref = refs[sides + 2 :]
     blocks = hi_ref.shape[0]
     near = []
     for ref in cells:
@@ -364,6 +374,7 @@
             rows = slice(row * BS, (row + 1) * BS)
             if o <= REACH or sides == 1:
                 sim_ref[m, rows, :] = similar
+                full_ref[m, rows, :] = kernel
             hi_ref[m, rows, :] = head
             lo_ref[m, rows, :] = (kernel - head.astype(f32)).astype(bf16)
 
@@ -426,9 +437,9 @@
     return jnp.concatenate([pack_ref[SYS:, :], z], axis=0)
 
 
-def build_own_kernel(own_ref, extra_ref, hi_ref, lo_ref, sim_ref, part_ref):
+def build_own_kernel(own_ref, extra_ref, hi_ref, lo_ref, sim_ref, full_ref, part_ref):
     build_kernel(
-        own_ref, own_ref, extra_ref, hi_ref, lo_ref, sim_ref, places=own_places, sides=1
+        own_ref, own_ref, extra_ref, hi_ref, lo_ref, sim_ref, full_ref, places=own_places, sides=1
     )
     coarse = part_ref.shape[0] - (own_ref.shape[0] - SYS)
     noise = extra_ref[TASKS : TASKS + 1, :]
@@ -560,7 +571,7 @@
 def final_kernel(
     gram_ref, own_ref, left_ref, d1_ref, d1l_ref, cargo_ref, cargol_ref, *refs, sides, points,
 ):
-    kernel_refs, (sol_ref, grad_ref) = refs[:6], refs[6:]
+    kernel_refs, (sol_ref, grad_ref) = refs[:4], refs[4:]
     width = own_ref.shape[1]
     count = own_ref.shape[0] - SYS
     rows = d1_ref.shape[0]
@@ -659,7 +670,7 @@
     if deep > 3 * step:
         parts.append(jnp.zeros((count, deep - 3 * step), f32))
         planes.append(jnp.zeros((deep - 3 * step, span), f32))
-    planes = [plane.astype(bf16) for plane in split(jnp.concatenate(planes, axis=0), 3)]
+    planes = halves(jnp.concatenate(planes, axis=0), 3)
     x = smooth_pieces(jnp.concatenate(parts, axis=1), planes)
     x = x + scalars(answer, 0) * q0 + scalars(answer, 1) * d1[:count]
     x = x + scalars(answer, 2) * d2[:count]
@@ -701,18 +712,17 @@
         places = [(1, row, j + REACH) for row, j, _ in own_places(m)]
         places += [(2, row, j) for row, j, _ in halo_places(m) if j < REACH]
         for orders, row, block in places:
-            hi_ref, lo_ref, sim_ref = kernel_refs[3 * orders - 3 : 3 * orders]
+            full_ref, sim_ref = kernel_refs[2 * orders - 2 : 2 * orders]
             j = slice(block * BS, (block + 1) * BS)
             rows_at = slice(row * BS, (row + 1) * BS)
             outers = [dot(near[j], mate[:, at]) for mate in mates[:orders]]
-            kernel = hi_ref[m, rows_at, :].astype(f32) + lo_ref[m, rows_at, :].astype(f32)
             similar = sim_ref[m, rows_at, :]
-            energy = sum(outers) * kernel
-            e0, e1 = (part.astype(bf16) for part in split(energy, 2))
+            energy = sum(outers[1:], outers[0]) * full_ref[m, rows_at, :]
+            e0, e1 = halves(energy, 2)
             first = dot(both[:, j], e0)
             sums = sums + first[:high] + first[high:] + dot(heads[:, j], e1)
             for k in range(orders):
-                h0, h1 = (part.astype(bf16) for part in split(outers[k] * similar, 2))
+                h0, h1 = halves(outers[k] * similar, 2)
                 held_sums[k] = held_sums[k] + dot(tables[:, j], h0) + dot(tables[:, j], h1)
         mid = slice(width + m * BS, width + (m + 1) * BS)
         left = scaled[:, mid]
@@ -826,16 +836,17 @@
             shape(blocks, deep, BS, kind=bf16),
             shape(blocks, deep, BS, kind=bf16),
             shape(blocks, deep, BS),
+            shape(blocks, deep, BS),
         ]
 
-    own_hi, own_lo, own_sim, part = call(
+    own_hi, own_lo, own_sim, own_full, part = call(
         build_own_kernel,
         cells_of(width) + [shape(rows, width)],
         [pack, extra],
         "build_own",
         flops=10**9,
     )
-    halo_hi, halo_lo, halo_sim = call(
+    halo_hi, halo_lo, halo_sim, halo_full = call(
         functools.partial(build_kernel, places=halo_places, sides=2),
         cells_of(BAND - width),
         [pack_l, pack_r, pack, extra],
@@ -881,7 +892,7 @@
         flops=10**9,
     )
     gram = lax.all_to_all(gram, "pts", 0, 0, tiled=True)
-    cells = [own_hi, own_lo, own_sim, halo_hi, halo_lo, halo_sim]
+    cells = [own_full, own_sim, halo_full, halo_sim]
     answer, grads = call(
         functools.partial(final_kernel, sides=sides * count, points=ranks * width),
         [shape(count, width), shape(ranks * sides, FEAT, LANES)],

time: 75.9 us -> 75.8 us (level)
  no operation moved by 1% of the time
where the time goes in v19:
time: 75.8 us; the launch traced here: 75.5 us
  Pallas kernels  25.8 us (34%)
  blocking collectives  23.2 us (31%)
  starting transfers between devices  17.7 us (23%)
  waiting for transfers between devices  8.1 us (11%)
  between operations  0.77 us (1%)
    pallas_call x10, Pallas kernels, call(): pl.pallas_call(body, out_shape=outs, in_specs=[sm] * smem + [vm] * (len(a...  25.8 us
    all_to_all x1, blocking collectives, shards(): gram = lax.all_to_all(gram, 'pts', 0, 0, tiled=True)  13.7 us
    ppermute x4, starting transfers between devices, both_sides(): return (lax.ppermute(cells, 'pts', up), lax.ppermute(cells, 'pts', down))  13.3 us
    all_to_all x1, blocking collectives, shards(): grads = lax.all_to_all(grads, ('pts', 'probe'), 0, 0, tiled=True)  9.53 us
    ppermute x4, waiting for transfers between devices, both_sides(): return (lax.ppermute(cells, 'pts', up), lax.ppermute(cells, 'pts', down))  5.08 us
    ppermute x1, starting transfers between devices, from_left(): return lax.ppermute(cells, 'pts', [(i, i + 1) for i in range(count - 1)])  4.4 us
    ppermute x1, waiting for transfers between devices, from_left(): return lax.ppermute(cells, 'pts', [(i, i + 1) for i in range(count - 1)])  3.01 us
  transfers between devices with their start and end apart: 5, of which 4 were waited for; matrix products, arithmetic and copies ran while one was open for 0% of the time, Pallas kernels for 4%

profile of v19, /device:TPU:0, one launch (start us, length us, event | category | flops | bytes accessed | tf_op | source)
XLA Modules:
  0.0 75.5 jit_solution(10245802551913717221)
XLA Ops:
  0.6 12.0 %invert.1 = (bf16[3,3,256,256]{3,2,1,0:T(8,128)(2,1)S(1)}, f32[32,768]{1,0:T(8,128)S(1)}, f32[24,768]{1,0:T(8,128)S(1)}) custom-call(s32[1]{0:T(128)} %bitcast.place_ref, s32[1]{0:T(128)} %bitcast.1.probe_ref, f32[8,768]{1,0:T(8,128)} %feat_hbm.1, s32[768]{0:T(1024)} %ids_hbm.1, s32[768]{0:T(1024)} %agg_hbm.1, f32[16,768]{1,0:T(8,128)} %sys_ref.3, ...), custom_call_target="tpu_custom_call" | custom-call | flops 10000000000 | bytes 1048576 | tf_op jit(solution)/shard_map/invert/pallas_call | solution.py:769
  12.7 1.3 %collective-permute-start.1 = (f32[32,768]{1,0:T(8,128)S(1)}, f32[32,768]{1,0:T(8,128)S(1)}, u32[]{:S(2)}, u32[]{:S(2)}) collective-permute-start(f32[32,768]{1,0:T(8,128)S(1)} %get-tuple-element.28.own_ref.refs_2_), channel_id=1, source_target_pairs={{2,0},{4,2},{6,4},{8,6},{10,8},{12,10},{14,12},{3,1},{5,3},{7,5},{... | collective-permute-start | bytes 294920 | tf_op jit(solution)/shard_map/ppermute | solution.py:785
  14.0 5.7 %collective-permute-start = (f32[32,768]{1,0:T(8,128)S(1)}, f32[32,768]{1,0:T(8,128)S(1)}, u32[]{:S(2)}, u32[]{:S(2)}) collective-permute-start(f32[32,768]{1,0:T(8,128)S(1)} %get-tuple-element.28.own_ref.refs_2_), channel_id=1, source_target_pairs={{0,2},{2,4},{4,6},{6,8},{8,10},{10,12},{12,14},{1,3},{3,5},{5,7},{... | collective-permute-start | bytes 294920 | tf_op jit(solution)/shard_map/ppermute | solution.py:785
  19.7 1.4 %build_own.1 = (bf16[3,768,256]{2,1,0:T(8,128)(2,1)S(1)}, bf16[3,768,256]{2,1,0:T(8,128)(2,1)S(1)}, f32[3,768,256]{2,1,0:T(8,128)S(1)}, f32[3,768,256]{2,1,0:T(8,128)S(1)}, f32[40,768]{1,0:T(8,128)S(1)}) custom-call(f32[32,768]{1,0:T(8,128)S(1)} %get-tuple-element.28.own_ref.refs_2_, f32[24,768]{1,0:T(8,128)S(1)} %get-tuple-element.27.extra_ref.refs_3_), custom_call_target="tpu_custom_call" | custom-call | flops 1000000000 | bytes 1048576 | tf_op jit(solution)/shard_map/build_own/pallas_call | solution.py:769
  21.1 0.0 collective-permute-done.1.refs_1_.right_ref
  21.1 1.5 %collective-permute-done.refs_0_.left_ref = f32[32,768]{1,0:T(8,128)S(1)} collective-permute-done((f32[32,768]{1,0:T(8,128)S(1)}, f32[32,768]{1,0:T(8,128)S(1)}, u32[]{:S(2)}, u32[]{:S(2)}) %collective-permute-start) | collective-permute-done | bytes 98336 | tf_op jit(solution)/shard_map/ppermute | solution.py:785
  22.6 1.4 %build_halo.1 = (bf16[3,1024,256]{2,1,0:T(8,128)(2,1)S(1)}, bf16[3,1024,256]{2,1,0:T(8,128)(2,1)S(1)}, f32[3,1024,256]{2,1,0:T(8,128)S(1)}, f32[3,1024,256]{2,1,0:T(8,128)S(1)}) custom-call(f32[32,768]{1,0:T(8,128)S(1)} %collective-permute-done.refs_0_.left_ref, f32[32,768]{1,0:T(8,128)S(1)} %collective-permute-done.1.refs_1_.right_ref, ...), custom_call_target="tpu_custom_call" | custom-call | flops 1000000000 | bytes 1048576 | tf_op jit(solution)/shard_map/build_halo/pallas_call | solution.py:769
  24.0 0.0 copy-start
  24.0 0.8 %first.1 = (f32[40,768]{1,0:T(8,128)S(1)}, f32[40,768]{1,0:T(8,128)S(1)}) custom-call(f32[40,768]{1,0:T(8,128)S(1)} %get-tuple-element.29.part_ref, f32[32,768]{1,0:T(8,128)S(1)} %collective-permute-done.refs_0_.left_ref, f32[32,768]{1,0:T(8,128)S(1)} %collective-permute-done.1.refs_1_.right_ref, bf16[3,1024,256]{2,1,0:T(8,128)(2,1)S(1)} %get-tuple-element.30.hi_ref, ...), custom_call_target="tpu_custom_call" | custom-call | flops 1000000000 | bytes 1048576 | tf_op jit(solution)/shard_map/first/pallas_call | solution.py:769
  24.9 1.3 %collective-permute-start.3 = (f32[40,768]{1,0:T(8,128)S(1)}, f32[40,768]{1,0:T(8,128)S(1)}, u32[]{:S(2)}, u32[]{:S(2)}) collective-permute-start(f32[40,768]{1,0:T(8,128)S(1)} %get-tuple-element.33.d1_ref), channel_id=1, source_target_pairs={{2,0},{4,2},{6,4},{8,6},{10,8},{12,10},{14,12},{3,1},{5,3},{7,5},{... | collective-permute-start | bytes 368648 | tf_op jit(solution)/shard_map/ppermute | solution.py:785
  26.2 5.0 %collective-permute-start.2 = (f32[40,768]{1,0:T(8,128)S(1)}, f32[40,768]{1,0:T(8,128)S(1)}, u32[]{:S(2)}, u32[]{:S(2)}) collective-permute-start(f32[40,768]{1,0:T(8,128)S(1)} %get-tuple-element.33.d1_ref), channel_id=1, source_target_pairs={{0,2},{2,4},{4,6},{6,8},{8,10},{10,12},{12,14},{1,3},{3,5},{5,7},{... | collective-permute-start | bytes 368648 | tf_op jit(solution)/shard_map/ppermute | solution.py:785
  31.2 0.0 copy-done
  31.2 0.7 early.1
  32.0 0.8 %collective-permute-done.3.right_ref = f32[40,768]{1,0:T(8,128)S(1)} collective-permute-done((f32[40,768]{1,0:T(8,128)S(1)}, f32[40,768]{1,0:T(8,128)S(1)}, u32[]{:S(2)}, u32[]{:S(2)}) %collective-permute-start.3) | collective-permute-done | bytes 122912 | tf_op jit(solution)/shard_map/ppermute | solution.py:785
  32.7 2.8 %collective-permute-done.2.left_ref.d1l_ref = f32[40,768]{1,0:T(8,128)S(1)} collective-permute-done((f32[40,768]{1,0:T(8,128)S(1)}, f32[40,768]{1,0:T(8,128)S(1)}, u32[]{:S(2)}, u32[]{:S(2)}) %collective-permute-start.2) | collective-permute-done | bytes 122912 | tf_op jit(solution)/shard_map/ppermute | solution.py:785
  35.5 0.8 %second.1 = (f32[40,768]{1,0:T(8,128)S(1)}, f32[56,768]{1,0:T(8,128)S(1)}) custom-call(f32[40,768]{1,0:T(8,128)S(1)} %get-tuple-element.38.part_ref, f32[40,768]{1,0:T(8,128)S(1)} %collective-permute-done.2.left_ref.d1l_ref, f32[40,768]{1,0:T(8,128)S(1)} %collective-permute-done.3.right_ref, f32[16,768]{1,0:T(8,128)S(1)} %copy-done, ...), custom_call_target="tpu_custom_call" | custom-call | flops 1000000000 | bytes 1048576 | tf_op jit(solution)/shard_map/second/pallas_call | solution.py:769
  36.3 4.4 %collective-permute-start.4 = (f32[56,768]{1,0:T(8,128)S(1)}, f32[56,768]{1,0:T(8,128)S(1)}, u32[]{:S(2)}, u32[]{:S(2)}) collective-permute-start(f32[56,768]{1,0:T(8,128)S(1)} %get-tuple-element.39.cargo_ref), channel_id=1, source_target_pairs={{0,2},{2,4},{4,6},{6,8},{8,10},{10,12},{12,14},{1,3},{3,5},{5,7},{... | collective-permute-start | bytes 516104 | tf_op jit(solution)/shard_map/ppermute | solution.py:790
  40.7 0.8 %late.1 = (f32[40,128]{1,0:T(8,128)S(1)}, f32[40,768]{1,0:T(8,128)S(1)}) custom-call(f32[40,128]{1,0:T(8,128)S(1)} %get-tuple-element.37.before_ref, f32[40,768]{1,0:T(8,128)S(1)} %get-tuple-element.33.d1_ref, f32[56,768]{1,0:T(8,128)S(1)} %get-tuple-element.39.cargo_ref, f32[40,768]{1,0:T(8,128)S(1)} %get-tuple-element.40.v1_ref, ...), custom_call_target="tpu_custom_call" | custom-call | flops 1000000000 | bytes 1048576 | tf_op jit(solution)/shard_map/late/pallas_call | solution.py:769
  41.5 3.0 %collective-permute-done.4.left_ref.cargol_ref = f32[56,768]{1,0:T(8,128)S(1)} collective-permute-done((f32[56,768]{1,0:T(8,128)S(1)}, f32[56,768]{1,0:T(8,128)S(1)}, u32[]{:S(2)}, u32[]{:S(2)}) %collective-permute-start.4) | collective-permute-done | bytes 172064 | tf_op jit(solution)/shard_map/ppermute | solution.py:790
  44.5 0.6 third.1
  45.2 13.7 %all_to_all.10.gram_ref = f32[8,40,128]{2,1,0:T(8,128)S(1)} all-to-all(f32[8,40,128]{2,1,0:T(8,128)S(1)} %third.1), channel_id=1, replica_groups=mesh['groups'=2,'pts'=8,'probe'=2] {'pts'}, dimensions={0} | all-to-all | bytes 327680 | tf_op jit(solution)/shard_map/all_to_all | solution.py:894
  58.8 6.5 %final.1 = (f32[16,768]{1,0:T(8,128)}, f32[16,8,128]{2,1,0:T(8,128)S(1)}) custom-call(f32[8,40,128]{2,1,0:T(8,128)S(1)} %all_to_all.10.gram_ref, f32[32,768]{1,0:T(8,128)S(1)} %get-tuple-element.28.own_ref.refs_2_, f32[32,768]{1,0:T(8,128)S(1)} %collective-permute-done.refs_0_.left_ref, f32[40,768]{1,0:T(8,128)S(1)} %get-tuple-element.33.d1_ref, ...), custom_call_target="tpu_custom_call" | custom-call | flops 1000000000 | bytes 1048576 | tf_op jit(solution)/shard_map/final/pallas_call | solution.py:769
  65.3 9.5 %all_to_all.11.parts_ref = f32[16,8,128]{2,1,0:T(8,128)S(1)} all-to-all(f32[16,8,128]{2,1,0:T(8,128)S(1)} %get-tuple-element.48), channel_id=1, replica_groups=mesh['groups'=2,'pts'=8,'probe'=2] {'pts','probe'}, dimensions={0} | all-to-all | bytes 131072 | tf_op jit(solution)/shard_map/all_to_all | solution.py:903
  74.8 0.7 tail.1
Async XLA Ops:
  12.7 8.4 %collective-permute-start.1 = (f32[32,768]{1,0:T(8,128)S(1)}, f32[32,768]{1,0:T(8,128)S(1)}, u32[]{:S(2)}, u32[]{:S(2)}) collective-permute-start(f32[32,768]{1,0:T(8,128)S(1)} %get-tuple-element.28.own_ref.refs_2_), channel_id=1, source_target_pairs={{2,0},{4,2},{6,4},{8,6},{10,8},{12,10},{14,12},{3,1},{5,3},{7,5},{... | collective-permute-start | bytes 294920 | tf_op jit(solution)/shard_map/ppermute | solution.py:785
  14.0 8.6 %collective-permute-start = (f32[32,768]{1,0:T(8,128)S(1)}, f32[32,768]{1,0:T(8,128)S(1)}, u32[]{:S(2)}, u32[]{:S(2)}) collective-permute-start(f32[32,768]{1,0:T(8,128)S(1)} %get-tuple-element.28.own_ref.refs_2_), channel_id=1, source_target_pairs={{0,2},{2,4},{4,6},{6,8},{8,10},{10,12},{12,14},{1,3},{3,5},{5,7},{... | collective-permute-start | bytes 294920 | tf_op jit(solution)/shard_map/ppermute | solution.py:785
  24.0 7.2 %copy-start = (f32[16,768]{1,0:T(8,128)S(1)}, f32[16,768]{1,0:T(8,128)}, u32[]{:S(2)}) copy-start(f32[16,768]{1,0:T(8,128)} %sys_ref.3) | copy-start | bytes 147460
  24.9 7.8 %collective-permute-start.3 = (f32[40,768]{1,0:T(8,128)S(1)}, f32[40,768]{1,0:T(8,128)S(1)}, u32[]{:S(2)}, u32[]{:S(2)}) collective-permute-start(f32[40,768]{1,0:T(8,128)S(1)} %get-tuple-element.33.d1_ref), channel_id=1, source_target_pairs={{2,0},{4,2},{6,4},{8,6},{10,8},{12,10},{14,12},{3,1},{5,3},{7,5},{... | collective-permute-start | bytes 368648 | tf_op jit(solution)/shard_map/ppermute | solution.py:785
  26.2 9.3 %collective-permute-start.2 = (f32[40,768]{1,0:T(8,128)S(1)}, f32[40,768]{1,0:T(8,128)S(1)}, u32[]{:S(2)}, u32[]{:S(2)}) collective-permute-start(f32[40,768]{1,0:T(8,128)S(1)} %get-tuple-element.33.d1_ref), channel_id=1, source_target_pairs={{0,2},{2,4},{4,6},{6,8},{8,10},{10,12},{12,14},{1,3},{3,5},{5,7},{... | collective-permute-start | bytes 368648 | tf_op jit(solution)/shard_map/ppermute | solution.py:785
  36.3 8.2 %collective-permute-start.4 = (f32[56,768]{1,0:T(8,128)S(1)}, f32[56,768]{1,0:T(8,128)S(1)}, u32[]{:S(2)}, u32[]{:S(2)}) collective-permute-start(f32[56,768]{1,0:T(8,128)S(1)} %get-tuple-element.39.cargo_ref), channel_id=1, source_target_pairs={{0,2},{2,4},{4,6},{6,8},{8,10},{10,12},{12,14},{1,3},{3,5},{5,7},{... | collective-permute-start | bytes 516104 | tf_op jit(solution)/shard_map/ppermute | solution.py:790

commit v20 on v19

--- a/solution.py
+++ b/solution.py
@@ -571,7 +571,7 @@
 def final_kernel(
     gram_ref, own_ref, left_ref, d1_ref, d1l_ref, cargo_ref, cargol_ref, *refs, sides, points,
 ):
-    kernel_refs, (sol_ref, grad_ref) = refs[:4], refs[4:]
+    kernel_refs, (grad_ref, sol_hbm, sol_ref, sem) = refs[:4], refs[4:]
     width = own_ref.shape[1]
     count = own_ref.shape[0] - SYS
     rows = d1_ref.shape[0]
@@ -619,36 +619,47 @@
     def total(x):
         return jnp.sum(x, axis=1, keepdims=True)
 
-    def scalars(u, i):
-        return total(jnp.where(lane == i * pitch + coarse, u, 0.0))
-
-    def metric(u):
-        out = dot(jnp.where(is_vec, u, 0.0), hankel, precision=highest)
+    hankel, inverse = halves(hankel, 3), halves(inverse, 3)
+
+    def metric(u, chain):
+        vec = smooth_pieces(jnp.where(is_vec, u, 0.0), hankel)
         for j in range(3):
-            out = out + scalars(u, j) * own[j]
-        out = jnp.where(is_vec, out, 0.0)
+            vec = vec + chain[j] * own[j]
+        vec = jnp.where(is_vec, vec, 0.0)
+        picked = [total(u * own[i]) for i in range(3)]
+        out = vec
         for i in range(3):
-            out = jnp.where(lane == i * pitch + coarse, total(u * own[i]), out)
-        return out
+            out = jnp.where(lane == i * pitch + coarse, picked[i], out)
+        curve = total(u * vec)
+        for i in range(3):
+            curve = curve + chain[i] * picked[i]
+        return out, curve
 
     def corrected(w):
-        return dot(jnp.where(lane < coarse, w, 0.0), inverse, precision=highest)
-
+        return smooth_pieces(jnp.where(lane < coarse, w, 0.0), inverse)
+
+    one, zero = jnp.ones((count, 1), f32), jnp.zeros((count, 1), f32)
     pre = corrected(against) + jnp.where(lane == coarse, 1.0, 0.0)
-    direction = pre
+    pre_chain = [one, zero, zero]
+    direction, chain = pre, pre_chain
     gamma = total(pre * against)
     answer = jnp.zeros_like(pre)
+    answer_chain = [zero] * 3
     image_sum = jnp.zeros_like(pre)
     for step in range(ITERS):
-        image = metric(direction)
-        alpha = gamma / total(direction * image)
+        image, curve = metric(direction, chain)
+        alpha = gamma / curve
         answer = answer + alpha * direction
+        answer_chain = [a + alpha * c for a, c in zip(answer_chain, chain)]
         if step + 1 < ITERS:
             image_sum = image_sum + alpha * image
             moved_on = jnp.where(live & (slot > 0), pltpu.roll(direction, pitch, axis=1), 0.0)
             pre = pre - alpha * (moved_on + corrected(image))
+            pre_chain = [p - alpha * c for p, c in zip(pre_chain, [zero] + chain[:2])]
             gamma_new = total(pre * (against - image_sum))
-            direction = pre + (gamma_new / gamma) * direction
+            beta = gamma_new / gamma
+            direction = pre + beta * direction
+            chain = [p + beta * c for p, c in zip(pre_chain, chain)]
             gamma = gamma_new
 
     pack = jnp.concatenate([left_ref[...], own_ref[...]], axis=1)
@@ -672,10 +683,11 @@
         planes.append(jnp.zeros((deep - 3 * step, span), f32))
     planes = halves(jnp.concatenate(planes, axis=0), 3)
     x = smooth_pieces(jnp.concatenate(parts, axis=1), planes)
-    x = x + scalars(answer, 0) * q0 + scalars(answer, 1) * d1[:count]
-    x = x + scalars(answer, 2) * d2[:count]
+    x = x + answer_chain[0] * q0 + answer_chain[1] * d1[:count] + answer_chain[2] * d2[:count]
     mine = slice(width, 2 * width)
     sol_ref[...] = x[:, mine]
+    leave = pltpu.make_async_copy(sol_ref, sol_hbm, sem)
+    leave.start()
 
     probe = own_ref[FEAT + 2 : FEAT + 3, 0:1]
     line = iota((count, 1), 0).astype(f32) + probe * count
@@ -743,6 +755,7 @@
     )
     for c in range(grad_ref.shape[0]):
         grad_ref[c] = value
+    leave.wait()
 
 
 def tail_kernel(parts_ref, length_ref, task_ref):
@@ -893,11 +906,13 @@
     )
     gram = lax.all_to_all(gram, "pts", 0, 0, tiled=True)
     cells = [own_full, own_sim, halo_full, halo_sim]
-    answer, grads = call(
+    grads, answer = call(
         functools.partial(final_kernel, sides=sides * count, points=ranks * width),
-        [shape(count, width), shape(ranks * sides, FEAT, LANES)],
+        [shape(ranks * sides, FEAT, LANES), shape(count, width)],
         [gram, pack, pack_l, d1, d1_l, cargo, cargo_l] + cells,
         "final",
+        far_outs=1,
+        scratch=[pltpu.VMEM((count, width), f32), pltpu.SemaphoreType.DMA],
         flops=10**9,
     )
     grads = lax.all_to_all(grads, ("pts", "probe"), 0, 0, tiled=True)

time: 75.8 us -> 76 us (level)
  no operation moved by 1% of the time
where the time goes in v20:
time: 76 us; the launch traced here: 75.6 us
  Pallas kernels  25.9 us (34%)
  blocking collectives  23.1 us (30%)
  starting transfers between devices  17.7 us (23%)
  waiting for transfers between devices  8.1 us (11%)
  between operations  0.77 us (1%)
    pallas_call x10, Pallas kernels, call(): pl.pallas_call(body, out_shape=outs, in_specs=[sm] * smem + [vm] * (len(a...  25.9 us
    all_to_all x1, blocking collectives, shards(): gram = lax.all_to_all(gram, 'pts', 0, 0, tiled=True)  13.7 us
    ppermute x4, starting transfers between devices, both_sides(): return (lax.ppermute(cells, 'pts', up), lax.ppermute(cells, 'pts', down))  13.3 us
    all_to_all x1, blocking collectives, shards(): grads = lax.all_to_all(grads, ('pts', 'probe'), 0, 0, tiled=True)  9.48 us
    ppermute x4, waiting for transfers between devices, both_sides(): return (lax.ppermute(cells, 'pts', up), lax.ppermute(cells, 'pts', down))  5.08 us
    ppermute x1, starting transfers between devices, from_left(): return lax.ppermute(cells, 'pts', [(i, i + 1) for i in range(count - 1)])  4.4 us
    ppermute x1, waiting for transfers between devices, from_left(): return lax.ppermute(cells, 'pts', [(i, i + 1) for i in range(count - 1)])  3.01 us
  transfers between devices with their start and end apart: 5, of which 4 were waited for; matrix products, arithmetic and copies ran while one was open for 0% of the time, Pallas kernels for 4%

profile of v20, /device:TPU:0, one launch (start us, length us, event | category | flops | bytes accessed | tf_op | source)
XLA Modules:
  0.0 75.6 jit_solution(7571960971309064099)
XLA Ops:
  0.6 12.0 %invert.1 = (bf16[3,3,256,256]{3,2,1,0:T(8,128)(2,1)S(1)}, f32[32,768]{1,0:T(8,128)S(1)}, f32[24,768]{1,0:T(8,128)S(1)}) custom-call(s32[1]{0:T(128)} %bitcast.place_ref, s32[1]{0:T(128)} %bitcast.1.probe_ref, f32[8,768]{1,0:T(8,128)} %feat_hbm.1, s32[768]{0:T(1024)} %ids_hbm.1, s32[768]{0:T(1024)} %agg_hbm.1, f32[16,768]{1,0:T(8,128)} %sys_ref.3, ...), custom_call_target="tpu_custom_call" | custom-call | flops 10000000000 | bytes 1048576 | tf_op jit(solution)/shard_map/invert/pallas_call | solution.py:782
  12.7 1.3 %collective-permute-start.1 = (f32[32,768]{1,0:T(8,128)S(1)}, f32[32,768]{1,0:T(8,128)S(1)}, u32[]{:S(2)}, u32[]{:S(2)}) collective-permute-start(f32[32,768]{1,0:T(8,128)S(1)} %get-tuple-element.28.own_ref.refs_2_), channel_id=1, source_target_pairs={{2,0},{4,2},{6,4},{8,6},{10,8},{12,10},{14,12},{3,1},{5,3},{7,5},{... | collective-permute-start | bytes 294920 | tf_op jit(solution)/shard_map/ppermute | solution.py:798
  14.0 5.7 %collective-permute-start = (f32[32,768]{1,0:T(8,128)S(1)}, f32[32,768]{1,0:T(8,128)S(1)}, u32[]{:S(2)}, u32[]{:S(2)}) collective-permute-start(f32[32,768]{1,0:T(8,128)S(1)} %get-tuple-element.28.own_ref.refs_2_), channel_id=1, source_target_pairs={{0,2},{2,4},{4,6},{6,8},{8,10},{10,12},{12,14},{1,3},{3,5},{5,7},{... | collective-permute-start | bytes 294920 | tf_op jit(solution)/shard_map/ppermute | solution.py:798
  19.7 1.4 %build_own.1 = (bf16[3,768,256]{2,1,0:T(8,128)(2,1)S(1)}, bf16[3,768,256]{2,1,0:T(8,128)(2,1)S(1)}, f32[3,768,256]{2,1,0:T(8,128)S(1)}, f32[3,768,256]{2,1,0:T(8,128)S(1)}, f32[40,768]{1,0:T(8,128)S(1)}) custom-call(f32[32,768]{1,0:T(8,128)S(1)} %get-tuple-element.28.own_ref.refs_2_, f32[24,768]{1,0:T(8,128)S(1)} %get-tuple-element.27.extra_ref.refs_3_), custom_call_target="tpu_custom_call" | custom-call | flops 1000000000 | bytes 1048576 | tf_op jit(solution)/shard_map/build_own/pallas_call | solution.py:782
  21.1 0.0 collective-permute-done.1.refs_1_.right_ref
  21.1 1.5 %collective-permute-done.refs_0_.left_ref = f32[32,768]{1,0:T(8,128)S(1)} collective-permute-done((f32[32,768]{1,0:T(8,128)S(1)}, f32[32,768]{1,0:T(8,128)S(1)}, u32[]{:S(2)}, u32[]{:S(2)}) %collective-permute-start) | collective-permute-done | bytes 98336 | tf_op jit(solution)/shard_map/ppermute | solution.py:798
  22.6 1.4 %build_halo.1 = (bf16[3,1024,256]{2,1,0:T(8,128)(2,1)S(1)}, bf16[3,1024,256]{2,1,0:T(8,128)(2,1)S(1)}, f32[3,1024,256]{2,1,0:T(8,128)S(1)}, f32[3,1024,256]{2,1,0:T(8,128)S(1)}) custom-call(f32[32,768]{1,0:T(8,128)S(1)} %collective-permute-done.refs_0_.left_ref, f32[32,768]{1,0:T(8,128)S(1)} %collective-permute-done.1.refs_1_.right_ref, ...), custom_call_target="tpu_custom_call" | custom-call | flops 1000000000 | bytes 1048576 | tf_op jit(solution)/shard_map/build_halo/pallas_call | solution.py:782
  24.0 0.0 copy-start
  24.0 0.8 %first.1 = (f32[40,768]{1,0:T(8,128)S(1)}, f32[40,768]{1,0:T(8,128)S(1)}) custom-call(f32[40,768]{1,0:T(8,128)S(1)} %get-tuple-element.29.part_ref, f32[32,768]{1,0:T(8,128)S(1)} %collective-permute-done.refs_0_.left_ref, f32[32,768]{1,0:T(8,128)S(1)} %collective-permute-done.1.refs_1_.right_ref, bf16[3,1024,256]{2,1,0:T(8,128)(2,1)S(1)} %get-tuple-element.30.hi_ref, ...), custom_call_target="tpu_custom_call" | custom-call | flops 1000000000 | bytes 1048576 | tf_op jit(solution)/shard_map/first/pallas_call | solution.py:782
  24.9 1.3 %collective-permute-start.3 = (f32[40,768]{1,0:T(8,128)S(1)}, f32[40,768]{1,0:T(8,128)S(1)}, u32[]{:S(2)}, u32[]{:S(2)}) collective-permute-start(f32[40,768]{1,0:T(8,128)S(1)} %get-tuple-element.33.d1_ref), channel_id=1, source_target_pairs={{2,0},{4,2},{6,4},{8,6},{10,8},{12,10},{14,12},{3,1},{5,3},{7,5},{... | collective-permute-start | bytes 368648 | tf_op jit(solution)/shard_map/ppermute | solution.py:798
  26.2 5.0 %collective-permute-start.2 = (f32[40,768]{1,0:T(8,128)S(1)}, f32[40,768]{1,0:T(8,128)S(1)}, u32[]{:S(2)}, u32[]{:S(2)}) collective-permute-start(f32[40,768]{1,0:T(8,128)S(1)} %get-tuple-element.33.d1_ref), channel_id=1, source_target_pairs={{0,2},{2,4},{4,6},{6,8},{8,10},{10,12},{12,14},{1,3},{3,5},{5,7},{... | collective-permute-start | bytes 368648 | tf_op jit(solution)/shard_map/ppermute | solution.py:798
  31.2 0.0 copy-done
  31.2 0.7 early.1
  32.0 0.8 %collective-permute-done.3.right_ref = f32[40,768]{1,0:T(8,128)S(1)} collective-permute-done((f32[40,768]{1,0:T(8,128)S(1)}, f32[40,768]{1,0:T(8,128)S(1)}, u32[]{:S(2)}, u32[]{:S(2)}) %collective-permute-start.3) | collective-permute-done | bytes 122912 | tf_op jit(solution)/shard_map/ppermute | solution.py:798
  32.7 2.8 %collective-permute-done.2.left_ref.d1l_ref = f32[40,768]{1,0:T(8,128)S(1)} collective-permute-done((f32[40,768]{1,0:T(8,128)S(1)}, f32[40,768]{1,0:T(8,128)S(1)}, u32[]{:S(2)}, u32[]{:S(2)}) %collective-permute-start.2) | collective-permute-done | bytes 122912 | tf_op jit(solution)/shard_map/ppermute | solution.py:798
  35.5 0.8 %second.1 = (f32[40,768]{1,0:T(8,128)S(1)}, f32[56,768]{1,0:T(8,128)S(1)}) custom-call(f32[40,768]{1,0:T(8,128)S(1)} %get-tuple-element.38.part_ref, f32[40,768]{1,0:T(8,128)S(1)} %collective-permute-done.2.left_ref.d1l_ref, f32[40,768]{1,0:T(8,128)S(1)} %collective-permute-done.3.right_ref, f32[16,768]{1,0:T(8,128)S(1)} %copy-done, ...), custom_call_target="tpu_custom_call" | custom-call | flops 1000000000 | bytes 1048576 | tf_op jit(solution)/shard_map/second/pallas_call | solution.py:782
  36.3 4.4 %collective-permute-start.4 = (f32[56,768]{1,0:T(8,128)S(1)}, f32[56,768]{1,0:T(8,128)S(1)}, u32[]{:S(2)}, u32[]{:S(2)}) collective-permute-start(f32[56,768]{1,0:T(8,128)S(1)} %get-tuple-element.39.cargo_ref), channel_id=1, source_target_pairs={{0,2},{2,4},{4,6},{6,8},{8,10},{10,12},{12,14},{1,3},{3,5},{5,7},{... | collective-permute-start | bytes 516104 | tf_op jit(solution)/shard_map/ppermute | solution.py:803
  40.7 0.8 %late.1 = (f32[40,128]{1,0:T(8,128)S(1)}, f32[40,768]{1,0:T(8,128)S(1)}) custom-call(f32[40,128]{1,0:T(8,128)S(1)} %get-tuple-element.37.before_ref, f32[40,768]{1,0:T(8,128)S(1)} %get-tuple-element.33.d1_ref, f32[56,768]{1,0:T(8,128)S(1)} %get-tuple-element.39.cargo_ref, f32[40,768]{1,0:T(8,128)S(1)} %get-tuple-element.40.v1_ref, ...), custom_call_target="tpu_custom_call" | custom-call | flops 1000000000 | bytes 1048576 | tf_op jit(solution)/shard_map/late/pallas_call | solution.py:782
  41.5 3.0 %collective-permute-done.4.left_ref.cargol_ref = f32[56,768]{1,0:T(8,128)S(1)} collective-permute-done((f32[56,768]{1,0:T(8,128)S(1)}, f32[56,768]{1,0:T(8,128)S(1)}, u32[]{:S(2)}, u32[]{:S(2)}) %collective-permute-start.4) | collective-permute-done | bytes 172064 | tf_op jit(solution)/shard_map/ppermute | solution.py:803
  44.5 0.6 third.1
  45.2 13.7 %all_to_all.10.gram_ref = f32[8,40,128]{2,1,0:T(8,128)S(1)} all-to-all(f32[8,40,128]{2,1,0:T(8,128)S(1)} %third.1), channel_id=1, replica_groups=mesh['groups'=2,'pts'=8,'probe'=2] {'pts'}, dimensions={0} | all-to-all | bytes 327680 | tf_op jit(solution)/shard_map/all_to_all | solution.py:907
  58.8 6.6 %final.1 = (f32[16,8,128]{2,1,0:T(8,128)S(1)}, f32[16,768]{1,0:T(8,128)}) custom-call(f32[8,40,128]{2,1,0:T(8,128)S(1)} %all_to_all.10.gram_ref, f32[32,768]{1,0:T(8,128)S(1)} %get-tuple-element.28.own_ref.refs_2_, f32[32,768]{1,0:T(8,128)S(1)} %collective-permute-done.refs_0_.left_ref, f32[40,768]{1,0:T(8,128)S(1)} %get-tuple-element.33.d1_ref, ...), custom_call_target="tpu_custom_call" | custom-call | flops 1000000000 | bytes 1048576 | tf_op jit(solution)/shard_map/final/pallas_call | solution.py:782
  65.5 9.5 %all_to_all.11.parts_ref = f32[16,8,128]{2,1,0:T(8,128)S(1)} all-to-all(f32[16,8,128]{2,1,0:T(8,128)S(1)} %get-tuple-element.48), channel_id=1, replica_groups=mesh['groups'=2,'pts'=8,'probe'=2] {'pts','probe'}, dimensions={0} | all-to-all | bytes 131072 | tf_op jit(solution)/shard_map/all_to_all | solution.py:918
  74.9 0.7 tail.1
Async XLA Ops:
  12.7 8.4 %collective-permute-start.1 = (f32[32,768]{1,0:T(8,128)S(1)}, f32[32,768]{1,0:T(8,128)S(1)}, u32[]{:S(2)}, u32[]{:S(2)}) collective-permute-start(f32[32,768]{1,0:T(8,128)S(1)} %get-tuple-element.28.own_ref.refs_2_), channel_id=1, source_target_pairs={{2,0},{4,2},{6,4},{8,6},{10,8},{12,10},{14,12},{3,1},{5,3},{7,5},{... | collective-permute-start | bytes 294920 | tf_op jit(solution)/shard_map/ppermute | solution.py:798
  14.0 8.6 %collective-permute-start = (f32[32,768]{1,0:T(8,128)S(1)}, f32[32,768]{1,0:T(8,128)S(1)}, u32[]{:S(2)}, u32[]{:S(2)}) collective-permute-start(f32[32,768]{1,0:T(8,128)S(1)} %get-tuple-element.28.own_ref.refs_2_), channel_id=1, source_target_pairs={{0,2},{2,4},{4,6},{6,8},{8,10},{10,12},{12,14},{1,3},{3,5},{5,7},{... | collective-permute-start | bytes 294920 | tf_op jit(solution)/shard_map/ppermute | solution.py:798
  24.0 7.2 %copy-start = (f32[16,768]{1,0:T(8,128)S(1)}, f32[16,768]{1,0:T(8,128)}, u32[]{:S(2)}) copy-start(f32[16,768]{1,0:T(8,128)} %sys_ref.3) | copy-start | bytes 147460
  24.9 7.8 %collective-permute-start.3 = (f32[40,768]{1,0:T(8,128)S(1)}, f32[40,768]{1,0:T(8,128)S(1)}, u32[]{:S(2)}, u32[]{:S(2)}) collective-permute-start(f32[40,768]{1,0:T(8,128)S(1)} %get-tuple-element.33.d1_ref), channel_id=1, source_target_pairs={{2,0},{4,2},{6,4},{8,6},{10,8},{12,10},{14,12},{3,1},{5,3},{7,5},{... | collective-permute-start | bytes 368648 | tf_op jit(solution)/shard_map/ppermute | solution.py:798
  26.2 9.3 %collective-permute-start.2 = (f32[40,768]{1,0:T(8,128)S(1)}, f32[40,768]{1,0:T(8,128)S(1)}, u32[]{:S(2)}, u32[]{:S(2)}) collective-permute-start(f32[40,768]{1,0:T(8,128)S(1)} %get-tuple-element.33.d1_ref), channel_id=1, source_target_pairs={{0,2},{2,4},{4,6},{6,8},{8,10},{10,12},{12,14},{1,3},{3,5},{5,7},{... | collective-permute-start | bytes 368648 | tf_op jit(solution)/shard_map/ppermute | solution.py:798
  36.3 8.2 %collective-permute-start.4 = (f32[56,768]{1,0:T(8,128)S(1)}, f32[56,768]{1,0:T(8,128)S(1)}, u32[]{:S(2)}, u32[]{:S(2)}) collective-permute-start(f32[56,768]{1,0:T(8,128)S(1)} %get-tuple-element.39.cargo_ref), channel_id=1, source_target_pairs={{0,2},{2,4},{4,6},{6,8},{8,10},{10,12},{12,14},{1,3},{3,5},{5,7},{... | collective-permute-start | bytes 516104 | tf_op jit(solution)/shard_map/ppermute | solution.py:803
